TPU v7x, 512 devices: a whole 4x4x16 slice. The times are simulated.
512 devices in a mesh: enc: 16 (over x_hi, y, core), dp: 32 (over z, x_lo).
Axes of the slice: x: 4 (x_hi: 2, x_lo: 2; x = x_hi * 2 + x_lo), y: 4, z: 16, core: 2. Of those that a mesh axis runs over, the one named last changes fastest.
Arguments:
- mel: bfloat16 [8192, 16, 128], P(('enc', 'dp')), may hold values from -6 to 6
- lengths: int32 [8192], P(('enc', 'dp')), may hold values from 1 to 16
- routes: int32 [8192, 1], P(('enc', 'dp')), may hold values from 0 to 15; in each aligned block of 16 rows (0 to 15, 16 to 31, ...) at most 2 rows name the same one
- conv1_weight: bfloat16 [384, 1280], replicated, may hold values from -0.3125 to 0.3125
- conv1_bias: float32 [1280], replicated, may hold values from -3 to 3
- conv2_weight: bfloat16 [1280, 1920], P('enc'), may hold values from -0.09375 to 0.09375
- conv2_bias: float32 [640], replicated, may hold values from -3 to 3
- out_grad: bfloat16 [8192, 8, 640], P(('enc', 'dp')), may hold values from -6 to 6
Outputs:
- packed_features: bfloat16 [16384, 8, 640], P(('enc', 'dp'))
- grad_conv1_weight: float32 [384, 1280], replicated
- grad_conv1_bias: float32 [1280], replicated
- grad_conv2_bias: float32 [640], replicated
- grad_conv2_weight: float32 [1280, 1920], P('enc')
Inputs may be any that keep to these rules, and one draw needn't show every extreme that they name: `routes`: among the clips of one device at most 2 name the same owner.
All inputs are finite; a program needn't handle non-finite values.
Results may differ from a plain program's by a relative error of at most 0.007.
Values may be sent and summed in bfloat16 or wider, within the bound.
No kernel may reach another device: no remote copies, remote signals or barrier semaphores. Data moves between devices by JAX's collectives and lax.ppermute only.
A program may use at most 128 MiB of HBM per device.

v0:
```python
import jax
import jax.numpy as jnp
from jax import lax
from jax.sharding import PartitionSpec as P

inv_root_two = 0.7071067811865476
inv_root_tau = 0.3989422804014327


def gelu_value(values):
    return 0.5 * values * (1.0 + lax.erf(values * inv_root_two))


def gelu_slope(values):
    return (
        0.5 * (1.0 + lax.erf(values * inv_root_two))
        + values * jnp.exp(-0.5 * values * values) * inv_root_tau
    )


def grad_to_act(second_grad, weight):
    clip_count, half_frames, out_width = second_grad.shape
    flat = second_grad.reshape(clip_count * half_frames, out_width)
    numbers = (((1,), (1,)), ((), ()))
    width = weight.shape[0]
    even_part = lax.dot_general(
        flat, weight[:, out_width : 2 * out_width], numbers, preferred_element_type=jnp.float32
    )
    odd_part = lax.dot_general(
        flat, weight[:, 2 * out_width :], numbers, preferred_element_type=jnp.float32
    )
    from_next = lax.dot_general(
        flat, weight[:, :out_width], numbers, preferred_element_type=jnp.float32
    )
    from_next = jnp.pad(
        from_next.reshape(clip_count, half_frames, width)[:, 1:], ((0, 0), (0, 1), (0, 0))
    )
    odd_part = odd_part.reshape(clip_count, half_frames, width) + from_next
    even_part = even_part.reshape(clip_count, half_frames, width)
    return jnp.stack([even_part, odd_part], axis=2).reshape(clip_count * half_frames * 2, width)


def stem_block(mel, length_f, out_grad, first_weight, first_bias, second_bias, project, backward):
    clip_count, frames, mel_bins = mel.shape
    half_frames = frames // 2
    out_width = second_bias.shape[0]
    live_first = jnp.arange(frames, dtype=jnp.float32)[None, :] < length_f[:, None]
    masked = jnp.where(live_first[:, :, None], mel, jnp.zeros_like(mel))
    padded = jnp.pad(masked, ((0, 0), (1, 1), (0, 0)))
    columns = jnp.concatenate(
        [padded[:, :frames], padded[:, 1 : frames + 1], padded[:, 2:]], axis=2
    )
    columns = columns.reshape(clip_count * frames, 3 * mel_bins)
    live_rows = live_first.reshape(clip_count * frames, 1).astype(jnp.float32)
    first_pre = jnp.dot(columns, first_weight, preferred_element_type=jnp.float32) + first_bias
    first_act = (gelu_value(first_pre) * live_rows).astype(jnp.bfloat16)
    taps_out = project(first_act).reshape(clip_count, half_frames, 2, 3, out_width)
    earlier = jnp.pad(taps_out[:, :-1, 1, 0], ((0, 0), (1, 0), (0, 0)))
    second_pre = earlier + taps_out[:, :, 0, 1] + taps_out[:, :, 1, 2] + second_bias
    live_second = (
        2.0 * jnp.arange(half_frames, dtype=jnp.float32)[None, :] < length_f[:, None]
    ).astype(jnp.float32)[:, :, None]
    features = (gelu_value(second_pre) * live_second).astype(jnp.bfloat16)
    second_grad = (out_grad.astype(jnp.float32) * gelu_slope(second_pre) * live_second).astype(
        jnp.bfloat16
    )
    act_grad = backward(second_grad)
    first_grad = (act_grad * gelu_slope(first_pre) * live_rows).astype(jnp.bfloat16)
    weight_grad = lax.dot_general(
        columns, first_grad, (((0,), (0,)), ((), ())), preferred_element_type=jnp.float32
    )
    bias_grad = jnp.sum(first_grad.astype(jnp.float32), axis=0)
    second_bias_grad = jnp.sum(second_grad.astype(jnp.float32), axis=(0, 1))
    return (features, weight_grad, bias_grad, second_bias_grad, first_act, second_grad)


def local(mel, lengths, routes, conv1_weight, conv1_bias, conv2_weight, conv2_bias, out_grad):
    clip_count, frames, mel_bins = mel.shape
    half_frames = frames // 2
    out_width = conv2_bias.shape[0]
    owners = lax.axis_size("enc")
    slot_count = 2 * clip_count // owners
    owner_of = routes[:, 0]
    owner_hits = (owner_of[:, None] == jnp.arange(owners, dtype=jnp.int32)[None, :]).astype(
        jnp.int32
    )
    slot_rank = jnp.sum((jnp.cumsum(owner_hits, axis=0) - owner_hits) * owner_hits, axis=1)
    slot_of = owner_of * slot_count + slot_rank
    placing = (
        jnp.arange(owners * slot_count, dtype=jnp.int32)[:, None] == slot_of[None, :]
    ).astype(jnp.bfloat16)
    whole_weight = lax.all_gather(conv2_weight, "enc", axis=0, tiled=True)

    def project(first_act):
        return jnp.dot(first_act, whole_weight, preferred_element_type=jnp.float32)

    def backward(second_grad):
        return grad_to_act(second_grad, whole_weight)

    send_mel = jnp.dot(
        placing, mel.reshape(clip_count, frames * mel_bins), preferred_element_type=jnp.float32
    ).astype(jnp.bfloat16)
    send_grad = jnp.dot(
        placing,
        out_grad.reshape(clip_count, half_frames * out_width),
        preferred_element_type=jnp.float32,
    ).astype(jnp.bfloat16)
    send_length = jnp.dot(
        placing, lengths.astype(jnp.bfloat16)[:, None], preferred_element_type=jnp.float32
    ).astype(jnp.bfloat16)
    got_mel, got_grad, got_length = (
        lax.all_to_all(send_mel, "enc", split_axis=0, concat_axis=0, tiled=True),
        lax.all_to_all(send_grad, "enc", split_axis=0, concat_axis=0, tiled=True),
        lax.all_to_all(send_length, "enc", split_axis=0, concat_axis=0, tiled=True),
    )
    slot_total = got_mel.shape[0]
    packed, weight_grad, bias_grad, second_bias_grad, first_act, second_grad = stem_block(
        got_mel.reshape(slot_total, frames, mel_bins),
        got_length[:, 0].astype(jnp.float32),
        got_grad.reshape(slot_total, half_frames, out_width),
        conv1_weight,
        conv1_bias,
        conv2_bias,
        project,
        backward,
    )
    act_parts = lax.all_to_all(first_act, "enc", split_axis=1, concat_axis=0, tiled=True)
    numbers = (((0,), (0,)), ((), ()))
    grad_piece = lax.all_gather(second_grad, "enc", axis=0, tiled=True)
    piece_clips = grad_piece.shape[0]
    width = act_parts.shape[1]
    act_pairs = act_parts.reshape(piece_clips, half_frames, 2, width)
    even_act = act_pairs[:, :, 0].reshape(piece_clips * half_frames, width)
    odd_here = act_pairs[:, :, 1]
    odd_act = odd_here.reshape(piece_clips * half_frames, width)
    prior_act = jnp.pad(odd_here[:, :-1], ((0, 0), (1, 0), (0, 0))).reshape(
        piece_clips * half_frames, width
    )
    flat_grad = grad_piece.reshape(piece_clips * half_frames, grad_piece.shape[2])
    tap_zero = lax.dot_general(prior_act, flat_grad, numbers, preferred_element_type=jnp.float32)
    tap_one = lax.dot_general(even_act, flat_grad, numbers, preferred_element_type=jnp.float32)
    tap_two = lax.dot_general(odd_act, flat_grad, numbers, preferred_element_type=jnp.float32)
    conv2_rows_grad = jnp.concatenate([tap_zero, tap_one, tap_two], axis=1)
    weight_grad, bias_grad, second_bias_grad = lax.psum(
        (weight_grad, bias_grad, second_bias_grad), ("enc", "dp")
    )
    conv2_rows_grad = lax.psum(conv2_rows_grad, "dp")
    return (packed, weight_grad, bias_grad, second_bias_grad, conv2_rows_grad)


def solution(mesh):
    placed = (
        P(("enc", "dp"), None, None),
        P(("enc", "dp")),
        P(("enc", "dp"), None),
        P(),
        P(),
        P("enc", None),
        P(),
        P(("enc", "dp"), None, None),
    )
    return jax.shard_map(
        local,
        mesh=mesh,
        in_specs=placed,
        out_specs=(P(("enc", "dp"), None, None), P(), P(), P(), P("enc", None)),
        check_vma=False,
    )
```

profile of v0, /device:TPU:4, one launch (start us, length us, event | category | flops | bytes accessed | tf_op | source)
XLA Modules:
  0.0 942.8 jit_solution(10839624494853902295)
XLA Ops:
  7.2 0.7 all-gather.3.cloned.1.call-update
  7.9 0.7 fusion.35
  8.7 0.8 select_reduce_fusion
  9.5 0.7 multiply_add_fusion
  10.2 0.8 fusion.15
  11.0 0.7 all_to_all.39
  11.7 9.2 all-to-all-start
  20.9 1.0 convolution_convert_fusion.1
  21.9 0.8 all_to_all.32
  22.6 0.9 copy.57
  23.8 0.8 all_to_all.34
  24.7 0.8 all-to-all-done
  25.5 6.4 all-to-all-start.1
  32.3 5.0 all-to-all-done.1
  37.2 6.4 all-to-all-start.2
  44.0 0.7 copy-done.5
  44.8 2.2 multiply_convert_fusion
  47.0 4.1 all-to-all-done.2
  51.2 36.6 %all-gather.3.cloned.1.call-done = bf16[1280,1920]{1,0:T(8,128)(2,1)} async-done(((bf16[80,1920]{1,0:T(8,128)(2,1)}), bf16[1280,1920]{1,0:T(8,128)(2,1)}) %all-gather.3.cloned.1.call-update) | async-done | bytes 4915216 | tf_op jit(solution)/shard_map/all_gather | solution.py:92
  87.8 7.2 fusion.43
  95.0 6.9 reshape.158
  101.9 3.9 fusion.41
  105.8 2.1 slice.50
  107.9 1.4 convert_reduce_fusion.1
  109.4 1.6 copy.44
  111.0 27.6 %all_to_all.44 = bf16[512,16,80]{0,2,1:T(8,128)(2,1)} all-to-all(bf16[512,16,80]{0,2,1:T(8,128)(2,1)S(1)} %bitcast.80), channel_id=1, replica_groups=mesh['enc'=16,'dp'=32] {'enc'}, dimensions={1} | all-to-all | bytes 2621440 | tf_op jit(solution)/shard_map/all_to_all | solution.py:127
  138.6 2.9 copy.45
  141.5 4.2 fusion.42
  145.6 5.7 copy.54
  151.5 2.1 convolution_bitcast_fusion
  153.6 2.3 fusion.14
  155.9 2.2 fusion.6
  158.3 3.6 copy.43
  161.9 4.5 reshape.160
  166.4 3.3 convert_reduce_fusion
  169.7 2.0 fusion.44
  172.0 13.4 %all-gather.5.cloned.1.call-done = bf16[512,8,640]{2,0,1:T(8,128)(2,1)} async-done(((bf16[32,8,640]{2,0,1:T(8,128)(2,1)}), bf16[512,8,640]{2,0,1:T(8,128)(2,1)}) %all-gather.5.cloned.1.call-update) | async-done | bytes 5242896 | tf_op jit(solution)/shard_map/all_gather | solution.py:129
  185.4 5.9 fusion
  191.3 1.0 convolution_bitcast_fusion.1
  192.4 0.5 copy-done.7
  192.9 3.2 fusion.2
  196.1 0.9 pad_maximum_fusion.1
  197.0 0.8 copy.49
  197.9 105.2 %all-reduce.4 = (f32[1280]{0:T(1024)}, f32[640]{0:T(1024)}) all-reduce(f32[1280]{0:T(1024)S(1)} %get-tuple-element.24, f32[640]{0:T(1024)S(1)} %get-tuple-element.22), channel_id=1, replica_groups=mesh['enc'=16,'dp'=32] {'enc','dp'}, use_global_device_ids=true, to_apply=%region_4.5 | all-reduce | flops 1920 | bytes 15360 | tf_op jit(solution)/shard_map/psum | solution.py:144
  303.1 366.1 %all-reduce.8.cloned.1.call-done = f32[384,1280]{1,0:T(8,128)} async-done(((f32[384,1280]{1,0:T(8,128)}), f32[384,1280]{1,0:T(8,128)}) %all-reduce.8.cloned.1.call-update) | async-done | bytes 1966096 | tf_op jit(solution)/shard_map/psum | solution.py:144
  669.1 263.3 %all-reduce.10.cloned.1.call-done = f32[80,1920]{1,0:T(8,128)} async-done(((f32[80,1920]{1,0:T(8,128)}), f32[80,1920]{1,0:T(8,128)}) %all-reduce.10.cloned.1.call-update) | async-done | bytes 614416 | tf_op jit(solution)/shard_map/psum | solution.py:147
  932.4 3.0 copy.106
  935.4 0.8 copy.107
  (47 shorter events, 1.9 us)
Async XLA Ops:
  7.2 37.6 %copy-start = (bf16[384,1280]{1,0:T(8,128)(2,1)S(1)}, bf16[384,1280]{1,0:T(8,128)(2,1)}, u32[]{:S(2)}) copy-start(bf16[384,1280]{1,0:T(8,128)(2,1)} %param.11) | copy-start | bytes 2949124
  7.2 37.6 %copy-start.12 = (f32[1280]{0:T(1024)S(1)}, f32[1280]{0:T(1024)}, u32[]{:S(2)}) copy-start(f32[1280]{0:T(1024)} %param.12) | copy-start | bytes 15364
  7.2 80.6 %all-gather.3.cloned.1.call-start = ((), (), s32[]{:S(2)}) async-start(), calls=%async_computation.4 | async-start | bytes 5222400 | tf_op jit(solution)/shard_map/all_gather | solution.py:92
  11.7 13.8 %all-to-all-start = ((bf16[16,2,1]{1,2,0:T(2,128)(2,1)}), bf16[16,2,1]{1,2,0:T(2,128)(2,1)S(1)}, u32[]{:S(2)}, u32[]{:S(2)}) async-start(bf16[16,2,1]{1,2,0:T(2,128)(2,1)} %all_to_all.39), calls=%async_computation | async-start | bytes 16384 | tf_op jit(solution)/shard_map/all_to_all | solution.py:114
  25.5 11.7 %all-to-all-start.1 = ((bf16[16,2,2048]{2,1,0:T(2,128)(2,1)}), bf16[16,2,2048]{2,1,0:T(2,128)(2,1)S(1)}, u32[]{:S(2)}, u32[]{:S(2)}) async-start(bf16[16,2,2048]{2,1,0:T(2,128)(2,1)} %all_to_all.32), calls=%async_computation.1 | async-start | bytes 262144 | tf_op jit(solution)/shard_map/all_to_all | solution.py:112
  37.2 13.8 %all-to-all-start.2 = ((bf16[16,2,5120]{2,1,0:T(2,128)(2,1)}), bf16[16,2,5120]{2,1,0:T(2,128)(2,1)S(1)}, u32[]{:S(2)}, u32[]{:S(2)}) async-start(bf16[16,2,5120]{2,1,0:T(2,128)(2,1)} %all_to_all.34), calls=%async_computation.2 | async-start | bytes 655360 | tf_op jit(solution)/shard_map/all_to_all | solution.py:113
  43.6 141.8 %all-gather.5.cloned.1.call-start = ((), (), s32[]{:S(2)}) async-start(), calls=%async_computation.6 | async-start | bytes 5570560 | tf_op jit(solution)/shard_map/all_gather | solution.py:129
  44.0 0.7 copy-start.5
  47.0 48.0 %copy-start.9 = (bf16[512,1280]{1,0:T(8,128)(2,1)}, bf16[512,1280]{1,0:T(8,128)(2,1)S(1)}, u32[]{:S(2)}) copy-start(bf16[512,1280]{1,0:T(8,128)(2,1)S(1)} %get-tuple-element.35) | copy-start | bytes 3932164
  101.9 6.0 copy-start.11
  109.4 559.8 %all-reduce.8.cloned.1.call-start = ((), (), s32[]{:S(2)}) async-start(), calls=%async_computation.5 | async-start | bytes 3932160 | tf_op jit(solution)/shard_map/psum | solution.py:144
  145.6 5.7 copy-start.2
  166.4 3.3 copy-start.6
  169.7 15.7 %copy-start.1 = (bf16[512,8,1,80]{3,2,1,0:T(2,128)(2,1)S(1)}, bf16[512,8,1,80]{3,2,1,0:T(2,128)(2,1)}, u32[]{:S(2)}) copy-start(bf16[512,8,1,80]{3,2,1,0:T(2,128)(2,1)} %get-tuple-element.29) | copy-start | bytes 1966084
  171.7 760.7 %all-reduce.10.cloned.1.call-start = ((), (), s32[]{:S(2)}) async-start(), calls=%async_computation.7 | async-start | bytes 1228800 | tf_op jit(solution)/shard_map/psum | solution.py:147
  185.4 5.9 copy-start.3
  185.4 5.9 copy-start.4
  191.3 1.6 copy-start.7
  192.9 4.1 copy-start.8
  932.4 3.0 copy-start.10
Sparse Core Ops, SparseCore 0:
  11.3 76.4 all-gather.2
  109.5 75.8 all-gather.4
  191.2 477.8 all-reduce.7
  672.5 259.8 all-reduce.9
where the time goes:
time: 944 us; the launch traced here: 943 us
  waiting for transfers between devices  690 us (73%)
  blocking collectives  133 us (14%)
  local copies, waits for them, and re-layouts  45.2 us (5%)
  matrix products  30.2 us (3%)
  starting transfers between devices  22.3 us (2%)
  between operations  14 us (1%)
    psum x1, waiting for transfers between devices, local(): lax.psum((weight_grad, bias_grad, second_bias_grad), ('enc', 'dp'))  366 us
    psum x1, waiting for transfers between devices, local(): conv2_rows_grad = lax.psum(conv2_rows_grad, 'dp')  263 us
    psum x1, blocking collectives, local(): lax.psum((weight_grad, bias_grad, second_bias_grad), ('enc', 'dp'))  105 us
    all_gather x1, waiting for transfers between devices, local(): whole_weight = lax.all_gather(conv2_weight, 'enc', axis=0, tiled=True)  36.6 us
    all_to_all x1, blocking collectives, local(): lax.all_to_all(first_act, 'enc', split_axis=1, concat_axis=0, tiled=True)  27.6 us
  transfers between devices with their start and end apart: 7, of which 7 were waited for; matrix products, arithmetic and copies ran while one was open for 6% of the time, Pallas kernels for 0%

commit v1 on v0

v1 whole, which is shorter than its diff:
```python
import functools

import jax
import jax.numpy as jnp
from jax import lax
from jax.experimental import pallas as pl
from jax.experimental.pallas import tpu as pltpu
from jax.sharding import Mesh
from jax.sharding import PartitionSpec as P

inv_root_two = 0.7071067811865476
inv_root_tau = 0.3989422804014327

MEL = 128
D2 = 640
ROWS = 80
LANES = 128
CHIPS = 8
CLIPS = 16
HALF = 8
STEPS = CLIPS * HALF
SLOTS = 2 * CLIPS
PACK = 1536
TILES = 19
VMEM = 56 * 1024 * 1024
ALL_AXES = ("xh", "y", "c", "z", "xl")
ENC = ("xh", "y", "c")
CHIP = ("xh", "y")
F32 = jnp.float32
BF16 = jnp.bfloat16


def gelu_both(values):
    cdf = 0.5 * (1.0 + lax.erf(values * inv_root_two))
    return values * cdf, cdf + values * jnp.exp(-0.5 * values * values) * inv_root_tau


def shift_down(values):
    rows, width = values.shape
    t = lax.broadcasted_iota(jnp.int32, (rows, width), 0) & (HALF - 1)
    clips = values.reshape(rows // HALF, HALF, width)
    moved = pltpu.roll(clips, 1, 1).reshape(rows, width)
    return jnp.where(t == 0, 0.0, moved)


def shift_up(values):
    rows, width = values.shape
    t = lax.broadcasted_iota(jnp.int32, (rows, width), 0) & (HALF - 1)
    clips = values.reshape(rows // HALF, HALF, width)
    moved = pltpu.roll(clips, HALF - 1, 1).reshape(rows, width)
    return jnp.where(t == HALF - 1, 0.0, moved)


def dot(left, right):
    return jnp.dot(left, right, preferred_element_type=F32)


def dot_nt(left, right):
    return lax.dot_general(left, right, (((1,), (1,)), ((), ())), preferred_element_type=F32)


def dot_tn(left, right):
    return lax.dot_general(left, right, (((0,), (0,)), ((), ())), preferred_element_type=F32)


def forward_kernel(pay_ref, w1_ref, b1_ref, w2_ref, part_ref, cols_ref, act_ref, slope_ref):
    spread = (
        lax.broadcasted_iota(jnp.int32, (STEPS, CLIPS), 0) >> 3
        == lax.broadcasted_iota(jnp.int32, (STEPS, CLIPS), 1)
    ).astype(F32).astype(BF16)
    length = dot(spread, pay_ref[0, STEPS : STEPS + CLIPS, :LANES])
    t = (lax.broadcasted_iota(jnp.int32, (STEPS, LANES), 0) & (HALF - 1)).astype(F32)
    live_even, live_odd = 2.0 * t < length, 2.0 * t + 1.0 < length
    even = jnp.where(live_even, pay_ref[0, :STEPS, :LANES].astype(F32), 0.0)
    odd = jnp.where(live_odd, pay_ref[0, :STEPS, LANES:].astype(F32), 0.0)
    cols_ref[0, :, :LANES] = shift_down(odd).astype(BF16)
    cols_ref[0, :, LANES : 2 * LANES] = even.astype(BF16)
    cols_ref[0, :, 2 * LANES : 3 * LANES] = odd.astype(BF16)
    cols_ref[0, :, 3 * LANES :] = shift_up(even).astype(BF16)
    bias = b1_ref[...]
    mask_even = jnp.where(live_even, 1.0, 0.0)
    mask_odd = jnp.where(live_odd, 1.0, 0.0)
    mask_even = jnp.concatenate([mask_even, mask_even], axis=1)
    mask_odd = jnp.concatenate([mask_odd, mask_odd], axis=1)
    act, slope = gelu_both(dot(cols_ref[0, :, : 3 * LANES], w1_ref[...]) + bias)
    act_even = (act * mask_even).astype(BF16)
    slope_ref[0, 0] = slope * mask_even
    act, slope = gelu_both(dot(cols_ref[0, :, LANES:], w1_ref[...]) + bias)
    act = act * mask_odd
    act_odd = act.astype(BF16)
    slope_ref[0, 1] = slope * mask_odd
    act_prior = shift_down(act).astype(BF16)
    act_ref[0, 0] = act_prior
    act_ref[0, 1] = act_even
    act_ref[0, 2] = act_odd
    total = dot(act_prior, w2_ref[:, :D2])
    total = total + dot(act_even, w2_ref[:, D2 : 2 * D2])
    total = total + dot(act_odd, w2_ref[:, 2 * D2 :])
    part_ref[0] = total.astype(BF16)


def middle_kernel(part_ref, grad_ref, b2_ref, length_ref, owner_col_ref, owner_row_ref, rep_ref, placed_ref):
    pre = part_ref[0].astype(F32)
    for source in range(1, CHIPS):
        pre = pre + part_ref[source].astype(F32)
    pre = pre + b2_ref[...]
    t = (lax.broadcasted_iota(jnp.int32, (STEPS, 1), 0) & (HALF - 1)).astype(F32)
    live = jnp.where(2.0 * t < length_ref[...], 1.0, 0.0)
    value, slope = gelu_both(pre)
    features = (value * live).astype(BF16)
    second_grad = (grad_ref[...].astype(F32) * slope * live).astype(BF16)
    for target in range(CHIPS):
        rep_ref[target] = second_grad
    here = lax.broadcasted_iota(jnp.int32, (STEPS, STEPS), 0)
    there = lax.broadcasted_iota(jnp.int32, (STEPS, STEPS), 1)
    same = (owner_col_ref[...] == owner_row_ref[...]) & ((here >> 3) < (there >> 3))
    same = same & ((here & (HALF - 1)) == 0)
    rank = jnp.sum(jnp.where(same, 1.0, 0.0), axis=0, keepdims=True).astype(jnp.int32)
    place = lax.broadcasted_iota(jnp.int32, (1, STEPS), 1) & (HALF - 1)
    place = (owner_row_ref[...] * 2 + rank) * HALF + place
    wanted = lax.broadcasted_iota(jnp.int32, (SLOTS * HALF, STEPS), 0) == place
    placed_ref[...] = dot(jnp.where(wanted, 1.0, 0.0).astype(BF16), features).astype(BF16)


def backward_kernel(
    where_ref, grad_ref, w2_ref, cols_ref, act_ref, slope_ref, pack_ref,
    conv2_sum, conv1_sum, bias1_sum, bias2_sum, bias2_col,
):
    step = pl.program_id(0)

    @pl.when(step == 0)
    def _():
        conv2_sum[...] = jnp.zeros_like(conv2_sum)
        conv1_sum[...] = jnp.zeros_like(conv1_sum)
        bias1_sum[...] = jnp.zeros_like(bias1_sum)
        bias2_sum[...] = jnp.zeros_like(bias2_sum)

    rows = 2 * STEPS
    grad = grad_ref[...].reshape(rows, D2)
    bias2_sum[...] += jnp.sum(grad.astype(F32), axis=0, keepdims=True)
    even = dot_nt(grad, w2_ref[:, D2 : 2 * D2])
    odd = dot_nt(grad, w2_ref[:, 2 * D2 :]) + shift_up(dot_nt(grad, w2_ref[:, :D2]))
    even = (even * slope_ref[:, 0].reshape(rows, 2 * LANES)).astype(BF16)
    odd = (odd * slope_ref[:, 1].reshape(rows, 2 * LANES)).astype(BF16)
    cols = cols_ref[...].reshape(rows, 4 * LANES)
    conv1_sum[...] += dot_tn(even, cols[:, : 3 * LANES]) + dot_tn(odd, cols[:, LANES:])
    ones = jnp.ones((rows, LANES), BF16)
    bias1_sum[...] += dot_tn(even, ones) + dot_tn(odd, ones)
    for tap in range(3):
        conv2_sum[:, tap * D2 : (tap + 1) * D2] += dot_tn(
            act_ref[:, tap].reshape(rows, 2 * LANES), grad
        )

    @pl.when(step == pl.num_programs(0) - 1)
    def _():
        core, place = where_ref[0], where_ref[1]
        for tile in range(D2 // LANES):
            block = bias2_sum[:, tile * LANES : (tile + 1) * LANES]
            bias2_col[tile * LANES : (tile + 1) * LANES, :] = jnp.broadcast_to(block, (LANES, LANES)).T
        lane = lax.broadcasted_iota(jnp.int32, (ROWS, LANES), 1)
        for side in range(2):
            target = core if side == 0 else 1 - core
            first = side * LANES
            for tile in range(15):
                block = conv2_sum[first : first + ROWS, tile * LANES : (tile + 1) * LANES]
                pack_ref[target, tile * ROWS : (tile + 1) * ROWS, :] = block.astype(BF16)
            for tile in range(3):
                block = conv1_sum[first : first + ROWS, tile * LANES : (tile + 1) * LANES]
                pack_ref[target, (15 + tile) * ROWS : (16 + tile) * ROWS, :] = block.astype(BF16)
            holder = 2 * place + target
            start = pl.multiple_of(jnp.minimum(holder, CHIPS - 1) * ROWS, 16)
            second = jnp.where(holder < CHIPS, bias2_col[pl.ds(start, ROWS), :], 0.0)
            block = jnp.where(lane == 0, bias1_sum[first : first + ROWS, :], jnp.where(lane == 1, second, 0.0))
            pack_ref[target, 18 * ROWS : 19 * ROWS, :] = block.astype(BF16)
            pack_ref[target, 19 * ROWS :, :] = jnp.zeros((PACK - 19 * ROWS, LANES), BF16)


def unpack_kernel(pack_ref, out_ref):
    for tile in range(15):
        out_ref[:, tile * LANES : (tile + 1) * LANES] = pack_ref[tile * ROWS : (tile + 1) * ROWS, :].astype(F32)


def last_kernel(got_ref, weight_ref, bias1_ref, bias2_ref, whole):
    for tile in range(4):
        for source in range(16):
            whole[source * ROWS : (source + 1) * ROWS, :] = got_ref[
                source, tile * ROWS : (tile + 1) * ROWS, :
            ].astype(F32)
        for block in range(10):
            turned = whole[block * LANES : (block + 1) * LANES, :].T
            if tile < 3:
                weight_ref[tile * LANES : (tile + 1) * LANES, block * LANES : (block + 1) * LANES] = turned
            else:
                bias1_ref[:, block * LANES : (block + 1) * LANES] = turned[0:1, :]
                if block < D2 // LANES:
                    bias2_ref[:, block * LANES : (block + 1) * LANES] = turned[1:2, :]


def exchange(values, axes):
    return lax.all_to_all(values, axes, split_axis=0, concat_axis=0, tiled=True)


def spread_to(values, count):
    return jnp.broadcast_to(values[None], (count,) + values.shape)


def vmem():
    return pl.BlockSpec(memory_space=pltpu.VMEM)


def params(*semantics):
    return pltpu.CompilerParams(vmem_limit_bytes=VMEM, dimension_semantics=semantics or None)


def local(mel, lengths, routes, conv1_weight, conv1_bias, conv2_weight, conv2_bias, out_grad):
    core = lax.axis_index("c")
    chip = lax.axis_index(CHIP)
    place = 2 * chip + core

    def shape(*dims, dtype=BF16):
        return jax.ShapeDtypeStruct(dims, dtype)

    other_weight = lax.ppermute(conv2_weight, "c", [(0, 1), (1, 0)])
    lengths_bf = lengths.astype(BF16)
    pay = jnp.concatenate(
        [mel.reshape(STEPS, 2 * MEL), jnp.broadcast_to(lengths_bf[:, None], (CLIPS, 2 * MEL))], axis=0
    )
    pay_rows = pay.shape[0]
    got_pay = exchange(spread_to(pay, CHIPS), CHIP)

    def side(index):
        weight = lax.dynamic_slice(conv1_weight, (0, index * ROWS), (3 * MEL, ROWS))
        bias = lax.dynamic_slice(conv1_bias, (index * ROWS,), (ROWS,))
        return jnp.pad(weight, ((0, 0), (0, LANES - ROWS))), jnp.pad(bias, (0, LANES - ROWS))

    own_w1, own_b1 = side(place)
    other_w1, other_b1 = side(2 * chip + 1 - core)
    w1 = jnp.concatenate([own_w1, other_w1], axis=1)
    b1 = jnp.concatenate([own_b1, other_b1])[None]
    gap = jnp.zeros((LANES - ROWS, 3 * D2), BF16)
    w2 = jnp.concatenate([conv2_weight, gap, other_weight, gap], axis=0)

    wide = 2 * LANES
    parts, cols, acts, slopes = pl.pallas_call(
        forward_kernel,
        grid=(CHIPS,),
        in_specs=[
            pl.BlockSpec((1, pay_rows, 2 * MEL), lambda i: (i, 0, 0)),
            pl.BlockSpec((3 * MEL, wide), lambda i: (0, 0)),
            pl.BlockSpec((1, wide), lambda i: (0, 0)),
            pl.BlockSpec((wide, 3 * D2), lambda i: (0, 0)),
        ],
        out_specs=[
            pl.BlockSpec((1, STEPS, D2), lambda i: (i, 0, 0)),
            pl.BlockSpec((1, STEPS, 4 * LANES), lambda i: (i, 0, 0)),
            pl.BlockSpec((1, 3, STEPS, wide), lambda i: (i, 0, 0, 0)),
            pl.BlockSpec((1, 2, STEPS, wide), lambda i: (i, 0, 0, 0)),
        ],
        out_shape=[
            shape(CHIPS, STEPS, D2),
            shape(CHIPS, STEPS, 4 * LANES),
            shape(CHIPS, 3, STEPS, wide),
            shape(CHIPS, 2, STEPS, wide, dtype=F32),
        ],
        compiler_params=params("arbitrary"),
        name="stem_forward",
    )(got_pay.reshape(CHIPS, pay_rows, 2 * MEL), w1, b1, w2)

    got_parts = exchange(parts, CHIP)
    owner = jnp.repeat(routes[:, 0], HALF)
    rep, placed = pl.pallas_call(
        middle_kernel,
        in_specs=[vmem()] * 6,
        out_specs=[vmem()] * 2,
        out_shape=[shape(CHIPS, STEPS, D2), shape(SLOTS * HALF, D2)],
        compiler_params=params(),
        name="stem_middle",
    )(
        got_parts,
        out_grad.reshape(STEPS, D2),
        conv2_bias[None],
        jnp.repeat(lengths.astype(F32), HALF)[:, None],
        owner[:, None],
        owner[None],
    )
    got_grad = exchange(rep, CHIP)
    packed = exchange(placed.reshape(16, 2 * HALF, D2), ENC).reshape(SLOTS, HALF, D2)

    pair = lambda i: (i, 0, 0)
    pair4 = lambda i: (i, 0, 0, 0)
    pack = pl.pallas_call(
        backward_kernel,
        grid=(CHIPS // 2,),
        in_specs=[
            pl.BlockSpec(memory_space=pltpu.SMEM),
            pl.BlockSpec((2, STEPS, D2), pair),
            pl.BlockSpec((wide, 3 * D2), lambda i: (0, 0)),
            pl.BlockSpec((2, STEPS, 4 * LANES), pair),
            pl.BlockSpec((2, 3, STEPS, wide), pair4),
            pl.BlockSpec((2, 2, STEPS, wide), pair4),
        ],
        out_specs=pl.BlockSpec((2, PACK, LANES), lambda i: (0, 0, 0)),
        out_shape=shape(2, PACK, LANES),
        scratch_shapes=[
            pltpu.VMEM((wide, 3 * D2), F32),
            pltpu.VMEM((wide, 3 * LANES), F32),
            pltpu.VMEM((wide, LANES), F32),
            pltpu.VMEM((1, D2), F32),
            pltpu.VMEM((D2, LANES), F32),
        ],
        compiler_params=params("arbitrary"),
        name="stem_backward",
    )(jnp.stack([core, chip]).astype(jnp.int32), got_grad, w2, cols, acts, slopes)

    quarters = exchange(pack.reshape(4, PACK // 2, LANES), ("c", "xl"))
    half = jnp.sum(quarters.astype(F32), axis=0).astype(BF16)
    pieces = exchange(half.reshape(16, PACK // 32, LANES), "z")
    piece = jnp.sum(pieces.astype(F32), axis=0).astype(BF16)
    half = exchange(spread_to(piece, 16), "z").reshape(PACK // 2, LANES)
    whole = exchange(spread_to(half, 2), "xl").reshape(PACK, LANES)
    conv2_rows_grad = pl.pallas_call(
        unpack_kernel,
        in_specs=[vmem()],
        out_specs=vmem(),
        out_shape=shape(ROWS, 3 * D2, dtype=F32),
        compiler_params=params(),
        name="conv2_unpack",
    )(whole)
    shares = exchange(spread_to(whole[15 * ROWS : 19 * ROWS], 16), ENC)
    weight_grad, bias_grad, second_bias_grad = pl.pallas_call(
        last_kernel,
        in_specs=[vmem()],
        out_specs=[vmem()] * 3,
        out_shape=[
            shape(3 * MEL, 16 * ROWS, dtype=F32),
            shape(1, 16 * ROWS, dtype=F32),
            shape(1, D2, dtype=F32),
        ],
        scratch_shapes=[pltpu.VMEM((16 * ROWS, LANES), F32)],
        compiler_params=params(),
        name="conv1_unpack",
    )(shares)
    return (packed, weight_grad, bias_grad[0], second_bias_grad[0], conv2_rows_grad)


def solution(mesh):
    fine = Mesh(mesh.devices.reshape(2, 4, 2, 16, 2), ALL_AXES)
    placed = (
        P(ALL_AXES, None, None),
        P(ALL_AXES),
        P(ALL_AXES, None),
        P(),
        P(),
        P(ENC, None),
        P(),
        P(ALL_AXES, None, None),
    )
    return jax.shard_map(
        local,
        mesh=fine,
        in_specs=placed,
        out_specs=(P(ALL_AXES, None, None), P(), P(), P(), P(ENC, None)),
        check_vma=False,
    )
```

time: 944 us -> 218 us (0.23)
  the two profiles are of different devices: /device:TPU:4 before, /device:TPU:1 now
where the time goes in v1:
time: 218 us; the launch traced here: 217 us
  blocking collectives  69.1 us (32%)
  waiting for transfers between devices  65 us (30%)
  starting transfers between devices  37.9 us (17%)
  Pallas kernels  24.7 us (11%)
  local copies, waits for them, and re-layouts  12.7 us (6%)
  other arithmetic  6.53 us (3%)
    all_to_all x4, blocking collectives, exchange(): return lax.all_to_all(values, axes, split_axis=0, concat_axis=0, tiled=True)  69.1 us
    all_to_all x5, waiting for transfers between devices, exchange(): return lax.all_to_all(values, axes, split_axis=0, concat_axis=0, tiled=True)  65 us
    all_to_all x5, starting transfers between devices, exchange(): return lax.all_to_all(values, axes, split_axis=0, concat_axis=0, tiled=True)  29 us
    ppermute x1, starting transfers between devices, local(): other_weight = lax.ppermute(conv2_weight, 'c', [(0, 1), (1, 0)])  8.92 us
    pallas_call x1, Pallas kernels, local(): pl.pallas_call(backward_kernel, grid=(CHIPS // 2,), in_specs=[pl.BlockSpe...  8.7 us
    pallas_call x1, Pallas kernels, local(): pl.pallas_call(forward_kernel, grid=(CHIPS,), in_specs=[pl.BlockSpec((1,...  8.17 us
    unnamed x17, local copies, waits for them, and re-layouts  4.76 us
  transfers between devices with their start and end apart: 6, of which 5 were waited for; matrix products, arithmetic and copies ran while one was open for 5% of the time, Pallas kernels for 1%

profile of v1, /device:TPU:1, one launch (start us, length us, event | category | flops | bytes accessed | tf_op | source)
XLA Modules:
  0.0 216.7 jit_solution(11686051085851625520)
XLA Ops:
  0.6 0.0 copy-start.5
  0.6 8.9 %collective-permute-start = (bf16[80,1920]{1,0:T(8,128)(2,1)}, bf16[80,1920]{1,0:T(8,128)(2,1)S(1)}, u32[]{:S(2)}, u32[]{:S(2)}) collective-permute-start(bf16[80,1920]{1,0:T(8,128)(2,1)} %param.13), channel_id=1, source_target_pairs={{0,32},{32,0},{1,33},{33,1},{2,34},{34,2},{3,35},{35,3},{4,36},{36... | collective-permute-start | bytes 921608 | tf_op jit(solution)/shard_map/ppermute | solution.py:223
  9.6 0.7 fusion.5
  10.3 0.9 reshape.36
  11.2 0.1 pad_maximum_fusion.1
  11.3 0.9 broadcast_in_dim.23
  12.1 3.5 %all-to-all-start = ((bf16[8,144,256]{2,1,0:T(8,128)(2,1)}), bf16[8,144,256]{2,1,0:T(8,128)(2,1)S(1)}, u32[]{:S(2)}, u32[]{:S(2)}) async-start(bf16[8,144,256]{2,1,0:T(8,128)(2,1)} %broadcast_in_dim.23), calls=%async_computation | async-start | bytes 1179648 | tf_op jit(solution)/shard_map/all_to_all | solution.py:200
  15.7 0.9 fusion.4
  16.5 0.6 fusion.3
  17.1 1.1 constant_dynamic-slice_fusion.1
  18.3 0.7 fusion.2.w1_ref
  19.0 0.0 collective-permute-done
  19.0 1.0 pad_maximum_fusion.w2_ref
  20.0 6.4 %all-to-all-done.pay_ref = bf16[8,144,256]{2,1,0:T(8,128)(2,1)S(1)} async-done(((bf16[8,144,256]{2,1,0:T(8,128)(2,1)}), bf16[8,144,256]{2,1,0:T(8,128)(2,1)S(1)}, u32[]{:S(2)}, u32[]{:S(2)}) %all-to-all-start) | async-done | bytes 589856 | tf_op jit(solution)/shard_map/all_to_all | solution.py:200
  26.5 0.8 copy-done.3
  27.3 8.2 %stem_forward.1 = (bf16[8,128,640]{2,1,0:T(8,128)(2,1)}, bf16[8,128,512]{2,1,0:T(8,128)(2,1)}, bf16[8,3,128,256]{3,2,1,0:T(8,128)(2,1)}, f32[8,2,128,256]{3,2,1,0:T(8,128)}) custom-call(bf16[8,144,256]{2,1,0:T(8,128)(2,1)} %copy-done.3, bf16[384,256]{1,0:T(8,128)(2,1)} %fusion.2.w1_ref, f32[1,256]{1,0:T(1,128)} %bitcast.18, ...), custom_call_target="tpu_custom_call" | custom-call | tf_op jit(solution)/shard_map/stem_forward/pallas_call | solution.py:244
  35.5 4.4 %all-to-all-start.1 = ((bf16[8,128,640]{2,1,0:T(8,128)(2,1)}), bf16[8,128,640]{2,1,0:T(8,128)(2,1)S(1)}, u32[]{:S(2)}, u32[]{:S(2)}) async-start(bf16[8,128,640]{2,1,0:T(8,128)(2,1)} %get-tuple-element.14), calls=%async_computation.1 | async-start | bytes 2621440 | tf_op jit(solution)/shard_map/all_to_all | solution.py:200
  39.8 0.1 broadcast_in_dim.52
  39.9 0.7 broadcast_in_dim_reshape.12.owner_row_ref
  40.6 0.7 broadcast_in_dim_reshape.14.owner_col_ref
  41.3 0.0 copy-done.6
  41.3 0.6 broadcast_in_dim.50.b2_ref
  41.9 0.1 broadcast_in_dim.51
  42.0 0.7 broadcast_in_dim_reshape.13.length_ref
  42.7 14.5 %all-to-all-done.1.part_ref = bf16[8,128,640]{2,1,0:T(8,128)(2,1)S(1)} async-done(((bf16[8,128,640]{2,1,0:T(8,128)(2,1)}), bf16[8,128,640]{2,1,0:T(8,128)(2,1)S(1)}, u32[]{:S(2)}, u32[]{:S(2)}) %all-to-all-start.1) | async-done | bytes 1310752 | tf_op jit(solution)/shard_map/all_to_all | solution.py:200
  57.1 1.1 copy-done
  58.2 3.0 %stem_middle.1 = (bf16[8,128,640]{2,1,0:T(8,128)(2,1)}, bf16[256,640]{1,0:T(8,128)(2,1)}) custom-call(bf16[8,128,640]{2,1,0:T(8,128)(2,1)} %copy-done, bf16[128,640]{1,0:T(8,128)(2,1)} %bitcast.17, f32[1,640]{1,0:T(1,128)} %broadcast_in_dim.50.b2_ref, f32[128,1]{1,0:T(8,128)} %broadcast_in_dim_reshape.13.length_ref, ...), custom_call_target="tpu_custom_call" | custom-call | tf_op jit(solution)/shard_map/stem_middle/pallas_call | solution.py:271
  61.2 5.6 %all-to-all-start.3 = ((bf16[8,128,640]{2,1,0:T(8,128)(2,1)}), bf16[8,128,640]{2,1,0:T(8,128)(2,1)S(1)}, u32[]{:S(2)}, u32[]{:S(2)}) async-start(bf16[8,128,640]{2,1,0:T(8,128)(2,1)} %get-tuple-element.16), calls=%async_computation.3 | async-start | bytes 2621440 | tf_op jit(solution)/shard_map/all_to_all | solution.py:200
  66.9 0.6 pad_add_fusion.where_ref
  67.4 16.6 %all-to-all-done.3.grad_ref = bf16[8,128,640]{2,1,0:T(8,128)(2,1)S(1)} async-done(((bf16[8,128,640]{2,1,0:T(8,128)(2,1)}), bf16[8,128,640]{2,1,0:T(8,128)(2,1)S(1)}, u32[]{:S(2)}, u32[]{:S(2)}) %all-to-all-start.3) | async-done | bytes 1310752 | tf_op jit(solution)/shard_map/all_to_all | solution.py:200
  84.1 1.1 copy-done.2
  85.1 8.7 %stem_backward.1 = bf16[2,1536,128]{2,1,0:T(8,128)(2,1)} custom-call(s32[2]{0:T(128)} %pad_add_fusion.where_ref, bf16[8,128,640]{2,1,0:T(8,128)(2,1)} %copy-done.2, bf16[256,1920]{1,0:T(8,128)(2,1)} %pad_maximum_fusion.w2_ref, bf16[8,128,512]{2,1,0:T(8,128)(2,1)} %get-tuple-element.17.cols_ref, bf16[8,3,128,256]{3,2,1,0:T(8,128)(2,1)} %get-tuple-element.18.act_ref, ...), custom_call_target="tpu_custom_call" | custom-call | tf_op jit(solution)/shard_map/stem_backward/pallas_call | solution.py:291
  93.9 15.8 %all_to_all.45 = bf16[4,768,128]{2,1,0:T(8,128)(2,1)S(1)} all-to-all(bf16[4,768,128]{2,1,0:T(8,128)(2,1)} %bitcast.11), channel_id=1, replica_groups=mesh['xh'=2,'y'=4,'c'=2,'z'=16,'xl'=2] {'c','xl'}, dimensions={0} | all-to-all | bytes 1572864 | tf_op jit(solution)/shard_map/all_to_all | solution.py:200
  109.6 0.2 reduce_sum.24
  109.8 24.9 %all_to_all.46 = bf16[16,48,128]{2,1,0:T(8,128)(2,1)S(1)} all-to-all(bf16[16,48,128]{2,1,0:T(8,128)(2,1)S(1)} %bitcast.15), channel_id=1, replica_groups=mesh['xh'=2,'y'=4,'c'=2,'z'=16,'xl'=2] {'z'}, dimensions={0} | all-to-all | bytes 393216 | tf_op jit(solution)/shard_map/all_to_all | solution.py:200
  134.8 21.4 %all_to_all.47 = bf16[16,48,128]{2,1,0:T(8,128)(2,1)S(1)} all-to-all(bf16[16,48,128]{2,1,0:T(8,128)(2,1)S(1)} %broadcast_in_dim.53), channel_id=1, replica_groups=mesh['xh'=2,'y'=4,'c'=2,'z'=16,'xl'=2] {'z'}, dimensions={0} | all-to-all | bytes 393216 | tf_op jit(solution)/shard_map/all_to_all | solution.py:200
  156.1 7.1 %all_to_all.48 = bf16[2,768,128]{2,1,0:T(8,128)(2,1)S(1)} all-to-all(bf16[2,768,128]{2,1,0:T(8,128)(2,1)S(1)} %broadcast_in_dim.55), channel_id=1, replica_groups=mesh['xh'=2,'y'=4,'c'=2,'z'=16,'xl'=2] {'xl'}, dimensions={0} | all-to-all | bytes 786432 | tf_op jit(solution)/shard_map/all_to_all | solution.py:200
  163.3 10.8 %all-to-all-start.2 = ((bf16[16,16,640]{2,1,0:T(8,128)(2,1)}), bf16[16,16,640]{2,1,0:T(8,128)(2,1)S(1)}, u32[]{:S(2)}, u32[]{:S(2)}) async-start(bf16[16,16,640]{2,1,0:T(8,128)(2,1)} %bitcast.3), calls=%async_computation.2 | async-start | bytes 655360 | tf_op jit(solution)/shard_map/all_to_all | solution.py:200
  174.0 9.2 %all-to-all-done.2 = bf16[16,16,640]{2,1,0:T(8,128)(2,1)S(1)} async-done(((bf16[16,16,640]{2,1,0:T(8,128)(2,1)}), bf16[16,16,640]{2,1,0:T(8,128)(2,1)S(1)}, u32[]{:S(2)}, u32[]{:S(2)}) %all-to-all-start.2) | async-done | bytes 327712 | tf_op jit(solution)/shard_map/all_to_all | solution.py:200
  183.2 1.3 broadcast_in_dim.56
  184.5 4.7 %all-to-all-start.8 = ((bf16[16,320,128]{2,1,0:T(8,128)(2,1)}), bf16[16,320,128]{2,1,0:T(8,128)(2,1)S(1)}, u32[]{:S(2)}, u32[]{:S(2)}) async-start(bf16[16,320,128]{2,1,0:T(8,128)(2,1)} %broadcast_in_dim.56), calls=%async_computation.8 | async-start | bytes 2621440 | tf_op jit(solution)/shard_map/all_to_all | solution.py:200
  189.2 1.9 conv2_unpack.1
  191.1 18.3 %all-to-all-done.8.got_ref = bf16[16,320,128]{2,1,0:T(8,128)(2,1)S(1)} async-done(((bf16[16,320,128]{2,1,0:T(8,128)(2,1)}), bf16[16,320,128]{2,1,0:T(8,128)(2,1)S(1)}, u32[]{:S(2)}, u32[]{:S(2)}) %all-to-all-start.8) | async-done | bytes 1310752 | tf_op jit(solution)/shard_map/all_to_all | solution.py:200
  209.3 1.1 copy-done.1
  210.4 2.9 %conv1_unpack.1 = (f32[384,1280]{1,0:T(8,128)}, f32[1,1280]{1,0:T(1,128)}, f32[1,640]{1,0:T(1,128)}) custom-call(bf16[16,320,128]{2,1,0:T(8,128)(2,1)} %copy-done.1), custom_call_target="tpu_custom_call" | custom-call | tf_op jit(solution)/shard_map/conv1_unpack/pallas_call | solution.py:330
  213.3 1.3 reduce.3
  214.6 1.3 reduce.2
  215.9 0.7 copy.20
  (16 shorter events, 0.1 us)
Async XLA Ops:
  0.6 18.4 %copy-start.5 = (bf16[80,1920]{1,0:T(8,128)(2,1)S(1)}, bf16[80,1920]{1,0:T(8,128)(2,1)}, u32[]{:S(2)}) copy-start(bf16[80,1920]{1,0:T(8,128)(2,1)} %param.13) | copy-start | bytes 921604
  0.6 18.3 %collective-permute-start = (bf16[80,1920]{1,0:T(8,128)(2,1)}, bf16[80,1920]{1,0:T(8,128)(2,1)S(1)}, u32[]{:S(2)}, u32[]{:S(2)}) collective-permute-start(bf16[80,1920]{1,0:T(8,128)(2,1)} %param.13), channel_id=1, source_target_pairs={{0,32},{32,0},{1,33},{33,1},{2,34},{34,2},{3,35},{35,3},{4,36},{36... | collective-permute-start | bytes 921608 | tf_op jit(solution)/shard_map/ppermute | solution.py:223
  12.1 14.4 %all-to-all-start = ((bf16[8,144,256]{2,1,0:T(8,128)(2,1)}), bf16[8,144,256]{2,1,0:T(8,128)(2,1)S(1)}, u32[]{:S(2)}, u32[]{:S(2)}) async-start(bf16[8,144,256]{2,1,0:T(8,128)(2,1)} %broadcast_in_dim.23), calls=%async_computation | async-start | bytes 1179648 | tf_op jit(solution)/shard_map/all_to_all | solution.py:200
  26.5 0.8 copy-start.3
  27.3 12.5 %copy-start.7 = (s32[16,1]{0,1:T(1,128)S(1)}, s32[16,1]{0,1:T(1,128)}, u32[]{:S(2)}) copy-start(s32[16,1]{0,1:T(1,128)} %param.10) | copy-start | bytes 196
  27.3 14.0 %copy-start.6 = (f32[640]{0:T(1024)S(1)}, f32[640]{0:T(1024)}, u32[]{:S(2)}) copy-start(f32[640]{0:T(1024)} %param.14) | copy-start | bytes 7684
  35.5 21.7 %all-to-all-start.1 = ((bf16[8,128,640]{2,1,0:T(8,128)(2,1)}), bf16[8,128,640]{2,1,0:T(8,128)(2,1)S(1)}, u32[]{:S(2)}, u32[]{:S(2)}) async-start(bf16[8,128,640]{2,1,0:T(8,128)(2,1)} %get-tuple-element.14), calls=%async_computation.1 | async-start | bytes 2621440 | tf_op jit(solution)/shard_map/all_to_all | solution.py:200
  57.1 1.1 copy-start
  61.2 22.9 %all-to-all-start.3 = ((bf16[8,128,640]{2,1,0:T(8,128)(2,1)}), bf16[8,128,640]{2,1,0:T(8,128)(2,1)S(1)}, u32[]{:S(2)}, u32[]{:S(2)}) async-start(bf16[8,128,640]{2,1,0:T(8,128)(2,1)} %get-tuple-element.16), calls=%async_computation.3 | async-start | bytes 2621440 | tf_op jit(solution)/shard_map/all_to_all | solution.py:200
  84.1 1.1 copy-start.2
  163.3 21.3 %copy-start.4 = (bf16[2,768,128]{2,1,0:T(8,128)(2,1)}, bf16[2,768,128]{2,1,0:T(8,128)(2,1)S(1)}, u32[]{:S(2)}) copy-start(bf16[2,768,128]{2,1,0:T(8,128)(2,1)S(1)} %all_to_all.48) | copy-start | bytes 1179652
  163.3 19.9 %all-to-all-start.2 = ((bf16[16,16,640]{2,1,0:T(8,128)(2,1)}), bf16[16,16,640]{2,1,0:T(8,128)(2,1)S(1)}, u32[]{:S(2)}, u32[]{:S(2)}) async-start(bf16[16,16,640]{2,1,0:T(8,128)(2,1)} %bitcast.3), calls=%async_computation.2 | async-start | bytes 655360 | tf_op jit(solution)/shard_map/all_to_all | solution.py:200
  184.5 24.8 %all-to-all-start.8 = ((bf16[16,320,128]{2,1,0:T(8,128)(2,1)}), bf16[16,320,128]{2,1,0:T(8,128)(2,1)S(1)}, u32[]{:S(2)}, u32[]{:S(2)}) async-start(bf16[16,320,128]{2,1,0:T(8,128)(2,1)} %broadcast_in_dim.56), calls=%async_computation.8 | async-start | bytes 2621440 | tf_op jit(solution)/shard_map/all_to_all | solution.py:200
  209.3 1.1 copy-start.1

commit v2 on v1

v2 whole, which is shorter than its diff:
```python
import functools

import jax
import jax.numpy as jnp
from jax import lax
from jax.experimental import pallas as pl
from jax.experimental.pallas import tpu as pltpu
from jax.sharding import Mesh
from jax.sharding import PartitionSpec as P

inv_root_two = 0.7071067811865476
inv_root_tau = 0.3989422804014327

MEL = 128
D2 = 640
ROWS = 80
LANES = 128
HOLDERS = 4
BLOCKS = 4
WIDE = 384
CLIPS = 16
HALF = 8
STEPS = CLIPS * HALF
SLOTS = 2 * CLIPS
PACK = 896
HALF_ROWS = 8 * ROWS
VMEM = 56 * 1024 * 1024
ALL_AXES = ("xh", "y", "c", "z", "xl")
ENC = ("xh", "y", "c")
F32 = jnp.float32
BF16 = jnp.bfloat16


def gelu_both(values):
    cdf = 0.5 * (1.0 + lax.erf(values * inv_root_two))
    return values * cdf, cdf + values * jnp.exp(-0.5 * values * values) * inv_root_tau


def shift_down(values):
    rows, width = values.shape
    t = lax.broadcasted_iota(jnp.int32, (rows, width), 0) & (HALF - 1)
    clips = values.reshape(rows // HALF, HALF, width)
    moved = pltpu.roll(clips, 1, 1).reshape(rows, width)
    return jnp.where(t == 0, 0.0, moved)


def shift_up(values):
    rows, width = values.shape
    t = lax.broadcasted_iota(jnp.int32, (rows, width), 0) & (HALF - 1)
    clips = values.reshape(rows // HALF, HALF, width)
    moved = pltpu.roll(clips, HALF - 1, 1).reshape(rows, width)
    return jnp.where(t == HALF - 1, 0.0, moved)


def dot(left, right):
    return jnp.dot(left, right, preferred_element_type=F32)


def dot_nt(left, right):
    return lax.dot_general(left, right, (((1,), (1,)), ((), ())), preferred_element_type=F32)


def dot_tn(left, right):
    return lax.dot_general(left, right, (((0,), (0,)), ((), ())), preferred_element_type=F32)


def stack_weights(refs, w2_ref):
    @pl.when(pl.program_id(0) == 0)
    def _():
        for block, ref in enumerate(refs):
            w2_ref[block * ROWS : (block + 1) * ROWS, :] = ref[...]
        w2_ref[BLOCKS * ROWS :, :] = jnp.zeros((WIDE - BLOCKS * ROWS, 3 * D2), BF16)


def forward_kernel(
    pay_ref, w1_ref, b1_ref, own_ref, side_ref, far_ref, both_ref, part_ref, cols_ref, act_ref, slope_ref, w2_ref
):
    stack_weights((own_ref, side_ref, far_ref, both_ref), w2_ref)
    spread = (
        lax.broadcasted_iota(jnp.int32, (STEPS, CLIPS), 0) >> 3
        == lax.broadcasted_iota(jnp.int32, (STEPS, CLIPS), 1)
    ).astype(F32).astype(BF16)
    length = dot(spread, pay_ref[0, STEPS : STEPS + CLIPS, :LANES])
    t = (lax.broadcasted_iota(jnp.int32, (STEPS, LANES), 0) & (HALF - 1)).astype(F32)
    live_even, live_odd = 2.0 * t < length, 2.0 * t + 1.0 < length
    even = jnp.where(live_even, pay_ref[0, :STEPS, :LANES].astype(F32), 0.0)
    odd = jnp.where(live_odd, pay_ref[0, :STEPS, LANES:].astype(F32), 0.0)
    cols_ref[0, :, :LANES] = shift_down(odd).astype(BF16)
    cols_ref[0, :, LANES : 2 * LANES] = even.astype(BF16)
    cols_ref[0, :, 2 * LANES : 3 * LANES] = odd.astype(BF16)
    cols_ref[0, :, 3 * LANES :] = shift_up(even).astype(BF16)
    bias = b1_ref[...]
    mask_even = jnp.where(live_even, 1.0, 0.0)
    mask_odd = jnp.where(live_odd, 1.0, 0.0)
    mask_even = jnp.concatenate([mask_even] * (WIDE // LANES), axis=1)
    mask_odd = jnp.concatenate([mask_odd] * (WIDE // LANES), axis=1)
    act, slope = gelu_both(dot(cols_ref[0, :, : 3 * LANES], w1_ref[...]) + bias)
    act_even = (act * mask_even).astype(BF16)
    slope_ref[0, 0] = slope * mask_even
    act, slope = gelu_both(dot(cols_ref[0, :, LANES:], w1_ref[...]) + bias)
    act = act * mask_odd
    act_odd = act.astype(BF16)
    slope_ref[0, 1] = slope * mask_odd
    act_prior = shift_down(act).astype(BF16)
    act_ref[0, 0] = act_prior
    act_ref[0, 1] = act_even
    act_ref[0, 2] = act_odd
    total = dot(act_prior, w2_ref[:, :D2])
    total = total + dot(act_even, w2_ref[:, D2 : 2 * D2])
    total = total + dot(act_odd, w2_ref[:, 2 * D2 :])
    part_ref[0] = total.astype(BF16)


def middle_kernel(part_ref, grad_ref, b2_ref, length_ref, owner_col_ref, owner_row_ref, rep_ref, placed_ref):
    pre = part_ref[0].astype(F32)
    for source in range(1, HOLDERS):
        pre = pre + part_ref[source].astype(F32)
    pre = pre + b2_ref[...]
    t = (lax.broadcasted_iota(jnp.int32, (STEPS, 1), 0) & (HALF - 1)).astype(F32)
    live = jnp.where(2.0 * t < length_ref[...], 1.0, 0.0)
    value, slope = gelu_both(pre)
    features = (value * live).astype(BF16)
    second_grad = (grad_ref[...].astype(F32) * slope * live).astype(BF16)
    for target in range(HOLDERS):
        rep_ref[target] = second_grad
    here = lax.broadcasted_iota(jnp.int32, (STEPS, STEPS), 0)
    there = lax.broadcasted_iota(jnp.int32, (STEPS, STEPS), 1)
    same = (owner_col_ref[...] == owner_row_ref[...]) & ((here >> 3) < (there >> 3))
    same = same & ((here & (HALF - 1)) == 0)
    rank = jnp.sum(jnp.where(same, 1.0, 0.0), axis=0, keepdims=True).astype(jnp.int32)
    place = lax.broadcasted_iota(jnp.int32, (1, STEPS), 1) & (HALF - 1)
    place = (owner_row_ref[...] * 2 + rank) * HALF + place
    wanted = lax.broadcasted_iota(jnp.int32, (SLOTS * HALF, STEPS), 0) == place
    placed_ref[...] = dot(jnp.where(wanted, 1.0, 0.0).astype(BF16), features).astype(BF16)


def backward_kernel(
    where_ref, grad_ref, own_ref, side_ref, far_ref, both_ref, cols_ref, act_ref, slope_ref, keep_ref, send_ref,
    w2_ref, conv2_sum, conv1_sum, bias1_sum, bias2_sum,
):
    stack_weights((own_ref, side_ref, far_ref, both_ref), w2_ref)
    step = pl.program_id(0)

    @pl.when(step == 0)
    def _():
        conv2_sum[...] = jnp.zeros_like(conv2_sum)
        conv1_sum[...] = jnp.zeros_like(conv1_sum)
        bias1_sum[...] = jnp.zeros_like(bias1_sum)
        bias2_sum[...] = jnp.zeros_like(bias2_sum)

    rows = 2 * STEPS
    grad = grad_ref[...].reshape(rows, D2)
    bias2_sum[...] += jnp.sum(grad.astype(F32), axis=0, keepdims=True)
    even = dot_nt(grad, w2_ref[:, D2 : 2 * D2])
    odd = dot_nt(grad, w2_ref[:, 2 * D2 :]) + shift_up(dot_nt(grad, w2_ref[:, :D2]))
    even = (even * slope_ref[:, 0].reshape(rows, WIDE)).astype(BF16)
    odd = (odd * slope_ref[:, 1].reshape(rows, WIDE)).astype(BF16)
    cols = cols_ref[...].reshape(rows, 4 * LANES)
    conv1_sum[...] += dot_tn(even, cols[:, : 3 * LANES]) + dot_tn(odd, cols[:, LANES:])
    bias1_sum[...] += jnp.sum(even.astype(F32) + odd.astype(F32), axis=0, keepdims=True)
    for tap in range(3):
        conv2_sum[:, tap * D2 : (tap + 1) * D2] += dot_tn(act_ref[:, tap].reshape(rows, WIDE), grad)

    @pl.when(step == pl.num_programs(0) - 1)
    def _():
        mine = where_ref[0]
        for block in range(BLOCKS):
            target = mine if block < 2 else 1 - mine
            out = keep_ref if block % 2 == 0 else send_ref
            first = block * ROWS
            for tile in range(15):
                half, spot = tile // 8, tile % 8
                piece = conv2_sum[first : first + ROWS, tile * LANES : (tile + 1) * LANES]
                out[target, half, spot * ROWS : (spot + 1) * ROWS, :] = piece.astype(out.dtype)
            out[target, 1, 7 * ROWS : 8 * ROWS, :] = jnp.zeros((ROWS, LANES), out.dtype)
            biases = [jnp.concatenate([bias1_sum[:, first : first + ROWS], jnp.zeros((1, LANES - ROWS), F32)], axis=1)]
            for tile in range(D2 // LANES):
                biases.append(bias2_sum[:, tile * LANES : (tile + 1) * LANES])
            biases.append(jnp.zeros((16 - len(biases), LANES), F32))
            biases = jnp.concatenate(biases, axis=0).astype(out.dtype)
            for half in range(2):
                for tile in range(3):
                    piece = conv1_sum[first : first + ROWS, tile * LANES : (tile + 1) * LANES]
                    out[target, half, (8 + tile) * ROWS : (9 + tile) * ROWS, :] = piece.astype(out.dtype)
                out[target, half, 11 * ROWS :, :] = biases


def sum_kernel(got_ref, out_ref):
    total = got_ref[0].astype(F32)
    for source in range(1, got_ref.shape[0]):
        total = total + got_ref[source].astype(F32)
    total = total.astype(BF16)
    if len(out_ref.shape) == 2:
        out_ref[...] = total
    else:
        for target in range(out_ref.shape[0]):
            out_ref[target] = total


def unpack_kernel(where_ref, own_ref, other_ref, out_ref):
    first = where_ref[1] == 0
    for tile in range(15):
        half, spot = tile // 8, tile % 8
        rows = slice(spot * ROWS, (spot + 1) * ROWS)
        own, other = own_ref[rows, :].astype(F32), other_ref[rows, :].astype(F32)
        picked = jnp.where(first, own, other) if half == 0 else jnp.where(first, other, own)
        out_ref[:, tile * LANES : (tile + 1) * LANES] = picked


def last_kernel(got_ref, weight_ref, bias1_ref, bias2_ref, whole):
    for tile in range(3):
        for source in range(16):
            whole[source * ROWS : (source + 1) * ROWS, :] = got_ref[
                source, tile * ROWS : (tile + 1) * ROWS, :
            ].astype(F32)
        for block in range(10):
            weight_ref[tile * LANES : (tile + 1) * LANES, block * LANES : (block + 1) * LANES] = whole[
                block * LANES : (block + 1) * LANES, :
            ].T
    pieces = [got_ref[source, 3 * ROWS :, :].astype(F32) for source in range(16)]
    bias1_ref[...] = jnp.concatenate([piece[0:1, :ROWS] for piece in pieces], axis=1)
    bias2_ref[...] = jnp.concatenate([pieces[0][1 + tile : 2 + tile, :] for tile in range(D2 // LANES)], axis=1)


def exchange(values, axes):
    return lax.all_to_all(values, axes, split_axis=0, concat_axis=0, tiled=True)


def spread_to(values, count):
    return jnp.broadcast_to(values[None], (count,) + values.shape)


def vmem():
    return pl.BlockSpec(memory_space=pltpu.VMEM)


def params(*semantics):
    return pltpu.CompilerParams(vmem_limit_bytes=VMEM, dimension_semantics=semantics or None)


def local(mel, lengths, routes, conv1_weight, conv1_bias, conv2_weight, conv2_bias, out_grad):
    x_hi, y, core = lax.axis_index("xh"), lax.axis_index("y"), lax.axis_index("c")
    where = jnp.stack([x_hi, lax.axis_index("xl")]).astype(jnp.int32)

    def shape(*dims, dtype=BF16):
        return jax.ShapeDtypeStruct(dims, dtype)

    weights = [
        conv2_weight,
        lax.ppermute(conv2_weight, "c", [(0, 1), (1, 0)]),
        lax.ppermute(conv2_weight, "xh", [(0, 1), (1, 0)]),
        lax.ppermute(conv2_weight, ("xh", "c"), [(0, 3), (3, 0), (1, 2), (2, 1)]),
    ]
    lengths_bf = lengths.astype(BF16)
    pay = jnp.concatenate(
        [mel.reshape(STEPS, 2 * MEL), jnp.broadcast_to(lengths_bf[:, None], (CLIPS, 2 * MEL))], axis=0
    )
    pay_rows = pay.shape[0]
    got_pay = exchange(spread_to(pay, HOLDERS), "y")

    w1, b1 = [], []
    for flip_x, flip_c in ((0, 0), (0, 1), (1, 0), (1, 1)):
        place = ((x_hi ^ flip_x) * HOLDERS + y) * 2 + (core ^ flip_c)
        w1.append(lax.dynamic_slice(conv1_weight, (0, place * ROWS), (3 * MEL, ROWS)))
        b1.append(lax.dynamic_slice(conv1_bias, (place * ROWS,), (ROWS,)))
    gap = WIDE - BLOCKS * ROWS
    w1 = jnp.concatenate(w1 + [jnp.zeros((3 * MEL, gap), BF16)], axis=1)
    b1 = jnp.concatenate(b1 + [jnp.zeros((gap,), F32)])[None]

    parts, cols, acts, slopes = pl.pallas_call(
        forward_kernel,
        grid=(HOLDERS,),
        in_specs=[
            pl.BlockSpec((1, pay_rows, 2 * MEL), lambda i: (i, 0, 0)),
            pl.BlockSpec((3 * MEL, WIDE), lambda i: (0, 0)),
            pl.BlockSpec((1, WIDE), lambda i: (0, 0)),
            *[pl.BlockSpec((ROWS, 3 * D2), lambda i: (0, 0))] * BLOCKS,
        ],
        out_specs=[
            pl.BlockSpec((1, STEPS, D2), lambda i: (i, 0, 0)),
            pl.BlockSpec((1, STEPS, 4 * LANES), lambda i: (i, 0, 0)),
            pl.BlockSpec((1, 3, STEPS, WIDE), lambda i: (i, 0, 0, 0)),
            pl.BlockSpec((1, 2, STEPS, WIDE), lambda i: (i, 0, 0, 0)),
        ],
        out_shape=[
            shape(HOLDERS, STEPS, D2),
            shape(HOLDERS, STEPS, 4 * LANES),
            shape(HOLDERS, 3, STEPS, WIDE),
            shape(HOLDERS, 2, STEPS, WIDE, dtype=F32),
        ],
        scratch_shapes=[pltpu.VMEM((WIDE, 3 * D2), BF16)],
        compiler_params=params("arbitrary"),
        name="stem_forward",
    )(got_pay.reshape(HOLDERS, pay_rows, 2 * MEL), w1, b1, *weights)

    got_parts = exchange(parts, "y")
    owner = jnp.repeat(routes[:, 0], HALF)
    rep, placed = pl.pallas_call(
        middle_kernel,
        in_specs=[vmem()] * 6,
        out_specs=[vmem()] * 2,
        out_shape=[shape(HOLDERS, STEPS, D2), shape(SLOTS * HALF, D2)],
        compiler_params=params(),
        name="stem_middle",
    )(
        got_parts,
        out_grad.reshape(STEPS, D2),
        conv2_bias[None],
        jnp.repeat(lengths.astype(F32), HALF)[:, None],
        owner[:, None],
        owner[None],
    )
    got_grad = exchange(rep, "y")
    packed = exchange(placed.reshape(16, 2 * HALF, D2), ENC)

    pair = lambda i: (i, 0, 0)
    pair4 = lambda i: (i, 0, 0, 0)
    whole = lambda i: (0, 0, 0, 0)
    keep, send = pl.pallas_call(
        backward_kernel,
        grid=(HOLDERS // 2,),
        in_specs=[
            pl.BlockSpec(memory_space=pltpu.SMEM),
            pl.BlockSpec((2, STEPS, D2), pair),
            *[pl.BlockSpec((ROWS, 3 * D2), lambda i: (0, 0))] * BLOCKS,
            pl.BlockSpec((2, STEPS, 4 * LANES), pair),
            pl.BlockSpec((2, 3, STEPS, WIDE), pair4),
            pl.BlockSpec((2, 2, STEPS, WIDE), pair4),
        ],
        out_specs=[pl.BlockSpec((2, 2, PACK, LANES), whole)] * 2,
        out_shape=[shape(2, 2, PACK, LANES, dtype=F32), shape(2, 2, PACK, LANES)],
        scratch_shapes=[
            pltpu.VMEM((WIDE, 3 * D2), BF16),
            pltpu.VMEM((WIDE, 3 * D2), F32),
            pltpu.VMEM((WIDE, 3 * LANES), F32),
            pltpu.VMEM((1, WIDE), F32),
            pltpu.VMEM((1, D2), F32),
        ],
        compiler_params=params("arbitrary"),
        cost_estimate=pl.CostEstimate(flops=24 * 10**8, bytes_accessed=8 * 10**6, transcendentals=0),
        name="stem_backward",
    )(where, got_grad, *weights, cols, acts, slopes)
    send, packed = lax.optimization_barrier((send, packed))
    got = lax.ppermute(send, "c", [(0, 1), (1, 0)])
    quarters = exchange((keep + got.astype(F32)).astype(BF16).reshape(4, PACK, LANES), ("xh", "xl"))

    def summed(values, *dims):
        return pl.pallas_call(
            sum_kernel,
            in_specs=[vmem()],
            out_specs=vmem(),
            out_shape=shape(*dims),
            compiler_params=params(),
            name="gradient_sum",
        )(values)

    half = summed(quarters, PACK, LANES)
    pieces = exchange(half.reshape(16, PACK // 16, LANES), "z")
    half = exchange(summed(pieces, 16, PACK // 16, LANES), "z").reshape(PACK, LANES)
    shares = exchange(spread_to(half[HALF_ROWS:], 16), ENC)
    own = half[:HALF_ROWS]
    conv2_rows_grad = pl.pallas_call(
        unpack_kernel,
        in_specs=[pl.BlockSpec(memory_space=pltpu.SMEM), vmem(), vmem()],
        out_specs=vmem(),
        out_shape=shape(ROWS, 3 * D2, dtype=F32),
        compiler_params=params(),
        name="conv2_unpack",
    )(where, own, lax.ppermute(own, "xl", [(0, 1), (1, 0)]))
    weight_grad, bias_grad, second_bias_grad = pl.pallas_call(
        last_kernel,
        in_specs=[vmem()],
        out_specs=[vmem()] * 3,
        out_shape=[
            shape(3 * MEL, 16 * ROWS, dtype=F32),
            shape(1, 16 * ROWS, dtype=F32),
            shape(1, D2, dtype=F32),
        ],
        scratch_shapes=[pltpu.VMEM((16 * ROWS, LANES), F32)],
        compiler_params=params(),
        name="conv1_unpack",
    )(shares)
    return (
        packed.reshape(SLOTS, HALF, D2),
        weight_grad,
        bias_grad[0],
        second_bias_grad[0],
        conv2_rows_grad,
    )


def solution(mesh):
    fine = Mesh(mesh.devices.reshape(2, 4, 2, 16, 2), ALL_AXES)
    placed = (
        P(ALL_AXES, None, None),
        P(ALL_AXES),
        P(ALL_AXES, None),
        P(),
        P(),
        P(ENC, None),
        P(),
        P(ALL_AXES, None, None),
    )
    return jax.shard_map(
        local,
        mesh=fine,
        in_specs=placed,
        out_specs=(P(ALL_AXES, None, None), P(), P(), P(), P(ENC, None)),
        check_vma=False,
    )
```

time: 218 us -> 191 us (0.88)
  waiting for transfers between devices: 65 us -> 33.5 us
  starting transfers between devices: 37.9 us -> 48.8 us
  blocking collectives: 69.1 us -> 62.3 us
    all_to_all x5, waiting for transfers between devices: 65 us -> 17.2 us  [exchange(): return lax.all_to_all(values, axes, split_axis=0, concat_axis=0, tiled=True)]
    ppermute x1 -> x5, waiting for transfers between devices: 0.01 us -> 16.3 us  [the longest x1 14 us: local(): lax.ppermute(own, 'xl', [(0, 1), (1, 0)])]
    ppermute x1 -> x5, starting transfers between devices: 8.92 us -> 20.7 us  [the longest x1 7.51 us: local(): lax.ppermute(conv2_weight, 'xh', [(0, 1), (1, 0)])]
    all_to_all x4 -> x3, blocking collectives: 69.1 us -> 62.3 us  [exchange(): return lax.all_to_all(values, axes, split_axis=0, concat_axis=0, tiled=True)]
    concatenate x3 -> x0, other arithmetic: 2.32 us -> none  [the longest x1 1.04 us: local(): w2 = jnp.concatenate([conv2_weight, gap, other_weight, gap], axis=0)]
    pallas_call x3 -> x5, Pallas kernels: 18.7 us -> 18.9 us  [the longest x1 7.54 us: local(): pl.pallas_call(backward_kernel, grid=(HOLDERS // 2,), in_specs=[pl.BlockS...]
    unnamed x17 -> x23, local copies, waits for them, and re-layouts: 4.76 us -> 4.87 us
  transfers between devices with their start and end apart: 6 -> 10, of which waited for: 5 -> 6; matrix products, arithmetic and copies ran while one was open for 5% -> 5% of each run, Pallas kernels for 1% -> 5%
where the time goes in v2:
time: 191 us; the launch traced here: 190 us
  blocking collectives  62.3 us (33%)
  starting transfers between devices  48.8 us (26%)
  waiting for transfers between devices  33.5 us (18%)
  Pallas kernels  24.2 us (13%)
  local copies, waits for them, and re-layouts  14.4 us (8%)
  other arithmetic  5.79 us (3%)
    all_to_all x3, blocking collectives, exchange(): return lax.all_to_all(values, axes, split_axis=0, concat_axis=0, tiled=True)  62.3 us
    all_to_all x5, starting transfers between devices, exchange(): return lax.all_to_all(values, axes, split_axis=0, concat_axis=0, tiled=True)  28 us
    all_to_all x5, waiting for transfers between devices, exchange(): return lax.all_to_all(values, axes, split_axis=0, concat_axis=0, tiled=True)  17.2 us
    ppermute x1, waiting for transfers between devices, local(): lax.ppermute(own, 'xl', [(0, 1), (1, 0)])  14 us
    pallas_call x1, Pallas kernels, local(): pl.pallas_call(backward_kernel, grid=(HOLDERS // 2,), in_specs=[pl.BlockS...  7.54 us
    ppermute x1, starting transfers between devices, local(): lax.ppermute(conv2_weight, 'xh', [(0, 1), (1, 0)])  7.51 us
    ppermute x1, starting transfers between devices, local(): lax.ppermute(conv2_weight, ('xh', 'c'), [(0, 3), (3, 0), (1, 2), (2, 1)])  6.04 us
    pallas_call x1, Pallas kernels, local(): pl.pallas_call(forward_kernel, grid=(HOLDERS,), in_specs=[pl.BlockSpec((1...  5.8 us
  transfers between devices with their start and end apart: 10, of which 6 were waited for; matrix products, arithmetic and copies ran while one was open for 5% of the time, Pallas kernels for 5%

profile of v2, /device:TPU:1, one launch (start us, length us, event | category | flops | bytes accessed | tf_op | source)
XLA Modules:
  0.0 189.7 jit_solution(18320242284432514944)
XLA Ops:
  0.6 6.0 %collective-permute-start.2 = (bf16[80,1920]{1,0:T(8,128)(2,1)}, bf16[80,1920]{1,0:T(8,128)(2,1)S(1)}, u32[]{:S(2)}, u32[]{:S(2)}) collective-permute-start(bf16[80,1920]{1,0:T(8,128)(2,1)} %own_ref.3), channel_id=1, source_target_pairs={{0,288},{288,0},{32,256},{256,32},{1,289},{289,1},{33,257},{257,33... | collective-permute-start | bytes 921608 | tf_op jit(solution)/shard_map/ppermute | solution.py:252
  6.7 7.5 %collective-permute-start.1 = (bf16[80,1920]{1,0:T(8,128)(2,1)}, bf16[80,1920]{1,0:T(8,128)(2,1)S(1)}, u32[]{:S(2)}, u32[]{:S(2)}) collective-permute-start(bf16[80,1920]{1,0:T(8,128)(2,1)} %own_ref.3), channel_id=1, source_target_pairs={{0,256},{256,0},{1,257},{257,1},{2,258},{258,2},{3,259},{259,3},{4... | collective-permute-start | bytes 921608 | tf_op jit(solution)/shard_map/ppermute | solution.py:251
  14.2 1.9 %collective-permute-start = (bf16[80,1920]{1,0:T(8,128)(2,1)}, bf16[80,1920]{1,0:T(8,128)(2,1)S(1)}, u32[]{:S(2)}, u32[]{:S(2)}) collective-permute-start(bf16[80,1920]{1,0:T(8,128)(2,1)} %own_ref.3), channel_id=1, source_target_pairs={{0,32},{32,0},{1,33},{33,1},{2,34},{34,2},{3,35},{35,3},{4,36},{36... | collective-permute-start | bytes 921608 | tf_op jit(solution)/shard_map/ppermute | solution.py:250
  16.1 0.7 fusion.1
  16.9 0.9 reshape.34
  17.8 0.7 broadcast_in_dim.37
  18.6 3.5 %all-to-all-start = ((bf16[4,144,256]{2,1,0:T(8,128)(2,1)}), bf16[4,144,256]{2,1,0:T(8,128)(2,1)S(1)}, u32[]{:S(2)}, u32[]{:S(2)}) async-start(bf16[4,144,256]{2,1,0:T(8,128)(2,1)} %broadcast_in_dim.37), calls=%async_computation | async-start | bytes 589824 | tf_op jit(solution)/shard_map/all_to_all | solution.py:226
  22.1 0.9 fusion
  23.1 0.6 broadcast_in_dim.40.b1_ref
  23.7 1.4 constant_dynamic-slice_fusion
  25.1 1.0 concatenate.10.w1_ref
  26.1 2.3 %all-to-all-done.pay_ref = bf16[4,144,256]{2,1,0:T(8,128)(2,1)S(1)} async-done(((bf16[4,144,256]{2,1,0:T(8,128)(2,1)}), bf16[4,144,256]{2,1,0:T(8,128)(2,1)S(1)}, u32[]{:S(2)}, u32[]{:S(2)}) %all-to-all-start) | async-done | bytes 294944 | tf_op jit(solution)/shard_map/all_to_all | solution.py:226
  28.4 0.7 copy-done.2
  29.3 0.7 copy-done.7
  30.0 5.8 %stem_forward.1 = (bf16[4,128,640]{2,1,0:T(8,128)(2,1)}, bf16[4,128,512]{2,1,0:T(8,128)(2,1)}, bf16[4,3,128,384]{3,2,1,0:T(8,128)(2,1)}, f32[4,2,128,384]{3,2,1,0:T(8,128)}) custom-call(bf16[4,144,256]{2,1,0:T(8,128)(2,1)} %copy-done.2, bf16[384,384]{1,0:T(8,128)(2,1)} %concatenate.10.w1_ref, f32[1,384]{1,0:T(1,128)} %broadcast_in_dim.40.b1_ref, ...), custom_call_target="tpu_custom_call" | custom-call | tf_op jit(solution)/shard_map/stem_forward/pallas_call | solution.py:270
  35.8 3.5 %all-to-all-start.1 = ((bf16[4,128,640]{2,1,0:T(8,128)(2,1)}), bf16[4,128,640]{2,1,0:T(8,128)(2,1)S(1)}, u32[]{:S(2)}, u32[]{:S(2)}) async-start(bf16[4,128,640]{2,1,0:T(8,128)(2,1)} %get-tuple-element.18), calls=%async_computation.1 | async-start | bytes 1310720 | tf_op jit(solution)/shard_map/all_to_all | solution.py:226
  39.4 0.6 broadcast_in_dim_reshape.11.owner_row_ref
  40.0 0.7 broadcast_in_dim_reshape.13.owner_col_ref
  40.7 0.6 broadcast_in_dim.41.b2_ref
  41.3 0.7 broadcast_in_dim_reshape.12.length_ref
  42.0 6.2 %all-to-all-done.1.part_ref = bf16[4,128,640]{2,1,0:T(8,128)(2,1)S(1)} async-done(((bf16[4,128,640]{2,1,0:T(8,128)(2,1)}), bf16[4,128,640]{2,1,0:T(8,128)(2,1)S(1)}, u32[]{:S(2)}, u32[]{:S(2)}) %all-to-all-start.1) | async-done | bytes 655392 | tf_op jit(solution)/shard_map/all_to_all | solution.py:226
  48.2 0.8 copy-done.1
  49.1 2.5 %stem_middle.1 = (bf16[4,128,640]{2,1,0:T(8,128)(2,1)}, bf16[256,640]{1,0:T(8,128)(2,1)}) custom-call(bf16[4,128,640]{2,1,0:T(8,128)(2,1)} %copy-done.1, bf16[128,640]{1,0:T(8,128)(2,1)} %bitcast.15, f32[1,640]{1,0:T(1,128)} %broadcast_in_dim.41.b2_ref, f32[128,1]{1,0:T(8,128)} %broadcast_in_dim_reshape.12.length_ref, ...), custom_call_target="tpu_custom_call" | custom-call | tf_op jit(solution)/shard_map/stem_middle/pallas_call | solution.py:298
  51.5 3.5 %all-to-all-start.2 = ((bf16[4,128,640]{2,1,0:T(8,128)(2,1)}), bf16[4,128,640]{2,1,0:T(8,128)(2,1)S(1)}, u32[]{:S(2)}, u32[]{:S(2)}) async-start(bf16[4,128,640]{2,1,0:T(8,128)(2,1)} %get-tuple-element.19), calls=%async_computation.2 | async-start | bytes 1310720 | tf_op jit(solution)/shard_map/all_to_all | solution.py:226
  55.0 7.7 %all-to-all-done.2.grad_ref = bf16[4,128,640]{2,1,0:T(8,128)(2,1)S(1)} async-done(((bf16[4,128,640]{2,1,0:T(8,128)(2,1)}), bf16[4,128,640]{2,1,0:T(8,128)(2,1)S(1)}, u32[]{:S(2)}, u32[]{:S(2)}) %all-to-all-start.2) | async-done | bytes 655392 | tf_op jit(solution)/shard_map/all_to_all | solution.py:226
  62.8 8.3 %all-to-all-start.3 = ((bf16[16,16,640]{2,1,0:T(8,128)(2,1)}), bf16[16,16,640]{2,1,0:T(8,128)(2,1)S(1)}, u32[]{:S(2)}, u32[]{:S(2)}) async-start(bf16[16,16,640]{2,1,0:T(8,128)(2,1)} %bitcast.14), calls=%async_computation.3 | async-start | bytes 655360 | tf_op jit(solution)/shard_map/all_to_all | solution.py:226
  71.1 0.7 pad_add_fusion.where_ref
  71.7 7.5 %stem_backward.1 = (f32[2,2,896,128]{3,2,1,0:T(8,128)}, bf16[2,2,896,128]{3,2,1,0:T(8,128)(2,1)}) custom-call(s32[2]{0:T(128)} %pad_add_fusion.where_ref, bf16[4,128,640]{2,1,0:T(8,128)(2,1)} %copy-done.4, bf16[80,1920]{1,0:T(8,128)(2,1)} %own_ref.3, bf16[80,1920]{1,0:T(8,128)(2,1)} %copy-done.7, bf16[80,1920]{1,0:T(8,128)(2,1)} %copy-done.6, ...), custom_call_target="tpu_custom_call" | custom-call | flops 2400000000 | bytes 8000000 | tf_op jit(solution)/shard_map/stem_backward/pallas_call | solution.py:319
  79.3 1.0 all-to-all-done.3
  80.3 3.1 %collective-permute-start.3 = (bf16[2,2,896,128]{3,2,1,0:T(8,128)(2,1)}, bf16[2,2,896,128]{3,2,1,0:T(8,128)(2,1)S(1)}, u32[]{:S(2)}, u32[]{:S(2)}) collective-permute-start(bf16[2,2,896,128]{3,2,1,0:T(8,128)(2,1)} %get-tuple-element.27), channel_id=1, source_target_pairs={{0,32},{32,0},{1,33},{33,1},{2,34},{34,2},{3,35},{35,3},{4,36},{36... | collective-permute-start | bytes 2752520 | tf_op jit(solution)/shard_map/ppermute | solution.py:344
  83.4 2.3 %collective-permute-done.3 = bf16[2,2,896,128]{3,2,1,0:T(8,128)(2,1)S(1)} collective-permute-done((bf16[2,2,896,128]{3,2,1,0:T(8,128)(2,1)}, bf16[2,2,896,128]{3,2,1,0:T(8,128)(2,1)S(1)}, u32[]{:S(2)}, u32[]{:S(2)}) %collective-permute-start.3) | collective-permute-done | bytes 917536 | tf_op jit(solution)/shard_map/ppermute | solution.py:344
  85.6 1.7 add_convert_fusion
  87.4 16.6 %all_to_all.40.got_ref = bf16[4,896,128]{2,1,0:T(8,128)(2,1)} all-to-all(bf16[4,896,128]{2,1,0:T(8,128)(2,1)S(1)} %bitcast.9), channel_id=1, replica_groups=mesh['xh'=2,'y'=4,'c'=2,'z'=16,'xl'=2] {'xh','xl'}, dimensions={0} | all-to-all | bytes 1835008 | tf_op jit(solution)/shard_map/all_to_all | solution.py:226
  103.9 2.0 %gradient_sum.2 = bf16[896,128]{1,0:T(8,128)(2,1)} custom-call(bf16[4,896,128]{2,1,0:T(8,128)(2,1)} %all_to_all.40.got_ref), custom_call_target="tpu_custom_call" | custom-call | tf_op jit(solution)/shard_map/gradient_sum/pallas_call | solution.py:348
  105.9 23.4 %all_to_all.41.got_ref = bf16[16,56,128]{2,1,0:T(8,128)(2,1)} all-to-all(bf16[16,56,128]{2,1,0:T(8,128)(2,1)} %bitcast.13), channel_id=1, replica_groups=mesh['xh'=2,'y'=4,'c'=2,'z'=16,'xl'=2] {'z'}, dimensions={0} | all-to-all | bytes 458752 | tf_op jit(solution)/shard_map/all_to_all | solution.py:226
  129.3 1.7 gradient_sum.3
  131.0 22.3 %all_to_all.42 = bf16[16,56,128]{2,1,0:T(8,128)(2,1)S(1)} all-to-all(bf16[16,56,128]{2,1,0:T(8,128)(2,1)} %gradient_sum.3), channel_id=1, replica_groups=mesh['xh'=2,'y'=4,'c'=2,'z'=16,'xl'=2] {'z'}, dimensions={0} | all-to-all | bytes 458752 | tf_op jit(solution)/shard_map/all_to_all | solution.py:226
  153.3 1.2 broadcast_in_dim.44
  154.5 9.3 %all-to-all-start.7 = ((bf16[16,256,128]{2,1,0:T(8,128)(2,1)}), bf16[16,256,128]{2,1,0:T(8,128)(2,1)S(1)}, u32[]{:S(2)}, u32[]{:S(2)}) async-start(bf16[16,256,128]{2,1,0:T(8,128)(2,1)} %broadcast_in_dim.44), calls=%async_computation.7 | async-start | bytes 2097152 | tf_op jit(solution)/shard_map/all_to_all | solution.py:226
  163.8 2.2 %collective-permute-start.4 = (bf16[640,128]{1,0:T(8,128)(2,1)S(1)}, bf16[640,128]{1,0:T(8,128)(2,1)S(1)}, u32[]{:S(2)}, u32[]{:S(2)}) collective-permute-start(bf16[640,128]{1,0:T(8,128)(2,1)S(1)} %slice.9.own_ref), channel_id=1, source_target_pairs={{0,1},{1,0},{2,3},{3,2},{4,5},{5,4},{6,7},{7,6},{8,9},{9,8},{10,11... | collective-permute-start | bytes 491528 | tf_op jit(solution)/shard_map/ppermute | solution.py:369
  166.0 14.0 %collective-permute-done.4.other_ref = bf16[640,128]{1,0:T(8,128)(2,1)S(1)} collective-permute-done((bf16[640,128]{1,0:T(8,128)(2,1)S(1)}, bf16[640,128]{1,0:T(8,128)(2,1)S(1)}, u32[]{:S(2)}, u32[]{:S(2)}) %collective-permute-start.4) | collective-permute-done | bytes 163872 | tf_op jit(solution)/shard_map/ppermute | solution.py:369
  180.0 0.7 copy-done.8
  180.7 1.9 conv2_unpack.1
  182.6 1.0 copy-done
  183.6 2.8 %conv1_unpack.1 = (f32[384,1280]{1,0:T(8,128)}, f32[1,1280]{1,0:T(1,128)}, f32[1,640]{1,0:T(1,128)}) custom-call(bf16[16,256,128]{2,1,0:T(8,128)(2,1)} %copy-done), custom_call_target="tpu_custom_call" | custom-call | tf_op jit(solution)/shard_map/conv1_unpack/pallas_call | solution.py:370
  186.4 1.3 reduce.1
  187.7 1.3 reduce
  189.0 0.7 copy.18
  (30 shorter events, 0.6 us)
Async XLA Ops:
  0.6 27.7 %collective-permute-start.2 = (bf16[80,1920]{1,0:T(8,128)(2,1)}, bf16[80,1920]{1,0:T(8,128)(2,1)S(1)}, u32[]{:S(2)}, u32[]{:S(2)}) collective-permute-start(bf16[80,1920]{1,0:T(8,128)(2,1)} %own_ref.3), channel_id=1, source_target_pairs={{0,288},{288,0},{32,256},{256,32},{1,289},{289,1},{33,257},{257,33... | collective-permute-start | bytes 921608 | tf_op jit(solution)/shard_map/ppermute | solution.py:252
  6.7 21.7 %collective-permute-start.1 = (bf16[80,1920]{1,0:T(8,128)(2,1)}, bf16[80,1920]{1,0:T(8,128)(2,1)S(1)}, u32[]{:S(2)}, u32[]{:S(2)}) collective-permute-start(bf16[80,1920]{1,0:T(8,128)(2,1)} %own_ref.3), channel_id=1, source_target_pairs={{0,256},{256,0},{1,257},{257,1},{2,258},{258,2},{3,259},{259,3},{4... | collective-permute-start | bytes 921608 | tf_op jit(solution)/shard_map/ppermute | solution.py:251
  14.2 14.2 %collective-permute-start = (bf16[80,1920]{1,0:T(8,128)(2,1)}, bf16[80,1920]{1,0:T(8,128)(2,1)S(1)}, u32[]{:S(2)}, u32[]{:S(2)}) collective-permute-start(bf16[80,1920]{1,0:T(8,128)(2,1)} %own_ref.3), channel_id=1, source_target_pairs={{0,32},{32,0},{1,33},{33,1},{2,34},{34,2},{3,35},{35,3},{4,36},{36... | collective-permute-start | bytes 921608 | tf_op jit(solution)/shard_map/ppermute | solution.py:250
  18.6 9.8 %all-to-all-start = ((bf16[4,144,256]{2,1,0:T(8,128)(2,1)}), bf16[4,144,256]{2,1,0:T(8,128)(2,1)S(1)}, u32[]{:S(2)}, u32[]{:S(2)}) async-start(bf16[4,144,256]{2,1,0:T(8,128)(2,1)} %broadcast_in_dim.37), calls=%async_computation | async-start | bytes 589824 | tf_op jit(solution)/shard_map/all_to_all | solution.py:226
  25.1 14.2 %copy-start.10 = (s32[16,1]{0,1:T(1,128)S(1)}, s32[16,1]{0,1:T(1,128)}, u32[]{:S(2)}) copy-start(s32[16,1]{0,1:T(1,128)} %param.10) | copy-start | bytes 196
  25.1 15.6 %copy-start.9 = (f32[640]{0:T(1024)S(1)}, f32[640]{0:T(1024)}, u32[]{:S(2)}) copy-start(f32[640]{0:T(1024)} %param.14) | copy-start | bytes 7684
  28.3 0.7 copy-start.2
  28.3 0.8 copy-start.5
  28.3 0.9 copy-start.6
  29.2 0.7 copy-start.7
  35.8 12.4 %all-to-all-start.1 = ((bf16[4,128,640]{2,1,0:T(8,128)(2,1)}), bf16[4,128,640]{2,1,0:T(8,128)(2,1)S(1)}, u32[]{:S(2)}, u32[]{:S(2)}) async-start(bf16[4,128,640]{2,1,0:T(8,128)(2,1)} %get-tuple-element.18), calls=%async_computation.1 | async-start | bytes 1310720 | tf_op jit(solution)/shard_map/all_to_all | solution.py:226
  48.2 0.8 copy-start.1
  51.5 11.2 %all-to-all-start.2 = ((bf16[4,128,640]{2,1,0:T(8,128)(2,1)}), bf16[4,128,640]{2,1,0:T(8,128)(2,1)S(1)}, u32[]{:S(2)}, u32[]{:S(2)}) async-start(bf16[4,128,640]{2,1,0:T(8,128)(2,1)} %get-tuple-element.19), calls=%async_computation.2 | async-start | bytes 1310720 | tf_op jit(solution)/shard_map/all_to_all | solution.py:226
  62.8 9.0 %copy-start.4 = (bf16[4,128,640]{2,1,0:T(8,128)(2,1)}, bf16[4,128,640]{2,1,0:T(8,128)(2,1)S(1)}, u32[]{:S(2)}) copy-start(bf16[4,128,640]{2,1,0:T(8,128)(2,1)S(1)} %all-to-all-done.2.grad_ref) | copy-start | bytes 1966084
  62.8 17.5 %all-to-all-start.3 = ((bf16[16,16,640]{2,1,0:T(8,128)(2,1)}), bf16[16,16,640]{2,1,0:T(8,128)(2,1)S(1)}, u32[]{:S(2)}, u32[]{:S(2)}) async-start(bf16[16,16,640]{2,1,0:T(8,128)(2,1)} %bitcast.14), calls=%async_computation.3 | async-start | bytes 655360 | tf_op jit(solution)/shard_map/all_to_all | solution.py:226
  80.3 5.4 %collective-permute-start.3 = (bf16[2,2,896,128]{3,2,1,0:T(8,128)(2,1)}, bf16[2,2,896,128]{3,2,1,0:T(8,128)(2,1)S(1)}, u32[]{:S(2)}, u32[]{:S(2)}) collective-permute-start(bf16[2,2,896,128]{3,2,1,0:T(8,128)(2,1)} %get-tuple-element.27), channel_id=1, source_target_pairs={{0,32},{32,0},{1,33},{33,1},{2,34},{34,2},{3,35},{35,3},{4,36},{36... | collective-permute-start | bytes 2752520 | tf_op jit(solution)/shard_map/ppermute | solution.py:344
  154.5 28.1 %all-to-all-start.7 = ((bf16[16,256,128]{2,1,0:T(8,128)(2,1)}), bf16[16,256,128]{2,1,0:T(8,128)(2,1)S(1)}, u32[]{:S(2)}, u32[]{:S(2)}) async-start(bf16[16,256,128]{2,1,0:T(8,128)(2,1)} %broadcast_in_dim.44), calls=%async_computation.7 | async-start | bytes 2097152 | tf_op jit(solution)/shard_map/all_to_all | solution.py:226
  163.8 16.2 %copy-start.3 = (bf16[640,128]{1,0:T(8,128)(2,1)}, bf16[640,128]{1,0:T(8,128)(2,1)S(1)}, u32[]{:S(2)}) copy-start(bf16[640,128]{1,0:T(8,128)(2,1)S(1)} %slice.9.own_ref) | copy-start | bytes 491524
  163.8 16.2 %collective-permute-start.4 = (bf16[640,128]{1,0:T(8,128)(2,1)S(1)}, bf16[640,128]{1,0:T(8,128)(2,1)S(1)}, u32[]{:S(2)}, u32[]{:S(2)}) collective-permute-start(bf16[640,128]{1,0:T(8,128)(2,1)S(1)} %slice.9.own_ref), channel_id=1, source_target_pairs={{0,1},{1,0},{2,3},{3,2},{4,5},{5,4},{6,7},{7,6},{8,9},{9,8},{10,11... | collective-permute-start | bytes 491528 | tf_op jit(solution)/shard_map/ppermute | solution.py:369
  180.0 0.7 copy-start.8
  182.6 1.0 copy-start

commit v3 on v2

--- a/solution.py
+++ b/solution.py
@@ -25,7 +25,7 @@
 PACK = 896
 HALF_ROWS = 8 * ROWS
 VMEM = 56 * 1024 * 1024
-ALL_AXES = ("xh", "y", "c", "z", "xl")
+ALL_AXES = ("xh", "y", "c", "zh", "zl", "xl")
 ENC = ("xh", "y", "c")
 F32 = jnp.float32
 BF16 = jnp.bfloat16
@@ -72,19 +72,31 @@
         w2_ref[BLOCKS * ROWS :, :] = jnp.zeros((WIDE - BLOCKS * ROWS, 3 * D2), BF16)
 
 
+def prepare_kernel(length_ref, mel_ref, pay_ref):
+    clip = lax.broadcasted_iota(jnp.int32, (CLIPS, MEL), 0)
+    length = jnp.zeros((CLIPS, MEL), F32)
+    for index in range(CLIPS):
+        length = jnp.where(clip == index, length_ref[index].astype(F32), length)
+    for target in range(HOLDERS):
+        pay_ref[target, :CLIPS] = mel_ref[...]
+        pay_ref[target, CLIPS] = length.astype(BF16)
+
+
 def forward_kernel(
-    pay_ref, w1_ref, b1_ref, own_ref, side_ref, far_ref, both_ref, part_ref, cols_ref, act_ref, slope_ref, w2_ref
+    pay_ref, w1_ref, b1_ref, own_ref, side_ref, far_ref, both_ref, part_ref, cols_ref, act_ref, slope_ref, w2_ref,
+    frames_ref,
 ):
     stack_weights((own_ref, side_ref, far_ref, both_ref), w2_ref)
     spread = (
         lax.broadcasted_iota(jnp.int32, (STEPS, CLIPS), 0) >> 3
         == lax.broadcasted_iota(jnp.int32, (STEPS, CLIPS), 1)
     ).astype(F32).astype(BF16)
-    length = dot(spread, pay_ref[0, STEPS : STEPS + CLIPS, :LANES])
+    length = dot(spread, pay_ref[0, CLIPS])
+    frames_ref[...] = pay_ref[0, :CLIPS].astype(F32).reshape(2 * STEPS, MEL)
     t = (lax.broadcasted_iota(jnp.int32, (STEPS, LANES), 0) & (HALF - 1)).astype(F32)
     live_even, live_odd = 2.0 * t < length, 2.0 * t + 1.0 < length
-    even = jnp.where(live_even, pay_ref[0, :STEPS, :LANES].astype(F32), 0.0)
-    odd = jnp.where(live_odd, pay_ref[0, :STEPS, LANES:].astype(F32), 0.0)
+    even = jnp.where(live_even, frames_ref[pl.ds(0, STEPS, 2), :], 0.0)
+    odd = jnp.where(live_odd, frames_ref[pl.ds(1, STEPS, 2), :], 0.0)
     cols_ref[0, :, :LANES] = shift_down(odd).astype(BF16)
     cols_ref[0, :, LANES : 2 * LANES] = even.astype(BF16)
     cols_ref[0, :, 2 * LANES : 3 * LANES] = odd.astype(BF16)
@@ -111,7 +123,7 @@
     part_ref[0] = total.astype(BF16)
 
 
-def middle_kernel(part_ref, grad_ref, b2_ref, length_ref, owner_col_ref, owner_row_ref, rep_ref, placed_ref):
+def middle_kernel(part_ref, grad_ref, b2_ref, length_ref, owner_col_ref, owner_row_ref, rep_ref, feature_ref):
     pre = part_ref[0].astype(F32)
     for source in range(1, HOLDERS):
         pre = pre + part_ref[source].astype(F32)
@@ -127,11 +139,23 @@
     there = lax.broadcasted_iota(jnp.int32, (STEPS, STEPS), 1)
     same = (owner_col_ref[...] == owner_row_ref[...]) & ((here >> 3) < (there >> 3))
     same = same & ((here & (HALF - 1)) == 0)
-    rank = jnp.sum(jnp.where(same, 1.0, 0.0), axis=0, keepdims=True).astype(jnp.int32)
-    place = lax.broadcasted_iota(jnp.int32, (1, STEPS), 1) & (HALF - 1)
-    place = (owner_row_ref[...] * 2 + rank) * HALF + place
-    wanted = lax.broadcasted_iota(jnp.int32, (SLOTS * HALF, STEPS), 0) == place
-    placed_ref[...] = dot(jnp.where(wanted, 1.0, 0.0).astype(BF16), features).astype(BF16)
+    rank = jnp.sum(jnp.where(same, 1.0, 0.0), axis=0, keepdims=True)
+    slot = owner_row_ref[...].astype(F32) * 2.0 + rank
+    feature_ref[:STEPS, :] = features
+    feature_ref[STEPS:, :] = jnp.zeros((16, D2), BF16)
+    feature_ref[STEPS:, :LANES] = jnp.broadcast_to(slot, (16, LANES)).astype(BF16)
+
+
+def place_kernel(where_ref, got_ref, out_ref):
+    row = lax.broadcasted_iota(jnp.int32, (16, STEPS), 0)
+    lane = lax.broadcasted_iota(jnp.int32, (16, STEPS), 1)
+    same = (row & (HALF - 1)) == (lane & (HALF - 1))
+    first = where_ref[2] * 2
+    for source in range(16):
+        start = source * (STEPS + 16)
+        slot = got_ref[start + STEPS : start + STEPS + 16, :LANES].astype(F32).astype(jnp.int32)
+        wanted = jnp.where(same & (slot == first + (row >> 3)), 1.0, 0.0).astype(BF16)
+        out_ref[source * 16 : (source + 1) * 16, :] = dot(wanted, got_ref[start : start + STEPS, :]).astype(BF16)
 
 
 def backward_kernel(
@@ -197,29 +221,29 @@
             out_ref[target] = total
 
 
-def unpack_kernel(where_ref, own_ref, other_ref, out_ref):
-    first = where_ref[1] == 0
-    for tile in range(15):
-        half, spot = tile // 8, tile % 8
-        rows = slice(spot * ROWS, (spot + 1) * ROWS)
-        own, other = own_ref[rows, :].astype(F32), other_ref[rows, :].astype(F32)
-        picked = jnp.where(first, own, other) if half == 0 else jnp.where(first, other, own)
-        out_ref[:, tile * LANES : (tile + 1) * LANES] = picked
-
-
-def last_kernel(got_ref, weight_ref, bias1_ref, bias2_ref, whole):
-    for tile in range(3):
-        for source in range(16):
-            whole[source * ROWS : (source + 1) * ROWS, :] = got_ref[
-                source, tile * ROWS : (tile + 1) * ROWS, :
-            ].astype(F32)
-        for block in range(10):
-            weight_ref[tile * LANES : (tile + 1) * LANES, block * LANES : (block + 1) * LANES] = whole[
-                block * LANES : (block + 1) * LANES, :
-            ].T
-    pieces = [got_ref[source, 3 * ROWS :, :].astype(F32) for source in range(16)]
-    bias1_ref[...] = jnp.concatenate([piece[0:1, :ROWS] for piece in pieces], axis=1)
-    bias2_ref[...] = jnp.concatenate([pieces[0][1 + tile : 2 + tile, :] for tile in range(D2 // LANES)], axis=1)
+def last_kernel(
+    where_ref, got_ref, bias_ref, own_ref, other_ref, weight_ref, bias1_ref, bias2_ref, conv2_ref, whole
+):
+    for source in range(16):
+        whole[source * ROWS : (source + 1) * ROWS, :] = got_ref[source].astype(F32)
+    for block in range(10):
+        columns = slice(block * LANES, (block + 1) * LANES)
+        weight_ref[:, columns] = whole[columns, :].T
+
+    @pl.when(pl.program_id(0) == 0)
+    def _():
+        pieces = [bias_ref[source].astype(F32) for source in range(16)]
+        bias1 = jnp.concatenate([piece[0:1, :ROWS] for piece in pieces], axis=1)
+        bias1_ref[...] = bias1.reshape(16 * ROWS)
+        bias2 = jnp.concatenate([pieces[0][1 + tile : 2 + tile, :] for tile in range(D2 // LANES)], axis=1)
+        bias2_ref[...] = bias2.reshape(D2)
+        first = where_ref[1] == 0
+        for tile in range(15):
+            half, spot = tile // 8, tile % 8
+            rows = slice(spot * ROWS, (spot + 1) * ROWS)
+            own, other = own_ref[rows, :].astype(F32), other_ref[rows, :].astype(F32)
+            picked = jnp.where(first, own, other) if half == 0 else jnp.where(first, other, own)
+            conv2_ref[:, tile * LANES : (tile + 1) * LANES] = picked
 
 
 def exchange(values, axes):
@@ -240,23 +264,26 @@
 
 def local(mel, lengths, routes, conv1_weight, conv1_bias, conv2_weight, conv2_bias, out_grad):
     x_hi, y, core = lax.axis_index("xh"), lax.axis_index("y"), lax.axis_index("c")
-    where = jnp.stack([x_hi, lax.axis_index("xl")]).astype(jnp.int32)
+    where = jnp.stack([x_hi, lax.axis_index("xl"), (x_hi * HOLDERS + y) * 2 + core]).astype(jnp.int32)
 
     def shape(*dims, dtype=BF16):
         return jax.ShapeDtypeStruct(dims, dtype)
 
+    pay = pl.pallas_call(
+        prepare_kernel,
+        in_specs=[pl.BlockSpec(memory_space=pltpu.SMEM), vmem()],
+        out_specs=vmem(),
+        out_shape=shape(HOLDERS, CLIPS + 1, 2 * HALF, MEL),
+        compiler_params=params(),
+        name="mel_payload",
+    )(lengths, mel)
+    got_pay = exchange(pay, "y")
     weights = [
         conv2_weight,
         lax.ppermute(conv2_weight, "c", [(0, 1), (1, 0)]),
-        lax.ppermute(conv2_weight, "xh", [(0, 1), (1, 0)]),
-        lax.ppermute(conv2_weight, ("xh", "c"), [(0, 3), (3, 0), (1, 2), (2, 1)]),
+        lax.ppermute(conv2_weight, ("xh", "xl"), [(0, 3), (3, 0), (1, 2), (2, 1)]),
+        lax.ppermute(conv2_weight, ("xh", "c", "xl"), [(i, 7 - i) for i in range(8)]),
     ]
-    lengths_bf = lengths.astype(BF16)
-    pay = jnp.concatenate(
-        [mel.reshape(STEPS, 2 * MEL), jnp.broadcast_to(lengths_bf[:, None], (CLIPS, 2 * MEL))], axis=0
-    )
-    pay_rows = pay.shape[0]
-    got_pay = exchange(spread_to(pay, HOLDERS), "y")
 
     w1, b1 = [], []
     for flip_x, flip_c in ((0, 0), (0, 1), (1, 0), (1, 1)):
@@ -271,7 +298,7 @@
         forward_kernel,
         grid=(HOLDERS,),
         in_specs=[
-            pl.BlockSpec((1, pay_rows, 2 * MEL), lambda i: (i, 0, 0)),
+            pl.BlockSpec((1, CLIPS + 1, 2 * HALF, MEL), lambda i: (i, 0, 0, 0)),
             pl.BlockSpec((3 * MEL, WIDE), lambda i: (0, 0)),
             pl.BlockSpec((1, WIDE), lambda i: (0, 0)),
             *[pl.BlockSpec((ROWS, 3 * D2), lambda i: (0, 0))] * BLOCKS,
@@ -288,18 +315,18 @@
             shape(HOLDERS, 3, STEPS, WIDE),
             shape(HOLDERS, 2, STEPS, WIDE, dtype=F32),
         ],
-        scratch_shapes=[pltpu.VMEM((WIDE, 3 * D2), BF16)],
+        scratch_shapes=[pltpu.VMEM((WIDE, 3 * D2), BF16), pltpu.VMEM((2 * STEPS, MEL), F32)],
         compiler_params=params("arbitrary"),
         name="stem_forward",
-    )(got_pay.reshape(HOLDERS, pay_rows, 2 * MEL), w1, b1, *weights)
+    )(got_pay, w1, b1, *weights)
 
     got_parts = exchange(parts, "y")
     owner = jnp.repeat(routes[:, 0], HALF)
-    rep, placed = pl.pallas_call(
+    rep, features = pl.pallas_call(
         middle_kernel,
         in_specs=[vmem()] * 6,
         out_specs=[vmem()] * 2,
-        out_shape=[shape(HOLDERS, STEPS, D2), shape(SLOTS * HALF, D2)],
+        out_shape=[shape(HOLDERS, STEPS, D2), shape(STEPS + 16, D2)],
         compiler_params=params(),
         name="stem_middle",
     )(
@@ -311,7 +338,6 @@
         owner[None],
     )
     got_grad = exchange(rep, "y")
-    packed = exchange(placed.reshape(16, 2 * HALF, D2), ENC)
 
     pair = lambda i: (i, 0, 0)
     pair4 = lambda i: (i, 0, 0, 0)
@@ -337,10 +363,8 @@
             pltpu.VMEM((1, D2), F32),
         ],
         compiler_params=params("arbitrary"),
-        cost_estimate=pl.CostEstimate(flops=24 * 10**8, bytes_accessed=8 * 10**6, transcendentals=0),
         name="stem_backward",
     )(where, got_grad, *weights, cols, acts, slopes)
-    send, packed = lax.optimization_barrier((send, packed))
     got = lax.ppermute(send, "c", [(0, 1), (1, 0)])
     quarters = exchange((keep + got.astype(F32)).astype(BF16).reshape(4, PACK, LANES), ("xh", "xl"))
 
@@ -355,42 +379,55 @@
         )(values)
 
     half = summed(quarters, PACK, LANES)
-    pieces = exchange(half.reshape(16, PACK // 16, LANES), "z")
-    half = exchange(summed(pieces, 16, PACK // 16, LANES), "z").reshape(PACK, LANES)
+    half, features = lax.optimization_barrier((half, features))
+    got_features = lax.all_gather(features, ENC, axis=0, tiled=True)
+    quarter = PACK // 4
+    near = summed(exchange(half.reshape(4, quarter, LANES), "zl"), 4, quarter, LANES)
+    far = summed(exchange(near, "zh"), 4, quarter, LANES)
+    half = exchange(far, "zl").reshape(PACK, LANES)
     shares = exchange(spread_to(half[HALF_ROWS:], 16), ENC)
     own = half[:HALF_ROWS]
-    conv2_rows_grad = pl.pallas_call(
-        unpack_kernel,
-        in_specs=[pl.BlockSpec(memory_space=pltpu.SMEM), vmem(), vmem()],
+    other = lax.ppermute(own, "xl", [(0, 1), (1, 0)])
+    packed = pl.pallas_call(
+        place_kernel,
+        in_specs=[pl.BlockSpec(memory_space=pltpu.SMEM), vmem()],
         out_specs=vmem(),
-        out_shape=shape(ROWS, 3 * D2, dtype=F32),
+        out_shape=shape(SLOTS * HALF, D2),
         compiler_params=params(),
-        name="conv2_unpack",
-    )(where, own, lax.ppermute(own, "xl", [(0, 1), (1, 0)]))
-    weight_grad, bias_grad, second_bias_grad = pl.pallas_call(
+        name="features_place",
+    )(where, got_features)
+    shares, packed = lax.optimization_barrier((shares, packed))
+    weight_grad, bias_grad, second_bias_grad, conv2_rows_grad = pl.pallas_call(
         last_kernel,
-        in_specs=[vmem()],
-        out_specs=[vmem()] * 3,
+        grid=(3,),
+        in_specs=[
+            pl.BlockSpec(memory_space=pltpu.SMEM),
+            pl.BlockSpec((16, ROWS, LANES), lambda i: (0, i, 0)),
+            pl.BlockSpec((16, 16, LANES), lambda i: (0, 3 * ROWS // 16, 0)),
+            pl.BlockSpec((HALF_ROWS, LANES), lambda i: (0, 0)),
+            pl.BlockSpec((HALF_ROWS, LANES), lambda i: (0, 0)),
+        ],
+        out_specs=[
+            pl.BlockSpec((LANES, 16 * ROWS), lambda i: (i, 0)),
+            pl.BlockSpec((16 * ROWS,), lambda i: (0,)),
+            pl.BlockSpec((D2,), lambda i: (0,)),
+            pl.BlockSpec((ROWS, 3 * D2), lambda i: (0, 0)),
+        ],
         out_shape=[
             shape(3 * MEL, 16 * ROWS, dtype=F32),
-            shape(1, 16 * ROWS, dtype=F32),
-            shape(1, D2, dtype=F32),
+            shape(16 * ROWS, dtype=F32),
+            shape(D2, dtype=F32),
+            shape(ROWS, 3 * D2, dtype=F32),
         ],
         scratch_shapes=[pltpu.VMEM((16 * ROWS, LANES), F32)],
-        compiler_params=params(),
-        name="conv1_unpack",
-    )(shares)
-    return (
-        packed.reshape(SLOTS, HALF, D2),
-        weight_grad,
-        bias_grad[0],
-        second_bias_grad[0],
-        conv2_rows_grad,
-    )
+        compiler_params=params("arbitrary"),
+        name="gradient_unpack",
+    )(where, shares, shares, own, other)
+    return packed.reshape(SLOTS, HALF, D2), weight_grad, bias_grad, second_bias_grad, conv2_rows_grad
 
 
 def solution(mesh):
-    fine = Mesh(mesh.devices.reshape(2, 4, 2, 16, 2), ALL_AXES)
+    fine = Mesh(mesh.devices.reshape(2, 4, 2, 4, 4, 2), ALL_AXES)
     placed = (
         P(ALL_AXES, None, None),
         P(ALL_AXES),

time: 191 us -> 194 us (1.016)
  between operations: 0.84 us -> 14.3 us
  starting transfers between devices: 48.8 us -> 42.1 us
  Pallas kernels: 24.2 us -> 29.6 us
  waiting for transfers between devices: 33.5 us -> 29.3 us
  other arithmetic: 5.79 us -> 2.33 us
    ppermute x3, waiting for transfers between devices: 14 us -> 0.01 us  [the longest x1 0.01 us: local(): lax.ppermute(conv2_weight, ('xh', 'c', 'xl'), [(i, 7 - i) for i in range(...]
    all_to_all x5 -> x4, starting transfers between devices: 28 us -> 18.5 us  [exchange(): return lax.all_to_all(values, axes, split_axis=0, concat_axis=0, tiled=True)]
    all_to_all x5 -> x4, waiting for transfers between devices: 17.2 us -> 25 us  [exchange(): return lax.all_to_all(values, axes, split_axis=0, concat_axis=0, tiled=True)]
    pallas_call x2 -> x3, Pallas kernels: 4.73 us -> 8.56 us  [the longest x1 3.87 us: local(): pl.pallas_call(last_kernel, grid=(3,), in_specs=[pl.BlockSpec(memory_spac...]
    ppermute x1, starting transfers between devices: 3.06 us -> 5.97 us  [local(): got = lax.ppermute(send, 'c', [(0, 1), (1, 0)])]
    pallas_call x2 -> x0, other arithmetic: 2.59 us -> none  [local(): pl.pallas_call(last_kernel, in_specs=[vmem()], out_specs=[vmem()] * 3, ou...]
    all_gather x0 -> x1, waiting for transfers between devices: none -> 2 us  [local(): got_features = lax.all_gather(features, ENC, axis=0, tiled=True)]
    pallas_call x2 -> x3, Pallas kernels: 3.65 us -> 5.29 us  [summed(): pl.pallas_call(sum_kernel, in_specs=[vmem()], out_specs=vmem(), out_shape...]
  transfers between devices with their start and end apart: 10 -> 10, of which waited for: 6 -> 6; matrix products, arithmetic and copies ran while one was open for 5% -> 4% of each run, Pallas kernels for 5% -> 4%
where the time goes in v3:
time: 194 us; the launch traced here: 193 us
  blocking collectives  62.4 us (32%)
  starting transfers between devices  42.1 us (22%)
  Pallas kernels  29.6 us (15%)
  waiting for transfers between devices  29.3 us (15%)
  between operations  14.3 us (7%)
  local copies, waits for them, and re-layouts  12.9 us (7%)
  other arithmetic  2.33 us (1%)
    all_to_all x4, blocking collectives, exchange(): return lax.all_to_all(values, axes, split_axis=0, concat_axis=0, tiled=True)  62.4 us
    all_to_all x4, waiting for transfers between devices, exchange(): return lax.all_to_all(values, axes, split_axis=0, concat_axis=0, tiled=True)  25 us
    all_to_all x4, starting transfers between devices, exchange(): return lax.all_to_all(values, axes, split_axis=0, concat_axis=0, tiled=True)  18.5 us
    pallas_call x1, Pallas kernels, local(): pl.pallas_call(backward_kernel, grid=(HOLDERS // 2,), in_specs=[pl.BlockS...  7.54 us
    ppermute x1, starting transfers between devices, local(): lax.ppermute(conv2_weight, ('xh', 'xl'), [(0, 3), (3, 0), (1, 2), (2, 1)])  7.48 us
    ppermute x1, starting transfers between devices, local(): got = lax.ppermute(send, 'c', [(0, 1), (1, 0)])  5.97 us
    pallas_call x1, Pallas kernels, local(): pl.pallas_call(forward_kernel, grid=(HOLDERS,), in_specs=[pl.BlockSpec((1...  5.8 us
    ppermute x1, starting transfers between devices, local(): lax.ppermute(conv2_weight, ('xh', 'c', 'xl'), [(i, 7 - i) for i in range(...  5.78 us
  transfers between devices with their start and end apart: 10, of which 6 were waited for; matrix products, arithmetic and copies ran while one was open for 4% of the time, Pallas kernels for 4%

profile of v3, /device:TPU:1, one launch (start us, length us, event | category | flops | bytes accessed | tf_op | source)
XLA Modules:
  0.0 192.9 jit_solution(13593369357644803961)
XLA Ops:
  7.2 5.8 %collective-permute-start.2 = (bf16[80,1920]{1,0:T(8,128)(2,1)}, bf16[80,1920]{1,0:T(8,128)(2,1)S(1)}, u32[]{:S(2)}, u32[]{:S(2)}) collective-permute-start(bf16[80,1920]{1,0:T(8,128)(2,1)} %own_ref.3), channel_id=1, source_target_pairs={{0,289},{1,288},{32,257},{33,256},{256,33},{257,32},{288,1},{289,0... | collective-permute-start | bytes 921608 | tf_op jit(solution)/shard_map/ppermute | solution.py:285
  13.0 7.5 %collective-permute-start.1 = (bf16[80,1920]{1,0:T(8,128)(2,1)}, bf16[80,1920]{1,0:T(8,128)(2,1)S(1)}, u32[]{:S(2)}, u32[]{:S(2)}) collective-permute-start(bf16[80,1920]{1,0:T(8,128)(2,1)} %own_ref.3), channel_id=1, source_target_pairs={{0,257},{257,0},{1,256},{256,1},{2,259},{259,2},{3,258},{258,3},{4... | collective-permute-start | bytes 921608 | tf_op jit(solution)/shard_map/ppermute | solution.py:284
  20.4 1.9 collective-permute-start
  22.4 1.6 mel_payload.1
  24.0 3.5 %all-to-all-start = ((bf16[4,17,16,128]{3,2,1,0:T(8,128)(2,1)}), bf16[4,17,16,128]{3,2,1,0:T(8,128)(2,1)S(1)}, u32[]{:S(2)}, u32[]{:S(2)}) async-start(bf16[4,17,16,128]{3,2,1,0:T(8,128)(2,1)} %mel_payload.1), calls=%async_computation | async-start | bytes 557056 | tf_op jit(solution)/shard_map/all_to_all | solution.py:250
  27.5 0.9 fusion
  28.4 0.1 concatenate.7
  28.5 0.6 broadcast_in_dim.26.b1_ref
  29.0 1.4 constant_dynamic-slice_fusion
  30.5 1.0 concatenate.6.w1_ref
  31.5 2.1 %all-to-all-done.pay_ref = bf16[4,17,16,128]{3,2,1,0:T(8,128)(2,1)S(1)} async-done(((bf16[4,17,16,128]{3,2,1,0:T(8,128)(2,1)}), bf16[4,17,16,128]{3,2,1,0:T(8,128)(2,1)S(1)}, u32[]{:S(2)}, u32[]{:S(2)}) %all-to-all-start) | async-done | bytes 278560 | tf_op jit(solution)/shard_map/all_to_all | solution.py:250
  33.6 0.7 copy-done.6
  34.3 0.1 copy-done.3
  34.4 0.1 copy-done.4
  34.5 0.7 copy-done.5
  35.2 5.8 %stem_forward.1 = (bf16[4,128,640]{2,1,0:T(8,128)(2,1)}, bf16[4,128,512]{2,1,0:T(8,128)(2,1)}, bf16[4,3,128,384]{3,2,1,0:T(8,128)(2,1)}, f32[4,2,128,384]{3,2,1,0:T(8,128)}) custom-call(bf16[4,17,16,128]{3,2,1,0:T(8,128)(2,1)} %copy-done.6, bf16[384,384]{1,0:T(8,128)(2,1)} %concatenate.6.w1_ref, f32[1,384]{1,0:T(1,128)} %broadcast_in_dim.26.b1_ref, ...), custom_call_target="tpu_custom_call" | custom-call | tf_op jit(solution)/shard_map/stem_forward/pallas_call | solution.py:297
  41.0 3.5 %all-to-all-start.1 = ((bf16[4,128,640]{2,1,0:T(8,128)(2,1)}), bf16[4,128,640]{2,1,0:T(8,128)(2,1)S(1)}, u32[]{:S(2)}, u32[]{:S(2)}) async-start(bf16[4,128,640]{2,1,0:T(8,128)(2,1)} %get-tuple-element.21), calls=%async_computation.1 | async-start | bytes 1310720 | tf_op jit(solution)/shard_map/all_to_all | solution.py:250
  44.6 0.7 broadcast_in_dim_reshape.11.owner_row_ref
  45.3 0.7 broadcast_in_dim_reshape.13.owner_col_ref
  46.0 0.6 broadcast_in_dim.27.b2_ref
  46.7 0.7 broadcast_in_dim_reshape.12.length_ref
  47.4 6.1 %all-to-all-done.1.part_ref = bf16[4,128,640]{2,1,0:T(8,128)(2,1)S(1)} async-done(((bf16[4,128,640]{2,1,0:T(8,128)(2,1)}), bf16[4,128,640]{2,1,0:T(8,128)(2,1)S(1)}, u32[]{:S(2)}, u32[]{:S(2)}) %all-to-all-start.1) | async-done | bytes 655392 | tf_op jit(solution)/shard_map/all_to_all | solution.py:250
  53.5 0.8 copy-done.1
  54.3 2.5 %stem_middle.1 = (bf16[4,128,640]{2,1,0:T(8,128)(2,1)}, bf16[144,640]{1,0:T(8,128)(2,1)}) custom-call(bf16[4,128,640]{2,1,0:T(8,128)(2,1)} %copy-done.1, bf16[128,640]{1,0:T(8,128)(2,1)} %bitcast.14, f32[1,640]{1,0:T(1,128)} %broadcast_in_dim.27.b2_ref, f32[128,1]{1,0:T(8,128)} %broadcast_in_dim_reshape.12.length_ref, ...), custom_call_target="tpu_custom_call" | custom-call | tf_op jit(solution)/shard_map/stem_middle/pallas_call | solution.py:325
  56.8 3.5 %all-to-all-start.2 = ((bf16[4,128,640]{2,1,0:T(8,128)(2,1)}), bf16[4,128,640]{2,1,0:T(8,128)(2,1)S(1)}, u32[]{:S(2)}, u32[]{:S(2)}) async-start(bf16[4,128,640]{2,1,0:T(8,128)(2,1)} %get-tuple-element.22), calls=%async_computation.2 | async-start | bytes 1310720 | tf_op jit(solution)/shard_map/all_to_all | solution.py:250
  60.3 0.6 pad_add_fusion.where_ref
  60.9 7.1 %all-to-all-done.2.grad_ref = bf16[4,128,640]{2,1,0:T(8,128)(2,1)S(1)} async-done(((bf16[4,128,640]{2,1,0:T(8,128)(2,1)}), bf16[4,128,640]{2,1,0:T(8,128)(2,1)S(1)}, u32[]{:S(2)}, u32[]{:S(2)}) %all-to-all-start.2) | async-done | bytes 655392 | tf_op jit(solution)/shard_map/all_to_all | solution.py:250
  68.0 0.8 copy-done.2
  68.8 7.5 %stem_backward.1 = (f32[2,2,896,128]{3,2,1,0:T(8,128)}, bf16[2,2,896,128]{3,2,1,0:T(8,128)(2,1)}) custom-call(s32[3]{0:T(128)} %pad_add_fusion.where_ref, bf16[4,128,640]{2,1,0:T(8,128)(2,1)} %copy-done.2, bf16[80,1920]{1,0:T(8,128)(2,1)} %own_ref.3, bf16[80,1920]{1,0:T(8,128)(2,1)} %copy-done.5, bf16[80,1920]{1,0:T(8,128)(2,1)} %copy-done.4, ...), custom_call_target="tpu_custom_call" | custom-call | tf_op jit(solution)/shard_map/stem_backward/pallas_call | solution.py:345
  76.4 6.0 %collective-permute-start.3 = (bf16[2,2,896,128]{3,2,1,0:T(8,128)(2,1)}, bf16[2,2,896,128]{3,2,1,0:T(8,128)(2,1)S(1)}, u32[]{:S(2)}, u32[]{:S(2)}) collective-permute-start(bf16[2,2,896,128]{3,2,1,0:T(8,128)(2,1)} %get-tuple-element.27), channel_id=1, source_target_pairs={{0,32},{32,0},{1,33},{33,1},{2,34},{34,2},{3,35},{35,3},{4,36},{36... | collective-permute-start | bytes 2752520 | tf_op jit(solution)/shard_map/ppermute | solution.py:368
  82.3 2.3 %collective-permute-done.3 = bf16[2,2,896,128]{3,2,1,0:T(8,128)(2,1)S(1)} collective-permute-done((bf16[2,2,896,128]{3,2,1,0:T(8,128)(2,1)}, bf16[2,2,896,128]{3,2,1,0:T(8,128)(2,1)S(1)}, u32[]{:S(2)}, u32[]{:S(2)}) %collective-permute-start.3) | collective-permute-done | bytes 917536 | tf_op jit(solution)/shard_map/ppermute | solution.py:368
  84.6 1.7 add_convert_fusion
  86.4 16.1 %all_to_all.40.got_ref = bf16[4,896,128]{2,1,0:T(8,128)(2,1)} all-to-all(bf16[4,896,128]{2,1,0:T(8,128)(2,1)S(1)} %bitcast.9), channel_id=1, replica_groups=mesh['xh'=2,'y'=4,'c'=2,'zh'=4,'zl'=4,'xl'=2] {'xh','xl'}, dimensions={0} | all-to-all | bytes 1835008 | tf_op jit(solution)/shard_map/all_to_all | solution.py:250
  102.4 2.0 %gradient_sum.3 = bf16[896,128]{1,0:T(8,128)(2,1)} custom-call(bf16[4,896,128]{2,1,0:T(8,128)(2,1)} %all_to_all.40.got_ref), custom_call_target="tpu_custom_call" | custom-call | tf_op jit(solution)/shard_map/gradient_sum/pallas_call | solution.py:372
  104.4 9.9 %all_to_all.41.got_ref = bf16[4,224,128]{2,1,0:T(8,128)(2,1)} all-to-all(bf16[4,224,128]{2,1,0:T(8,128)(2,1)} %bitcast.12), channel_id=1, replica_groups=mesh['xh'=2,'y'=4,'c'=2,'zh'=4,'zl'=4,'xl'=2] {'zl'}, dimensions={0} | all-to-all | bytes 458752 | tf_op jit(solution)/shard_map/all_to_all | solution.py:250
  114.3 1.7 gradient_sum.4
  116.0 25.9 %all_to_all.42.got_ref = bf16[4,224,128]{2,1,0:T(8,128)(2,1)} all-to-all(bf16[4,224,128]{2,1,0:T(8,128)(2,1)} %gradient_sum.4), channel_id=1, replica_groups=mesh['xh'=2,'y'=4,'c'=2,'zh'=4,'zl'=4,'xl'=2] {'zh'}, dimensions={0} | all-to-all | bytes 458752 | tf_op jit(solution)/shard_map/all_to_all | solution.py:250
  141.9 1.7 gradient_sum.5
  143.5 10.5 %all_to_all.43 = bf16[4,224,128]{2,1,0:T(8,128)(2,1)S(1)} all-to-all(bf16[4,224,128]{2,1,0:T(8,128)(2,1)} %gradient_sum.5), channel_id=1, replica_groups=mesh['xh'=2,'y'=4,'c'=2,'zh'=4,'zl'=4,'xl'=2] {'zl'}, dimensions={0} | all-to-all | bytes 458752 | tf_op jit(solution)/shard_map/all_to_all | solution.py:250
  154.1 1.2 broadcast_in_dim.30
  155.2 8.0 %all-to-all-start.7 = ((bf16[16,256,128]{2,1,0:T(8,128)(2,1)}), bf16[16,256,128]{2,1,0:T(8,128)(2,1)S(1)}, u32[]{:S(2)}, u32[]{:S(2)}) async-start(bf16[16,256,128]{2,1,0:T(8,128)(2,1)} %broadcast_in_dim.30), calls=%async_computation.7 | async-start | bytes 2097152 | tf_op jit(solution)/shard_map/all_to_all | solution.py:250
  163.3 2.4 %collective-permute-start.4 = (bf16[640,128]{1,0:T(8,128)(2,1)S(1)}, bf16[640,128]{1,0:T(8,128)(2,1)S(1)}, u32[]{:S(2)}, u32[]{:S(2)}) collective-permute-start(bf16[640,128]{1,0:T(8,128)(2,1)S(1)} %slice.9.own_ref), channel_id=1, source_target_pairs={{0,1},{1,0},{2,3},{3,2},{4,5},{5,4},{6,7},{7,6},{8,9},{9,8},{10,11... | collective-permute-start | bytes 491528 | tf_op jit(solution)/shard_map/ppermute | solution.py:390
  165.7 2.0 %all-gather.2.cloned.1.call-done.got_ref = bf16[2304,640]{1,0:T(8,128)(2,1)} async-done(((bf16[144,640]{1,0:T(8,128)(2,1)}), bf16[2304,640]{1,0:T(8,128)(2,1)}) %all-gather.2.cloned.1.call-update) | async-done | bytes 2949136 | tf_op jit(solution)/shard_map/all_gather | solution.py:383
  167.7 3.1 %features_place.1 = bf16[256,640]{1,0:T(8,128)(2,1)} custom-call(s32[3]{0:T(128)} %pad_add_fusion.where_ref, bf16[2304,640]{1,0:T(8,128)(2,1)} %all-gather.2.cloned.1.call-done.got_ref), custom_call_target="tpu_custom_call" | custom-call | tf_op jit(solution)/shard_map/features_place/pallas_call | solution.py:391
  170.8 9.7 %all-to-all-done.7.got_ref.bias_ref = bf16[16,256,128]{2,1,0:T(8,128)(2,1)S(1)} async-done(((bf16[16,256,128]{2,1,0:T(8,128)(2,1)}), bf16[16,256,128]{2,1,0:T(8,128)(2,1)S(1)}, u32[]{:S(2)}, u32[]{:S(2)}) %all-to-all-start.7) | async-done | bytes 1048608 | tf_op jit(solution)/shard_map/all_to_all | solution.py:250
  180.6 1.0 copy-done
  181.5 0.7 copy-done.8
  182.2 3.9 %gradient_unpack.1 = (f32[384,1280]{1,0:T(8,128)}, f32[1280]{0:T(1024)}, f32[640]{0:T(1024)}, f32[80,1920]{1,0:T(8,128)}) custom-call(s32[3]{0:T(128)} %pad_add_fusion.where_ref, bf16[16,256,128]{2,1,0:T(8,128)(2,1)} %copy-done, bf16[16,256,128]{2,1,0:T(8,128)(2,1)} %copy-done, bf16[640,128]{1,0:T(8,128)(2,1)} %copy-done.7, bf16[640,128]{1,0:T(8,128)(2,1)} %copy-done.8), custom_call_target="tpu_custom_call" | custom-call | tf_op jit(solution)/shard_map/gradient_unpack/pallas_call | solution.py:400
  (29 shorter events, 0.3 us)
Async XLA Ops:
  7.2 26.4 %collective-permute-start.2 = (bf16[80,1920]{1,0:T(8,128)(2,1)}, bf16[80,1920]{1,0:T(8,128)(2,1)S(1)}, u32[]{:S(2)}, u32[]{:S(2)}) collective-permute-start(bf16[80,1920]{1,0:T(8,128)(2,1)} %own_ref.3), channel_id=1, source_target_pairs={{0,289},{1,288},{32,257},{33,256},{256,33},{257,32},{288,1},{289,0... | collective-permute-start | bytes 921608 | tf_op jit(solution)/shard_map/ppermute | solution.py:285
  13.0 20.6 %collective-permute-start.1 = (bf16[80,1920]{1,0:T(8,128)(2,1)}, bf16[80,1920]{1,0:T(8,128)(2,1)S(1)}, u32[]{:S(2)}, u32[]{:S(2)}) collective-permute-start(bf16[80,1920]{1,0:T(8,128)(2,1)} %own_ref.3), channel_id=1, source_target_pairs={{0,257},{257,0},{1,256},{256,1},{2,259},{259,2},{3,258},{258,3},{4... | collective-permute-start | bytes 921608 | tf_op jit(solution)/shard_map/ppermute | solution.py:284
  20.4 13.1 %collective-permute-start = (bf16[80,1920]{1,0:T(8,128)(2,1)}, bf16[80,1920]{1,0:T(8,128)(2,1)S(1)}, u32[]{:S(2)}, u32[]{:S(2)}) collective-permute-start(bf16[80,1920]{1,0:T(8,128)(2,1)} %own_ref.3), channel_id=1, source_target_pairs={{0,32},{32,0},{1,33},{33,1},{2,34},{34,2},{3,35},{35,3},{4,36},{36... | collective-permute-start | bytes 921608 | tf_op jit(solution)/shard_map/ppermute | solution.py:283
  24.0 9.6 %all-to-all-start = ((bf16[4,17,16,128]{3,2,1,0:T(8,128)(2,1)}), bf16[4,17,16,128]{3,2,1,0:T(8,128)(2,1)S(1)}, u32[]{:S(2)}, u32[]{:S(2)}) async-start(bf16[4,17,16,128]{3,2,1,0:T(8,128)(2,1)} %mel_payload.1), calls=%async_computation | async-start | bytes 557056 | tf_op jit(solution)/shard_map/all_to_all | solution.py:250
  30.5 14.1 %copy-start.10 = (s32[16]{0:T(128)S(1)}, s32[16]{0:T(128)}, u32[]{:S(2)}) copy-start(s32[16]{0:T(128)} %length_ref.1) | copy-start | bytes 196
  30.5 14.1 %copy-start.11 = (s32[16,1]{0,1:T(1,128)S(1)}, s32[16,1]{0,1:T(1,128)}, u32[]{:S(2)}) copy-start(s32[16,1]{0,1:T(1,128)} %param.10) | copy-start | bytes 196
  30.5 15.5 %copy-start.9 = (f32[640]{0:T(1024)S(1)}, f32[640]{0:T(1024)}, u32[]{:S(2)}) copy-start(f32[640]{0:T(1024)} %param.14) | copy-start | bytes 7684
  33.5 0.7 copy-start.6
  33.6 0.8 copy-start.3
  33.6 0.9 copy-start.4
  34.5 0.7 copy-start.5
  41.0 12.4 %all-to-all-start.1 = ((bf16[4,128,640]{2,1,0:T(8,128)(2,1)}), bf16[4,128,640]{2,1,0:T(8,128)(2,1)S(1)}, u32[]{:S(2)}, u32[]{:S(2)}) async-start(bf16[4,128,640]{2,1,0:T(8,128)(2,1)} %get-tuple-element.21), calls=%async_computation.1 | async-start | bytes 1310720 | tf_op jit(solution)/shard_map/all_to_all | solution.py:250
  53.5 0.8 copy-start.1
  56.8 11.2 %all-to-all-start.2 = ((bf16[4,128,640]{2,1,0:T(8,128)(2,1)}), bf16[4,128,640]{2,1,0:T(8,128)(2,1)S(1)}, u32[]{:S(2)}, u32[]{:S(2)}) async-start(bf16[4,128,640]{2,1,0:T(8,128)(2,1)} %get-tuple-element.22), calls=%async_computation.2 | async-start | bytes 1310720 | tf_op jit(solution)/shard_map/all_to_all | solution.py:250
  60.2 107.5 %all-gather.2.cloned.1.call-start = ((), (), s32[]{:S(2)}) async-start(), calls=%async_computation.8 | async-start | bytes 3133440 | tf_op jit(solution)/shard_map/all_gather | solution.py:383
  68.0 0.8 copy-start.2
  76.4 8.3 %collective-permute-start.3 = (bf16[2,2,896,128]{3,2,1,0:T(8,128)(2,1)}, bf16[2,2,896,128]{3,2,1,0:T(8,128)(2,1)S(1)}, u32[]{:S(2)}, u32[]{:S(2)}) collective-permute-start(bf16[2,2,896,128]{3,2,1,0:T(8,128)(2,1)} %get-tuple-element.27), channel_id=1, source_target_pairs={{0,32},{32,0},{1,33},{33,1},{2,34},{34,2},{3,35},{35,3},{4,36},{36... | collective-permute-start | bytes 2752520 | tf_op jit(solution)/shard_map/ppermute | solution.py:368
  155.2 25.3 %all-to-all-start.7 = ((bf16[16,256,128]{2,1,0:T(8,128)(2,1)}), bf16[16,256,128]{2,1,0:T(8,128)(2,1)S(1)}, u32[]{:S(2)}, u32[]{:S(2)}) async-start(bf16[16,256,128]{2,1,0:T(8,128)(2,1)} %broadcast_in_dim.30), calls=%async_computation.7 | async-start | bytes 2097152 | tf_op jit(solution)/shard_map/all_to_all | solution.py:250
  163.3 17.3 %copy-start.7 = (bf16[640,128]{1,0:T(8,128)(2,1)}, bf16[640,128]{1,0:T(8,128)(2,1)S(1)}, u32[]{:S(2)}) copy-start(bf16[640,128]{1,0:T(8,128)(2,1)S(1)} %slice.9.own_ref) | copy-start | bytes 491524
  163.3 17.3 %collective-permute-start.4 = (bf16[640,128]{1,0:T(8,128)(2,1)S(1)}, bf16[640,128]{1,0:T(8,128)(2,1)S(1)}, u32[]{:S(2)}, u32[]{:S(2)}) collective-permute-start(bf16[640,128]{1,0:T(8,128)(2,1)S(1)} %slice.9.own_ref), channel_id=1, source_target_pairs={{0,1},{1,0},{2,3},{3,2},{4,5},{5,4},{6,7},{7,6},{8,9},{9,8},{10,11... | collective-permute-start | bytes 491528 | tf_op jit(solution)/shard_map/ppermute | solution.py:390
  180.5 1.0 copy-start
  181.5 0.7 copy-start.8
Sparse Core Ops, SparseCore 0:
  104.6 63.1 all-gather.1

commit v4 on v3

--- a/solution.py
+++ b/solution.py
@@ -82,11 +82,7 @@
         pay_ref[target, CLIPS] = length.astype(BF16)
 
 
-def forward_kernel(
-    pay_ref, w1_ref, b1_ref, own_ref, side_ref, far_ref, both_ref, part_ref, cols_ref, act_ref, slope_ref, w2_ref,
-    frames_ref,
-):
-    stack_weights((own_ref, side_ref, far_ref, both_ref), w2_ref)
+def first_kernel(pay_ref, w1_ref, b1_ref, cols_ref, act_ref, slope_ref, frames_ref):
     spread = (
         lax.broadcasted_iota(jnp.int32, (STEPS, CLIPS), 0) >> 3
         == lax.broadcasted_iota(jnp.int32, (STEPS, CLIPS), 1)
@@ -117,10 +113,15 @@
     act_ref[0, 0] = act_prior
     act_ref[0, 1] = act_even
     act_ref[0, 2] = act_odd
-    total = dot(act_prior, w2_ref[:, :D2])
-    total = total + dot(act_even, w2_ref[:, D2 : 2 * D2])
-    total = total + dot(act_odd, w2_ref[:, 2 * D2 :])
-    part_ref[0] = total.astype(BF16)
+
+
+def second_kernel(act_ref, own_ref, side_ref, far_ref, both_ref, part_ref, w2_ref):
+    stack_weights((own_ref, side_ref, far_ref, both_ref), w2_ref)
+    rows = 2 * STEPS
+    total = dot(act_ref[:, 0].reshape(rows, WIDE), w2_ref[:, :D2])
+    total = total + dot(act_ref[:, 1].reshape(rows, WIDE), w2_ref[:, D2 : 2 * D2])
+    total = total + dot(act_ref[:, 2].reshape(rows, WIDE), w2_ref[:, 2 * D2 :])
+    part_ref[...] = total.astype(BF16).reshape(2, STEPS, D2)
 
 
 def middle_kernel(part_ref, grad_ref, b2_ref, length_ref, owner_col_ref, owner_row_ref, rep_ref, feature_ref):
@@ -140,22 +141,15 @@
     same = (owner_col_ref[...] == owner_row_ref[...]) & ((here >> 3) < (there >> 3))
     same = same & ((here & (HALF - 1)) == 0)
     rank = jnp.sum(jnp.where(same, 1.0, 0.0), axis=0, keepdims=True)
-    slot = owner_row_ref[...].astype(F32) * 2.0 + rank
-    feature_ref[:STEPS, :] = features
-    feature_ref[STEPS:, :] = jnp.zeros((16, D2), BF16)
-    feature_ref[STEPS:, :LANES] = jnp.broadcast_to(slot, (16, LANES)).astype(BF16)
-
-
-def place_kernel(where_ref, got_ref, out_ref):
-    row = lax.broadcasted_iota(jnp.int32, (16, STEPS), 0)
-    lane = lax.broadcasted_iota(jnp.int32, (16, STEPS), 1)
-    same = (row & (HALF - 1)) == (lane & (HALF - 1))
-    first = where_ref[2] * 2
-    for source in range(16):
-        start = source * (STEPS + 16)
-        slot = got_ref[start + STEPS : start + STEPS + 16, :LANES].astype(F32).astype(jnp.int32)
-        wanted = jnp.where(same & (slot == first + (row >> 3)), 1.0, 0.0).astype(BF16)
-        out_ref[source * 16 : (source + 1) * 16, :] = dot(wanted, got_ref[start : start + STEPS, :]).astype(BF16)
+    place = lax.broadcasted_iota(jnp.int32, (1, STEPS), 1) & (HALF - 1)
+    place = (owner_row_ref[...] * 2 + rank.astype(jnp.int32)) * HALF + place
+    wanted = lax.broadcasted_iota(jnp.int32, (SLOTS * HALF, STEPS), 0) == place
+    placed = dot(jnp.where(wanted, 1.0, 0.0).astype(BF16), features).astype(BF16)
+    for target in range(16):
+        for tile in range(D2 // LANES):
+            feature_ref[target, tile * 16 : (tile + 1) * 16, :] = placed[
+                target * 16 : (target + 1) * 16, tile * LANES : (tile + 1) * LANES
+            ]
 
 
 def backward_kernel(
@@ -222,7 +216,8 @@
 
 
 def last_kernel(
-    where_ref, got_ref, bias_ref, own_ref, other_ref, weight_ref, bias1_ref, bias2_ref, conv2_ref, whole
+    where_ref, got_ref, feature_ref, bias_ref, own_ref, other_ref,
+    weight_ref, bias1_ref, bias2_ref, conv2_ref, packed_ref, whole,
 ):
     for source in range(16):
         whole[source * ROWS : (source + 1) * ROWS, :] = got_ref[source].astype(F32)
@@ -237,6 +232,11 @@
         bias1_ref[...] = bias1.reshape(16 * ROWS)
         bias2 = jnp.concatenate([pieces[0][1 + tile : 2 + tile, :] for tile in range(D2 // LANES)], axis=1)
         bias2_ref[...] = bias2.reshape(D2)
+        for source in range(16):
+            for tile in range(D2 // LANES):
+                packed_ref[source * 16 : (source + 1) * 16, tile * LANES : (tile + 1) * LANES] = feature_ref[
+                    source, tile * 16 : (tile + 1) * 16, :
+                ]
         first = where_ref[1] == 0
         for tile in range(15):
             half, spot = tile // 8, tile % 8
@@ -294,31 +294,42 @@
     w1 = jnp.concatenate(w1 + [jnp.zeros((3 * MEL, gap), BF16)], axis=1)
     b1 = jnp.concatenate(b1 + [jnp.zeros((gap,), F32)])[None]
 
-    parts, cols, acts, slopes = pl.pallas_call(
-        forward_kernel,
+    pair = lambda i: (i, 0, 0)
+    pair4 = lambda i: (i, 0, 0, 0)
+    weight_spec = pl.BlockSpec((ROWS, 3 * D2), lambda i: (0, 0))
+    cols, acts, slopes = pl.pallas_call(
+        first_kernel,
         grid=(HOLDERS,),
         in_specs=[
-            pl.BlockSpec((1, CLIPS + 1, 2 * HALF, MEL), lambda i: (i, 0, 0, 0)),
+            pl.BlockSpec((1, CLIPS + 1, 2 * HALF, MEL), pair4),
             pl.BlockSpec((3 * MEL, WIDE), lambda i: (0, 0)),
             pl.BlockSpec((1, WIDE), lambda i: (0, 0)),
-            *[pl.BlockSpec((ROWS, 3 * D2), lambda i: (0, 0))] * BLOCKS,
         ],
         out_specs=[
-            pl.BlockSpec((1, STEPS, D2), lambda i: (i, 0, 0)),
-            pl.BlockSpec((1, STEPS, 4 * LANES), lambda i: (i, 0, 0)),
-            pl.BlockSpec((1, 3, STEPS, WIDE), lambda i: (i, 0, 0, 0)),
-            pl.BlockSpec((1, 2, STEPS, WIDE), lambda i: (i, 0, 0, 0)),
+            pl.BlockSpec((1, STEPS, 4 * LANES), pair),
+            pl.BlockSpec((1, 3, STEPS, WIDE), pair4),
+            pl.BlockSpec((1, 2, STEPS, WIDE), pair4),
         ],
         out_shape=[
-            shape(HOLDERS, STEPS, D2),
             shape(HOLDERS, STEPS, 4 * LANES),
             shape(HOLDERS, 3, STEPS, WIDE),
             shape(HOLDERS, 2, STEPS, WIDE, dtype=F32),
         ],
-        scratch_shapes=[pltpu.VMEM((WIDE, 3 * D2), BF16), pltpu.VMEM((2 * STEPS, MEL), F32)],
+        scratch_shapes=[pltpu.VMEM((2 * STEPS, MEL), F32)],
         compiler_params=params("arbitrary"),
-        name="stem_forward",
-    )(got_pay, w1, b1, *weights)
+        cost_estimate=pl.CostEstimate(flops=302 * 10**6, bytes_accessed=10**7, transcendentals=8 * 10**5),
+        name="stem_first",
+    )(got_pay, w1, b1)
+    parts = pl.pallas_call(
+        second_kernel,
+        grid=(HOLDERS // 2,),
+        in_specs=[pl.BlockSpec((2, 3, STEPS, WIDE), pair4), *[weight_spec] * BLOCKS],
+        out_specs=pl.BlockSpec((2, STEPS, D2), pair),
+        out_shape=shape(HOLDERS, STEPS, D2),
+        scratch_shapes=[pltpu.VMEM((WIDE, 3 * D2), BF16)],
+        compiler_params=params("arbitrary"),
+        name="stem_second",
+    )(acts, *weights)
 
     got_parts = exchange(parts, "y")
     owner = jnp.repeat(routes[:, 0], HALF)
@@ -326,7 +337,7 @@
         middle_kernel,
         in_specs=[vmem()] * 6,
         out_specs=[vmem()] * 2,
-        out_shape=[shape(HOLDERS, STEPS, D2), shape(STEPS + 16, D2)],
+        out_shape=[shape(HOLDERS, STEPS, D2), shape(16, ROWS, LANES)],
         compiler_params=params(),
         name="stem_middle",
     )(
@@ -339,8 +350,6 @@
     )
     got_grad = exchange(rep, "y")
 
-    pair = lambda i: (i, 0, 0)
-    pair4 = lambda i: (i, 0, 0, 0)
     whole = lambda i: (0, 0, 0, 0)
     keep, send = pl.pallas_call(
         backward_kernel,
@@ -348,7 +357,7 @@
         in_specs=[
             pl.BlockSpec(memory_space=pltpu.SMEM),
             pl.BlockSpec((2, STEPS, D2), pair),
-            *[pl.BlockSpec((ROWS, 3 * D2), lambda i: (0, 0))] * BLOCKS,
+            *[weight_spec] * BLOCKS,
             pl.BlockSpec((2, STEPS, 4 * LANES), pair),
             pl.BlockSpec((2, 3, STEPS, WIDE), pair4),
             pl.BlockSpec((2, 2, STEPS, WIDE), pair4),
@@ -379,31 +388,21 @@
         )(values)
 
     half = summed(quarters, PACK, LANES)
-    half, features = lax.optimization_barrier((half, features))
-    got_features = lax.all_gather(features, ENC, axis=0, tiled=True)
     quarter = PACK // 4
     near = summed(exchange(half.reshape(4, quarter, LANES), "zl"), 4, quarter, LANES)
     far = summed(exchange(near, "zh"), 4, quarter, LANES)
     half = exchange(far, "zl").reshape(PACK, LANES)
-    shares = exchange(spread_to(half[HALF_ROWS:], 16), ENC)
     own = half[:HALF_ROWS]
     other = lax.ppermute(own, "xl", [(0, 1), (1, 0)])
-    packed = pl.pallas_call(
-        place_kernel,
-        in_specs=[pl.BlockSpec(memory_space=pltpu.SMEM), vmem()],
-        out_specs=vmem(),
-        out_shape=shape(SLOTS * HALF, D2),
-        compiler_params=params(),
-        name="features_place",
-    )(where, got_features)
-    shares, packed = lax.optimization_barrier((shares, packed))
-    weight_grad, bias_grad, second_bias_grad, conv2_rows_grad = pl.pallas_call(
+    shares = exchange(jnp.concatenate([features, spread_to(half[HALF_ROWS:], 16)], axis=1), ENC)
+    weight_grad, bias_grad, second_bias_grad, conv2_rows_grad, packed = pl.pallas_call(
         last_kernel,
         grid=(3,),
         in_specs=[
             pl.BlockSpec(memory_space=pltpu.SMEM),
-            pl.BlockSpec((16, ROWS, LANES), lambda i: (0, i, 0)),
-            pl.BlockSpec((16, 16, LANES), lambda i: (0, 3 * ROWS // 16, 0)),
+            pl.BlockSpec((16, ROWS, LANES), lambda i: (0, i + 1, 0)),
+            pl.BlockSpec((16, ROWS, LANES), lambda i: (0, 0, 0)),
+            pl.BlockSpec((16, 16, LANES), lambda i: (0, 4 * ROWS // 16, 0)),
             pl.BlockSpec((HALF_ROWS, LANES), lambda i: (0, 0)),
             pl.BlockSpec((HALF_ROWS, LANES), lambda i: (0, 0)),
         ],
@@ -412,17 +411,19 @@
             pl.BlockSpec((16 * ROWS,), lambda i: (0,)),
             pl.BlockSpec((D2,), lambda i: (0,)),
             pl.BlockSpec((ROWS, 3 * D2), lambda i: (0, 0)),
+            pl.BlockSpec((SLOTS * HALF, D2), lambda i: (0, 0)),
         ],
         out_shape=[
             shape(3 * MEL, 16 * ROWS, dtype=F32),
             shape(16 * ROWS, dtype=F32),
             shape(D2, dtype=F32),
             shape(ROWS, 3 * D2, dtype=F32),
+            shape(SLOTS * HALF, D2),
         ],
         scratch_shapes=[pltpu.VMEM((16 * ROWS, LANES), F32)],
         compiler_params=params("arbitrary"),
         name="gradient_unpack",
-    )(where, shares, shares, own, other)
+    )(where, shares, shares, shares, own, other)
     return packed.reshape(SLOTS, HALF, D2), weight_grad, bias_grad, second_bias_grad, conv2_rows_grad
 
 

time: 194 us -> 188 us (0.969)
  between operations: 14.3 us -> 0.86 us
  waiting for transfers between devices: 29.3 us -> 36.1 us
    ppermute x1, waiting for transfers between devices: 0.01 us -> 17.5 us  [local(): other = lax.ppermute(own, 'xl', [(0, 1), (1, 0)])]
    all_to_all x4, waiting for transfers between devices: 25 us -> 16.3 us  [exchange(): return lax.all_to_all(values, axes, split_axis=0, concat_axis=0, tiled=True)]
    all_gather x1 -> x0, waiting for transfers between devices: 2 us -> none  [local(): got_features = lax.all_gather(features, ENC, axis=0, tiled=True)]
    unnamed x24 -> x26, local copies, waits for them, and re-layouts: 4.97 us -> 4.45 us
  transfers between devices with their start and end apart: 10 -> 9, of which waited for: 6 -> 6; matrix products, arithmetic and copies ran while one was open for 4% -> 4% of each run, Pallas kernels for 4% -> 3%
where the time goes in v4:
time: 188 us; the launch traced here: 186 us
  blocking collectives  62.1 us (33%)
  starting transfers between devices  42.4 us (23%)
  waiting for transfers between devices  36.1 us (19%)
  Pallas kernels  29.5 us (16%)
  local copies, waits for them, and re-layouts  11.4 us (6%)
  other arithmetic  3.49 us (2%)
    all_to_all x4, blocking collectives, exchange(): return lax.all_to_all(values, axes, split_axis=0, concat_axis=0, tiled=True)  62.1 us
    all_to_all x4, starting transfers between devices, exchange(): return lax.all_to_all(values, axes, split_axis=0, concat_axis=0, tiled=True)  18.9 us
    ppermute x1, waiting for transfers between devices, local(): other = lax.ppermute(own, 'xl', [(0, 1), (1, 0)])  17.5 us
    all_to_all x4, waiting for transfers between devices, exchange(): return lax.all_to_all(values, axes, split_axis=0, concat_axis=0, tiled=True)  16.3 us
    pallas_call x1, Pallas kernels, local(): pl.pallas_call(backward_kernel, grid=(HOLDERS // 2,), in_specs=[pl.BlockS...  7.54 us
    ppermute x1, starting transfers between devices, local(): lax.ppermute(conv2_weight, ('xh', 'xl'), [(0, 3), (3, 0), (1, 2), (2, 1)])  7.48 us
    ppermute x1, starting transfers between devices, local(): got = lax.ppermute(send, 'c', [(0, 1), (1, 0)])  5.95 us
    ppermute x1, starting transfers between devices, local(): lax.ppermute(conv2_weight, ('xh', 'c', 'xl'), [(i, 7 - i) for i in range(...  5.78 us
  transfers between devices with their start and end apart: 9, of which 6 were waited for; matrix products, arithmetic and copies ran while one was open for 4% of the time, Pallas kernels for 3%

profile of v4, /device:TPU:1, one launch (start us, length us, event | category | flops | bytes accessed | tf_op | source)
XLA Modules:
  0.0 185.8 jit_solution(3666790779343711386)
XLA Ops:
  0.6 5.8 %collective-permute-start.2 = (bf16[80,1920]{1,0:T(8,128)(2,1)}, bf16[80,1920]{1,0:T(8,128)(2,1)S(1)}, u32[]{:S(2)}, u32[]{:S(2)}) collective-permute-start(bf16[80,1920]{1,0:T(8,128)(2,1)} %own_ref.3), channel_id=1, source_target_pairs={{0,289},{1,288},{32,257},{33,256},{256,33},{257,32},{288,1},{289,0... | collective-permute-start | bytes 921608 | tf_op jit(solution)/shard_map/ppermute | solution.py:285
  6.4 7.5 %collective-permute-start.1 = (bf16[80,1920]{1,0:T(8,128)(2,1)}, bf16[80,1920]{1,0:T(8,128)(2,1)S(1)}, u32[]{:S(2)}, u32[]{:S(2)}) collective-permute-start(bf16[80,1920]{1,0:T(8,128)(2,1)} %own_ref.3), channel_id=1, source_target_pairs={{0,257},{257,0},{1,256},{256,1},{2,259},{259,2},{3,258},{258,3},{4... | collective-permute-start | bytes 921608 | tf_op jit(solution)/shard_map/ppermute | solution.py:284
  13.9 1.9 %collective-permute-start = (bf16[80,1920]{1,0:T(8,128)(2,1)}, bf16[80,1920]{1,0:T(8,128)(2,1)S(1)}, u32[]{:S(2)}, u32[]{:S(2)}) collective-permute-start(bf16[80,1920]{1,0:T(8,128)(2,1)} %own_ref.3), channel_id=1, source_target_pairs={{0,32},{32,0},{1,33},{33,1},{2,34},{34,2},{3,35},{35,3},{4,36},{36... | collective-permute-start | bytes 921608 | tf_op jit(solution)/shard_map/ppermute | solution.py:283
  15.8 1.6 mel_payload.1
  17.4 3.5 %all-to-all-start = ((bf16[4,17,16,128]{3,2,1,0:T(8,128)(2,1)}), bf16[4,17,16,128]{3,2,1,0:T(8,128)(2,1)S(1)}, u32[]{:S(2)}, u32[]{:S(2)}) async-start(bf16[4,17,16,128]{3,2,1,0:T(8,128)(2,1)} %mel_payload.1), calls=%async_computation | async-start | bytes 557056 | tf_op jit(solution)/shard_map/all_to_all | solution.py:250
  20.9 0.9 fusion
  21.9 0.1 concatenate.10
  21.9 0.6 broadcast_in_dim.26.b1_ref
  22.5 1.4 constant_dynamic-slice_fusion
  23.9 1.0 concatenate.9.w1_ref
  24.9 2.1 %all-to-all-done.pay_ref = bf16[4,17,16,128]{3,2,1,0:T(8,128)(2,1)S(1)} async-done(((bf16[4,17,16,128]{3,2,1,0:T(8,128)(2,1)}), bf16[4,17,16,128]{3,2,1,0:T(8,128)(2,1)S(1)}, u32[]{:S(2)}, u32[]{:S(2)}) %all-to-all-start) | async-done | bytes 278560 | tf_op jit(solution)/shard_map/all_to_all | solution.py:250
  27.0 0.7 copy-done.8
  27.7 4.7 %stem_first.1 = (bf16[4,128,512]{2,1,0:T(8,128)(2,1)}, bf16[4,3,128,384]{3,2,1,0:T(8,128)(2,1)}, f32[4,2,128,384]{3,2,1,0:T(8,128)}) custom-call(bf16[4,17,16,128]{3,2,1,0:T(8,128)(2,1)} %copy-done.8, bf16[384,384]{1,0:T(8,128)(2,1)} %concatenate.9.w1_ref, f32[1,384]{1,0:T(1,128)} %broadcast_in_dim.26.b1_ref), custom_call_target="tpu_custom_call" | custom-call | flops 302000000 | bytes 10000000 | tf_op jit(solution)/shard_map/stem_first/pallas_call | solution.py:300
  32.5 0.7 copy-done.3
  33.2 0.1 copy-done.4
  33.3 0.1 copy-done.5
  33.4 3.8 %stem_second.1 = bf16[4,128,640]{2,1,0:T(8,128)(2,1)} custom-call(bf16[4,3,128,384]{3,2,1,0:T(8,128)(2,1)} %get-tuple-element.17.act_ref, bf16[80,1920]{1,0:T(8,128)(2,1)} %own_ref.3, bf16[80,1920]{1,0:T(8,128)(2,1)} %copy-done.5, bf16[80,1920]{1,0:T(8,128)(2,1)} %copy-done.4, bf16[80,1920]{1,0:T(8,128)(2,1)} %copy-done.3), custom_call_target="tpu_custom_call" | custom-call | tf_op jit(solution)/shard_map/stem_second/pallas_call | solution.py:323
  37.2 3.5 %all-to-all-start.1 = ((bf16[4,128,640]{2,1,0:T(8,128)(2,1)}), bf16[4,128,640]{2,1,0:T(8,128)(2,1)S(1)}, u32[]{:S(2)}, u32[]{:S(2)}) async-start(bf16[4,128,640]{2,1,0:T(8,128)(2,1)} %stem_second.1), calls=%async_computation.1 | async-start | bytes 1310720 | tf_op jit(solution)/shard_map/all_to_all | solution.py:250
  40.8 0.6 broadcast_in_dim_reshape.11.owner_row_ref
  41.4 0.7 broadcast_in_dim_reshape.13.owner_col_ref
  42.1 0.6 broadcast_in_dim.27.b2_ref
  42.8 0.7 broadcast_in_dim_reshape.12.length_ref
  43.5 6.2 %all-to-all-done.1.part_ref = bf16[4,128,640]{2,1,0:T(8,128)(2,1)S(1)} async-done(((bf16[4,128,640]{2,1,0:T(8,128)(2,1)}), bf16[4,128,640]{2,1,0:T(8,128)(2,1)S(1)}, u32[]{:S(2)}, u32[]{:S(2)}) %all-to-all-start.1) | async-done | bytes 655392 | tf_op jit(solution)/shard_map/all_to_all | solution.py:250
  49.6 0.8 copy-done.1
  50.5 2.5 %stem_middle.1 = (bf16[4,128,640]{2,1,0:T(8,128)(2,1)}, bf16[16,80,128]{2,1,0:T(8,128)(2,1)}) custom-call(bf16[4,128,640]{2,1,0:T(8,128)(2,1)} %copy-done.1, bf16[128,640]{1,0:T(8,128)(2,1)} %bitcast.13, f32[1,640]{1,0:T(1,128)} %broadcast_in_dim.27.b2_ref, f32[128,1]{1,0:T(8,128)} %broadcast_in_dim_reshape.12.length_ref, ...), custom_call_target="tpu_custom_call" | custom-call | tf_op jit(solution)/shard_map/stem_middle/pallas_call | solution.py:336
  53.0 3.5 %all-to-all-start.2 = ((bf16[4,128,640]{2,1,0:T(8,128)(2,1)}), bf16[4,128,640]{2,1,0:T(8,128)(2,1)S(1)}, u32[]{:S(2)}, u32[]{:S(2)}) async-start(bf16[4,128,640]{2,1,0:T(8,128)(2,1)} %get-tuple-element.19), calls=%async_computation.2 | async-start | bytes 1310720 | tf_op jit(solution)/shard_map/all_to_all | solution.py:250
  56.5 0.6 pad_add_fusion.where_ref
  57.1 7.2 %all-to-all-done.2.grad_ref = bf16[4,128,640]{2,1,0:T(8,128)(2,1)S(1)} async-done(((bf16[4,128,640]{2,1,0:T(8,128)(2,1)}), bf16[4,128,640]{2,1,0:T(8,128)(2,1)S(1)}, u32[]{:S(2)}, u32[]{:S(2)}) %all-to-all-start.2) | async-done | bytes 655392 | tf_op jit(solution)/shard_map/all_to_all | solution.py:250
  64.2 0.8 copy-done.2
  65.0 7.5 %stem_backward.1 = (f32[2,2,896,128]{3,2,1,0:T(8,128)}, bf16[2,2,896,128]{3,2,1,0:T(8,128)(2,1)}) custom-call(s32[3]{0:T(128)} %pad_add_fusion.where_ref, bf16[4,128,640]{2,1,0:T(8,128)(2,1)} %copy-done.2, bf16[80,1920]{1,0:T(8,128)(2,1)} %own_ref.3, bf16[80,1920]{1,0:T(8,128)(2,1)} %copy-done.5, bf16[80,1920]{1,0:T(8,128)(2,1)} %copy-done.4, ...), custom_call_target="tpu_custom_call" | custom-call | tf_op jit(solution)/shard_map/stem_backward/pallas_call | solution.py:354
  72.6 5.9 %collective-permute-start.3 = (bf16[2,2,896,128]{3,2,1,0:T(8,128)(2,1)}, bf16[2,2,896,128]{3,2,1,0:T(8,128)(2,1)S(1)}, u32[]{:S(2)}, u32[]{:S(2)}) collective-permute-start(bf16[2,2,896,128]{3,2,1,0:T(8,128)(2,1)} %get-tuple-element.23), channel_id=1, source_target_pairs={{0,32},{32,0},{1,33},{33,1},{2,34},{34,2},{3,35},{35,3},{4,36},{36... | collective-permute-start | bytes 2752520 | tf_op jit(solution)/shard_map/ppermute | solution.py:377
  78.5 2.3 %collective-permute-done.3 = bf16[2,2,896,128]{3,2,1,0:T(8,128)(2,1)S(1)} collective-permute-done((bf16[2,2,896,128]{3,2,1,0:T(8,128)(2,1)}, bf16[2,2,896,128]{3,2,1,0:T(8,128)(2,1)S(1)}, u32[]{:S(2)}, u32[]{:S(2)}) %collective-permute-start.3) | collective-permute-done | bytes 917536 | tf_op jit(solution)/shard_map/ppermute | solution.py:377
  80.8 1.7 add_convert_fusion
  82.6 16.1 %all_to_all.40.got_ref = bf16[4,896,128]{2,1,0:T(8,128)(2,1)} all-to-all(bf16[4,896,128]{2,1,0:T(8,128)(2,1)S(1)} %bitcast.9), channel_id=1, replica_groups=mesh['xh'=2,'y'=4,'c'=2,'zh'=4,'zl'=4,'xl'=2] {'xh','xl'}, dimensions={0} | all-to-all | bytes 1835008 | tf_op jit(solution)/shard_map/all_to_all | solution.py:250
  98.6 2.0 %gradient_sum.3 = bf16[896,128]{1,0:T(8,128)(2,1)} custom-call(bf16[4,896,128]{2,1,0:T(8,128)(2,1)} %all_to_all.40.got_ref), custom_call_target="tpu_custom_call" | custom-call | tf_op jit(solution)/shard_map/gradient_sum/pallas_call | solution.py:381
  100.6 10.0 %all_to_all.41.got_ref = bf16[4,224,128]{2,1,0:T(8,128)(2,1)} all-to-all(bf16[4,224,128]{2,1,0:T(8,128)(2,1)} %bitcast.12), channel_id=1, replica_groups=mesh['xh'=2,'y'=4,'c'=2,'zh'=4,'zl'=4,'xl'=2] {'zl'}, dimensions={0} | all-to-all | bytes 458752 | tf_op jit(solution)/shard_map/all_to_all | solution.py:250
  110.6 1.7 gradient_sum.4
  112.2 25.9 %all_to_all.42.got_ref = bf16[4,224,128]{2,1,0:T(8,128)(2,1)} all-to-all(bf16[4,224,128]{2,1,0:T(8,128)(2,1)} %gradient_sum.4), channel_id=1, replica_groups=mesh['xh'=2,'y'=4,'c'=2,'zh'=4,'zl'=4,'xl'=2] {'zh'}, dimensions={0} | all-to-all | bytes 458752 | tf_op jit(solution)/shard_map/all_to_all | solution.py:250
  138.1 1.7 gradient_sum.5
  139.8 10.1 %all_to_all.43 = bf16[4,224,128]{2,1,0:T(8,128)(2,1)S(1)} all-to-all(bf16[4,224,128]{2,1,0:T(8,128)(2,1)} %gradient_sum.5), channel_id=1, replica_groups=mesh['xh'=2,'y'=4,'c'=2,'zh'=4,'zl'=4,'xl'=2] {'zl'}, dimensions={0} | all-to-all | bytes 458752 | tf_op jit(solution)/shard_map/all_to_all | solution.py:250
  149.9 0.2 broadcast_in_dim.30
  150.1 1.2 pad_maximum_fusion
  151.3 8.5 %all-to-all-start.7 = ((bf16[16,336,128]{2,1,0:T(8,128)(2,1)}), bf16[16,336,128]{2,1,0:T(8,128)(2,1)S(1)}, u32[]{:S(2)}, u32[]{:S(2)}) async-start(bf16[16,336,128]{2,1,0:T(8,128)(2,1)} %pad_maximum_fusion), calls=%async_computation.7 | async-start | bytes 2752512 | tf_op jit(solution)/shard_map/all_to_all | solution.py:250
  159.8 2.4 %collective-permute-start.4 = (bf16[640,128]{1,0:T(8,128)(2,1)S(1)}, bf16[640,128]{1,0:T(8,128)(2,1)S(1)}, u32[]{:S(2)}, u32[]{:S(2)}) collective-permute-start(bf16[640,128]{1,0:T(8,128)(2,1)S(1)} %slice.9.own_ref), channel_id=1, source_target_pairs={{0,1},{1,0},{2,3},{3,2},{4,5},{5,4},{6,7},{7,6},{8,9},{9,8},{10,11... | collective-permute-start | bytes 491528 | tf_op jit(solution)/shard_map/ppermute | solution.py:396
  162.2 17.5 %collective-permute-done.4.other_ref = bf16[640,128]{1,0:T(8,128)(2,1)S(1)} collective-permute-done((bf16[640,128]{1,0:T(8,128)(2,1)S(1)}, bf16[640,128]{1,0:T(8,128)(2,1)S(1)}, u32[]{:S(2)}, u32[]{:S(2)}) %collective-permute-start.4) | collective-permute-done | bytes 163872 | tf_op jit(solution)/shard_map/ppermute | solution.py:396
  179.7 0.9 all-to-all-done.7.got_ref.feature_ref.bias_ref
  180.6 1.1 copy-done
  181.7 4.1 %gradient_unpack.1 = (f32[384,1280]{1,0:T(8,128)}, f32[1280]{0:T(1024)}, f32[640]{0:T(1024)}, f32[80,1920]{1,0:T(8,128)}, bf16[256,640]{1,0:T(8,128)(2,1)}) custom-call(s32[3]{0:T(128)} %pad_add_fusion.where_ref, bf16[16,336,128]{2,1,0:T(8,128)(2,1)} %copy-done, bf16[16,336,128]{2,1,0:T(8,128)(2,1)} %copy-done, bf16[16,336,128]{2,1,0:T(8,128)(2,1)} %copy-done, ...), custom_call_target="tpu_custom_call" | custom-call | tf_op jit(solution)/shard_map/gradient_unpack/pallas_call | solution.py:398
  (29 shorter events, 0.2 us)
Async XLA Ops:
  0.6 31.8 %collective-permute-start.2 = (bf16[80,1920]{1,0:T(8,128)(2,1)}, bf16[80,1920]{1,0:T(8,128)(2,1)S(1)}, u32[]{:S(2)}, u32[]{:S(2)}) collective-permute-start(bf16[80,1920]{1,0:T(8,128)(2,1)} %own_ref.3), channel_id=1, source_target_pairs={{0,289},{1,288},{32,257},{33,256},{256,33},{257,32},{288,1},{289,0... | collective-permute-start | bytes 921608 | tf_op jit(solution)/shard_map/ppermute | solution.py:285
  6.4 26.0 %collective-permute-start.1 = (bf16[80,1920]{1,0:T(8,128)(2,1)}, bf16[80,1920]{1,0:T(8,128)(2,1)S(1)}, u32[]{:S(2)}, u32[]{:S(2)}) collective-permute-start(bf16[80,1920]{1,0:T(8,128)(2,1)} %own_ref.3), channel_id=1, source_target_pairs={{0,257},{257,0},{1,256},{256,1},{2,259},{259,2},{3,258},{258,3},{4... | collective-permute-start | bytes 921608 | tf_op jit(solution)/shard_map/ppermute | solution.py:284
  13.9 18.5 %collective-permute-start = (bf16[80,1920]{1,0:T(8,128)(2,1)}, bf16[80,1920]{1,0:T(8,128)(2,1)S(1)}, u32[]{:S(2)}, u32[]{:S(2)}) collective-permute-start(bf16[80,1920]{1,0:T(8,128)(2,1)} %own_ref.3), channel_id=1, source_target_pairs={{0,32},{32,0},{1,33},{33,1},{2,34},{34,2},{3,35},{35,3},{4,36},{36... | collective-permute-start | bytes 921608 | tf_op jit(solution)/shard_map/ppermute | solution.py:283
  17.4 9.6 %all-to-all-start = ((bf16[4,17,16,128]{3,2,1,0:T(8,128)(2,1)}), bf16[4,17,16,128]{3,2,1,0:T(8,128)(2,1)S(1)}, u32[]{:S(2)}, u32[]{:S(2)}) async-start(bf16[4,17,16,128]{3,2,1,0:T(8,128)(2,1)} %mel_payload.1), calls=%async_computation | async-start | bytes 557056 | tf_op jit(solution)/shard_map/all_to_all | solution.py:250
  27.0 0.7 copy-start.8
  32.4 0.7 copy-start.3
  32.4 0.8 copy-start.4
  32.5 0.9 copy-start.5
  33.4 7.3 %copy-start.11 = (s32[16]{0:T(128)S(1)}, s32[16]{0:T(128)}, u32[]{:S(2)}) copy-start(s32[16]{0:T(128)} %length_ref.1) | copy-start | bytes 196
  33.4 7.3 %copy-start.12 = (s32[16,1]{0,1:T(1,128)S(1)}, s32[16,1]{0,1:T(1,128)}, u32[]{:S(2)}) copy-start(s32[16,1]{0,1:T(1,128)} %param.10) | copy-start | bytes 196
  33.4 8.7 %copy-start.10 = (f32[640]{0:T(1024)S(1)}, f32[640]{0:T(1024)}, u32[]{:S(2)}) copy-start(f32[640]{0:T(1024)} %param.14) | copy-start | bytes 7684
  37.2 12.5 %all-to-all-start.1 = ((bf16[4,128,640]{2,1,0:T(8,128)(2,1)}), bf16[4,128,640]{2,1,0:T(8,128)(2,1)S(1)}, u32[]{:S(2)}, u32[]{:S(2)}) async-start(bf16[4,128,640]{2,1,0:T(8,128)(2,1)} %stem_second.1), calls=%async_computation.1 | async-start | bytes 1310720 | tf_op jit(solution)/shard_map/all_to_all | solution.py:250
  49.6 0.8 copy-start.1
  53.0 11.2 %all-to-all-start.2 = ((bf16[4,128,640]{2,1,0:T(8,128)(2,1)}), bf16[4,128,640]{2,1,0:T(8,128)(2,1)S(1)}, u32[]{:S(2)}, u32[]{:S(2)}) async-start(bf16[4,128,640]{2,1,0:T(8,128)(2,1)} %get-tuple-element.19), calls=%async_computation.2 | async-start | bytes 1310720 | tf_op jit(solution)/shard_map/all_to_all | solution.py:250
  64.2 0.8 copy-start.2
  72.6 8.2 %collective-permute-start.3 = (bf16[2,2,896,128]{3,2,1,0:T(8,128)(2,1)}, bf16[2,2,896,128]{3,2,1,0:T(8,128)(2,1)S(1)}, u32[]{:S(2)}, u32[]{:S(2)}) collective-permute-start(bf16[2,2,896,128]{3,2,1,0:T(8,128)(2,1)} %get-tuple-element.23), channel_id=1, source_target_pairs={{0,32},{32,0},{1,33},{33,1},{2,34},{34,2},{3,35},{35,3},{4,36},{36... | collective-permute-start | bytes 2752520 | tf_op jit(solution)/shard_map/ppermute | solution.py:377
  100.6 49.5 %copy-start.7 = (bf16[16,80,128]{2,1,0:T(8,128)(2,1)S(1)}, bf16[16,80,128]{2,1,0:T(8,128)(2,1)}, u32[]{:S(2)}) copy-start(bf16[16,80,128]{2,1,0:T(8,128)(2,1)} %get-tuple-element.18) | copy-start | bytes 983044
  151.3 29.3 %all-to-all-start.7 = ((bf16[16,336,128]{2,1,0:T(8,128)(2,1)}), bf16[16,336,128]{2,1,0:T(8,128)(2,1)S(1)}, u32[]{:S(2)}, u32[]{:S(2)}) async-start(bf16[16,336,128]{2,1,0:T(8,128)(2,1)} %pad_maximum_fusion), calls=%async_computation.7 | async-start | bytes 2752512 | tf_op jit(solution)/shard_map/all_to_all | solution.py:250
  159.8 20.8 %copy-start.6 = (bf16[640,128]{1,0:T(8,128)(2,1)}, bf16[640,128]{1,0:T(8,128)(2,1)S(1)}, u32[]{:S(2)}) copy-start(bf16[640,128]{1,0:T(8,128)(2,1)S(1)} %slice.9.own_ref) | copy-start | bytes 491524
  159.8 19.9 %collective-permute-start.4 = (bf16[640,128]{1,0:T(8,128)(2,1)S(1)}, bf16[640,128]{1,0:T(8,128)(2,1)S(1)}, u32[]{:S(2)}, u32[]{:S(2)}) collective-permute-start(bf16[640,128]{1,0:T(8,128)(2,1)S(1)} %slice.9.own_ref), channel_id=1, source_target_pairs={{0,1},{1,0},{2,3},{3,2},{4,5},{5,4},{6,7},{7,6},{8,9},{9,8},{10,11... | collective-permute-start | bytes 491528 | tf_op jit(solution)/shard_map/ppermute | solution.py:396
  179.7 0.9 copy-start.9
  180.6 1.1 copy-start

commit v5 on v4

--- a/solution.py
+++ b/solution.py
@@ -24,7 +24,7 @@
 SLOTS = 2 * CLIPS
 PACK = 896
 HALF_ROWS = 8 * ROWS
-VMEM = 56 * 1024 * 1024
+MIB = 1024 * 1024
 ALL_AXES = ("xh", "y", "c", "zh", "zl", "xl")
 ENC = ("xh", "y", "c")
 F32 = jnp.float32
@@ -82,7 +82,11 @@
         pay_ref[target, CLIPS] = length.astype(BF16)
 
 
-def first_kernel(pay_ref, w1_ref, b1_ref, cols_ref, act_ref, slope_ref, frames_ref):
+def forward_kernel(
+    pay_ref, w1_ref, b1_ref, own_ref, side_ref, far_ref, both_ref, part_ref, cols_ref, act_ref, slope_ref, w2_ref,
+    frames_ref,
+):
+    stack_weights((own_ref, side_ref, far_ref, both_ref), w2_ref)
     spread = (
         lax.broadcasted_iota(jnp.int32, (STEPS, CLIPS), 0) >> 3
         == lax.broadcasted_iota(jnp.int32, (STEPS, CLIPS), 1)
@@ -113,15 +117,10 @@
     act_ref[0, 0] = act_prior
     act_ref[0, 1] = act_even
     act_ref[0, 2] = act_odd
-
-
-def second_kernel(act_ref, own_ref, side_ref, far_ref, both_ref, part_ref, w2_ref):
-    stack_weights((own_ref, side_ref, far_ref, both_ref), w2_ref)
-    rows = 2 * STEPS
-    total = dot(act_ref[:, 0].reshape(rows, WIDE), w2_ref[:, :D2])
-    total = total + dot(act_ref[:, 1].reshape(rows, WIDE), w2_ref[:, D2 : 2 * D2])
-    total = total + dot(act_ref[:, 2].reshape(rows, WIDE), w2_ref[:, 2 * D2 :])
-    part_ref[...] = total.astype(BF16).reshape(2, STEPS, D2)
+    total = dot(act_prior, w2_ref[:, :D2])
+    total = total + dot(act_even, w2_ref[:, D2 : 2 * D2])
+    total = total + dot(act_odd, w2_ref[:, 2 * D2 :])
+    part_ref[0] = total.astype(BF16)
 
 
 def middle_kernel(part_ref, grad_ref, b2_ref, length_ref, owner_col_ref, owner_row_ref, rep_ref, feature_ref):
@@ -258,23 +257,29 @@
     return pl.BlockSpec(memory_space=pltpu.VMEM)
 
 
-def params(*semantics):
-    return pltpu.CompilerParams(vmem_limit_bytes=VMEM, dimension_semantics=semantics or None)
+def params(mib, *semantics):
+    return pltpu.CompilerParams(vmem_limit_bytes=mib * MIB, dimension_semantics=semantics or None)
 
 
 def local(mel, lengths, routes, conv1_weight, conv1_bias, conv2_weight, conv2_bias, out_grad):
     x_hi, y, core = lax.axis_index("xh"), lax.axis_index("y"), lax.axis_index("c")
-    where = jnp.stack([x_hi, lax.axis_index("xl"), (x_hi * HOLDERS + y) * 2 + core]).astype(jnp.int32)
+    where = jnp.stack([x_hi, lax.axis_index("xl")]).astype(jnp.int32)
 
     def shape(*dims, dtype=BF16):
         return jax.ShapeDtypeStruct(dims, dtype)
+
+    def from_hbm(values):
+        return pltpu.with_memory_space_constraint(values, pltpu.HBM)
+
+    def in_hbm(*dims, dtype=BF16):
+        return pltpu.HBM(dims, dtype)
 
     pay = pl.pallas_call(
         prepare_kernel,
         in_specs=[pl.BlockSpec(memory_space=pltpu.SMEM), vmem()],
         out_specs=vmem(),
-        out_shape=shape(HOLDERS, CLIPS + 1, 2 * HALF, MEL),
-        compiler_params=params(),
+        out_shape=in_hbm(HOLDERS, CLIPS + 1, 2 * HALF, MEL),
+        compiler_params=params(60),
         name="mel_payload",
     )(lengths, mel)
     got_pay = exchange(pay, "y")
@@ -297,39 +302,31 @@
     pair = lambda i: (i, 0, 0)
     pair4 = lambda i: (i, 0, 0, 0)
     weight_spec = pl.BlockSpec((ROWS, 3 * D2), lambda i: (0, 0))
-    cols, acts, slopes = pl.pallas_call(
-        first_kernel,
+    parts, cols, acts, slopes = pl.pallas_call(
+        forward_kernel,
         grid=(HOLDERS,),
         in_specs=[
             pl.BlockSpec((1, CLIPS + 1, 2 * HALF, MEL), pair4),
             pl.BlockSpec((3 * MEL, WIDE), lambda i: (0, 0)),
             pl.BlockSpec((1, WIDE), lambda i: (0, 0)),
+            *[weight_spec] * BLOCKS,
         ],
         out_specs=[
+            pl.BlockSpec((1, STEPS, D2), pair),
             pl.BlockSpec((1, STEPS, 4 * LANES), pair),
             pl.BlockSpec((1, 3, STEPS, WIDE), pair4),
             pl.BlockSpec((1, 2, STEPS, WIDE), pair4),
         ],
         out_shape=[
-            shape(HOLDERS, STEPS, 4 * LANES),
-            shape(HOLDERS, 3, STEPS, WIDE),
-            shape(HOLDERS, 2, STEPS, WIDE, dtype=F32),
-        ],
-        scratch_shapes=[pltpu.VMEM((2 * STEPS, MEL), F32)],
-        compiler_params=params("arbitrary"),
-        cost_estimate=pl.CostEstimate(flops=302 * 10**6, bytes_accessed=10**7, transcendentals=8 * 10**5),
-        name="stem_first",
-    )(got_pay, w1, b1)
-    parts = pl.pallas_call(
-        second_kernel,
-        grid=(HOLDERS // 2,),
-        in_specs=[pl.BlockSpec((2, 3, STEPS, WIDE), pair4), *[weight_spec] * BLOCKS],
-        out_specs=pl.BlockSpec((2, STEPS, D2), pair),
-        out_shape=shape(HOLDERS, STEPS, D2),
-        scratch_shapes=[pltpu.VMEM((WIDE, 3 * D2), BF16)],
-        compiler_params=params("arbitrary"),
-        name="stem_second",
-    )(acts, *weights)
+            in_hbm(HOLDERS, STEPS, D2),
+            in_hbm(HOLDERS, STEPS, 4 * LANES),
+            in_hbm(HOLDERS, 3, STEPS, WIDE),
+            in_hbm(HOLDERS, 2, STEPS, WIDE, dtype=F32),
+        ],
+        scratch_shapes=[pltpu.VMEM((WIDE, 3 * D2), BF16), pltpu.VMEM((2 * STEPS, MEL), F32)],
+        compiler_params=params(20, "arbitrary"),
+        name="stem_forward",
+    )(got_pay, w1, b1, *weights)
 
     got_parts = exchange(parts, "y")
     owner = jnp.repeat(routes[:, 0], HALF)
@@ -337,14 +334,14 @@
         middle_kernel,
         in_specs=[vmem()] * 6,
         out_specs=[vmem()] * 2,
-        out_shape=[shape(HOLDERS, STEPS, D2), shape(16, ROWS, LANES)],
-        compiler_params=params(),
+        out_shape=[in_hbm(HOLDERS, STEPS, D2), in_hbm(16, ROWS, LANES)],
+        compiler_params=params(10),
         name="stem_middle",
     )(
         got_parts,
-        out_grad.reshape(STEPS, D2),
+        from_hbm(out_grad.reshape(STEPS, D2)),
         conv2_bias[None],
-        jnp.repeat(lengths.astype(F32), HALF)[:, None],
+        from_hbm(jnp.repeat(lengths.astype(F32), HALF)[:, None]),
         owner[:, None],
         owner[None],
     )
@@ -371,9 +368,9 @@
             pltpu.VMEM((1, WIDE), F32),
             pltpu.VMEM((1, D2), F32),
         ],
-        compiler_params=params("arbitrary"),
+        compiler_params=params(32, "arbitrary"),
         name="stem_backward",
-    )(where, got_grad, *weights, cols, acts, slopes)
+    )(where, got_grad, *weights, from_hbm(cols), from_hbm(acts), from_hbm(slopes))
     got = lax.ppermute(send, "c", [(0, 1), (1, 0)])
     quarters = exchange((keep + got.astype(F32)).astype(BF16).reshape(4, PACK, LANES), ("xh", "xl"))
 
@@ -383,7 +380,7 @@
             in_specs=[vmem()],
             out_specs=vmem(),
             out_shape=shape(*dims),
-            compiler_params=params(),
+            compiler_params=params(8),
             name="gradient_sum",
         )(values)
 
@@ -421,7 +418,7 @@
             shape(SLOTS * HALF, D2),
         ],
         scratch_shapes=[pltpu.VMEM((16 * ROWS, LANES), F32)],
-        compiler_params=params("arbitrary"),
+        compiler_params=params(16, "arbitrary"),
         name="gradient_unpack",
     )(where, shares, shares, shares, own, other)
     return packed.reshape(SLOTS, HALF, D2), weight_grad, bias_grad, second_bias_grad, conv2_rows_grad

time: 188 us -> 166 us (0.88)
  Pallas kernels: 29.5 us -> 17 us
  local copies, waits for them, and re-layouts: 11.4 us -> 3.97 us
  waiting for transfers between devices: 36.1 us -> 39.5 us
  blocking collectives: 62.1 us -> 59.7 us
  other arithmetic: 3.49 us -> 1.43 us
    pallas_call x3, Pallas kernels: 5.29 us -> 0.18 us  [summed(): pl.pallas_call(sum_kernel, in_specs=[vmem()], out_specs=vmem(), out_shape...]
    unnamed x26 -> x10, local copies, waits for them, and re-layouts: 4.45 us -> 0.03 us
    pallas_call x2 -> x1, Pallas kernels: 8.47 us -> 4.4 us  [local(): pl.pallas_call(forward_kernel, grid=(HOLDERS,), in_specs=[pl.BlockSpec((1...]
    all_to_all x4, waiting for transfers between devices: 16.3 us -> 20 us  [exchange(): return lax.all_to_all(values, axes, split_axis=0, concat_axis=0, tiled=True)]
    all_to_all x4, blocking collectives: 62.1 us -> 59.7 us  [exchange(): return lax.all_to_all(values, axes, split_axis=0, concat_axis=0, tiled=True)]
    pallas_call x1, Pallas kernels: 7.54 us -> 5.51 us  [local(): pl.pallas_call(backward_kernel, grid=(HOLDERS // 2,), in_specs=[pl.BlockS...]
  transfers between devices with their start and end apart: 9 -> 9, of which waited for: 6 -> 6; matrix products, arithmetic and copies ran while one was open for 4% -> 2% of each run, Pallas kernels for 3% -> 1%
where the time goes in v5:
time: 166 us
  blocking collectives  59.7 us (36%)
  starting transfers between devices  43.1 us (26%)
  waiting for transfers between devices  39.5 us (24%)
  Pallas kernels  17 us (10%)
  local copies, waits for them, and re-layouts  3.97 us (2%)
    all_to_all x4, blocking collectives, exchange(): return lax.all_to_all(values, axes, split_axis=0, concat_axis=0, tiled=True)  59.7 us
    all_to_all x4, waiting for transfers between devices, exchange(): return lax.all_to_all(values, axes, split_axis=0, concat_axis=0, tiled=True)  20 us
    all_to_all x4, starting transfers between devices, exchange(): return lax.all_to_all(values, axes, split_axis=0, concat_axis=0, tiled=True)  19.6 us
    ppermute x1, waiting for transfers between devices, local(): other = lax.ppermute(own, 'xl', [(0, 1), (1, 0)])  17.5 us
    ppermute x1, starting transfers between devices, local(): lax.ppermute(conv2_weight, ('xh', 'xl'), [(0, 3), (3, 0), (1, 2), (2, 1)])  7.48 us
    ppermute x1, starting transfers between devices, local(): got = lax.ppermute(send, 'c', [(0, 1), (1, 0)])  5.98 us
    ppermute x1, starting transfers between devices, local(): lax.ppermute(conv2_weight, ('xh', 'c', 'xl'), [(i, 7 - i) for i in range(...  5.91 us
    pallas_call x1, Pallas kernels, local(): pl.pallas_call(backward_kernel, grid=(HOLDERS // 2,), in_specs=[pl.BlockS...  5.51 us
  transfers between devices with their start and end apart: 9, of which 6 were waited for; matrix products, arithmetic and copies ran while one was open for 2% of the time, Pallas kernels for 1%

profile of v5, /device:TPU:1, one launch (start us, length us, event | category | flops | bytes accessed | tf_op | source)
XLA Modules:
  0.0 165.6 jit_solution(17255287884696026866)
XLA Ops:
  0.6 0.0 copy-start
  0.6 5.9 %collective-permute-start.2 = (bf16[80,1920]{1,0:T(8,128)(2,1)}, bf16[80,1920]{1,0:T(8,128)(2,1)S(1)}, u32[]{:S(2)}, u32[]{:S(2)}) collective-permute-start(bf16[80,1920]{1,0:T(8,128)(2,1)} %own_ref.3), channel_id=1, source_target_pairs={{0,289},{1,288},{32,257},{33,256},{256,33},{257,32},{288,1},{289,0... | collective-permute-start | bytes 921608 | tf_op jit(solution)/shard_map/ppermute | solution.py:290
  6.6 7.5 %collective-permute-start.1 = (bf16[80,1920]{1,0:T(8,128)(2,1)}, bf16[80,1920]{1,0:T(8,128)(2,1)S(1)}, u32[]{:S(2)}, u32[]{:S(2)}) collective-permute-start(bf16[80,1920]{1,0:T(8,128)(2,1)} %own_ref.3), channel_id=1, source_target_pairs={{0,257},{257,0},{1,256},{256,1},{2,259},{259,2},{3,258},{258,3},{4... | collective-permute-start | bytes 921608 | tf_op jit(solution)/shard_map/ppermute | solution.py:289
  14.0 1.9 %collective-permute-start = (bf16[80,1920]{1,0:T(8,128)(2,1)}, bf16[80,1920]{1,0:T(8,128)(2,1)S(1)}, u32[]{:S(2)}, u32[]{:S(2)}) collective-permute-start(bf16[80,1920]{1,0:T(8,128)(2,1)} %own_ref.3), channel_id=1, source_target_pairs={{0,32},{32,0},{1,33},{33,1},{2,34},{34,2},{3,35},{35,3},{4,36},{36... | collective-permute-start | bytes 921608 | tf_op jit(solution)/shard_map/ppermute | solution.py:288
  16.0 1.6 mel_payload.1
  17.6 3.5 %all-to-all-start = ((bf16[4,17,16,128]{3,2,1,0:T(8,128)(2,1)}), bf16[4,17,16,128]{3,2,1,0:T(8,128)(2,1)S(1)}, u32[]{:S(2)}, u32[]{:S(2)}) async-start(bf16[4,17,16,128]{3,2,1,0:T(8,128)(2,1)} %mel_payload.1), calls=%async_computation | async-start | bytes 557056 | tf_op jit(solution)/shard_map/all_to_all | solution.py:249
  21.1 0.9 fusion
  22.0 0.1 concatenate.10
  22.1 1.4 constant_dynamic-slice_fusion
  23.5 0.0 copy-start.3
  23.5 0.0 copy-start.4
  23.5 0.0 copy-start.2
  23.5 0.3 concatenate.9.w1_ref
  23.8 3.3 %all-to-all-done.pay_ref = bf16[4,17,16,128]{3,2,1,0:T(8,128)(2,1)S(1)} async-done(((bf16[4,17,16,128]{3,2,1,0:T(8,128)(2,1)}), bf16[4,17,16,128]{3,2,1,0:T(8,128)(2,1)S(1)}, u32[]{:S(2)}, u32[]{:S(2)}) %all-to-all-start) | async-done | bytes 278560 | tf_op jit(solution)/shard_map/all_to_all | solution.py:249
  27.1 0.0 collective-permute-done.2.both_ref
  27.2 0.0 collective-permute-done.1.far_ref
  27.2 0.0 collective-permute-done.side_ref
  27.2 0.0 copy-done
  27.2 4.4 %stem_forward.1 = (bf16[4,128,640]{2,1,0:T(8,128)(2,1)}, bf16[4,128,512]{2,1,0:T(8,128)(2,1)}, bf16[4,3,128,384]{3,2,1,0:T(8,128)(2,1)}, f32[4,2,128,384]{3,2,1,0:T(8,128)}) custom-call(bf16[4,17,16,128]{3,2,1,0:T(8,128)(2,1)S(1)} %all-to-all-done.pay_ref, bf16[384,384]{1,0:T(8,128)(2,1)S(1)} %concatenate.9.w1_ref, f32[1,384]{1,0:T(1,128)S(1)} %broadcast_in_dim.26.b1_ref, ...), custom_call_target="tpu_custom_call" | custom-call | tf_op jit(solution)/shard_map/stem_forward/pallas_call | solution.py:305
  31.6 3.5 %all-to-all-start.1 = ((bf16[4,128,640]{2,1,0:T(8,128)(2,1)}), bf16[4,128,640]{2,1,0:T(8,128)(2,1)S(1)}, u32[]{:S(2)}, u32[]{:S(2)}) async-start(bf16[4,128,640]{2,1,0:T(8,128)(2,1)} %get-tuple-element.18), calls=%async_computation.1 | async-start | bytes 1310720 | tf_op jit(solution)/shard_map/all_to_all | solution.py:249
  35.1 0.1 broadcast_in_dim.29
  35.2 0.1 broadcast_in_dim_reshape.11.owner_row_ref
  35.3 0.1 broadcast_in_dim_reshape.13.owner_col_ref
  35.3 0.0 copy-done.2
  35.4 0.1 broadcast_in_dim.28
  35.4 0.7 broadcast_in_dim_reshape.12.length_ref
  36.1 7.9 %all-to-all-done.1.part_ref = bf16[4,128,640]{2,1,0:T(8,128)(2,1)S(1)} async-done(((bf16[4,128,640]{2,1,0:T(8,128)(2,1)}), bf16[4,128,640]{2,1,0:T(8,128)(2,1)S(1)}, u32[]{:S(2)}, u32[]{:S(2)}) %all-to-all-start.1) | async-done | bytes 655392 | tf_op jit(solution)/shard_map/all_to_all | solution.py:249
  44.0 2.2 %stem_middle.1 = (bf16[4,128,640]{2,1,0:T(8,128)(2,1)}, bf16[16,80,128]{2,1,0:T(8,128)(2,1)}) custom-call(bf16[4,128,640]{2,1,0:T(8,128)(2,1)S(1)} %all-to-all-done.1.part_ref, bf16[128,640]{1,0:T(8,128)(2,1)} %bitcast.12, f32[1,640]{1,0:T(1,128)S(1)} %broadcast_in_dim.27.b2_ref, f32[128,1]{1,0:T(8,128)} %broadcast_in_dim_reshape.12.length_ref, ...), custom_call_target="tpu_custom_call" | custom-call | tf_op jit(solution)/shard_map/stem_middle/pallas_call | solution.py:333
  46.2 3.5 %all-to-all-start.2 = ((bf16[4,128,640]{2,1,0:T(8,128)(2,1)}), bf16[4,128,640]{2,1,0:T(8,128)(2,1)S(1)}, u32[]{:S(2)}, u32[]{:S(2)}) async-start(bf16[4,128,640]{2,1,0:T(8,128)(2,1)} %get-tuple-element.20), calls=%async_computation.2 | async-start | bytes 1310720 | tf_op jit(solution)/shard_map/all_to_all | solution.py:249
  49.7 0.1 pad_add_fusion.where_ref
  49.8 7.6 %all-to-all-done.2.grad_ref = bf16[4,128,640]{2,1,0:T(8,128)(2,1)S(1)} async-done(((bf16[4,128,640]{2,1,0:T(8,128)(2,1)}), bf16[4,128,640]{2,1,0:T(8,128)(2,1)S(1)}, u32[]{:S(2)}, u32[]{:S(2)}) %all-to-all-start.2) | async-done | bytes 655392 | tf_op jit(solution)/shard_map/all_to_all | solution.py:249
  57.4 5.5 %stem_backward.1 = (f32[2,2,896,128]{3,2,1,0:T(8,128)S(1)}, bf16[2,2,896,128]{3,2,1,0:T(8,128)(2,1)S(1)}) custom-call(s32[2]{0:T(128)S(1)} %pad_add_fusion.where_ref, bf16[4,128,640]{2,1,0:T(8,128)(2,1)S(1)} %all-to-all-done.2.grad_ref, bf16[80,1920]{1,0:T(8,128)(2,1)S(1)} %copy-done, bf16[80,1920]{1,0:T(8,128)(2,1)S(1)} %collective-permute-done.side_ref, ...), custom_call_target="tpu_custom_call" | custom-call | tf_op jit(solution)/shard_map/stem_backward/pallas_call | solution.py:351
  62.9 6.0 %collective-permute-start.3 = (bf16[2,2,896,128]{3,2,1,0:T(8,128)(2,1)S(1)}, bf16[2,2,896,128]{3,2,1,0:T(8,128)(2,1)S(1)}, u32[]{:S(2)}, u32[]{:S(2)}) collective-permute-start(bf16[2,2,896,128]{3,2,1,0:T(8,128)(2,1)S(1)} %get-tuple-element.25), channel_id=1, source_target_pairs={{0,32},{32,0},{1,33},{33,1},{2,34},{34,2},{3,35},{35,3},{4,36},{36... | collective-permute-start | bytes 2752520 | tf_op jit(solution)/shard_map/ppermute | solution.py:374
  68.9 2.1 %collective-permute-done.3 = bf16[2,2,896,128]{3,2,1,0:T(8,128)(2,1)S(1)} collective-permute-done((bf16[2,2,896,128]{3,2,1,0:T(8,128)(2,1)S(1)}, bf16[2,2,896,128]{3,2,1,0:T(8,128)(2,1)S(1)}, u32[]{:S(2)}, u32[]{:S(2)}) %collective-permute-start.3) | collective-permute-done | bytes 917536 | tf_op jit(solution)/shard_map/ppermute | solution.py:374
  71.0 0.2 add_convert_fusion
  71.2 16.0 %all_to_all.40.got_ref = bf16[4,896,128]{2,1,0:T(8,128)(2,1)S(1)} all-to-all(bf16[4,896,128]{2,1,0:T(8,128)(2,1)S(1)} %bitcast.9), channel_id=1, replica_groups=mesh['xh'=2,'y'=4,'c'=2,'zh'=4,'zl'=4,'xl'=2] {'xh','xl'}, dimensions={0} | all-to-all | bytes 1835008 | tf_op jit(solution)/shard_map/all_to_all | solution.py:249
  87.2 0.1 gradient_sum.3
  87.3 0.0 copy-start.1
  87.3 8.3 %all_to_all.41.got_ref = bf16[4,224,128]{2,1,0:T(8,128)(2,1)S(1)} all-to-all(bf16[4,224,128]{2,1,0:T(8,128)(2,1)S(1)} %bitcast.8), channel_id=1, replica_groups=mesh['xh'=2,'y'=4,'c'=2,'zh'=4,'zl'=4,'xl'=2] {'zl'}, dimensions={0} | all-to-all | bytes 458752 | tf_op jit(solution)/shard_map/all_to_all | solution.py:249
  95.6 27.3 %all_to_all.42.got_ref = bf16[4,224,128]{2,1,0:T(8,128)(2,1)S(1)} all-to-all(bf16[4,224,128]{2,1,0:T(8,128)(2,1)S(1)} %gradient_sum.4), channel_id=1, replica_groups=mesh['xh'=2,'y'=4,'c'=2,'zh'=4,'zl'=4,'xl'=2] {'zh'}, dimensions={0} | all-to-all | bytes 458752 | tf_op jit(solution)/shard_map/all_to_all | solution.py:249
  123.0 8.1 %all_to_all.43 = bf16[4,224,128]{2,1,0:T(8,128)(2,1)S(1)} all-to-all(bf16[4,224,128]{2,1,0:T(8,128)(2,1)S(1)} %gradient_sum.5), channel_id=1, replica_groups=mesh['xh'=2,'y'=4,'c'=2,'zh'=4,'zl'=4,'xl'=2] {'zl'}, dimensions={0} | all-to-all | bytes 458752 | tf_op jit(solution)/shard_map/all_to_all | solution.py:249
  131.1 0.2 broadcast_in_dim.30
  131.3 1.2 pad_maximum_fusion
  132.5 9.2 %all-to-all-start.7 = ((bf16[16,336,128]{2,1,0:T(8,128)(2,1)}), bf16[16,336,128]{2,1,0:T(8,128)(2,1)S(1)}, u32[]{:S(2)}, u32[]{:S(2)}) async-start(bf16[16,336,128]{2,1,0:T(8,128)(2,1)} %pad_maximum_fusion), calls=%async_computation.7 | async-start | bytes 2752512 | tf_op jit(solution)/shard_map/all_to_all | solution.py:249
  141.7 2.2 %collective-permute-start.4 = (bf16[640,128]{1,0:T(8,128)(2,1)S(1)}, bf16[640,128]{1,0:T(8,128)(2,1)S(1)}, u32[]{:S(2)}, u32[]{:S(2)}) collective-permute-start(bf16[640,128]{1,0:T(8,128)(2,1)S(1)} %slice.9.own_ref), channel_id=1, source_target_pairs={{0,1},{1,0},{2,3},{3,2},{4,5},{5,4},{6,7},{7,6},{8,9},{9,8},{10,11... | collective-permute-start | bytes 491528 | tf_op jit(solution)/shard_map/ppermute | solution.py:393
  143.9 17.5 %collective-permute-done.4.other_ref = bf16[640,128]{1,0:T(8,128)(2,1)S(1)} collective-permute-done((bf16[640,128]{1,0:T(8,128)(2,1)S(1)}, bf16[640,128]{1,0:T(8,128)(2,1)S(1)}, u32[]{:S(2)}, u32[]{:S(2)}) %collective-permute-start.4) | collective-permute-done | bytes 163872 | tf_op jit(solution)/shard_map/ppermute | solution.py:393
  161.4 1.1 all-to-all-done.7.got_ref.feature_ref.bias_ref
  162.5 3.1 %gradient_unpack.1 = (f32[384,1280]{1,0:T(8,128)}, f32[1280]{0:T(1024)}, f32[640]{0:T(1024)}, f32[80,1920]{1,0:T(8,128)}, bf16[256,640]{1,0:T(8,128)(2,1)}) custom-call(s32[2]{0:T(128)S(1)} %pad_add_fusion.where_ref, bf16[16,336,128]{2,1,0:T(8,128)(2,1)S(1)} %all-to-all-done.7.got_ref.feature_ref.bias_ref, ...), custom_call_target="tpu_custom_call" | custom-call | tf_op jit(solution)/shard_map/gradient_unpack/pallas_call | solution.py:395
  (12 shorter events, 0.1 us)
Async XLA Ops:
  0.6 26.5 %copy-start = (bf16[80,1920]{1,0:T(8,128)(2,1)S(1)}, bf16[80,1920]{1,0:T(8,128)(2,1)}, u32[]{:S(2)}) copy-start(bf16[80,1920]{1,0:T(8,128)(2,1)} %own_ref.3) | copy-start | bytes 921604
  0.6 26.5 %collective-permute-start.2 = (bf16[80,1920]{1,0:T(8,128)(2,1)}, bf16[80,1920]{1,0:T(8,128)(2,1)S(1)}, u32[]{:S(2)}, u32[]{:S(2)}) collective-permute-start(bf16[80,1920]{1,0:T(8,128)(2,1)} %own_ref.3), channel_id=1, source_target_pairs={{0,289},{1,288},{32,257},{33,256},{256,33},{257,32},{288,1},{289,0... | collective-permute-start | bytes 921608 | tf_op jit(solution)/shard_map/ppermute | solution.py:290
  6.6 20.6 %collective-permute-start.1 = (bf16[80,1920]{1,0:T(8,128)(2,1)}, bf16[80,1920]{1,0:T(8,128)(2,1)S(1)}, u32[]{:S(2)}, u32[]{:S(2)}) collective-permute-start(bf16[80,1920]{1,0:T(8,128)(2,1)} %own_ref.3), channel_id=1, source_target_pairs={{0,257},{257,0},{1,256},{256,1},{2,259},{259,2},{3,258},{258,3},{4... | collective-permute-start | bytes 921608 | tf_op jit(solution)/shard_map/ppermute | solution.py:289
  14.0 13.1 %collective-permute-start = (bf16[80,1920]{1,0:T(8,128)(2,1)}, bf16[80,1920]{1,0:T(8,128)(2,1)S(1)}, u32[]{:S(2)}, u32[]{:S(2)}) collective-permute-start(bf16[80,1920]{1,0:T(8,128)(2,1)} %own_ref.3), channel_id=1, source_target_pairs={{0,32},{32,0},{1,33},{33,1},{2,34},{34,2},{3,35},{35,3},{4,36},{36... | collective-permute-start | bytes 921608 | tf_op jit(solution)/shard_map/ppermute | solution.py:288
  17.6 9.6 %all-to-all-start = ((bf16[4,17,16,128]{3,2,1,0:T(8,128)(2,1)}), bf16[4,17,16,128]{3,2,1,0:T(8,128)(2,1)S(1)}, u32[]{:S(2)}, u32[]{:S(2)}) async-start(bf16[4,17,16,128]{3,2,1,0:T(8,128)(2,1)} %mel_payload.1), calls=%async_computation | async-start | bytes 557056 | tf_op jit(solution)/shard_map/all_to_all | solution.py:249
  23.5 11.6 %copy-start.3 = (s32[16]{0:T(128)S(1)}, s32[16]{0:T(128)}, u32[]{:S(2)}) copy-start(s32[16]{0:T(128)} %length_ref.1) | copy-start | bytes 196
  23.5 11.6 %copy-start.4 = (s32[16,1]{0,1:T(1,128)S(1)}, s32[16,1]{0,1:T(1,128)}, u32[]{:S(2)}) copy-start(s32[16,1]{0,1:T(1,128)} %param.10) | copy-start | bytes 196
  23.5 11.8 %copy-start.2 = (f32[640]{0:T(1024)S(1)}, f32[640]{0:T(1024)}, u32[]{:S(2)}) copy-start(f32[640]{0:T(1024)} %param.14) | copy-start | bytes 7684
  31.6 12.4 %all-to-all-start.1 = ((bf16[4,128,640]{2,1,0:T(8,128)(2,1)}), bf16[4,128,640]{2,1,0:T(8,128)(2,1)S(1)}, u32[]{:S(2)}, u32[]{:S(2)}) async-start(bf16[4,128,640]{2,1,0:T(8,128)(2,1)} %get-tuple-element.18), calls=%async_computation.1 | async-start | bytes 1310720 | tf_op jit(solution)/shard_map/all_to_all | solution.py:249
  46.2 11.2 %all-to-all-start.2 = ((bf16[4,128,640]{2,1,0:T(8,128)(2,1)}), bf16[4,128,640]{2,1,0:T(8,128)(2,1)S(1)}, u32[]{:S(2)}, u32[]{:S(2)}) async-start(bf16[4,128,640]{2,1,0:T(8,128)(2,1)} %get-tuple-element.20), calls=%async_computation.2 | async-start | bytes 1310720 | tf_op jit(solution)/shard_map/all_to_all | solution.py:249
  62.9 8.1 %collective-permute-start.3 = (bf16[2,2,896,128]{3,2,1,0:T(8,128)(2,1)S(1)}, bf16[2,2,896,128]{3,2,1,0:T(8,128)(2,1)S(1)}, u32[]{:S(2)}, u32[]{:S(2)}) collective-permute-start(bf16[2,2,896,128]{3,2,1,0:T(8,128)(2,1)S(1)} %get-tuple-element.25), channel_id=1, source_target_pairs={{0,32},{32,0},{1,33},{33,1},{2,34},{34,2},{3,35},{35,3},{4,36},{36... | collective-permute-start | bytes 2752520 | tf_op jit(solution)/shard_map/ppermute | solution.py:374
  87.3 44.0 %copy-start.1 = (bf16[16,80,128]{2,1,0:T(8,128)(2,1)S(1)}, bf16[16,80,128]{2,1,0:T(8,128)(2,1)}, u32[]{:S(2)}) copy-start(bf16[16,80,128]{2,1,0:T(8,128)(2,1)} %get-tuple-element.19) | copy-start | bytes 983044
  132.5 30.0 %all-to-all-start.7 = ((bf16[16,336,128]{2,1,0:T(8,128)(2,1)}), bf16[16,336,128]{2,1,0:T(8,128)(2,1)S(1)}, u32[]{:S(2)}, u32[]{:S(2)}) async-start(bf16[16,336,128]{2,1,0:T(8,128)(2,1)} %pad_maximum_fusion), calls=%async_computation.7 | async-start | bytes 2752512 | tf_op jit(solution)/shard_map/all_to_all | solution.py:249
  141.7 19.7 %collective-permute-start.4 = (bf16[640,128]{1,0:T(8,128)(2,1)S(1)}, bf16[640,128]{1,0:T(8,128)(2,1)S(1)}, u32[]{:S(2)}, u32[]{:S(2)}) collective-permute-start(bf16[640,128]{1,0:T(8,128)(2,1)S(1)} %slice.9.own_ref), channel_id=1, source_target_pairs={{0,1},{1,0},{2,3},{3,2},{4,5},{5,4},{6,7},{7,6},{8,9},{9,8},{10,11... | collective-permute-start | bytes 491528 | tf_op jit(solution)/shard_map/ppermute | solution.py:393

commit v6 on v5

--- a/solution.py
+++ b/solution.py
@@ -22,6 +22,8 @@
 HALF = 8
 STEPS = CLIPS * HALF
 SLOTS = 2 * CLIPS
+PAY = 26
+CHIPS = 8
 PACK = 896
 HALF_ROWS = 8 * ROWS
 MIB = 1024 * 1024
@@ -80,6 +82,7 @@
     for target in range(HOLDERS):
         pay_ref[target, :CLIPS] = mel_ref[...]
         pay_ref[target, CLIPS] = length.astype(BF16)
+        pay_ref[target, CLIPS + 1 :] = jnp.zeros((PAY - CLIPS - 1, 2 * HALF, MEL), BF16)
 
 
 def forward_kernel(
@@ -123,7 +126,9 @@
     part_ref[0] = total.astype(BF16)
 
 
-def middle_kernel(part_ref, grad_ref, b2_ref, length_ref, owner_col_ref, owner_row_ref, rep_ref, feature_ref):
+def middle_kernel(
+    where_ref, part_ref, grad_ref, b2_ref, length_ref, owner_col_ref, owner_row_ref, rep_ref, same_ref, cross_ref
+):
     pre = part_ref[0].astype(F32)
     for source in range(1, HOLDERS):
         pre = pre + part_ref[source].astype(F32)
@@ -143,12 +148,15 @@
     place = lax.broadcasted_iota(jnp.int32, (1, STEPS), 1) & (HALF - 1)
     place = (owner_row_ref[...] * 2 + rank.astype(jnp.int32)) * HALF + place
     wanted = lax.broadcasted_iota(jnp.int32, (SLOTS * HALF, STEPS), 0) == place
-    placed = dot(jnp.where(wanted, 1.0, 0.0).astype(BF16), features).astype(BF16)
-    for target in range(16):
+    placed = dot(jnp.where(wanted, 1.0, 0.0).astype(BF16), features)
+    first = where_ref[2] == 0
+    for chip in range(CHIPS):
         for tile in range(D2 // LANES):
-            feature_ref[target, tile * 16 : (tile + 1) * 16, :] = placed[
-                target * 16 : (target + 1) * 16, tile * LANES : (tile + 1) * LANES
-            ]
+            rows, columns = slice(tile * 16, (tile + 1) * 16), slice(tile * LANES, (tile + 1) * LANES)
+            left = placed[chip * 32 : chip * 32 + 16, columns]
+            right = placed[chip * 32 + 16 : chip * 32 + 32, columns]
+            same_ref[chip, rows, :] = jnp.where(first, left, right).astype(BF16)
+            cross_ref[chip, rows, :] = jnp.where(first, right, left).astype(BF16)
 
 
 def backward_kernel(
@@ -215,33 +223,45 @@
 
 
 def last_kernel(
-    where_ref, got_ref, feature_ref, bias_ref, own_ref, other_ref,
+    where_ref, got_ref, got_cross_ref, feature_ref, feature_cross_ref, bias_ref, bias_cross_ref, own_ref, other_ref,
     weight_ref, bias1_ref, bias2_ref, conv2_ref, packed_ref, whole,
 ):
-    for source in range(16):
-        whole[source * ROWS : (source + 1) * ROWS, :] = got_ref[source].astype(F32)
+    first = where_ref[2] == 0
+
+    def in_order(here, there):
+        here, there = here.astype(F32), there.astype(F32)
+        return jnp.where(first, here, there), jnp.where(first, there, here)
+
+    for chip in range(CHIPS):
+        start = 2 * chip * ROWS
+        left, right = in_order(got_ref[chip], got_cross_ref[chip])
+        whole[start : start + ROWS, :] = left
+        whole[start + ROWS : start + 2 * ROWS, :] = right
     for block in range(10):
         columns = slice(block * LANES, (block + 1) * LANES)
         weight_ref[:, columns] = whole[columns, :].T
 
     @pl.when(pl.program_id(0) == 0)
     def _():
-        pieces = [bias_ref[source].astype(F32) for source in range(16)]
+        pieces = []
+        for chip in range(CHIPS):
+            pieces.extend(in_order(bias_ref[chip], bias_cross_ref[chip]))
         bias1 = jnp.concatenate([piece[0:1, :ROWS] for piece in pieces], axis=1)
         bias1_ref[...] = bias1.reshape(16 * ROWS)
         bias2 = jnp.concatenate([pieces[0][1 + tile : 2 + tile, :] for tile in range(D2 // LANES)], axis=1)
         bias2_ref[...] = bias2.reshape(D2)
-        for source in range(16):
+        for chip in range(CHIPS):
+            left, right = in_order(feature_ref[chip], feature_cross_ref[chip])
             for tile in range(D2 // LANES):
-                packed_ref[source * 16 : (source + 1) * 16, tile * LANES : (tile + 1) * LANES] = feature_ref[
-                    source, tile * 16 : (tile + 1) * 16, :
-                ]
-        first = where_ref[1] == 0
+                rows, columns = slice(tile * 16, (tile + 1) * 16), slice(tile * LANES, (tile + 1) * LANES)
+                packed_ref[chip * 32 : chip * 32 + 16, columns] = left[rows, :].astype(BF16)
+                packed_ref[chip * 32 + 16 : chip * 32 + 32, columns] = right[rows, :].astype(BF16)
+        lower = where_ref[1] == 0
         for tile in range(15):
             half, spot = tile // 8, tile % 8
             rows = slice(spot * ROWS, (spot + 1) * ROWS)
             own, other = own_ref[rows, :].astype(F32), other_ref[rows, :].astype(F32)
-            picked = jnp.where(first, own, other) if half == 0 else jnp.where(first, other, own)
+            picked = jnp.where(lower, own, other) if half == 0 else jnp.where(lower, other, own)
             conv2_ref[:, tile * LANES : (tile + 1) * LANES] = picked
 
 
@@ -263,7 +283,7 @@
 
 def local(mel, lengths, routes, conv1_weight, conv1_bias, conv2_weight, conv2_bias, out_grad):
     x_hi, y, core = lax.axis_index("xh"), lax.axis_index("y"), lax.axis_index("c")
-    where = jnp.stack([x_hi, lax.axis_index("xl")]).astype(jnp.int32)
+    where = jnp.stack([x_hi, lax.axis_index("xl"), core]).astype(jnp.int32)
 
     def shape(*dims, dtype=BF16):
         return jax.ShapeDtypeStruct(dims, dtype)
@@ -278,7 +298,18 @@
         prepare_kernel,
         in_specs=[pl.BlockSpec(memory_space=pltpu.SMEM), vmem()],
         out_specs=vmem(),
-        out_shape=in_hbm(HOLDERS, CLIPS + 1, 2 * HALF, MEL),
+        out_shape=in_hbm(HOLDERS, PAY, 2 * HALF, MEL),
+        compiler_params=params(60),
+        name="mel_payload",
+    )(lengths, mel)
+    got_pay = exchange(pay, "y")
+    cores = [(0, 1), (1, 0)]
+    far_weight = lax.ppermute(conv2_weight, ("xh", "xl"), [(0, 3), (3, 0), (1, 2), (2, 1)])
+    pay = pl.pallas_call(
+        prepare_kernel,
+        in_specs=[pl.BlockSpec(memory_space=pltpu.SMEM), vmem()],
+        out_specs=vmem(),
+        out_shape=in_hbm(HOLDERS, PAY, 2 * HALF, MEL),
         compiler_params=params(60),
         name="mel_payload",
     )(lengths, mel)
@@ -298,6 +329,14 @@
     gap = WIDE - BLOCKS * ROWS
     w1 = jnp.concatenate(w1 + [jnp.zeros((3 * MEL, gap), BF16)], axis=1)
     b1 = jnp.concatenate(b1 + [jnp.zeros((gap,), F32)])[None]
+    own_weight, b1 = lax.optimization_barrier((conv2_weight, b1))
+    far_weight, b1 = lax.optimization_barrier((far_weight, b1))
+    weights = [
+        conv2_weight,
+        lax.ppermute(own_weight, "c", cores),
+        far_weight,
+        lax.ppermute(far_weight, "c", cores),
+    ]
 
     pair = lambda i: (i, 0, 0)
     pair4 = lambda i: (i, 0, 0, 0)
@@ -306,7 +345,7 @@
         forward_kernel,
         grid=(HOLDERS,),
         in_specs=[
-            pl.BlockSpec((1, CLIPS + 1, 2 * HALF, MEL), pair4),
+            pl.BlockSpec((1, PAY, 2 * HALF, MEL), pair4),
             pl.BlockSpec((3 * MEL, WIDE), lambda i: (0, 0)),
             pl.BlockSpec((1, WIDE), lambda i: (0, 0)),
             *[weight_spec] * BLOCKS,
@@ -330,14 +369,15 @@
 
     got_parts = exchange(parts, "y")
     owner = jnp.repeat(routes[:, 0], HALF)
-    rep, features = pl.pallas_call(
+    rep, same, cross = pl.pallas_call(
         middle_kernel,
-        in_specs=[vmem()] * 6,
-        out_specs=[vmem()] * 2,
-        out_shape=[in_hbm(HOLDERS, STEPS, D2), in_hbm(16, ROWS, LANES)],
+        in_specs=[pl.BlockSpec(memory_space=pltpu.SMEM)] + [vmem()] * 6,
+        out_specs=[vmem()] * 3,
+        out_shape=[in_hbm(HOLDERS, STEPS, D2), shape(CHIPS, ROWS, LANES), shape(CHIPS, ROWS, LANES)],
         compiler_params=params(10),
         name="stem_middle",
     )(
+        where,
         got_parts,
         from_hbm(out_grad.reshape(STEPS, D2)),
         conv2_bias[None],
@@ -371,7 +411,7 @@
         compiler_params=params(32, "arbitrary"),
         name="stem_backward",
     )(where, got_grad, *weights, from_hbm(cols), from_hbm(acts), from_hbm(slopes))
-    got = lax.ppermute(send, "c", [(0, 1), (1, 0)])
+    got = lax.ppermute(send, "c", cores)
     quarters = exchange((keep + got.astype(F32)).astype(BF16).reshape(4, PACK, LANES), ("xh", "xl"))
 
     def summed(values, *dims):
@@ -391,15 +431,21 @@
     half = exchange(far, "zl").reshape(PACK, LANES)
     own = half[:HALF_ROWS]
     other = lax.ppermute(own, "xl", [(0, 1), (1, 0)])
-    shares = exchange(jnp.concatenate([features, spread_to(half[HALF_ROWS:], 16)], axis=1), ENC)
+    conv1 = spread_to(half[HALF_ROWS:], CHIPS)
+    got = exchange(jnp.concatenate([same, conv1[:, : 3 * ROWS], cross, conv1[:, 3 * ROWS :]], axis=1), ("xh", "y"))
+    got, other = lax.optimization_barrier((got, other))
+    got_cross = lax.ppermute(got, "c", cores)
     weight_grad, bias_grad, second_bias_grad, conv2_rows_grad, packed = pl.pallas_call(
         last_kernel,
         grid=(3,),
         in_specs=[
             pl.BlockSpec(memory_space=pltpu.SMEM),
-            pl.BlockSpec((16, ROWS, LANES), lambda i: (0, i + 1, 0)),
-            pl.BlockSpec((16, ROWS, LANES), lambda i: (0, 0, 0)),
-            pl.BlockSpec((16, 16, LANES), lambda i: (0, 4 * ROWS // 16, 0)),
+            pl.BlockSpec((CHIPS, ROWS, LANES), lambda i: (0, i + 1, 0)),
+            pl.BlockSpec((CHIPS, ROWS, LANES), lambda i: (0, i + 1, 0)),
+            pl.BlockSpec((CHIPS, ROWS, LANES), lambda i: (0, 0, 0)),
+            pl.BlockSpec((CHIPS, ROWS, LANES), lambda i: (0, 4, 0)),
+            pl.BlockSpec((CHIPS, 16, LANES), lambda i: (0, 5 * ROWS // 16, 0)),
+            pl.BlockSpec((CHIPS, 16, LANES), lambda i: (0, 5 * ROWS // 16, 0)),
             pl.BlockSpec((HALF_ROWS, LANES), lambda i: (0, 0)),
             pl.BlockSpec((HALF_ROWS, LANES), lambda i: (0, 0)),
         ],
@@ -420,7 +466,7 @@
         scratch_shapes=[pltpu.VMEM((16 * ROWS, LANES), F32)],
         compiler_params=params(16, "arbitrary"),
         name="gradient_unpack",
-    )(where, shares, shares, shares, own, other)
+    )(where, got, got_cross, got, got_cross, got, got_cross, own, other)
     return packed.reshape(SLOTS, HALF, D2), weight_grad, bias_grad, second_bias_grad, conv2_rows_grad
 
 

time: 166 us -> 159 us (0.958)
  waiting for transfers between devices: 39.5 us -> 20.1 us
  blocking collectives: 59.7 us -> 74.5 us
  starting transfers between devices: 43.1 us -> 40.5 us
    all_to_all x4 -> x5, blocking collectives: 59.7 us -> 74.5 us  [exchange(): return lax.all_to_all(values, axes, split_axis=0, concat_axis=0, tiled=True)]
    all_to_all x4 -> x3, waiting for transfers between devices: 20 us -> 9.02 us  [exchange(): return lax.all_to_all(values, axes, split_axis=0, concat_axis=0, tiled=True)]
    ppermute x1, waiting for transfers between devices: 17.5 us -> 6.97 us  [local(): other = lax.ppermute(own, 'xl', [(0, 1), (1, 0)])]
    all_to_all x4 -> x3, starting transfers between devices: 19.6 us -> 12.1 us  [exchange(): return lax.all_to_all(values, axes, split_axis=0, concat_axis=0, tiled=True)]
    ppermute x3 -> x4, starting transfers between devices: 13.8 us -> 20.3 us  [the longest x1 8.9 us: local(): got_cross = lax.ppermute(got, 'c', cores)]
    ppermute x1, starting transfers between devices: 7.48 us -> 5.35 us  [local(): lax.ppermute(conv2_weight, ('xh', 'xl'), [(0, 3), (3, 0), (1, 2), (2, 1)])]
    ppermute x3 -> x4, waiting for transfers between devices: 2.08 us -> 4.07 us  [the longest x1 2.08 us: local(): got = lax.ppermute(send, 'c', cores)]
  transfers between devices with their start and end apart: 9 -> 9, of which waited for: 6 -> 4; matrix products, arithmetic and copies ran while one was open for 2% -> 2% of each run, Pallas kernels for 1% -> 1%
where the time goes in v6:
time: 159 us; the launch traced here: 158 us
  blocking collectives  74.5 us (47%)
  starting transfers between devices  40.5 us (25%)
  waiting for transfers between devices  20.1 us (13%)
  Pallas kernels  17 us (11%)
  local copies, waits for them, and re-layouts  3.86 us (2%)
    all_to_all x5, blocking collectives, exchange(): return lax.all_to_all(values, axes, split_axis=0, concat_axis=0, tiled=True)  74.5 us
    all_to_all x3, starting transfers between devices, exchange(): return lax.all_to_all(values, axes, split_axis=0, concat_axis=0, tiled=True)  12.1 us
    all_to_all x3, waiting for transfers between devices, exchange(): return lax.all_to_all(values, axes, split_axis=0, concat_axis=0, tiled=True)  9.02 us
    ppermute x1, starting transfers between devices, local(): got_cross = lax.ppermute(got, 'c', cores)  8.9 us
    ppermute x1, waiting for transfers between devices, local(): other = lax.ppermute(own, 'xl', [(0, 1), (1, 0)])  6.97 us
    pallas_call x1, Pallas kernels, local(): pl.pallas_call(backward_kernel, grid=(HOLDERS // 2,), in_specs=[pl.BlockS...  5.5 us
    ppermute x1, starting transfers between devices, local(): lax.ppermute(conv2_weight, ('xh', 'xl'), [(0, 3), (3, 0), (1, 2), (2, 1)])  5.35 us
    ppermute x1, starting transfers between devices, local(): lax.ppermute(own_weight, 'c', cores)  4.82 us
  transfers between devices with their start and end apart: 9, of which 4 were waited for; matrix products, arithmetic and copies ran while one was open for 2% of the time, Pallas kernels for 1%

profile of v6, /device:TPU:1, one launch (start us, length us, event | category | flops | bytes accessed | tf_op | source)
XLA Modules:
  0.0 158.1 jit_solution(8750849890488394592)
XLA Ops:
  0.6 0.0 copy-start
  0.6 5.3 %collective-permute-start = (bf16[80,1920]{1,0:T(8,128)(2,1)}, bf16[80,1920]{1,0:T(8,128)(2,1)S(1)}, u32[]{:S(2)}, u32[]{:S(2)}) collective-permute-start(bf16[80,1920]{1,0:T(8,128)(2,1)} %own_ref.3), channel_id=1, source_target_pairs={{0,257},{257,0},{1,256},{256,1},{2,259},{259,2},{3,258},{258,3},{4... | collective-permute-start | bytes 921608 | tf_op jit(solution)/shard_map/ppermute | solution.py:307
  6.0 1.7 %mel_payload.1 = bf16[4,26,16,128]{3,2,1,0:T(8,128)(2,1)} custom-call(s32[16]{0:T(128)} %length_ref.1, bf16[16,16,128]{2,1,0:T(8,128)(2,1)} %mel_ref.1), custom_call_target="tpu_custom_call" | custom-call | tf_op jit(solution)/shard_map/mel_payload/pallas_call | solution.py:308
  7.7 4.2 %all-to-all-start = ((bf16[4,26,16,128]{3,2,1,0:T(8,128)(2,1)}), bf16[4,26,16,128]{3,2,1,0:T(8,128)(2,1)S(1)}, u32[]{:S(2)}, u32[]{:S(2)}) async-start(bf16[4,26,16,128]{3,2,1,0:T(8,128)(2,1)} %mel_payload.1), calls=%async_computation | async-start | bytes 851968 | tf_op jit(solution)/shard_map/all_to_all | solution.py:269
  11.8 0.9 fusion
  12.8 0.1 concatenate.10
  12.9 4.8 %collective-permute-start.1 = (bf16[80,1920]{1,0:T(8,128)(2,1)}, bf16[80,1920]{1,0:T(8,128)(2,1)S(1)}, u32[]{:S(2)}, u32[]{:S(2)}) collective-permute-start(bf16[80,1920]{1,0:T(8,128)(2,1)} %own_ref.3), channel_id=1, source_target_pairs={{0,32},{32,0},{1,33},{33,1},{2,34},{34,2},{3,35},{35,3},{4,36},{36... | collective-permute-start | bytes 921608 | tf_op jit(solution)/shard_map/ppermute | solution.py:336
  17.7 0.0 collective-permute-done.far_ref
  17.7 2.0 %collective-permute-start.2 = (bf16[80,1920]{1,0:T(8,128)(2,1)S(1)}, bf16[80,1920]{1,0:T(8,128)(2,1)S(1)}, u32[]{:S(2)}, u32[]{:S(2)}) collective-permute-start(bf16[80,1920]{1,0:T(8,128)(2,1)S(1)} %collective-permute-done.far_ref), channel_id=1, source_target_pairs={{0,32},{32,0},{1,33},{33,1},{2,34},{34,2},{3,35},{35,3},{4,36},{36... | collective-permute-start | bytes 921608 | tf_op jit(solution)/shard_map/ppermute | solution.py:338
  19.7 1.4 constant_dynamic-slice_fusion
  21.2 0.3 concatenate.9.w1_ref
  21.5 0.0 copy-start.2
  21.5 0.0 copy-start.3
  21.5 0.0 copy-start.1
  21.5 0.0 collective-permute-done.1.side_ref
  21.5 0.0 all-to-all-done.pay_ref
  21.5 0.0 collective-permute-done.2.both_ref
  21.5 0.0 copy-done
  21.5 4.4 %stem_forward.1 = (bf16[4,128,640]{2,1,0:T(8,128)(2,1)}, bf16[4,128,512]{2,1,0:T(8,128)(2,1)}, bf16[4,3,128,384]{3,2,1,0:T(8,128)(2,1)}, f32[4,2,128,384]{3,2,1,0:T(8,128)}) custom-call(bf16[4,26,16,128]{3,2,1,0:T(8,128)(2,1)S(1)} %all-to-all-done.pay_ref, bf16[384,384]{1,0:T(8,128)(2,1)S(1)} %concatenate.9.w1_ref, f32[1,384]{1,0:T(1,128)S(1)} %broadcast_in_dim.28.b1_ref, ...), custom_call_target="tpu_custom_call" | custom-call | tf_op jit(solution)/shard_map/stem_forward/pallas_call | solution.py:344
  25.9 4.3 %all-to-all-start.1 = ((bf16[4,128,640]{2,1,0:T(8,128)(2,1)}), bf16[4,128,640]{2,1,0:T(8,128)(2,1)S(1)}, u32[]{:S(2)}, u32[]{:S(2)}) async-start(bf16[4,128,640]{2,1,0:T(8,128)(2,1)} %get-tuple-element.29), calls=%async_computation.1 | async-start | bytes 1310720 | tf_op jit(solution)/shard_map/all_to_all | solution.py:269
  30.3 0.0 copy-done.2
  30.3 0.1 broadcast_in_dim.31
  30.3 0.1 broadcast_in_dim_reshape.11.owner_row_ref
  30.4 0.1 broadcast_in_dim_reshape.13.owner_col_ref
  30.5 0.1 broadcast_in_dim.30
  30.6 0.7 broadcast_in_dim_reshape.12.length_ref
  31.3 0.1 pad_add_fusion.where_ref
  31.4 9.0 %all-to-all-done.1.part_ref = bf16[4,128,640]{2,1,0:T(8,128)(2,1)S(1)} async-done(((bf16[4,128,640]{2,1,0:T(8,128)(2,1)}), bf16[4,128,640]{2,1,0:T(8,128)(2,1)S(1)}, u32[]{:S(2)}, u32[]{:S(2)}) %all-to-all-start.1) | async-done | bytes 655392 | tf_op jit(solution)/shard_map/all_to_all | solution.py:269
  40.4 2.1 %stem_middle.1 = (bf16[4,128,640]{2,1,0:T(8,128)(2,1)}, bf16[8,80,128]{2,1,0:T(8,128)(2,1)S(1)}, bf16[8,80,128]{2,1,0:T(8,128)(2,1)S(1)}) custom-call(s32[3]{0:T(128)S(1)} %pad_add_fusion.where_ref, bf16[4,128,640]{2,1,0:T(8,128)(2,1)S(1)} %all-to-all-done.1.part_ref, bf16[128,640]{1,0:T(8,128)(2,1)} %bitcast.14, f32[1,640]{1,0:T(1,128)S(1)} %broadcast_in_dim.29.b2_ref, ...), custom_call_target="tpu_custom_call" | custom-call | tf_op jit(solution)/shard_map/stem_middle/pallas_call | solution.py:372
  42.5 12.7 %all_to_all.40.grad_ref = bf16[4,128,640]{2,1,0:T(8,128)(2,1)S(1)} all-to-all(bf16[4,128,640]{2,1,0:T(8,128)(2,1)} %get-tuple-element.31), channel_id=1, replica_groups=mesh['xh'=2,'y'=4,'c'=2,'zh'=4,'zl'=4,'xl'=2] {'y'}, dimensions={0} | all-to-all | bytes 1310720 | tf_op jit(solution)/shard_map/all_to_all | solution.py:269
  55.2 5.5 %stem_backward.1 = (f32[2,2,896,128]{3,2,1,0:T(8,128)S(1)}, bf16[2,2,896,128]{3,2,1,0:T(8,128)(2,1)S(1)}) custom-call(s32[3]{0:T(128)S(1)} %pad_add_fusion.where_ref, bf16[4,128,640]{2,1,0:T(8,128)(2,1)S(1)} %all_to_all.40.grad_ref, bf16[80,1920]{1,0:T(8,128)(2,1)S(1)} %copy-done, bf16[80,1920]{1,0:T(8,128)(2,1)S(1)} %collective-permute-done.1.side_ref, ...), custom_call_target="tpu_custom_call" | custom-call | tf_op jit(solution)/shard_map/stem_backward/pallas_call | solution.py:391
  60.7 4.5 %collective-permute-start.3 = (bf16[2,2,896,128]{3,2,1,0:T(8,128)(2,1)S(1)}, bf16[2,2,896,128]{3,2,1,0:T(8,128)(2,1)S(1)}, u32[]{:S(2)}, u32[]{:S(2)}) collective-permute-start(bf16[2,2,896,128]{3,2,1,0:T(8,128)(2,1)S(1)} %get-tuple-element.36), channel_id=1, source_target_pairs={{0,32},{32,0},{1,33},{33,1},{2,34},{34,2},{3,35},{35,3},{4,36},{36... | collective-permute-start | bytes 2752520 | tf_op jit(solution)/shard_map/ppermute | solution.py:414
  65.2 2.1 %collective-permute-done.3 = bf16[2,2,896,128]{3,2,1,0:T(8,128)(2,1)S(1)} collective-permute-done((bf16[2,2,896,128]{3,2,1,0:T(8,128)(2,1)S(1)}, bf16[2,2,896,128]{3,2,1,0:T(8,128)(2,1)S(1)}, u32[]{:S(2)}, u32[]{:S(2)}) %collective-permute-start.3) | collective-permute-done | bytes 917536 | tf_op jit(solution)/shard_map/ppermute | solution.py:414
  67.3 0.2 add_convert_fusion
  67.5 16.9 %all_to_all.41.got_ref = bf16[4,896,128]{2,1,0:T(8,128)(2,1)S(1)} all-to-all(bf16[4,896,128]{2,1,0:T(8,128)(2,1)S(1)} %bitcast.10), channel_id=1, replica_groups=mesh['xh'=2,'y'=4,'c'=2,'zh'=4,'zl'=4,'xl'=2] {'xh','xl'}, dimensions={0} | all-to-all | bytes 1835008 | tf_op jit(solution)/shard_map/all_to_all | solution.py:269
  84.4 0.1 gradient_sum.3
  84.5 8.1 %all_to_all.42.got_ref = bf16[4,224,128]{2,1,0:T(8,128)(2,1)S(1)} all-to-all(bf16[4,224,128]{2,1,0:T(8,128)(2,1)S(1)} %bitcast.9), channel_id=1, replica_groups=mesh['xh'=2,'y'=4,'c'=2,'zh'=4,'zl'=4,'xl'=2] {'zl'}, dimensions={0} | all-to-all | bytes 458752 | tf_op jit(solution)/shard_map/all_to_all | solution.py:269
  92.7 28.7 %all_to_all.43.got_ref = bf16[4,224,128]{2,1,0:T(8,128)(2,1)S(1)} all-to-all(bf16[4,224,128]{2,1,0:T(8,128)(2,1)S(1)} %gradient_sum.4), channel_id=1, replica_groups=mesh['xh'=2,'y'=4,'c'=2,'zh'=4,'zl'=4,'xl'=2] {'zh'}, dimensions={0} | all-to-all | bytes 458752 | tf_op jit(solution)/shard_map/all_to_all | solution.py:269
  121.4 8.1 %all_to_all.44 = bf16[4,224,128]{2,1,0:T(8,128)(2,1)S(1)} all-to-all(bf16[4,224,128]{2,1,0:T(8,128)(2,1)S(1)} %gradient_sum.5), channel_id=1, replica_groups=mesh['xh'=2,'y'=4,'c'=2,'zh'=4,'zl'=4,'xl'=2] {'zl'}, dimensions={0} | all-to-all | bytes 458752 | tf_op jit(solution)/shard_map/all_to_all | solution.py:269
  129.6 0.1 broadcast_in_dim.32
  129.6 1.0 pad_maximum_fusion
  130.6 3.6 %all-to-all-start.7 = ((bf16[8,416,128]{2,1,0:T(8,128)(2,1)}), bf16[8,416,128]{2,1,0:T(8,128)(2,1)S(1)}, u32[]{:S(2)}, u32[]{:S(2)}) async-start(bf16[8,416,128]{2,1,0:T(8,128)(2,1)} %pad_maximum_fusion), calls=%async_computation.7 | async-start | bytes 1703936 | tf_op jit(solution)/shard_map/all_to_all | solution.py:269
  134.2 2.9 %collective-permute-start.4 = (bf16[640,128]{1,0:T(8,128)(2,1)S(1)}, bf16[640,128]{1,0:T(8,128)(2,1)S(1)}, u32[]{:S(2)}, u32[]{:S(2)}) collective-permute-start(bf16[640,128]{1,0:T(8,128)(2,1)S(1)} %slice.20.own_ref), channel_id=1, source_target_pairs={{0,1},{1,0},{2,3},{3,2},{4,5},{5,4},{6,7},{7,6},{8,9},{9,8},{10,11... | collective-permute-start | bytes 491528 | tf_op jit(solution)/shard_map/ppermute | solution.py:433
  137.1 7.0 %collective-permute-done.4.other_ref = bf16[640,128]{1,0:T(8,128)(2,1)S(1)} collective-permute-done((bf16[640,128]{1,0:T(8,128)(2,1)S(1)}, bf16[640,128]{1,0:T(8,128)(2,1)S(1)}, u32[]{:S(2)}, u32[]{:S(2)}) %collective-permute-start.4) | collective-permute-done | bytes 163872 | tf_op jit(solution)/shard_map/ppermute | solution.py:433
  144.0 0.0 all-to-all-done.7.got_ref.feature_ref.bias_ref
  144.0 8.9 %collective-permute-start.5 = (bf16[8,416,128]{2,1,0:T(8,128)(2,1)S(1)}, bf16[8,416,128]{2,1,0:T(8,128)(2,1)S(1)}, u32[]{:S(2)}, u32[]{:S(2)}) collective-permute-start(bf16[8,416,128]{2,1,0:T(8,128)(2,1)S(1)} %all-to-all-done.7.got_ref.feature_ref.bias_ref), channel_id=1, source_target_pairs={{0,32},{32,0},{1,33},{33,1},{2,34},{34,2},{3,35},{35,3},{4,36},{36... | collective-permute-start | bytes 2555912 | tf_op jit(solution)/shard_map/ppermute | solution.py:437
  152.9 2.0 %collective-permute-done.5.got_cross_ref.feature_cross_ref.bias_cross_ref = bf16[8,416,128]{2,1,0:T(8,128)(2,1)S(1)} collective-permute-done((bf16[8,416,128]{2,1,0:T(8,128)(2,1)S(1)}, bf16[8,416,128]{2,1,0:T(8,128)(2,1)S(1)}, u32[]{:S(2)}, u32[]{:S(2)}) %collective-permute-start.5) | collective-permute-done | bytes 852000 | tf_op jit(solution)/shard_map/ppermute | solution.py:437
  154.9 3.1 %gradient_unpack.1 = (f32[384,1280]{1,0:T(8,128)}, f32[1280]{0:T(1024)}, f32[640]{0:T(1024)}, f32[80,1920]{1,0:T(8,128)}, bf16[256,640]{1,0:T(8,128)(2,1)}) custom-call(s32[3]{0:T(128)S(1)} %pad_add_fusion.where_ref, bf16[8,416,128]{2,1,0:T(8,128)(2,1)S(1)} %all-to-all-done.7.got_ref.feature_ref.bias_ref, ...), custom_call_target="tpu_custom_call" | custom-call | tf_op jit(solution)/shard_map/gradient_unpack/pallas_call | solution.py:438
  (13 shorter events, 0.1 us)
Async XLA Ops:
  0.6 20.9 %copy-start = (bf16[80,1920]{1,0:T(8,128)(2,1)S(1)}, bf16[80,1920]{1,0:T(8,128)(2,1)}, u32[]{:S(2)}) copy-start(bf16[80,1920]{1,0:T(8,128)(2,1)} %own_ref.3) | copy-start | bytes 921604
  0.6 17.0 %collective-permute-start = (bf16[80,1920]{1,0:T(8,128)(2,1)}, bf16[80,1920]{1,0:T(8,128)(2,1)S(1)}, u32[]{:S(2)}, u32[]{:S(2)}) collective-permute-start(bf16[80,1920]{1,0:T(8,128)(2,1)} %own_ref.3), channel_id=1, source_target_pairs={{0,257},{257,0},{1,256},{256,1},{2,259},{259,2},{3,258},{258,3},{4... | collective-permute-start | bytes 921608 | tf_op jit(solution)/shard_map/ppermute | solution.py:307
  7.7 13.8 %all-to-all-start = ((bf16[4,26,16,128]{3,2,1,0:T(8,128)(2,1)}), bf16[4,26,16,128]{3,2,1,0:T(8,128)(2,1)S(1)}, u32[]{:S(2)}, u32[]{:S(2)}) async-start(bf16[4,26,16,128]{3,2,1,0:T(8,128)(2,1)} %mel_payload.1), calls=%async_computation | async-start | bytes 851968 | tf_op jit(solution)/shard_map/all_to_all | solution.py:269
  12.9 8.6 %collective-permute-start.1 = (bf16[80,1920]{1,0:T(8,128)(2,1)}, bf16[80,1920]{1,0:T(8,128)(2,1)S(1)}, u32[]{:S(2)}, u32[]{:S(2)}) collective-permute-start(bf16[80,1920]{1,0:T(8,128)(2,1)} %own_ref.3), channel_id=1, source_target_pairs={{0,32},{32,0},{1,33},{33,1},{2,34},{34,2},{3,35},{35,3},{4,36},{36... | collective-permute-start | bytes 921608 | tf_op jit(solution)/shard_map/ppermute | solution.py:336
  17.7 3.8 %collective-permute-start.2 = (bf16[80,1920]{1,0:T(8,128)(2,1)S(1)}, bf16[80,1920]{1,0:T(8,128)(2,1)S(1)}, u32[]{:S(2)}, u32[]{:S(2)}) collective-permute-start(bf16[80,1920]{1,0:T(8,128)(2,1)S(1)} %collective-permute-done.far_ref), channel_id=1, source_target_pairs={{0,32},{32,0},{1,33},{33,1},{2,34},{34,2},{3,35},{35,3},{4,36},{36... | collective-permute-start | bytes 921608 | tf_op jit(solution)/shard_map/ppermute | solution.py:338
  21.5 8.8 %copy-start.2 = (s32[16]{0:T(128)S(1)}, s32[16]{0:T(128)}, u32[]{:S(2)}) copy-start(s32[16]{0:T(128)} %length_ref.1) | copy-start | bytes 196
  21.5 8.8 %copy-start.3 = (s32[16,1]{0,1:T(1,128)S(1)}, s32[16,1]{0,1:T(1,128)}, u32[]{:S(2)}) copy-start(s32[16,1]{0,1:T(1,128)} %param.10) | copy-start | bytes 196
  21.5 9.0 %copy-start.1 = (f32[640]{0:T(1024)S(1)}, f32[640]{0:T(1024)}, u32[]{:S(2)}) copy-start(f32[640]{0:T(1024)} %param.14) | copy-start | bytes 7684
  25.9 14.5 %all-to-all-start.1 = ((bf16[4,128,640]{2,1,0:T(8,128)(2,1)}), bf16[4,128,640]{2,1,0:T(8,128)(2,1)S(1)}, u32[]{:S(2)}, u32[]{:S(2)}) async-start(bf16[4,128,640]{2,1,0:T(8,128)(2,1)} %get-tuple-element.29), calls=%async_computation.1 | async-start | bytes 1310720 | tf_op jit(solution)/shard_map/all_to_all | solution.py:269
  60.7 6.6 %collective-permute-start.3 = (bf16[2,2,896,128]{3,2,1,0:T(8,128)(2,1)S(1)}, bf16[2,2,896,128]{3,2,1,0:T(8,128)(2,1)S(1)}, u32[]{:S(2)}, u32[]{:S(2)}) collective-permute-start(bf16[2,2,896,128]{3,2,1,0:T(8,128)(2,1)S(1)} %get-tuple-element.36), channel_id=1, source_target_pairs={{0,32},{32,0},{1,33},{33,1},{2,34},{34,2},{3,35},{35,3},{4,36},{36... | collective-permute-start | bytes 2752520 | tf_op jit(solution)/shard_map/ppermute | solution.py:414
  130.6 13.4 %all-to-all-start.7 = ((bf16[8,416,128]{2,1,0:T(8,128)(2,1)}), bf16[8,416,128]{2,1,0:T(8,128)(2,1)S(1)}, u32[]{:S(2)}, u32[]{:S(2)}) async-start(bf16[8,416,128]{2,1,0:T(8,128)(2,1)} %pad_maximum_fusion), calls=%async_computation.7 | async-start | bytes 1703936 | tf_op jit(solution)/shard_map/all_to_all | solution.py:269
  134.2 9.9 %collective-permute-start.4 = (bf16[640,128]{1,0:T(8,128)(2,1)S(1)}, bf16[640,128]{1,0:T(8,128)(2,1)S(1)}, u32[]{:S(2)}, u32[]{:S(2)}) collective-permute-start(bf16[640,128]{1,0:T(8,128)(2,1)S(1)} %slice.20.own_ref), channel_id=1, source_target_pairs={{0,1},{1,0},{2,3},{3,2},{4,5},{5,4},{6,7},{7,6},{8,9},{9,8},{10,11... | collective-permute-start | bytes 491528 | tf_op jit(solution)/shard_map/ppermute | solution.py:433
  144.0 10.9 %collective-permute-start.5 = (bf16[8,416,128]{2,1,0:T(8,128)(2,1)S(1)}, bf16[8,416,128]{2,1,0:T(8,128)(2,1)S(1)}, u32[]{:S(2)}, u32[]{:S(2)}) collective-permute-start(bf16[8,416,128]{2,1,0:T(8,128)(2,1)S(1)} %all-to-all-done.7.got_ref.feature_ref.bias_ref), channel_id=1, source_target_pairs={{0,32},{32,0},{1,33},{33,1},{2,34},{34,2},{3,35},{35,3},{4,36},{36... | collective-permute-start | bytes 2555912 | tf_op jit(solution)/shard_map/ppermute | solution.py:437

commit v7 on v6

--- a/solution.py
+++ b/solution.py
@@ -83,6 +83,21 @@
         pay_ref[target, :CLIPS] = mel_ref[...]
         pay_ref[target, CLIPS] = length.astype(BF16)
         pay_ref[target, CLIPS + 1 :] = jnp.zeros((PAY - CLIPS - 1, 2 * HALF, MEL), BF16)
+
+
+def columns_kernel(where_ref, weight_ref, bias_ref, w1_ref, b1_ref, picked):
+    picked[...] = jnp.zeros_like(picked)
+    b1_ref[...] = jnp.zeros_like(b1_ref)
+    for block, flip in enumerate((0, 1, 2 * HOLDERS, 2 * HOLDERS + 1)):
+        first = (where_ref[3] ^ flip) * ROWS
+        start = pl.multiple_of(jnp.minimum((first >> 7) << 7, 16 * ROWS - 2 * LANES), LANES)
+        shift = (2 * LANES - (first - start)) & (2 * LANES - 1)
+        lanes = slice(block * ROWS, (block + 1) * ROWS)
+        window = weight_ref[:, pl.ds(start, 2 * LANES)].astype(F32)
+        picked[:, lanes] = pltpu.roll(window, shift, 1)[:, :ROWS]
+        window = jnp.broadcast_to(bias_ref[:, pl.ds(start, 2 * LANES)], (8, 2 * LANES))
+        b1_ref[:, lanes] = pltpu.roll(window, shift, 1)[0:1, :ROWS]
+    w1_ref[...] = picked[...].astype(BF16)
 
 
 def forward_kernel(
@@ -126,9 +141,7 @@
     part_ref[0] = total.astype(BF16)
 
 
-def middle_kernel(
-    where_ref, part_ref, grad_ref, b2_ref, length_ref, owner_col_ref, owner_row_ref, rep_ref, same_ref, cross_ref
-):
+def middle_kernel(part_ref, grad_ref, b2_ref, length_ref, rep_ref, feature_ref):
     pre = part_ref[0].astype(F32)
     for source in range(1, HOLDERS):
         pre = pre + part_ref[source].astype(F32)
@@ -140,6 +153,10 @@
     second_grad = (grad_ref[...].astype(F32) * slope * live).astype(BF16)
     for target in range(HOLDERS):
         rep_ref[target] = second_grad
+    feature_ref[...] = features
+
+
+def place_kernel(where_ref, feature_ref, owner_col_ref, owner_row_ref, same_ref, cross_ref):
     here = lax.broadcasted_iota(jnp.int32, (STEPS, STEPS), 0)
     there = lax.broadcasted_iota(jnp.int32, (STEPS, STEPS), 1)
     same = (owner_col_ref[...] == owner_row_ref[...]) & ((here >> 3) < (there >> 3))
@@ -148,7 +165,7 @@
     place = lax.broadcasted_iota(jnp.int32, (1, STEPS), 1) & (HALF - 1)
     place = (owner_row_ref[...] * 2 + rank.astype(jnp.int32)) * HALF + place
     wanted = lax.broadcasted_iota(jnp.int32, (SLOTS * HALF, STEPS), 0) == place
-    placed = dot(jnp.where(wanted, 1.0, 0.0).astype(BF16), features)
+    placed = dot(jnp.where(wanted, 1.0, 0.0).astype(BF16), feature_ref[...])
     first = where_ref[2] == 0
     for chip in range(CHIPS):
         for tile in range(D2 // LANES):
@@ -223,39 +240,33 @@
 
 
 def last_kernel(
-    where_ref, got_ref, got_cross_ref, feature_ref, feature_cross_ref, bias_ref, bias_cross_ref, own_ref, other_ref,
-    weight_ref, bias1_ref, bias2_ref, conv2_ref, packed_ref, whole,
+    where_ref, got_ref, cross_ref, own_ref, other_ref, weight_ref, bias1_ref, bias2_ref, conv2_ref, packed_ref,
+    whole, biases,
 ):
-    first = where_ref[2] == 0
-
-    def in_order(here, there):
-        here, there = here.astype(F32), there.astype(F32)
-        return jnp.where(first, here, there), jnp.where(first, there, here)
-
+    step, core = pl.program_id(0), where_ref[2]
+    rows = pl.ds(pl.multiple_of((step + 1) * ROWS, 16), ROWS)
     for chip in range(CHIPS):
-        start = 2 * chip * ROWS
-        left, right = in_order(got_ref[chip], got_cross_ref[chip])
-        whole[start : start + ROWS, :] = left
-        whole[start + ROWS : start + 2 * ROWS, :] = right
+        whole[pl.ds(pl.multiple_of((2 * chip + core) * ROWS, 16), ROWS), :] = got_ref[chip, rows, :]
+        whole[pl.ds(pl.multiple_of((2 * chip + 1 - core) * ROWS, 16), ROWS), :] = cross_ref[chip, rows, :]
     for block in range(10):
         columns = slice(block * LANES, (block + 1) * LANES)
-        weight_ref[:, columns] = whole[columns, :].T
-
-    @pl.when(pl.program_id(0) == 0)
+        weight_ref[:, columns] = whole[columns, :].T.astype(F32)
+
+    @pl.when(step == 0)
     def _():
-        pieces = []
         for chip in range(CHIPS):
-            pieces.extend(in_order(bias_ref[chip], bias_cross_ref[chip]))
-        bias1 = jnp.concatenate([piece[0:1, :ROWS] for piece in pieces], axis=1)
+            biases[2 * chip + core] = got_ref[chip, 5 * ROWS :, :].astype(F32)
+            biases[2 * chip + 1 - core] = cross_ref[chip, 5 * ROWS :, :].astype(F32)
+            left = pl.ds(pl.multiple_of(chip * 32 + 16 * core, 16), 16)
+            right = pl.ds(pl.multiple_of(chip * 32 + 16 - 16 * core, 16), 16)
+            for tile in range(D2 // LANES):
+                columns = slice(tile * LANES, (tile + 1) * LANES)
+                packed_ref[left, columns] = got_ref[chip, tile * 16 : (tile + 1) * 16, :]
+                packed_ref[right, columns] = cross_ref[chip, 4 * ROWS + tile * 16 : 4 * ROWS + (tile + 1) * 16, :]
+        bias1 = jnp.concatenate([biases[source, 0:1, :ROWS] for source in range(16)], axis=1)
         bias1_ref[...] = bias1.reshape(16 * ROWS)
-        bias2 = jnp.concatenate([pieces[0][1 + tile : 2 + tile, :] for tile in range(D2 // LANES)], axis=1)
+        bias2 = jnp.concatenate([biases[0, 1 + tile : 2 + tile, :] for tile in range(D2 // LANES)], axis=1)
         bias2_ref[...] = bias2.reshape(D2)
-        for chip in range(CHIPS):
-            left, right = in_order(feature_ref[chip], feature_cross_ref[chip])
-            for tile in range(D2 // LANES):
-                rows, columns = slice(tile * 16, (tile + 1) * 16), slice(tile * LANES, (tile + 1) * LANES)
-                packed_ref[chip * 32 : chip * 32 + 16, columns] = left[rows, :].astype(BF16)
-                packed_ref[chip * 32 + 16 : chip * 32 + 32, columns] = right[rows, :].astype(BF16)
         lower = where_ref[1] == 0
         for tile in range(15):
             half, spot = tile // 8, tile % 8
@@ -283,7 +294,7 @@
 
 def local(mel, lengths, routes, conv1_weight, conv1_bias, conv2_weight, conv2_bias, out_grad):
     x_hi, y, core = lax.axis_index("xh"), lax.axis_index("y"), lax.axis_index("c")
-    where = jnp.stack([x_hi, lax.axis_index("xl"), core]).astype(jnp.int32)
+    where = jnp.stack([x_hi, lax.axis_index("xl"), core, (x_hi * HOLDERS + y) * 2 + core]).astype(jnp.int32)
 
     def shape(*dims, dtype=BF16):
         return jax.ShapeDtypeStruct(dims, dtype)
@@ -321,14 +332,15 @@
         lax.ppermute(conv2_weight, ("xh", "c", "xl"), [(i, 7 - i) for i in range(8)]),
     ]
 
-    w1, b1 = [], []
-    for flip_x, flip_c in ((0, 0), (0, 1), (1, 0), (1, 1)):
-        place = ((x_hi ^ flip_x) * HOLDERS + y) * 2 + (core ^ flip_c)
-        w1.append(lax.dynamic_slice(conv1_weight, (0, place * ROWS), (3 * MEL, ROWS)))
-        b1.append(lax.dynamic_slice(conv1_bias, (place * ROWS,), (ROWS,)))
-    gap = WIDE - BLOCKS * ROWS
-    w1 = jnp.concatenate(w1 + [jnp.zeros((3 * MEL, gap), BF16)], axis=1)
-    b1 = jnp.concatenate(b1 + [jnp.zeros((gap,), F32)])[None]
+    w1, b1 = pl.pallas_call(
+        columns_kernel,
+        in_specs=[pl.BlockSpec(memory_space=pltpu.SMEM), vmem(), vmem()],
+        out_specs=[vmem()] * 2,
+        out_shape=[shape(3 * MEL, WIDE), shape(1, WIDE, dtype=F32)],
+        scratch_shapes=[pltpu.VMEM((3 * MEL, WIDE), F32)],
+        compiler_params=params(10),
+        name="conv1_columns",
+    )(where, conv1_weight, conv1_bias[None])
     own_weight, b1 = lax.optimization_barrier((conv2_weight, b1))
     far_weight, b1 = lax.optimization_barrier((far_weight, b1))
     weights = [
@@ -340,15 +352,12 @@
 
     pair = lambda i: (i, 0, 0)
     pair4 = lambda i: (i, 0, 0, 0)
-    weight_spec = pl.BlockSpec((ROWS, 3 * D2), lambda i: (0, 0))
     parts, cols, acts, slopes = pl.pallas_call(
         forward_kernel,
         grid=(HOLDERS,),
         in_specs=[
             pl.BlockSpec((1, PAY, 2 * HALF, MEL), pair4),
-            pl.BlockSpec((3 * MEL, WIDE), lambda i: (0, 0)),
-            pl.BlockSpec((1, WIDE), lambda i: (0, 0)),
-            *[weight_spec] * BLOCKS,
+            *[vmem()] * (2 + BLOCKS),
         ],
         out_specs=[
             pl.BlockSpec((1, STEPS, D2), pair),
@@ -369,37 +378,42 @@
 
     got_parts = exchange(parts, "y")
     owner = jnp.repeat(routes[:, 0], HALF)
-    rep, same, cross = pl.pallas_call(
+    rep, features = pl.pallas_call(
         middle_kernel,
-        in_specs=[pl.BlockSpec(memory_space=pltpu.SMEM)] + [vmem()] * 6,
-        out_specs=[vmem()] * 3,
-        out_shape=[in_hbm(HOLDERS, STEPS, D2), shape(CHIPS, ROWS, LANES), shape(CHIPS, ROWS, LANES)],
+        in_specs=[vmem()] * 4,
+        out_specs=[vmem()] * 2,
+        out_shape=[in_hbm(HOLDERS, STEPS, D2), shape(STEPS, D2)],
         compiler_params=params(10),
         name="stem_middle",
     )(
-        where,
         got_parts,
         from_hbm(out_grad.reshape(STEPS, D2)),
         conv2_bias[None],
         from_hbm(jnp.repeat(lengths.astype(F32), HALF)[:, None]),
-        owner[:, None],
-        owner[None],
     )
     got_grad = exchange(rep, "y")
-
-    whole = lambda i: (0, 0, 0, 0)
+    same, cross = pl.pallas_call(
+        place_kernel,
+        in_specs=[pl.BlockSpec(memory_space=pltpu.SMEM), vmem(), vmem(), vmem()],
+        out_specs=[vmem()] * 2,
+        out_shape=[shape(CHIPS, ROWS, LANES)] * 2,
+        compiler_params=params(10),
+        name="features_place",
+    )(where, features, owner[:, None], owner[None])
+    got_grad, same = lax.optimization_barrier((got_grad, same))
+
     keep, send = pl.pallas_call(
         backward_kernel,
         grid=(HOLDERS // 2,),
         in_specs=[
             pl.BlockSpec(memory_space=pltpu.SMEM),
             pl.BlockSpec((2, STEPS, D2), pair),
-            *[weight_spec] * BLOCKS,
+            *[vmem()] * BLOCKS,
             pl.BlockSpec((2, STEPS, 4 * LANES), pair),
             pl.BlockSpec((2, 3, STEPS, WIDE), pair4),
             pl.BlockSpec((2, 2, STEPS, WIDE), pair4),
         ],
-        out_specs=[pl.BlockSpec((2, 2, PACK, LANES), whole)] * 2,
+        out_specs=[vmem()] * 2,
         out_shape=[shape(2, 2, PACK, LANES, dtype=F32), shape(2, 2, PACK, LANES)],
         scratch_shapes=[
             pltpu.VMEM((WIDE, 3 * D2), BF16),
@@ -440,14 +454,7 @@
         grid=(3,),
         in_specs=[
             pl.BlockSpec(memory_space=pltpu.SMEM),
-            pl.BlockSpec((CHIPS, ROWS, LANES), lambda i: (0, i + 1, 0)),
-            pl.BlockSpec((CHIPS, ROWS, LANES), lambda i: (0, i + 1, 0)),
-            pl.BlockSpec((CHIPS, ROWS, LANES), lambda i: (0, 0, 0)),
-            pl.BlockSpec((CHIPS, ROWS, LANES), lambda i: (0, 4, 0)),
-            pl.BlockSpec((CHIPS, 16, LANES), lambda i: (0, 5 * ROWS // 16, 0)),
-            pl.BlockSpec((CHIPS, 16, LANES), lambda i: (0, 5 * ROWS // 16, 0)),
-            pl.BlockSpec((HALF_ROWS, LANES), lambda i: (0, 0)),
-            pl.BlockSpec((HALF_ROWS, LANES), lambda i: (0, 0)),
+            *[vmem()] * 4,
         ],
         out_specs=[
             pl.BlockSpec((LANES, 16 * ROWS), lambda i: (i, 0)),
@@ -463,10 +470,10 @@
             shape(ROWS, 3 * D2, dtype=F32),
             shape(SLOTS * HALF, D2),
         ],
-        scratch_shapes=[pltpu.VMEM((16 * ROWS, LANES), F32)],
+        scratch_shapes=[pltpu.VMEM((16 * ROWS, LANES), BF16), pltpu.VMEM((16, 16, LANES), F32)],
         compiler_params=params(16, "arbitrary"),
         name="gradient_unpack",
-    )(where, got, got_cross, got, got_cross, got, got_cross, own, other)
+    )(where, got, got_cross, own, other)
     return packed.reshape(SLOTS, HALF, D2), weight_grad, bias_grad, second_bias_grad, conv2_rows_grad
 
 

time: 159 us -> 162 us (1.019)
  blocking collectives: 74.5 us -> 63.2 us
  waiting for transfers between devices: 20.1 us -> 31.2 us
  starting transfers between devices: 40.5 us -> 43.3 us
  Pallas kernels: 17 us -> 19.1 us
  local copies, waits for them, and re-layouts: 3.86 us -> 1.85 us
    all_to_all x5 -> x4, blocking collectives: 74.5 us -> 63.2 us  [exchange(): return lax.all_to_all(values, axes, split_axis=0, concat_axis=0, tiled=True)]
    all_to_all x3 -> x4, waiting for transfers between devices: 9.02 us -> 19 us  [exchange(): return lax.all_to_all(values, axes, split_axis=0, concat_axis=0, tiled=True)]
    all_to_all x3 -> x4, starting transfers between devices: 12.1 us -> 15.8 us  [exchange(): return lax.all_to_all(values, axes, split_axis=0, concat_axis=0, tiled=True)]
    dynamic_slice x2 -> x0, local copies, waits for them, and re-layouts: 2.34 us -> none  [the longest x1 1.42 us: local(): lax.dynamic_slice(conv1_weight, (0, place * ROWS), (3 * MEL, ROWS))]
    pallas_call x1 -> x3, Pallas kernels: 2.1 us -> 4.27 us  [the longest x1 2.2 us: local(): pl.pallas_call(middle_kernel, in_specs=[vmem()] * 4, out_specs=[vmem()] *...]
  transfers between devices with their start and end apart: 9 -> 10, of which waited for: 4 -> 7; matrix products, arithmetic and copies ran while one was open for 2% -> 1% of each run, Pallas kernels for 1% -> 2%
where the time goes in v7:
time: 162 us; the launch traced here: 161 us
  blocking collectives  63.2 us (39%)
  starting transfers between devices  43.3 us (27%)
  waiting for transfers between devices  31.2 us (19%)
  Pallas kernels  19.1 us (12%)
  local copies, waits for them, and re-layouts  1.85 us (1%)
    all_to_all x4, blocking collectives, exchange(): return lax.all_to_all(values, axes, split_axis=0, concat_axis=0, tiled=True)  63.2 us
    all_to_all x4, waiting for transfers between devices, exchange(): return lax.all_to_all(values, axes, split_axis=0, concat_axis=0, tiled=True)  19 us
    all_to_all x4, starting transfers between devices, exchange(): return lax.all_to_all(values, axes, split_axis=0, concat_axis=0, tiled=True)  15.8 us
    ppermute x1, starting transfers between devices, local(): got_cross = lax.ppermute(got, 'c', cores)  8.86 us
    ppermute x1, waiting for transfers between devices, local(): other = lax.ppermute(own, 'xl', [(0, 1), (1, 0)])  6.59 us
    pallas_call x1, Pallas kernels, local(): pl.pallas_call(backward_kernel, grid=(HOLDERS // 2,), in_specs=[pl.BlockS...  5.51 us
    ppermute x1, starting transfers between devices, local(): lax.ppermute(conv2_weight, ('xh', 'xl'), [(0, 3), (3, 0), (1, 2), (2, 1)])  5.35 us
    ppermute x1, starting transfers between devices, local(): lax.ppermute(own_weight, 'c', cores)  4.79 us
  transfers between devices with their start and end apart: 10, of which 7 were waited for; matrix products, arithmetic and copies ran while one was open for 1% of the time, Pallas kernels for 2%

profile of v7, /device:TPU:1, one launch (start us, length us, event | category | flops | bytes accessed | tf_op | source)
XLA Modules:
  0.0 160.8 jit_solution(8513685481251805527)
XLA Ops:
  0.6 0.0 copy-start
  0.6 0.0 copy-start.1
  0.7 5.3 %collective-permute-start = (bf16[80,1920]{1,0:T(8,128)(2,1)}, bf16[80,1920]{1,0:T(8,128)(2,1)S(1)}, u32[]{:S(2)}, u32[]{:S(2)}) collective-permute-start(bf16[80,1920]{1,0:T(8,128)(2,1)} %own_ref.3), channel_id=1, source_target_pairs={{0,257},{257,0},{1,256},{256,1},{2,259},{259,2},{3,258},{258,3},{4... | collective-permute-start | bytes 921608 | tf_op jit(solution)/shard_map/ppermute | solution.py:318
  6.0 1.7 %mel_payload.1 = bf16[4,26,16,128]{3,2,1,0:T(8,128)(2,1)} custom-call(s32[16]{0:T(128)} %length_ref.1, bf16[16,16,128]{2,1,0:T(8,128)(2,1)} %mel_ref.1), custom_call_target="tpu_custom_call" | custom-call | tf_op jit(solution)/shard_map/mel_payload/pallas_call | solution.py:319
  7.7 4.2 %all-to-all-start = ((bf16[4,26,16,128]{3,2,1,0:T(8,128)(2,1)}), bf16[4,26,16,128]{3,2,1,0:T(8,128)(2,1)S(1)}, u32[]{:S(2)}, u32[]{:S(2)}) async-start(bf16[4,26,16,128]{3,2,1,0:T(8,128)(2,1)} %mel_payload.1), calls=%async_computation | async-start | bytes 851968 | tf_op jit(solution)/shard_map/all_to_all | solution.py:280
  11.9 0.1 pad_add_fusion.where_ref
  11.9 0.7 broadcast_in_dim.20.bias_ref
  12.6 0.0 copy-done.1
  12.6 1.2 conv1_columns.1
  13.9 0.0 copy-start.3
  13.9 0.0 copy-start.2
  13.9 0.0 copy-done
  13.9 4.8 %collective-permute-start.1 = (bf16[80,1920]{1,0:T(8,128)(2,1)S(1)}, bf16[80,1920]{1,0:T(8,128)(2,1)S(1)}, u32[]{:S(2)}, u32[]{:S(2)}) collective-permute-start(bf16[80,1920]{1,0:T(8,128)(2,1)S(1)} %copy-done), channel_id=1, source_target_pairs={{0,32},{32,0},{1,33},{33,1},{2,34},{34,2},{3,35},{35,3},{4,36},{36... | collective-permute-start | bytes 921608 | tf_op jit(solution)/shard_map/ppermute | solution.py:348
  18.7 0.0 collective-permute-done.far_ref
  18.7 1.9 %collective-permute-start.2 = (bf16[80,1920]{1,0:T(8,128)(2,1)S(1)}, bf16[80,1920]{1,0:T(8,128)(2,1)S(1)}, u32[]{:S(2)}, u32[]{:S(2)}) collective-permute-start(bf16[80,1920]{1,0:T(8,128)(2,1)S(1)} %collective-permute-done.far_ref), channel_id=1, source_target_pairs={{0,32},{32,0},{1,33},{33,1},{2,34},{34,2},{3,35},{35,3},{4,36},{36... | collective-permute-start | bytes 921608 | tf_op jit(solution)/shard_map/ppermute | solution.py:350
  20.6 0.0 collective-permute-done.1.side_ref
  20.6 0.0 all-to-all-done.pay_ref
  20.6 1.5 collective-permute-done.2.both_ref
  22.2 4.4 %stem_forward.1 = (bf16[4,128,640]{2,1,0:T(8,128)(2,1)}, bf16[4,128,512]{2,1,0:T(8,128)(2,1)}, bf16[4,3,128,384]{3,2,1,0:T(8,128)(2,1)}, f32[4,2,128,384]{3,2,1,0:T(8,128)}) custom-call(bf16[4,26,16,128]{3,2,1,0:T(8,128)(2,1)S(1)} %all-to-all-done.pay_ref, bf16[384,384]{1,0:T(8,128)(2,1)S(1)} %get-tuple-element.30.w1_ref, ...), custom_call_target="tpu_custom_call" | custom-call | tf_op jit(solution)/shard_map/stem_forward/pallas_call | solution.py:355
  26.6 4.6 %all-to-all-start.1 = ((bf16[4,128,640]{2,1,0:T(8,128)(2,1)}), bf16[4,128,640]{2,1,0:T(8,128)(2,1)S(1)}, u32[]{:S(2)}, u32[]{:S(2)}) async-start(bf16[4,128,640]{2,1,0:T(8,128)(2,1)} %get-tuple-element.36), calls=%async_computation.1 | async-start | bytes 1310720 | tf_op jit(solution)/shard_map/all_to_all | solution.py:280
  31.2 0.1 broadcast_in_dim.22
  31.3 0.7 broadcast_in_dim_reshape.12.length_ref
  32.0 9.7 %all-to-all-done.1.part_ref = bf16[4,128,640]{2,1,0:T(8,128)(2,1)S(1)} async-done(((bf16[4,128,640]{2,1,0:T(8,128)(2,1)}), bf16[4,128,640]{2,1,0:T(8,128)(2,1)S(1)}, u32[]{:S(2)}, u32[]{:S(2)}) %all-to-all-start.1) | async-done | bytes 655392 | tf_op jit(solution)/shard_map/all_to_all | solution.py:280
  41.7 2.2 %stem_middle.1 = (bf16[4,128,640]{2,1,0:T(8,128)(2,1)}, bf16[128,640]{1,0:T(8,128)(2,1)S(1)}) custom-call(bf16[4,128,640]{2,1,0:T(8,128)(2,1)S(1)} %all-to-all-done.1.part_ref, bf16[128,640]{1,0:T(8,128)(2,1)} %bitcast.15, f32[1,640]{1,0:T(1,128)S(1)} %broadcast_in_dim.21.b2_ref, f32[128,1]{1,0:T(8,128)} %broadcast_in_dim_reshape.12.length_ref), custom_call_target="tpu_custom_call" | custom-call | tf_op jit(solution)/shard_map/stem_middle/pallas_call | solution.py:381
  43.9 3.5 %all-to-all-start.2 = ((bf16[4,128,640]{2,1,0:T(8,128)(2,1)}), bf16[4,128,640]{2,1,0:T(8,128)(2,1)S(1)}, u32[]{:S(2)}, u32[]{:S(2)}) async-start(bf16[4,128,640]{2,1,0:T(8,128)(2,1)} %get-tuple-element.37), calls=%async_computation.2 | async-start | bytes 1310720 | tf_op jit(solution)/shard_map/all_to_all | solution.py:280
  47.4 0.1 broadcast_in_dim.23
  47.5 0.1 broadcast_in_dim_reshape.11.owner_row_ref
  47.6 0.1 broadcast_in_dim_reshape.13.owner_col_ref
  47.7 0.9 features_place.1
  48.5 8.2 %all-to-all-done.2.grad_ref = bf16[4,128,640]{2,1,0:T(8,128)(2,1)S(1)} async-done(((bf16[4,128,640]{2,1,0:T(8,128)(2,1)}), bf16[4,128,640]{2,1,0:T(8,128)(2,1)S(1)}, u32[]{:S(2)}, u32[]{:S(2)}) %all-to-all-start.2) | async-done | bytes 655392 | tf_op jit(solution)/shard_map/all_to_all | solution.py:280
  56.7 5.5 %stem_backward.1 = (f32[2,2,896,128]{3,2,1,0:T(8,128)S(1)}, bf16[2,2,896,128]{3,2,1,0:T(8,128)(2,1)S(1)}) custom-call(s32[4]{0:T(128)S(1)} %pad_add_fusion.where_ref, bf16[4,128,640]{2,1,0:T(8,128)(2,1)S(1)} %all-to-all-done.2.grad_ref, bf16[80,1920]{1,0:T(8,128)(2,1)S(1)} %copy-done, bf16[80,1920]{1,0:T(8,128)(2,1)S(1)} %collective-permute-done.1.side_ref, ...), custom_call_target="tpu_custom_call" | custom-call | tf_op jit(solution)/shard_map/stem_backward/pallas_call | solution.py:405
  62.2 4.4 %collective-permute-start.3 = (bf16[2,2,896,128]{3,2,1,0:T(8,128)(2,1)S(1)}, bf16[2,2,896,128]{3,2,1,0:T(8,128)(2,1)S(1)}, u32[]{:S(2)}, u32[]{:S(2)}) collective-permute-start(bf16[2,2,896,128]{3,2,1,0:T(8,128)(2,1)S(1)} %get-tuple-element.46), channel_id=1, source_target_pairs={{0,32},{32,0},{1,33},{33,1},{2,34},{34,2},{3,35},{35,3},{4,36},{36... | collective-permute-start | bytes 2752520 | tf_op jit(solution)/shard_map/ppermute | solution.py:428
  66.6 2.1 %collective-permute-done.3 = bf16[2,2,896,128]{3,2,1,0:T(8,128)(2,1)S(1)} collective-permute-done((bf16[2,2,896,128]{3,2,1,0:T(8,128)(2,1)S(1)}, bf16[2,2,896,128]{3,2,1,0:T(8,128)(2,1)S(1)}, u32[]{:S(2)}, u32[]{:S(2)}) %collective-permute-start.3) | collective-permute-done | bytes 917536 | tf_op jit(solution)/shard_map/ppermute | solution.py:428
  68.7 0.2 add_convert_fusion
  68.9 16.9 %all_to_all.40.got_ref = bf16[4,896,128]{2,1,0:T(8,128)(2,1)S(1)} all-to-all(bf16[4,896,128]{2,1,0:T(8,128)(2,1)S(1)} %bitcast.11), channel_id=1, replica_groups=mesh['xh'=2,'y'=4,'c'=2,'zh'=4,'zl'=4,'xl'=2] {'xh','xl'}, dimensions={0} | all-to-all | bytes 1835008 | tf_op jit(solution)/shard_map/all_to_all | solution.py:280
  85.8 0.1 gradient_sum.3
  85.9 8.6 %all_to_all.41.got_ref = bf16[4,224,128]{2,1,0:T(8,128)(2,1)S(1)} all-to-all(bf16[4,224,128]{2,1,0:T(8,128)(2,1)S(1)} %bitcast.10), channel_id=1, replica_groups=mesh['xh'=2,'y'=4,'c'=2,'zh'=4,'zl'=4,'xl'=2] {'zl'}, dimensions={0} | all-to-all | bytes 458752 | tf_op jit(solution)/shard_map/all_to_all | solution.py:280
  94.6 27.6 %all_to_all.42.got_ref = bf16[4,224,128]{2,1,0:T(8,128)(2,1)S(1)} all-to-all(bf16[4,224,128]{2,1,0:T(8,128)(2,1)S(1)} %gradient_sum.4), channel_id=1, replica_groups=mesh['xh'=2,'y'=4,'c'=2,'zh'=4,'zl'=4,'xl'=2] {'zh'}, dimensions={0} | all-to-all | bytes 458752 | tf_op jit(solution)/shard_map/all_to_all | solution.py:280
  122.2 10.2 %all_to_all.43 = bf16[4,224,128]{2,1,0:T(8,128)(2,1)S(1)} all-to-all(bf16[4,224,128]{2,1,0:T(8,128)(2,1)S(1)} %gradient_sum.5), channel_id=1, replica_groups=mesh['xh'=2,'y'=4,'c'=2,'zh'=4,'zl'=4,'xl'=2] {'zl'}, dimensions={0} | all-to-all | bytes 458752 | tf_op jit(solution)/shard_map/all_to_all | solution.py:280
  132.4 0.1 broadcast_in_dim.24
  132.5 1.0 pad_maximum_fusion
  133.4 3.6 %all-to-all-start.7 = ((bf16[8,416,128]{2,1,0:T(8,128)(2,1)}), bf16[8,416,128]{2,1,0:T(8,128)(2,1)S(1)}, u32[]{:S(2)}, u32[]{:S(2)}) async-start(bf16[8,416,128]{2,1,0:T(8,128)(2,1)} %pad_maximum_fusion), calls=%async_computation.7 | async-start | bytes 1703936 | tf_op jit(solution)/shard_map/all_to_all | solution.py:280
  137.0 2.2 %collective-permute-start.4 = (bf16[640,128]{1,0:T(8,128)(2,1)S(1)}, bf16[640,128]{1,0:T(8,128)(2,1)S(1)}, u32[]{:S(2)}, u32[]{:S(2)}) collective-permute-start(bf16[640,128]{1,0:T(8,128)(2,1)S(1)} %slice.20.own_ref), channel_id=1, source_target_pairs={{0,1},{1,0},{2,3},{3,2},{4,5},{5,4},{6,7},{7,6},{8,9},{9,8},{10,11... | collective-permute-start | bytes 491528 | tf_op jit(solution)/shard_map/ppermute | solution.py:447
  139.2 6.6 %collective-permute-done.4.other_ref = bf16[640,128]{1,0:T(8,128)(2,1)S(1)} collective-permute-done((bf16[640,128]{1,0:T(8,128)(2,1)S(1)}, bf16[640,128]{1,0:T(8,128)(2,1)S(1)}, u32[]{:S(2)}, u32[]{:S(2)}) %collective-permute-start.4) | collective-permute-done | bytes 163872 | tf_op jit(solution)/shard_map/ppermute | solution.py:447
  145.8 1.1 all-to-all-done.7.got_ref
  146.9 8.9 %collective-permute-start.5 = (bf16[8,416,128]{2,1,0:T(8,128)(2,1)S(1)}, bf16[8,416,128]{2,1,0:T(8,128)(2,1)S(1)}, u32[]{:S(2)}, u32[]{:S(2)}) collective-permute-start(bf16[8,416,128]{2,1,0:T(8,128)(2,1)S(1)} %all-to-all-done.7.got_ref), channel_id=1, source_target_pairs={{0,32},{32,0},{1,33},{33,1},{2,34},{34,2},{3,35},{35,3},{4,36},{36... | collective-permute-start | bytes 2555912 | tf_op jit(solution)/shard_map/ppermute | solution.py:451
  155.8 2.0 %collective-permute-done.5.cross_ref = bf16[8,416,128]{2,1,0:T(8,128)(2,1)S(1)} collective-permute-done((bf16[8,416,128]{2,1,0:T(8,128)(2,1)S(1)}, bf16[8,416,128]{2,1,0:T(8,128)(2,1)S(1)}, u32[]{:S(2)}, u32[]{:S(2)}) %collective-permute-start.5) | collective-permute-done | bytes 852000 | tf_op jit(solution)/shard_map/ppermute | solution.py:451
  157.8 3.0 %gradient_unpack.1 = (f32[384,1280]{1,0:T(8,128)}, f32[1280]{0:T(1024)}, f32[640]{0:T(1024)}, f32[80,1920]{1,0:T(8,128)}, bf16[256,640]{1,0:T(8,128)(2,1)}) custom-call(s32[4]{0:T(128)S(1)} %pad_add_fusion.where_ref, bf16[8,416,128]{2,1,0:T(8,128)(2,1)S(1)} %all-to-all-done.7.got_ref, bf16[8,416,128]{2,1,0:T(8,128)(2,1)S(1)} %collective-permute-done.5.cross_ref, ...), custom_call_target="tpu_custom_call" | custom-call | tf_op jit(solution)/shard_map/gradient_unpack/pallas_call | solution.py:452
  (12 shorter events, 0.1 us)
Async XLA Ops:
  0.6 13.2 %copy-start = (bf16[80,1920]{1,0:T(8,128)(2,1)S(1)}, bf16[80,1920]{1,0:T(8,128)(2,1)}, u32[]{:S(2)}) copy-start(bf16[80,1920]{1,0:T(8,128)(2,1)} %own_ref.3) | copy-start | bytes 921604
  0.6 12.0 %copy-start.1 = (bf16[384,1280]{1,0:T(8,128)(2,1)S(1)}, bf16[384,1280]{1,0:T(8,128)(2,1)}, u32[]{:S(2)}) copy-start(bf16[384,1280]{1,0:T(8,128)(2,1)} %weight_ref.1) | copy-start | bytes 2949124
  0.7 18.0 %collective-permute-start = (bf16[80,1920]{1,0:T(8,128)(2,1)}, bf16[80,1920]{1,0:T(8,128)(2,1)S(1)}, u32[]{:S(2)}, u32[]{:S(2)}) collective-permute-start(bf16[80,1920]{1,0:T(8,128)(2,1)} %own_ref.3), channel_id=1, source_target_pairs={{0,257},{257,0},{1,256},{256,1},{2,259},{259,2},{3,258},{258,3},{4... | collective-permute-start | bytes 921608 | tf_op jit(solution)/shard_map/ppermute | solution.py:318
  7.7 13.0 %all-to-all-start = ((bf16[4,26,16,128]{3,2,1,0:T(8,128)(2,1)}), bf16[4,26,16,128]{3,2,1,0:T(8,128)(2,1)S(1)}, u32[]{:S(2)}, u32[]{:S(2)}) async-start(bf16[4,26,16,128]{3,2,1,0:T(8,128)(2,1)} %mel_payload.1), calls=%async_computation | async-start | bytes 851968 | tf_op jit(solution)/shard_map/all_to_all | solution.py:280
  13.9 17.3 %copy-start.3 = (s32[16]{0:T(128)S(1)}, s32[16]{0:T(128)}, u32[]{:S(2)}) copy-start(s32[16]{0:T(128)} %length_ref.1) | copy-start | bytes 196
  13.9 17.3 %copy-start.2 = (f32[640]{0:T(1024)S(1)}, f32[640]{0:T(1024)}, u32[]{:S(2)}) copy-start(f32[640]{0:T(1024)} %param.14) | copy-start | bytes 7684
  13.9 6.7 %collective-permute-start.1 = (bf16[80,1920]{1,0:T(8,128)(2,1)S(1)}, bf16[80,1920]{1,0:T(8,128)(2,1)S(1)}, u32[]{:S(2)}, u32[]{:S(2)}) collective-permute-start(bf16[80,1920]{1,0:T(8,128)(2,1)S(1)} %copy-done), channel_id=1, source_target_pairs={{0,32},{32,0},{1,33},{33,1},{2,34},{34,2},{3,35},{35,3},{4,36},{36... | collective-permute-start | bytes 921608 | tf_op jit(solution)/shard_map/ppermute | solution.py:348
  18.7 3.5 %collective-permute-start.2 = (bf16[80,1920]{1,0:T(8,128)(2,1)S(1)}, bf16[80,1920]{1,0:T(8,128)(2,1)S(1)}, u32[]{:S(2)}, u32[]{:S(2)}) collective-permute-start(bf16[80,1920]{1,0:T(8,128)(2,1)S(1)} %collective-permute-done.far_ref), channel_id=1, source_target_pairs={{0,32},{32,0},{1,33},{33,1},{2,34},{34,2},{3,35},{35,3},{4,36},{36... | collective-permute-start | bytes 921608 | tf_op jit(solution)/shard_map/ppermute | solution.py:350
  26.6 20.8 %copy-start.4 = (s32[16,1]{0,1:T(1,128)S(1)}, s32[16,1]{0,1:T(1,128)}, u32[]{:S(2)}) copy-start(s32[16,1]{0,1:T(1,128)} %param.10) | copy-start | bytes 196
  26.6 15.1 %all-to-all-start.1 = ((bf16[4,128,640]{2,1,0:T(8,128)(2,1)}), bf16[4,128,640]{2,1,0:T(8,128)(2,1)S(1)}, u32[]{:S(2)}, u32[]{:S(2)}) async-start(bf16[4,128,640]{2,1,0:T(8,128)(2,1)} %get-tuple-element.36), calls=%async_computation.1 | async-start | bytes 1310720 | tf_op jit(solution)/shard_map/all_to_all | solution.py:280
  43.9 12.8 %all-to-all-start.2 = ((bf16[4,128,640]{2,1,0:T(8,128)(2,1)}), bf16[4,128,640]{2,1,0:T(8,128)(2,1)S(1)}, u32[]{:S(2)}, u32[]{:S(2)}) async-start(bf16[4,128,640]{2,1,0:T(8,128)(2,1)} %get-tuple-element.37), calls=%async_computation.2 | async-start | bytes 1310720 | tf_op jit(solution)/shard_map/all_to_all | solution.py:280
  62.2 6.5 %collective-permute-start.3 = (bf16[2,2,896,128]{3,2,1,0:T(8,128)(2,1)S(1)}, bf16[2,2,896,128]{3,2,1,0:T(8,128)(2,1)S(1)}, u32[]{:S(2)}, u32[]{:S(2)}) collective-permute-start(bf16[2,2,896,128]{3,2,1,0:T(8,128)(2,1)S(1)} %get-tuple-element.46), channel_id=1, source_target_pairs={{0,32},{32,0},{1,33},{33,1},{2,34},{34,2},{3,35},{35,3},{4,36},{36... | collective-permute-start | bytes 2752520 | tf_op jit(solution)/shard_map/ppermute | solution.py:428
  133.4 13.5 %all-to-all-start.7 = ((bf16[8,416,128]{2,1,0:T(8,128)(2,1)}), bf16[8,416,128]{2,1,0:T(8,128)(2,1)S(1)}, u32[]{:S(2)}, u32[]{:S(2)}) async-start(bf16[8,416,128]{2,1,0:T(8,128)(2,1)} %pad_maximum_fusion), calls=%async_computation.7 | async-start | bytes 1703936 | tf_op jit(solution)/shard_map/all_to_all | solution.py:280
  137.0 8.8 %collective-permute-start.4 = (bf16[640,128]{1,0:T(8,128)(2,1)S(1)}, bf16[640,128]{1,0:T(8,128)(2,1)S(1)}, u32[]{:S(2)}, u32[]{:S(2)}) collective-permute-start(bf16[640,128]{1,0:T(8,128)(2,1)S(1)} %slice.20.own_ref), channel_id=1, source_target_pairs={{0,1},{1,0},{2,3},{3,2},{4,5},{5,4},{6,7},{7,6},{8,9},{9,8},{10,11... | collective-permute-start | bytes 491528 | tf_op jit(solution)/shard_map/ppermute | solution.py:447
  146.9 10.9 %collective-permute-start.5 = (bf16[8,416,128]{2,1,0:T(8,128)(2,1)S(1)}, bf16[8,416,128]{2,1,0:T(8,128)(2,1)S(1)}, u32[]{:S(2)}, u32[]{:S(2)}) collective-permute-start(bf16[8,416,128]{2,1,0:T(8,128)(2,1)S(1)} %all-to-all-done.7.got_ref), channel_id=1, source_target_pairs={{0,32},{32,0},{1,33},{33,1},{2,34},{34,2},{3,35},{35,3},{4,36},{36... | collective-permute-start | bytes 2555912 | tf_op jit(solution)/shard_map/ppermute | solution.py:451

commit v8 on v7

--- a/solution.py
+++ b/solution.py
@@ -24,6 +24,7 @@
 SLOTS = 2 * CLIPS
 PAY = 26
 CHIPS = 8
+DEAD = -1e30
 PACK = 896
 HALF_ROWS = 8 * ROWS
 MIB = 1024 * 1024
@@ -31,6 +32,10 @@
 ENC = ("xh", "y", "c")
 F32 = jnp.float32
 BF16 = jnp.bfloat16
+
+
+def gelu_value(values):
+    return values * (0.5 * (1.0 + lax.erf(values * inv_root_two)))
 
 
 def gelu_both(values):
@@ -95,13 +100,13 @@
         lanes = slice(block * ROWS, (block + 1) * ROWS)
         window = weight_ref[:, pl.ds(start, 2 * LANES)].astype(F32)
         picked[:, lanes] = pltpu.roll(window, shift, 1)[:, :ROWS]
-        window = jnp.broadcast_to(bias_ref[:, pl.ds(start, 2 * LANES)], (8, 2 * LANES))
+        window = jnp.broadcast_to(bias_ref[pl.ds(start, 2 * LANES)].reshape(1, 2 * LANES), (8, 2 * LANES))
         b1_ref[:, lanes] = pltpu.roll(window, shift, 1)[0:1, :ROWS]
     w1_ref[...] = picked[...].astype(BF16)
 
 
 def forward_kernel(
-    pay_ref, w1_ref, b1_ref, own_ref, side_ref, far_ref, both_ref, part_ref, cols_ref, act_ref, slope_ref, w2_ref,
+    pay_ref, w1_ref, b1_ref, own_ref, side_ref, far_ref, both_ref, part_ref, cols_ref, act_ref, pre_ref, w2_ref,
     frames_ref,
 ):
     stack_weights((own_ref, side_ref, far_ref, both_ref), w2_ref)
@@ -120,17 +125,15 @@
     cols_ref[0, :, 2 * LANES : 3 * LANES] = odd.astype(BF16)
     cols_ref[0, :, 3 * LANES :] = shift_up(even).astype(BF16)
     bias = b1_ref[...]
-    mask_even = jnp.where(live_even, 1.0, 0.0)
-    mask_odd = jnp.where(live_odd, 1.0, 0.0)
-    mask_even = jnp.concatenate([mask_even] * (WIDE // LANES), axis=1)
-    mask_odd = jnp.concatenate([mask_odd] * (WIDE // LANES), axis=1)
-    act, slope = gelu_both(dot(cols_ref[0, :, : 3 * LANES], w1_ref[...]) + bias)
-    act_even = (act * mask_even).astype(BF16)
-    slope_ref[0, 0] = slope * mask_even
-    act, slope = gelu_both(dot(cols_ref[0, :, LANES:], w1_ref[...]) + bias)
-    act = act * mask_odd
+    live_even = jnp.concatenate([live_even] * (WIDE // LANES), axis=1)
+    live_odd = jnp.concatenate([live_odd] * (WIDE // LANES), axis=1)
+    pre = dot(cols_ref[0, :, : 3 * LANES], w1_ref[...]) + bias
+    pre_ref[0, 0] = jnp.where(live_even, pre, DEAD)
+    act_even = jnp.where(live_even, gelu_value(pre), 0.0).astype(BF16)
+    pre = dot(cols_ref[0, :, LANES:], w1_ref[...]) + bias
+    pre_ref[0, 1] = jnp.where(live_odd, pre, DEAD)
+    act = jnp.where(live_odd, gelu_value(pre), 0.0)
     act_odd = act.astype(BF16)
-    slope_ref[0, 1] = slope * mask_odd
     act_prior = shift_down(act).astype(BF16)
     act_ref[0, 0] = act_prior
     act_ref[0, 1] = act_even
@@ -141,7 +144,17 @@
     part_ref[0] = total.astype(BF16)
 
 
-def middle_kernel(part_ref, grad_ref, b2_ref, length_ref, rep_ref, feature_ref):
+def slope_kernel(pre_ref, act_ref, slope_ref, turned_ref):
+    pre = pre_ref[0].reshape(2 * STEPS, WIDE)
+    slope = jnp.where(pre > 0.5 * DEAD, gelu_both(pre)[1], 0.0)
+    slope_ref[0] = slope.reshape(2, STEPS, WIDE)
+    for tap in range(3):
+        turned_ref[tap] = act_ref[0, tap].T
+
+
+def middle_kernel(
+    where_ref, part_ref, grad_ref, b2_ref, length_ref, owner_col_ref, owner_row_ref, rep_ref, same_ref, cross_ref
+):
     pre = part_ref[0].astype(F32)
     for source in range(1, HOLDERS):
         pre = pre + part_ref[source].astype(F32)
@@ -153,10 +166,6 @@
     second_grad = (grad_ref[...].astype(F32) * slope * live).astype(BF16)
     for target in range(HOLDERS):
         rep_ref[target] = second_grad
-    feature_ref[...] = features
-
-
-def place_kernel(where_ref, feature_ref, owner_col_ref, owner_row_ref, same_ref, cross_ref):
     here = lax.broadcasted_iota(jnp.int32, (STEPS, STEPS), 0)
     there = lax.broadcasted_iota(jnp.int32, (STEPS, STEPS), 1)
     same = (owner_col_ref[...] == owner_row_ref[...]) & ((here >> 3) < (there >> 3))
@@ -165,7 +174,7 @@
     place = lax.broadcasted_iota(jnp.int32, (1, STEPS), 1) & (HALF - 1)
     place = (owner_row_ref[...] * 2 + rank.astype(jnp.int32)) * HALF + place
     wanted = lax.broadcasted_iota(jnp.int32, (SLOTS * HALF, STEPS), 0) == place
-    placed = dot(jnp.where(wanted, 1.0, 0.0).astype(BF16), feature_ref[...])
+    placed = dot(jnp.where(wanted, 1.0, 0.0).astype(BF16), features)
     first = where_ref[2] == 0
     for chip in range(CHIPS):
         for tile in range(D2 // LANES):
@@ -201,7 +210,7 @@
     conv1_sum[...] += dot_tn(even, cols[:, : 3 * LANES]) + dot_tn(odd, cols[:, LANES:])
     bias1_sum[...] += jnp.sum(even.astype(F32) + odd.astype(F32), axis=0, keepdims=True)
     for tap in range(3):
-        conv2_sum[:, tap * D2 : (tap + 1) * D2] += dot_tn(act_ref[:, tap].reshape(rows, WIDE), grad)
+        conv2_sum[:, tap * D2 : (tap + 1) * D2] += dot(act_ref[tap], grad)
 
     @pl.when(step == pl.num_programs(0) - 1)
     def _():
@@ -237,6 +246,13 @@
     else:
         for target in range(out_ref.shape[0]):
             out_ref[target] = total
+
+
+def pairs_kernel(own_ref, near_ref, far_ref, both_ref, out_ref):
+    own, near, far, both = (ref[...].astype(F32) for ref in (own_ref, near_ref, far_ref, both_ref))
+    total = ((own + near) + (far + both)).astype(BF16)
+    for target in range(out_ref.shape[0]):
+        out_ref[target] = total
 
 
 def last_kernel(
@@ -340,9 +356,9 @@
         scratch_shapes=[pltpu.VMEM((3 * MEL, WIDE), F32)],
         compiler_params=params(10),
         name="conv1_columns",
-    )(where, conv1_weight, conv1_bias[None])
-    own_weight, b1 = lax.optimization_barrier((conv2_weight, b1))
-    far_weight, b1 = lax.optimization_barrier((far_weight, b1))
+    )(where, conv1_weight, conv1_bias)
+    own_weight, place = lax.optimization_barrier((conv2_weight, where))
+    far_weight, place = lax.optimization_barrier((far_weight, place))
     weights = [
         conv2_weight,
         lax.ppermute(own_weight, "c", cores),
@@ -352,7 +368,7 @@
 
     pair = lambda i: (i, 0, 0)
     pair4 = lambda i: (i, 0, 0, 0)
-    parts, cols, acts, slopes = pl.pallas_call(
+    parts, cols, acts, pres = pl.pallas_call(
         forward_kernel,
         grid=(HOLDERS,),
         in_specs=[
@@ -377,30 +393,34 @@
     )(got_pay, w1, b1, *weights)
 
     got_parts = exchange(parts, "y")
+    slopes, turned = pl.pallas_call(
+        slope_kernel,
+        grid=(HOLDERS,),
+        in_specs=[pl.BlockSpec((1, 2, STEPS, WIDE), pair4), pl.BlockSpec((1, 3, STEPS, WIDE), pair4)],
+        out_specs=[pl.BlockSpec((1, 2, STEPS, WIDE), pair4), pl.BlockSpec((3, WIDE, STEPS), lambda i: (0, 0, i))],
+        out_shape=[in_hbm(HOLDERS, 2, STEPS, WIDE, dtype=F32), in_hbm(3, WIDE, HOLDERS * STEPS)],
+        compiler_params=params(20, "arbitrary"),
+        name="stem_slopes",
+    )(from_hbm(pres), from_hbm(acts))
+    got_parts, slopes, turned = lax.optimization_barrier((got_parts, slopes, turned))
     owner = jnp.repeat(routes[:, 0], HALF)
-    rep, features = pl.pallas_call(
+    rep, same, cross = pl.pallas_call(
         middle_kernel,
-        in_specs=[vmem()] * 4,
-        out_specs=[vmem()] * 2,
-        out_shape=[in_hbm(HOLDERS, STEPS, D2), shape(STEPS, D2)],
+        in_specs=[pl.BlockSpec(memory_space=pltpu.SMEM)] + [vmem()] * 6,
+        out_specs=[vmem()] * 3,
+        out_shape=[in_hbm(HOLDERS, STEPS, D2), shape(CHIPS, ROWS, LANES), shape(CHIPS, ROWS, LANES)],
         compiler_params=params(10),
         name="stem_middle",
     )(
+        where,
         got_parts,
         from_hbm(out_grad.reshape(STEPS, D2)),
         conv2_bias[None],
         from_hbm(jnp.repeat(lengths.astype(F32), HALF)[:, None]),
+        owner[:, None],
+        owner[None],
     )
     got_grad = exchange(rep, "y")
-    same, cross = pl.pallas_call(
-        place_kernel,
-        in_specs=[pl.BlockSpec(memory_space=pltpu.SMEM), vmem(), vmem(), vmem()],
-        out_specs=[vmem()] * 2,
-        out_shape=[shape(CHIPS, ROWS, LANES)] * 2,
-        compiler_params=params(10),
-        name="features_place",
-    )(where, features, owner[:, None], owner[None])
-    got_grad, same = lax.optimization_barrier((got_grad, same))
 
     keep, send = pl.pallas_call(
         backward_kernel,
@@ -410,7 +430,7 @@
             pl.BlockSpec((2, STEPS, D2), pair),
             *[vmem()] * BLOCKS,
             pl.BlockSpec((2, STEPS, 4 * LANES), pair),
-            pl.BlockSpec((2, 3, STEPS, WIDE), pair4),
+            pl.BlockSpec((3, WIDE, 2 * STEPS), lambda i: (0, 0, i)),
             pl.BlockSpec((2, 2, STEPS, WIDE), pair4),
         ],
         out_specs=[vmem()] * 2,
@@ -424,7 +444,7 @@
         ],
         compiler_params=params(32, "arbitrary"),
         name="stem_backward",
-    )(where, got_grad, *weights, from_hbm(cols), from_hbm(acts), from_hbm(slopes))
+    )(where, got_grad, *weights, from_hbm(cols), from_hbm(turned), from_hbm(slopes))
     got = lax.ppermute(send, "c", cores)
     quarters = exchange((keep + got.astype(F32)).astype(BF16).reshape(4, PACK, LANES), ("xh", "xl"))
 
@@ -440,8 +460,16 @@
 
     half = summed(quarters, PACK, LANES)
     quarter = PACK // 4
-    near = summed(exchange(half.reshape(4, quarter, LANES), "zl"), 4, quarter, LANES)
-    far = summed(exchange(near, "zh"), 4, quarter, LANES)
+    near = summed(exchange(half.reshape(4, quarter, LANES), "zl"), quarter, LANES)
+    far = {flip: lax.ppermute(near, "zh", [(i, i ^ flip) for i in range(4)]) for flip in (2, 3, 1)}
+    far = pl.pallas_call(
+        pairs_kernel,
+        in_specs=[vmem()] * 4,
+        out_specs=vmem(),
+        out_shape=shape(4, quarter, LANES),
+        compiler_params=params(8),
+        name="gradient_pairs",
+    )(near, far[1], far[2], far[3])
     half = exchange(far, "zl").reshape(PACK, LANES)
     own = half[:HALF_ROWS]
     other = lax.ppermute(own, "xl", [(0, 1), (1, 0)])

time: 162 us -> 158 us (0.975)
  blocking collectives: 63.2 us -> 47 us
  starting transfers between devices: 43.3 us -> 58.5 us
  waiting for transfers between devices: 31.2 us -> 25.1 us
  Pallas kernels: 19.1 us -> 22.4 us
    ppermute x0 -> x3, starting transfers between devices: none -> 18.7 us  [local(): lax.ppermute(near, 'zh', [(i, i ^ flip) for i in range(4)])]
    all_to_all x4, blocking collectives: 63.2 us -> 47 us  [exchange(): return lax.all_to_all(values, axes, split_axis=0, concat_axis=0, tiled=True)]
    all_to_all x4 -> x3, waiting for transfers between devices: 19 us -> 5.61 us  [exchange(): return lax.all_to_all(values, axes, split_axis=0, concat_axis=0, tiled=True)]
    ppermute x0 -> x3, waiting for transfers between devices: none -> 8.65 us  [local(): lax.ppermute(near, 'zh', [(i, i ^ flip) for i in range(4)])]
    all_to_all x4 -> x3, starting transfers between devices: 15.8 us -> 11.2 us  [exchange(): return lax.all_to_all(values, axes, split_axis=0, concat_axis=0, tiled=True)]
    pallas_call x2 -> x3, Pallas kernels: 3.06 us -> 6.59 us  [the longest x1 4.45 us: local(): pl.pallas_call(slope_kernel, grid=(HOLDERS,), in_specs=[pl.BlockSpec((1,...]
  transfers between devices with their start and end apart: 10 -> 12, of which waited for: 7 -> 7; matrix products, arithmetic and copies ran while one was open for 1% -> 1% of each run, Pallas kernels for 2% -> 5%
where the time goes in v8:
time: 158 us; the launch traced here: 157 us
  starting transfers between devices  58.5 us (37%)
  blocking collectives  47 us (30%)
  waiting for transfers between devices  25.1 us (16%)
  Pallas kernels  22.4 us (14%)
  local copies, waits for them, and re-layouts  1.84 us (1%)
    all_to_all x4, blocking collectives, exchange(): return lax.all_to_all(values, axes, split_axis=0, concat_axis=0, tiled=True)  47 us
    ppermute x3, starting transfers between devices, local(): lax.ppermute(near, 'zh', [(i, i ^ flip) for i in range(4)])  18.7 us
    all_to_all x3, starting transfers between devices, exchange(): return lax.all_to_all(values, axes, split_axis=0, concat_axis=0, tiled=True)  11.2 us
    ppermute x1, starting transfers between devices, local(): got_cross = lax.ppermute(got, 'c', cores)  8.85 us
    ppermute x3, waiting for transfers between devices, local(): lax.ppermute(near, 'zh', [(i, i ^ flip) for i in range(4)])  8.65 us
    ppermute x1, waiting for transfers between devices, local(): other = lax.ppermute(own, 'xl', [(0, 1), (1, 0)])  6.78 us
    all_to_all x3, waiting for transfers between devices, exchange(): return lax.all_to_all(values, axes, split_axis=0, concat_axis=0, tiled=True)  5.61 us
    pallas_call x1, Pallas kernels, local(): pl.pallas_call(backward_kernel, grid=(HOLDERS // 2,), in_specs=[pl.BlockS...  5.51 us
  transfers between devices with their start and end apart: 12, of which 7 were waited for; matrix products, arithmetic and copies ran while one was open for 1% of the time, Pallas kernels for 5%

profile of v8, /device:TPU:1, one launch (start us, length us, event | category | flops | bytes accessed | tf_op | source)
XLA Modules:
  0.0 157.0 jit_solution(15096784797812842919)
XLA Ops:
  0.6 0.0 copy-start
  0.7 5.3 %collective-permute-start.1 = (bf16[80,1920]{1,0:T(8,128)(2,1)}, bf16[80,1920]{1,0:T(8,128)(2,1)S(1)}, u32[]{:S(2)}, u32[]{:S(2)}) collective-permute-start(bf16[80,1920]{1,0:T(8,128)(2,1)} %own_ref.3), channel_id=1, source_target_pairs={{0,257},{257,0},{1,256},{256,1},{2,259},{259,2},{3,258},{258,3},{4... | collective-permute-start | bytes 921608 | tf_op jit(solution)/shard_map/ppermute | solution.py:334
  6.0 1.7 %mel_payload.1 = bf16[4,26,16,128]{3,2,1,0:T(8,128)(2,1)} custom-call(s32[16]{0:T(128)} %length_ref.1, bf16[16,16,128]{2,1,0:T(8,128)(2,1)} %mel_ref.1), custom_call_target="tpu_custom_call" | custom-call | tf_op jit(solution)/shard_map/mel_payload/pallas_call | solution.py:335
  7.7 4.2 %all-to-all-start = ((bf16[4,26,16,128]{3,2,1,0:T(8,128)(2,1)}), bf16[4,26,16,128]{3,2,1,0:T(8,128)(2,1)S(1)}, u32[]{:S(2)}, u32[]{:S(2)}) async-start(bf16[4,26,16,128]{3,2,1,0:T(8,128)(2,1)} %mel_payload.1), calls=%async_computation | async-start | bytes 851968 | tf_op jit(solution)/shard_map/all_to_all | solution.py:296
  11.9 0.1 pad_add_fusion.where_ref
  11.9 4.8 %collective-permute-start = (bf16[80,1920]{1,0:T(8,128)(2,1)}, bf16[80,1920]{1,0:T(8,128)(2,1)S(1)}, u32[]{:S(2)}, u32[]{:S(2)}) collective-permute-start(bf16[80,1920]{1,0:T(8,128)(2,1)} %own_ref.3), channel_id=1, source_target_pairs={{0,32},{32,0},{1,33},{33,1},{2,34},{34,2},{3,35},{35,3},{4,36},{36... | collective-permute-start | bytes 921608 | tf_op jit(solution)/shard_map/ppermute | solution.py:364
  16.7 3.0 %collective-permute-start.2 = (bf16[80,1920]{1,0:T(8,128)(2,1)S(1)}, bf16[80,1920]{1,0:T(8,128)(2,1)S(1)}, u32[]{:S(2)}, u32[]{:S(2)}) collective-permute-start(bf16[80,1920]{1,0:T(8,128)(2,1)S(1)} %collective-permute-done.1.far_ref), channel_id=1, source_target_pairs={{0,32},{32,0},{1,33},{33,1},{2,34},{34,2},{3,35},{35,3},{4,36},{36... | collective-permute-start | bytes 921608 | tf_op jit(solution)/shard_map/ppermute | solution.py:366
  19.8 0.0 copy-start.2
  19.8 0.7 copy-done.2
  20.5 1.2 conv1_columns.1
  21.7 0.0 copy-start.4
  21.7 0.0 copy-start.5
  21.7 0.0 copy-start.3
  21.7 0.0 collective-permute-done.2.both_ref
  21.7 4.2 %stem_forward.1 = (bf16[4,128,640]{2,1,0:T(8,128)(2,1)}, bf16[4,128,512]{2,1,0:T(8,128)(2,1)}, bf16[4,3,128,384]{3,2,1,0:T(8,128)(2,1)}, f32[4,2,128,384]{3,2,1,0:T(8,128)}) custom-call(bf16[4,26,16,128]{3,2,1,0:T(8,128)(2,1)S(1)} %all-to-all-done.pay_ref, bf16[384,384]{1,0:T(8,128)(2,1)S(1)} %get-tuple-element.29.w1_ref, ...), custom_call_target="tpu_custom_call" | custom-call | tf_op jit(solution)/shard_map/stem_forward/pallas_call | solution.py:371
  26.0 3.5 %all-to-all-start.1 = ((bf16[4,128,640]{2,1,0:T(8,128)(2,1)}), bf16[4,128,640]{2,1,0:T(8,128)(2,1)S(1)}, u32[]{:S(2)}, u32[]{:S(2)}) async-start(bf16[4,128,640]{2,1,0:T(8,128)(2,1)} %get-tuple-element.32), calls=%async_computation.1 | async-start | bytes 1310720 | tf_op jit(solution)/shard_map/all_to_all | solution.py:296
  29.5 0.1 broadcast_in_dim.19
  29.6 0.1 broadcast_in_dim_reshape.11.owner_row_ref
  29.7 0.1 broadcast_in_dim_reshape.13.owner_col_ref
  29.8 0.1 broadcast_in_dim.18
  29.9 0.7 broadcast_in_dim_reshape.12.length_ref
  30.6 4.5 %stem_slopes.1 = (f32[4,2,128,384]{3,2,1,0:T(8,128)}, bf16[3,384,512]{2,1,0:T(8,128)(2,1)}) custom-call(f32[4,2,128,384]{3,2,1,0:T(8,128)} %get-tuple-element.33.pre_ref, bf16[4,3,128,384]{3,2,1,0:T(8,128)(2,1)} %get-tuple-element.34.act_ref), custom_call_target="tpu_custom_call" | custom-call | tf_op jit(solution)/shard_map/stem_slopes/pallas_call | solution.py:396
  35.0 4.7 %all-to-all-done.1.part_ref = bf16[4,128,640]{2,1,0:T(8,128)(2,1)S(1)} async-done(((bf16[4,128,640]{2,1,0:T(8,128)(2,1)}), bf16[4,128,640]{2,1,0:T(8,128)(2,1)S(1)}, u32[]{:S(2)}, u32[]{:S(2)}) %all-to-all-start.1) | async-done | bytes 655392 | tf_op jit(solution)/shard_map/all_to_all | solution.py:296
  39.7 2.1 %stem_middle.1 = (bf16[4,128,640]{2,1,0:T(8,128)(2,1)}, bf16[8,80,128]{2,1,0:T(8,128)(2,1)S(1)}, bf16[8,80,128]{2,1,0:T(8,128)(2,1)S(1)}) custom-call(s32[4]{0:T(128)S(1)} %pad_add_fusion.where_ref, bf16[4,128,640]{2,1,0:T(8,128)(2,1)S(1)} %all-to-all-done.1.part_ref, bf16[128,640]{1,0:T(8,128)(2,1)} %bitcast.15, f32[1,640]{1,0:T(1,128)S(1)} %broadcast_in_dim.17.b2_ref, ...), custom_call_target="tpu_custom_call" | custom-call | tf_op jit(solution)/shard_map/stem_middle/pallas_call | solution.py:407
  41.8 12.8 %all_to_all.35.grad_ref = bf16[4,128,640]{2,1,0:T(8,128)(2,1)S(1)} all-to-all(bf16[4,128,640]{2,1,0:T(8,128)(2,1)} %get-tuple-element.39), channel_id=1, replica_groups=mesh['xh'=2,'y'=4,'c'=2,'zh'=4,'zl'=4,'xl'=2] {'y'}, dimensions={0} | all-to-all | bytes 1310720 | tf_op jit(solution)/shard_map/all_to_all | solution.py:296
  54.6 5.5 %stem_backward.1 = (f32[2,2,896,128]{3,2,1,0:T(8,128)S(1)}, bf16[2,2,896,128]{3,2,1,0:T(8,128)(2,1)S(1)}) custom-call(s32[4]{0:T(128)S(1)} %pad_add_fusion.where_ref, bf16[4,128,640]{2,1,0:T(8,128)(2,1)S(1)} %all_to_all.35.grad_ref, bf16[80,1920]{1,0:T(8,128)(2,1)S(1)} %copy-done, bf16[80,1920]{1,0:T(8,128)(2,1)S(1)} %collective-permute-done.side_ref, ...), custom_call_target="tpu_custom_call" | custom-call | tf_op jit(solution)/shard_map/stem_backward/pallas_call | solution.py:425
  60.1 4.4 %collective-permute-start.3 = (bf16[2,2,896,128]{3,2,1,0:T(8,128)(2,1)S(1)}, bf16[2,2,896,128]{3,2,1,0:T(8,128)(2,1)S(1)}, u32[]{:S(2)}, u32[]{:S(2)}) collective-permute-start(bf16[2,2,896,128]{3,2,1,0:T(8,128)(2,1)S(1)} %get-tuple-element.44), channel_id=1, source_target_pairs={{0,32},{32,0},{1,33},{33,1},{2,34},{34,2},{3,35},{35,3},{4,36},{36... | collective-permute-start | bytes 2752520 | tf_op jit(solution)/shard_map/ppermute | solution.py:448
  64.5 2.1 %collective-permute-done.3 = bf16[2,2,896,128]{3,2,1,0:T(8,128)(2,1)S(1)} collective-permute-done((bf16[2,2,896,128]{3,2,1,0:T(8,128)(2,1)S(1)}, bf16[2,2,896,128]{3,2,1,0:T(8,128)(2,1)S(1)}, u32[]{:S(2)}, u32[]{:S(2)}) %collective-permute-start.3) | collective-permute-done | bytes 917536 | tf_op jit(solution)/shard_map/ppermute | solution.py:448
  66.6 0.2 add_convert_fusion
  66.8 16.7 %all_to_all.36.got_ref = bf16[4,896,128]{2,1,0:T(8,128)(2,1)S(1)} all-to-all(bf16[4,896,128]{2,1,0:T(8,128)(2,1)S(1)} %bitcast.11), channel_id=1, replica_groups=mesh['xh'=2,'y'=4,'c'=2,'zh'=4,'zl'=4,'xl'=2] {'xh','xl'}, dimensions={0} | all-to-all | bytes 1835008 | tf_op jit(solution)/shard_map/all_to_all | solution.py:296
  83.5 0.1 gradient_sum.2
  83.6 8.9 %all_to_all.37.got_ref = bf16[4,224,128]{2,1,0:T(8,128)(2,1)S(1)} all-to-all(bf16[4,224,128]{2,1,0:T(8,128)(2,1)S(1)} %bitcast.10), channel_id=1, replica_groups=mesh['xh'=2,'y'=4,'c'=2,'zh'=4,'zl'=4,'xl'=2] {'zl'}, dimensions={0} | all-to-all | bytes 458752 | tf_op jit(solution)/shard_map/all_to_all | solution.py:296
  92.6 9.8 %collective-permute-start.6 = (bf16[224,128]{1,0:T(8,128)(2,1)S(1)}, bf16[224,128]{1,0:T(8,128)(2,1)S(1)}, u32[]{:S(2)}, u32[]{:S(2)}) collective-permute-start(bf16[224,128]{1,0:T(8,128)(2,1)S(1)} %gradient_sum.3.own_ref), channel_id=1, source_target_pairs={{0,24},{8,16},{16,8},{24,0},{1,25},{9,17},{17,9},{25,1},{2,26},{10... | collective-permute-start | bytes 172040 | tf_op jit(solution)/shard_map/ppermute | solution.py:464
  102.4 6.1 %collective-permute-start.5 = (bf16[224,128]{1,0:T(8,128)(2,1)S(1)}, bf16[224,128]{1,0:T(8,128)(2,1)S(1)}, u32[]{:S(2)}, u32[]{:S(2)}) collective-permute-start(bf16[224,128]{1,0:T(8,128)(2,1)S(1)} %gradient_sum.3.own_ref), channel_id=1, source_target_pairs={{0,16},{8,24},{16,0},{24,8},{1,17},{9,25},{17,1},{25,9},{2,18},{10... | collective-permute-start | bytes 172040 | tf_op jit(solution)/shard_map/ppermute | solution.py:464
  108.4 2.9 %collective-permute-start.4 = (bf16[224,128]{1,0:T(8,128)(2,1)S(1)}, bf16[224,128]{1,0:T(8,128)(2,1)S(1)}, u32[]{:S(2)}, u32[]{:S(2)}) collective-permute-start(bf16[224,128]{1,0:T(8,128)(2,1)S(1)} %gradient_sum.3.own_ref), channel_id=1, source_target_pairs={{0,8},{8,0},{16,24},{24,16},{1,9},{9,1},{17,25},{25,17},{2,10},{10... | collective-permute-start | bytes 172040 | tf_op jit(solution)/shard_map/ppermute | solution.py:464
  111.3 0.0 collective-permute-done.6.both_ref
  111.3 5.4 %collective-permute-done.5.far_ref = bf16[224,128]{1,0:T(8,128)(2,1)S(1)} collective-permute-done((bf16[224,128]{1,0:T(8,128)(2,1)S(1)}, bf16[224,128]{1,0:T(8,128)(2,1)S(1)}, u32[]{:S(2)}, u32[]{:S(2)}) %collective-permute-start.5) | collective-permute-done | bytes 57376 | tf_op jit(solution)/shard_map/ppermute | solution.py:464
  116.7 3.3 %collective-permute-done.4.near_ref = bf16[224,128]{1,0:T(8,128)(2,1)S(1)} collective-permute-done((bf16[224,128]{1,0:T(8,128)(2,1)S(1)}, bf16[224,128]{1,0:T(8,128)(2,1)S(1)}, u32[]{:S(2)}, u32[]{:S(2)}) %collective-permute-start.4) | collective-permute-done | bytes 57376 | tf_op jit(solution)/shard_map/ppermute | solution.py:464
  120.0 8.6 %all_to_all.38 = bf16[4,224,128]{2,1,0:T(8,128)(2,1)S(1)} all-to-all(bf16[4,224,128]{2,1,0:T(8,128)(2,1)S(1)} %gradient_pairs.1), channel_id=1, replica_groups=mesh['xh'=2,'y'=4,'c'=2,'zh'=4,'zl'=4,'xl'=2] {'zl'}, dimensions={0} | all-to-all | bytes 458752 | tf_op jit(solution)/shard_map/all_to_all | solution.py:296
  128.6 0.1 broadcast_in_dim.20
  128.7 1.0 pad_maximum_fusion
  129.7 3.6 %all-to-all-start.6 = ((bf16[8,416,128]{2,1,0:T(8,128)(2,1)}), bf16[8,416,128]{2,1,0:T(8,128)(2,1)S(1)}, u32[]{:S(2)}, u32[]{:S(2)}) async-start(bf16[8,416,128]{2,1,0:T(8,128)(2,1)} %pad_maximum_fusion), calls=%async_computation.6 | async-start | bytes 1703936 | tf_op jit(solution)/shard_map/all_to_all | solution.py:296
  133.2 2.2 %collective-permute-start.7 = (bf16[640,128]{1,0:T(8,128)(2,1)S(1)}, bf16[640,128]{1,0:T(8,128)(2,1)S(1)}, u32[]{:S(2)}, u32[]{:S(2)}) collective-permute-start(bf16[640,128]{1,0:T(8,128)(2,1)S(1)} %slice.20.own_ref), channel_id=1, source_target_pairs={{0,1},{1,0},{2,3},{3,2},{4,5},{5,4},{6,7},{7,6},{8,9},{9,8},{10,11... | collective-permute-start | bytes 491528 | tf_op jit(solution)/shard_map/ppermute | solution.py:475
  135.4 6.8 %collective-permute-done.7.other_ref = bf16[640,128]{1,0:T(8,128)(2,1)S(1)} collective-permute-done((bf16[640,128]{1,0:T(8,128)(2,1)S(1)}, bf16[640,128]{1,0:T(8,128)(2,1)S(1)}, u32[]{:S(2)}, u32[]{:S(2)}) %collective-permute-start.7) | collective-permute-done | bytes 163872 | tf_op jit(solution)/shard_map/ppermute | solution.py:475
  142.2 0.9 all-to-all-done.6.got_ref
  143.2 8.8 %collective-permute-start.8 = (bf16[8,416,128]{2,1,0:T(8,128)(2,1)S(1)}, bf16[8,416,128]{2,1,0:T(8,128)(2,1)S(1)}, u32[]{:S(2)}, u32[]{:S(2)}) collective-permute-start(bf16[8,416,128]{2,1,0:T(8,128)(2,1)S(1)} %all-to-all-done.6.got_ref), channel_id=1, source_target_pairs={{0,32},{32,0},{1,33},{33,1},{2,34},{34,2},{3,35},{35,3},{4,36},{36... | collective-permute-start | bytes 2555912 | tf_op jit(solution)/shard_map/ppermute | solution.py:479
  152.0 2.0 %collective-permute-done.8.cross_ref = bf16[8,416,128]{2,1,0:T(8,128)(2,1)S(1)} collective-permute-done((bf16[8,416,128]{2,1,0:T(8,128)(2,1)S(1)}, bf16[8,416,128]{2,1,0:T(8,128)(2,1)S(1)}, u32[]{:S(2)}, u32[]{:S(2)}) %collective-permute-start.8) | collective-permute-done | bytes 852000 | tf_op jit(solution)/shard_map/ppermute | solution.py:479
  154.0 3.0 %gradient_unpack.1 = (f32[384,1280]{1,0:T(8,128)}, f32[1280]{0:T(1024)}, f32[640]{0:T(1024)}, f32[80,1920]{1,0:T(8,128)}, bf16[256,640]{1,0:T(8,128)(2,1)}) custom-call(s32[4]{0:T(128)S(1)} %pad_add_fusion.where_ref, bf16[8,416,128]{2,1,0:T(8,128)(2,1)S(1)} %all-to-all-done.6.got_ref, bf16[8,416,128]{2,1,0:T(8,128)(2,1)S(1)} %collective-permute-done.8.cross_ref, ...), custom_call_target="tpu_custom_call" | custom-call | tf_op jit(solution)/shard_map/gradient_unpack/pallas_call | solution.py:480
  (17 shorter events, 0.1 us)
Async XLA Ops:
  0.6 21.1 %copy-start = (bf16[80,1920]{1,0:T(8,128)(2,1)S(1)}, bf16[80,1920]{1,0:T(8,128)(2,1)}, u32[]{:S(2)}) copy-start(bf16[80,1920]{1,0:T(8,128)(2,1)} %own_ref.3) | copy-start | bytes 921604
  0.6 19.1 %copy-start.1 = (bf16[384,1280]{1,0:T(8,128)(2,1)S(1)}, bf16[384,1280]{1,0:T(8,128)(2,1)}, u32[]{:S(2)}) copy-start(bf16[384,1280]{1,0:T(8,128)(2,1)} %weight_ref.1) | copy-start | bytes 2949124
  0.7 16.1 %collective-permute-start.1 = (bf16[80,1920]{1,0:T(8,128)(2,1)}, bf16[80,1920]{1,0:T(8,128)(2,1)S(1)}, u32[]{:S(2)}, u32[]{:S(2)}) collective-permute-start(bf16[80,1920]{1,0:T(8,128)(2,1)} %own_ref.3), channel_id=1, source_target_pairs={{0,257},{257,0},{1,256},{256,1},{2,259},{259,2},{3,258},{258,3},{4... | collective-permute-start | bytes 921608 | tf_op jit(solution)/shard_map/ppermute | solution.py:334
  7.7 14.0 %all-to-all-start = ((bf16[4,26,16,128]{3,2,1,0:T(8,128)(2,1)}), bf16[4,26,16,128]{3,2,1,0:T(8,128)(2,1)S(1)}, u32[]{:S(2)}, u32[]{:S(2)}) async-start(bf16[4,26,16,128]{3,2,1,0:T(8,128)(2,1)} %mel_payload.1), calls=%async_computation | async-start | bytes 851968 | tf_op jit(solution)/shard_map/all_to_all | solution.py:296
  11.9 9.8 %collective-permute-start = (bf16[80,1920]{1,0:T(8,128)(2,1)}, bf16[80,1920]{1,0:T(8,128)(2,1)S(1)}, u32[]{:S(2)}, u32[]{:S(2)}) collective-permute-start(bf16[80,1920]{1,0:T(8,128)(2,1)} %own_ref.3), channel_id=1, source_target_pairs={{0,32},{32,0},{1,33},{33,1},{2,34},{34,2},{3,35},{35,3},{4,36},{36... | collective-permute-start | bytes 921608 | tf_op jit(solution)/shard_map/ppermute | solution.py:364
  16.7 5.0 %collective-permute-start.2 = (bf16[80,1920]{1,0:T(8,128)(2,1)S(1)}, bf16[80,1920]{1,0:T(8,128)(2,1)S(1)}, u32[]{:S(2)}, u32[]{:S(2)}) collective-permute-start(bf16[80,1920]{1,0:T(8,128)(2,1)S(1)} %collective-permute-done.1.far_ref), channel_id=1, source_target_pairs={{0,32},{32,0},{1,33},{33,1},{2,34},{34,2},{3,35},{35,3},{4,36},{36... | collective-permute-start | bytes 921608 | tf_op jit(solution)/shard_map/ppermute | solution.py:366
  19.8 0.7 copy-start.2
  21.7 7.8 %copy-start.4 = (s32[16]{0:T(128)S(1)}, s32[16]{0:T(128)}, u32[]{:S(2)}) copy-start(s32[16]{0:T(128)} %length_ref.1) | copy-start | bytes 196
  21.7 7.8 %copy-start.5 = (s32[16,1]{0,1:T(1,128)S(1)}, s32[16,1]{0,1:T(1,128)}, u32[]{:S(2)}) copy-start(s32[16,1]{0,1:T(1,128)} %param.10) | copy-start | bytes 196
  21.7 8.1 %copy-start.3 = (f32[640]{0:T(1024)S(1)}, f32[640]{0:T(1024)}, u32[]{:S(2)}) copy-start(f32[640]{0:T(1024)} %param.14) | copy-start | bytes 7684
  26.0 13.7 %all-to-all-start.1 = ((bf16[4,128,640]{2,1,0:T(8,128)(2,1)}), bf16[4,128,640]{2,1,0:T(8,128)(2,1)S(1)}, u32[]{:S(2)}, u32[]{:S(2)}) async-start(bf16[4,128,640]{2,1,0:T(8,128)(2,1)} %get-tuple-element.32), calls=%async_computation.1 | async-start | bytes 1310720 | tf_op jit(solution)/shard_map/all_to_all | solution.py:296
  60.1 6.5 %collective-permute-start.3 = (bf16[2,2,896,128]{3,2,1,0:T(8,128)(2,1)S(1)}, bf16[2,2,896,128]{3,2,1,0:T(8,128)(2,1)S(1)}, u32[]{:S(2)}, u32[]{:S(2)}) collective-permute-start(bf16[2,2,896,128]{3,2,1,0:T(8,128)(2,1)S(1)} %get-tuple-element.44), channel_id=1, source_target_pairs={{0,32},{32,0},{1,33},{33,1},{2,34},{34,2},{3,35},{35,3},{4,36},{36... | collective-permute-start | bytes 2752520 | tf_op jit(solution)/shard_map/ppermute | solution.py:448
  92.6 18.7 %collective-permute-start.6 = (bf16[224,128]{1,0:T(8,128)(2,1)S(1)}, bf16[224,128]{1,0:T(8,128)(2,1)S(1)}, u32[]{:S(2)}, u32[]{:S(2)}) collective-permute-start(bf16[224,128]{1,0:T(8,128)(2,1)S(1)} %gradient_sum.3.own_ref), channel_id=1, source_target_pairs={{0,24},{8,16},{16,8},{24,0},{1,25},{9,17},{17,9},{25,1},{2,26},{10... | collective-permute-start | bytes 172040 | tf_op jit(solution)/shard_map/ppermute | solution.py:464
  102.4 14.3 %collective-permute-start.5 = (bf16[224,128]{1,0:T(8,128)(2,1)S(1)}, bf16[224,128]{1,0:T(8,128)(2,1)S(1)}, u32[]{:S(2)}, u32[]{:S(2)}) collective-permute-start(bf16[224,128]{1,0:T(8,128)(2,1)S(1)} %gradient_sum.3.own_ref), channel_id=1, source_target_pairs={{0,16},{8,24},{16,0},{24,8},{1,17},{9,25},{17,1},{25,9},{2,18},{10... | collective-permute-start | bytes 172040 | tf_op jit(solution)/shard_map/ppermute | solution.py:464
  108.4 11.5 %collective-permute-start.4 = (bf16[224,128]{1,0:T(8,128)(2,1)S(1)}, bf16[224,128]{1,0:T(8,128)(2,1)S(1)}, u32[]{:S(2)}, u32[]{:S(2)}) collective-permute-start(bf16[224,128]{1,0:T(8,128)(2,1)S(1)} %gradient_sum.3.own_ref), channel_id=1, source_target_pairs={{0,8},{8,0},{16,24},{24,16},{1,9},{9,1},{17,25},{25,17},{2,10},{10... | collective-permute-start | bytes 172040 | tf_op jit(solution)/shard_map/ppermute | solution.py:464
  129.7 13.5 %all-to-all-start.6 = ((bf16[8,416,128]{2,1,0:T(8,128)(2,1)}), bf16[8,416,128]{2,1,0:T(8,128)(2,1)S(1)}, u32[]{:S(2)}, u32[]{:S(2)}) async-start(bf16[8,416,128]{2,1,0:T(8,128)(2,1)} %pad_maximum_fusion), calls=%async_computation.6 | async-start | bytes 1703936 | tf_op jit(solution)/shard_map/all_to_all | solution.py:296
  133.2 9.0 %collective-permute-start.7 = (bf16[640,128]{1,0:T(8,128)(2,1)S(1)}, bf16[640,128]{1,0:T(8,128)(2,1)S(1)}, u32[]{:S(2)}, u32[]{:S(2)}) collective-permute-start(bf16[640,128]{1,0:T(8,128)(2,1)S(1)} %slice.20.own_ref), channel_id=1, source_target_pairs={{0,1},{1,0},{2,3},{3,2},{4,5},{5,4},{6,7},{7,6},{8,9},{9,8},{10,11... | collective-permute-start | bytes 491528 | tf_op jit(solution)/shard_map/ppermute | solution.py:475
  143.2 10.8 %collective-permute-start.8 = (bf16[8,416,128]{2,1,0:T(8,128)(2,1)S(1)}, bf16[8,416,128]{2,1,0:T(8,128)(2,1)S(1)}, u32[]{:S(2)}, u32[]{:S(2)}) collective-permute-start(bf16[8,416,128]{2,1,0:T(8,128)(2,1)S(1)} %all-to-all-done.6.got_ref), channel_id=1, source_target_pairs={{0,32},{32,0},{1,33},{33,1},{2,34},{34,2},{3,35},{35,3},{4,36},{36... | collective-permute-start | bytes 2555912 | tf_op jit(solution)/shard_map/ppermute | solution.py:479

commit v9 on v8

--- a/solution.py
+++ b/solution.py
@@ -24,7 +24,6 @@
 SLOTS = 2 * CLIPS
 PAY = 26
 CHIPS = 8
-DEAD = -1e30
 PACK = 896
 HALF_ROWS = 8 * ROWS
 MIB = 1024 * 1024
@@ -72,11 +71,9 @@
 
 
 def stack_weights(refs, w2_ref):
-    @pl.when(pl.program_id(0) == 0)
-    def _():
-        for block, ref in enumerate(refs):
-            w2_ref[block * ROWS : (block + 1) * ROWS, :] = ref[...]
-        w2_ref[BLOCKS * ROWS :, :] = jnp.zeros((WIDE - BLOCKS * ROWS, 3 * D2), BF16)
+    for block, ref in enumerate(refs):
+        w2_ref[block * ROWS : (block + 1) * ROWS, :] = ref[...]
+    w2_ref[BLOCKS * ROWS :, :] = jnp.zeros((WIDE - BLOCKS * ROWS, 3 * D2), BF16)
 
 
 def prepare_kernel(length_ref, mel_ref, pay_ref):
@@ -105,51 +102,58 @@
     w1_ref[...] = picked[...].astype(BF16)
 
 
-def forward_kernel(
-    pay_ref, w1_ref, b1_ref, own_ref, side_ref, far_ref, both_ref, part_ref, cols_ref, act_ref, pre_ref, w2_ref,
-    frames_ref,
-):
-    stack_weights((own_ref, side_ref, far_ref, both_ref), w2_ref)
+def first_conv(pay_ref, w1_ref, b1_ref, cols_ref, frames_ref):
+    sources = pay_ref.shape[0]
     spread = (
         lax.broadcasted_iota(jnp.int32, (STEPS, CLIPS), 0) >> 3
         == lax.broadcasted_iota(jnp.int32, (STEPS, CLIPS), 1)
     ).astype(F32).astype(BF16)
-    length = dot(spread, pay_ref[0, CLIPS])
-    frames_ref[...] = pay_ref[0, :CLIPS].astype(F32).reshape(2 * STEPS, MEL)
     t = (lax.broadcasted_iota(jnp.int32, (STEPS, LANES), 0) & (HALF - 1)).astype(F32)
-    live_even, live_odd = 2.0 * t < length, 2.0 * t + 1.0 < length
-    even = jnp.where(live_even, frames_ref[pl.ds(0, STEPS, 2), :], 0.0)
-    odd = jnp.where(live_odd, frames_ref[pl.ds(1, STEPS, 2), :], 0.0)
-    cols_ref[0, :, :LANES] = shift_down(odd).astype(BF16)
-    cols_ref[0, :, LANES : 2 * LANES] = even.astype(BF16)
-    cols_ref[0, :, 2 * LANES : 3 * LANES] = odd.astype(BF16)
-    cols_ref[0, :, 3 * LANES :] = shift_up(even).astype(BF16)
-    bias = b1_ref[...]
-    live_even = jnp.concatenate([live_even] * (WIDE // LANES), axis=1)
-    live_odd = jnp.concatenate([live_odd] * (WIDE // LANES), axis=1)
-    pre = dot(cols_ref[0, :, : 3 * LANES], w1_ref[...]) + bias
-    pre_ref[0, 0] = jnp.where(live_even, pre, DEAD)
-    act_even = jnp.where(live_even, gelu_value(pre), 0.0).astype(BF16)
-    pre = dot(cols_ref[0, :, LANES:], w1_ref[...]) + bias
-    pre_ref[0, 1] = jnp.where(live_odd, pre, DEAD)
-    act = jnp.where(live_odd, gelu_value(pre), 0.0)
-    act_odd = act.astype(BF16)
-    act_prior = shift_down(act).astype(BF16)
-    act_ref[0, 0] = act_prior
-    act_ref[0, 1] = act_even
-    act_ref[0, 2] = act_odd
-    total = dot(act_prior, w2_ref[:, :D2])
-    total = total + dot(act_even, w2_ref[:, D2 : 2 * D2])
-    total = total + dot(act_odd, w2_ref[:, 2 * D2 :])
-    part_ref[0] = total.astype(BF16)
-
-
-def slope_kernel(pre_ref, act_ref, slope_ref, turned_ref):
-    pre = pre_ref[0].reshape(2 * STEPS, WIDE)
-    slope = jnp.where(pre > 0.5 * DEAD, gelu_both(pre)[1], 0.0)
-    slope_ref[0] = slope.reshape(2, STEPS, WIDE)
-    for tap in range(3):
-        turned_ref[tap] = act_ref[0, tap].T
+    lives_even, lives_odd = [], []
+    for source in range(sources):
+        rows = slice(source * STEPS, (source + 1) * STEPS)
+        length = dot(spread, pay_ref[source, CLIPS])
+        frames_ref[source] = pay_ref[source, :CLIPS].astype(F32).reshape(2 * STEPS, MEL)
+        live_even, live_odd = 2.0 * t < length, 2.0 * t + 1.0 < length
+        even = jnp.where(live_even, frames_ref[source, pl.ds(0, STEPS, 2), :], 0.0)
+        odd = jnp.where(live_odd, frames_ref[source, pl.ds(1, STEPS, 2), :], 0.0)
+        cols_ref[rows, :LANES] = shift_down(odd).astype(BF16)
+        cols_ref[rows, LANES : 2 * LANES] = even.astype(BF16)
+        cols_ref[rows, 2 * LANES : 3 * LANES] = odd.astype(BF16)
+        cols_ref[rows, 3 * LANES :] = shift_up(even).astype(BF16)
+        lives_even.append(jnp.concatenate([live_even] * (WIDE // LANES), axis=1))
+        lives_odd.append(jnp.concatenate([live_odd] * (WIDE // LANES), axis=1))
+    cols = jnp.concatenate([cols_ref[:, : 3 * LANES], cols_ref[:, LANES:]], axis=0)
+    pre = dot(cols, w1_ref[...]) + b1_ref[...]
+    half = sources * STEPS
+    return pre[:half], pre[half:], jnp.concatenate(lives_even, axis=0), jnp.concatenate(lives_odd, axis=0)
+
+
+def forward_kernel(
+    pay_ref, w1_ref, b1_ref, own_ref, side_ref, far_ref, both_ref, part_ref, w2_ref, cols_ref, frames_ref
+):
+    @pl.when(pl.program_id(0) == 0)
+    def _():
+        stack_weights((own_ref, side_ref, far_ref, both_ref), w2_ref)
+
+    pre_even, pre_odd, live_even, live_odd = first_conv(pay_ref, w1_ref, b1_ref, cols_ref, frames_ref)
+    odd = jnp.where(live_odd, gelu_value(pre_odd), 0.0)
+    total = dot(odd.astype(BF16), w2_ref[:, 2 * D2 :]) + dot(shift_down(odd).astype(BF16), w2_ref[:, :D2])
+    even = jnp.where(live_even, gelu_value(pre_even), 0.0)
+    total = total + dot(even.astype(BF16), w2_ref[:, D2 : 2 * D2])
+    part_ref[...] = total.astype(BF16).reshape(part_ref.shape)
+
+
+def slope_kernel(pay_ref, w1_ref, b1_ref, cols_ref, slope_ref, turned_ref, frames_ref):
+    pre_even, pre_odd, live_even, live_odd = first_conv(pay_ref, w1_ref, b1_ref, cols_ref, frames_ref)
+    value, slope = gelu_both(pre_odd)
+    odd = jnp.where(live_odd, value, 0.0)
+    slope_ref[1] = jnp.where(live_odd, slope, 0.0)
+    turned_ref[0] = shift_down(odd).astype(BF16).T
+    turned_ref[2] = odd.astype(BF16).T
+    value, slope = gelu_both(pre_even)
+    slope_ref[0] = jnp.where(live_even, slope, 0.0)
+    turned_ref[1] = jnp.where(live_even, value, 0.0).astype(BF16).T
 
 
 def middle_kernel(
@@ -186,54 +190,47 @@
 
 
 def backward_kernel(
-    where_ref, grad_ref, own_ref, side_ref, far_ref, both_ref, cols_ref, act_ref, slope_ref, keep_ref, send_ref,
-    w2_ref, conv2_sum, conv1_sum, bias1_sum, bias2_sum,
+    where_ref, grad_ref, own_ref, side_ref, far_ref, both_ref, cols_ref, turned_ref, slope_ref, keep_ref, send_ref,
+    w2_ref, conv_sum, cols_here, cols_done,
 ):
+    cols_copy = pltpu.make_async_copy(cols_ref, cols_here, cols_done)
+    cols_copy.start()
     stack_weights((own_ref, side_ref, far_ref, both_ref), w2_ref)
-    step = pl.program_id(0)
-
-    @pl.when(step == 0)
-    def _():
-        conv2_sum[...] = jnp.zeros_like(conv2_sum)
-        conv1_sum[...] = jnp.zeros_like(conv1_sum)
-        bias1_sum[...] = jnp.zeros_like(bias1_sum)
-        bias2_sum[...] = jnp.zeros_like(bias2_sum)
-
-    rows = 2 * STEPS
-    grad = grad_ref[...].reshape(rows, D2)
-    bias2_sum[...] += jnp.sum(grad.astype(F32), axis=0, keepdims=True)
+    mine = where_ref[0]
+    grad = grad_ref[...].reshape(HOLDERS * STEPS, D2)
+    places = []
+    for block in range(BLOCKS):
+        places.append((keep_ref if block % 2 == 0 else send_ref, mine if block < 2 else 1 - mine, block * ROWS))
+
+    for tap in range(3):
+        conv_sum[...] = dot(turned_ref[tap], grad)
+        for out, target, first in places:
+            for column in range(D2 // LANES):
+                tile = tap * (D2 // LANES) + column
+                piece = conv_sum[first : first + ROWS, column * LANES : (column + 1) * LANES]
+                out[target, tile // 8, (tile % 8) * ROWS : (tile % 8 + 1) * ROWS, :] = piece.astype(out.dtype)
+
     even = dot_nt(grad, w2_ref[:, D2 : 2 * D2])
+    even = (even * slope_ref[0]).astype(BF16)
     odd = dot_nt(grad, w2_ref[:, 2 * D2 :]) + shift_up(dot_nt(grad, w2_ref[:, :D2]))
-    even = (even * slope_ref[:, 0].reshape(rows, WIDE)).astype(BF16)
-    odd = (odd * slope_ref[:, 1].reshape(rows, WIDE)).astype(BF16)
-    cols = cols_ref[...].reshape(rows, 4 * LANES)
-    conv1_sum[...] += dot_tn(even, cols[:, : 3 * LANES]) + dot_tn(odd, cols[:, LANES:])
-    bias1_sum[...] += jnp.sum(even.astype(F32) + odd.astype(F32), axis=0, keepdims=True)
-    for tap in range(3):
-        conv2_sum[:, tap * D2 : (tap + 1) * D2] += dot(act_ref[tap], grad)
-
-    @pl.when(step == pl.num_programs(0) - 1)
-    def _():
-        mine = where_ref[0]
-        for block in range(BLOCKS):
-            target = mine if block < 2 else 1 - mine
-            out = keep_ref if block % 2 == 0 else send_ref
-            first = block * ROWS
-            for tile in range(15):
-                half, spot = tile // 8, tile % 8
-                piece = conv2_sum[first : first + ROWS, tile * LANES : (tile + 1) * LANES]
-                out[target, half, spot * ROWS : (spot + 1) * ROWS, :] = piece.astype(out.dtype)
-            out[target, 1, 7 * ROWS : 8 * ROWS, :] = jnp.zeros((ROWS, LANES), out.dtype)
-            biases = [jnp.concatenate([bias1_sum[:, first : first + ROWS], jnp.zeros((1, LANES - ROWS), F32)], axis=1)]
-            for tile in range(D2 // LANES):
-                biases.append(bias2_sum[:, tile * LANES : (tile + 1) * LANES])
-            biases.append(jnp.zeros((16 - len(biases), LANES), F32))
-            biases = jnp.concatenate(biases, axis=0).astype(out.dtype)
-            for half in range(2):
-                for tile in range(3):
-                    piece = conv1_sum[first : first + ROWS, tile * LANES : (tile + 1) * LANES]
-                    out[target, half, (8 + tile) * ROWS : (9 + tile) * ROWS, :] = piece.astype(out.dtype)
-                out[target, half, 11 * ROWS :, :] = biases
+    odd = (odd * slope_ref[1]).astype(BF16)
+    cols_copy.wait()
+    cols = cols_here[...]
+    conv_sum[:, : 3 * LANES] = dot_tn(even, cols[:, : 3 * LANES]) + dot_tn(odd, cols[:, LANES:])
+    bias1 = jnp.sum(even.astype(F32) + odd.astype(F32), axis=0, keepdims=True)
+    bias2 = jnp.sum(grad.astype(F32), axis=0, keepdims=True)
+    for out, target, first in places:
+        out[target, 1, 7 * ROWS : 8 * ROWS, :] = jnp.zeros((ROWS, LANES), out.dtype)
+        biases = [jnp.concatenate([bias1[:, first : first + ROWS], jnp.zeros((1, LANES - ROWS), F32)], axis=1)]
+        for tile in range(D2 // LANES):
+            biases.append(bias2[:, tile * LANES : (tile + 1) * LANES])
+        biases.append(jnp.zeros((16 - len(biases), LANES), F32))
+        biases = jnp.concatenate(biases, axis=0).astype(out.dtype)
+        for half in range(2):
+            for tile in range(3):
+                piece = conv_sum[first : first + ROWS, tile * LANES : (tile + 1) * LANES]
+                out[target, half, (8 + tile) * ROWS : (9 + tile) * ROWS, :] = piece.astype(out.dtype)
+            out[target, half, 11 * ROWS :, :] = biases
 
 
 def sum_kernel(got_ref, out_ref):
@@ -248,7 +245,7 @@
             out_ref[target] = total
 
 
-def pairs_kernel(own_ref, near_ref, far_ref, both_ref, out_ref):
+def pairs_kernel(own_ref, near_ref, both_ref, far_ref, out_ref):
     own, near, far, both = (ref[...].astype(F32) for ref in (own_ref, near_ref, far_ref, both_ref))
     total = ((own + near) + (far + both)).astype(BF16)
     for target in range(out_ref.shape[0]):
@@ -356,7 +353,7 @@
         scratch_shapes=[pltpu.VMEM((3 * MEL, WIDE), F32)],
         compiler_params=params(10),
         name="conv1_columns",
-    )(where, conv1_weight, conv1_bias)
+    )(where, conv1_weight, from_hbm(conv1_bias))
     own_weight, place = lax.optimization_barrier((conv2_weight, where))
     far_weight, place = lax.optimization_barrier((far_weight, place))
     weights = [
@@ -368,40 +365,39 @@
 
     pair = lambda i: (i, 0, 0)
     pair4 = lambda i: (i, 0, 0, 0)
-    parts, cols, acts, pres = pl.pallas_call(
+    rows, some = HOLDERS * STEPS, 2 * STEPS
+    frames = (2, 2 * STEPS, MEL)
+    pay_spec = pl.BlockSpec((2, PAY, 2 * HALF, MEL), pair4)
+    parts = pl.pallas_call(
         forward_kernel,
-        grid=(HOLDERS,),
-        in_specs=[
-            pl.BlockSpec((1, PAY, 2 * HALF, MEL), pair4),
-            *[vmem()] * (2 + BLOCKS),
-        ],
-        out_specs=[
-            pl.BlockSpec((1, STEPS, D2), pair),
-            pl.BlockSpec((1, STEPS, 4 * LANES), pair),
-            pl.BlockSpec((1, 3, STEPS, WIDE), pair4),
-            pl.BlockSpec((1, 2, STEPS, WIDE), pair4),
-        ],
-        out_shape=[
-            in_hbm(HOLDERS, STEPS, D2),
-            in_hbm(HOLDERS, STEPS, 4 * LANES),
-            in_hbm(HOLDERS, 3, STEPS, WIDE),
-            in_hbm(HOLDERS, 2, STEPS, WIDE, dtype=F32),
-        ],
-        scratch_shapes=[pltpu.VMEM((WIDE, 3 * D2), BF16), pltpu.VMEM((2 * STEPS, MEL), F32)],
+        grid=(HOLDERS // 2,),
+        in_specs=[pay_spec, *[vmem()] * (2 + BLOCKS)],
+        out_specs=pl.BlockSpec((2, STEPS, D2), pair),
+        out_shape=in_hbm(HOLDERS, STEPS, D2),
+        scratch_shapes=[
+            pltpu.VMEM((WIDE, 3 * D2), BF16),
+            pltpu.VMEM((some, 4 * LANES), BF16),
+            pltpu.VMEM(frames, F32),
+        ],
         compiler_params=params(20, "arbitrary"),
         name="stem_forward",
     )(got_pay, w1, b1, *weights)
 
     got_parts = exchange(parts, "y")
-    slopes, turned = pl.pallas_call(
+    cols, slopes, turned = pl.pallas_call(
         slope_kernel,
-        grid=(HOLDERS,),
-        in_specs=[pl.BlockSpec((1, 2, STEPS, WIDE), pair4), pl.BlockSpec((1, 3, STEPS, WIDE), pair4)],
-        out_specs=[pl.BlockSpec((1, 2, STEPS, WIDE), pair4), pl.BlockSpec((3, WIDE, STEPS), lambda i: (0, 0, i))],
-        out_shape=[in_hbm(HOLDERS, 2, STEPS, WIDE, dtype=F32), in_hbm(3, WIDE, HOLDERS * STEPS)],
+        grid=(HOLDERS // 2,),
+        in_specs=[pay_spec, vmem(), vmem()],
+        out_specs=[
+            pl.BlockSpec((some, 4 * LANES), lambda i: (i, 0)),
+            pl.BlockSpec((2, some, WIDE), lambda i: (0, i, 0)),
+            pl.BlockSpec((3, WIDE, some), lambda i: (0, 0, i)),
+        ],
+        out_shape=[in_hbm(rows, 4 * LANES), shape(2, rows, WIDE, dtype=F32), shape(3, WIDE, rows)],
+        scratch_shapes=[pltpu.VMEM(frames, F32)],
         compiler_params=params(20, "arbitrary"),
         name="stem_slopes",
-    )(from_hbm(pres), from_hbm(acts))
+    )(got_pay, w1, b1)
     got_parts, slopes, turned = lax.optimization_barrier((got_parts, slopes, turned))
     owner = jnp.repeat(routes[:, 0], HALF)
     rep, same, cross = pl.pallas_call(
@@ -424,27 +420,24 @@
 
     keep, send = pl.pallas_call(
         backward_kernel,
-        grid=(HOLDERS // 2,),
         in_specs=[
             pl.BlockSpec(memory_space=pltpu.SMEM),
-            pl.BlockSpec((2, STEPS, D2), pair),
-            *[vmem()] * BLOCKS,
-            pl.BlockSpec((2, STEPS, 4 * LANES), pair),
-            pl.BlockSpec((3, WIDE, 2 * STEPS), lambda i: (0, 0, i)),
-            pl.BlockSpec((2, 2, STEPS, WIDE), pair4),
+            *[vmem()] * (1 + BLOCKS),
+            pl.BlockSpec(memory_space=pl.ANY),
+            vmem(),
+            vmem(),
         ],
         out_specs=[vmem()] * 2,
         out_shape=[shape(2, 2, PACK, LANES, dtype=F32), shape(2, 2, PACK, LANES)],
         scratch_shapes=[
             pltpu.VMEM((WIDE, 3 * D2), BF16),
-            pltpu.VMEM((WIDE, 3 * D2), F32),
-            pltpu.VMEM((WIDE, 3 * LANES), F32),
-            pltpu.VMEM((1, WIDE), F32),
-            pltpu.VMEM((1, D2), F32),
-        ],
-        compiler_params=params(32, "arbitrary"),
+            pltpu.VMEM((WIDE, D2), F32),
+            pltpu.VMEM((rows, 4 * LANES), BF16),
+            pltpu.SemaphoreType.DMA,
+        ],
+        compiler_params=params(32),
         name="stem_backward",
-    )(where, got_grad, *weights, from_hbm(cols), from_hbm(turned), from_hbm(slopes))
+    )(where, got_grad, *weights, from_hbm(cols), turned, slopes)
     got = lax.ppermute(send, "c", cores)
     quarters = exchange((keep + got.astype(F32)).astype(BF16).reshape(4, PACK, LANES), ("xh", "xl"))
 
@@ -469,7 +462,7 @@
         out_shape=shape(4, quarter, LANES),
         compiler_params=params(8),
         name="gradient_pairs",
-    )(near, far[1], far[2], far[3])
+    )(near, far[1], far[3], far[2])
     half = exchange(far, "zl").reshape(PACK, LANES)
     own = half[:HALF_ROWS]
     other = lax.ppermute(own, "xl", [(0, 1), (1, 0)])

time: 158 us -> 153 us (0.968)
  Pallas kernels: 22.4 us -> 17.4 us
    pallas_call x3, Pallas kernels: 14.2 us -> 8.97 us  [the longest x1 3.45 us: local(): pl.pallas_call(backward_kernel, in_specs=[pl.BlockSpec(memory_space=pltpu...]
  transfers between devices with their start and end apart: 12 -> 12, of which waited for: 7 -> 7; matrix products, arithmetic and copies ran while one was open for 1% -> 1% of each run, Pallas kernels for 5% -> 3%
where the time goes in v9:
time: 153 us
  starting transfers between devices  59.2 us (39%)
  blocking collectives  47 us (31%)
  waiting for transfers between devices  23.6 us (15%)
  Pallas kernels  17.4 us (11%)
  local copies, waits for them, and re-layouts  3.14 us (2%)
    all_to_all x4, blocking collectives, exchange(): return lax.all_to_all(values, axes, split_axis=0, concat_axis=0, tiled=True)  47 us
    ppermute x3, starting transfers between devices, local(): lax.ppermute(near, 'zh', [(i, i ^ flip) for i in range(4)])  18.7 us
    all_to_all x3, starting transfers between devices, exchange(): return lax.all_to_all(values, axes, split_axis=0, concat_axis=0, tiled=True)  11.2 us
    ppermute x1, starting transfers between devices, local(): got_cross = lax.ppermute(got, 'c', cores)  8.88 us
    ppermute x3, waiting for transfers between devices, local(): lax.ppermute(near, 'zh', [(i, i ^ flip) for i in range(4)])  7.21 us
    ppermute x1, waiting for transfers between devices, local(): other = lax.ppermute(own, 'xl', [(0, 1), (1, 0)])  6.48 us
    all_to_all x3, waiting for transfers between devices, exchange(): return lax.all_to_all(values, axes, split_axis=0, concat_axis=0, tiled=True)  5.87 us
    ppermute x1, starting transfers between devices, local(): lax.ppermute(conv2_weight, ('xh', 'xl'), [(0, 3), (3, 0), (1, 2), (2, 1)])  5.35 us
  transfers between devices with their start and end apart: 12, of which 7 were waited for; matrix products, arithmetic and copies ran while one was open for 1% of the time, Pallas kernels for 3%

profile of v9, /device:TPU:1, one launch (start us, length us, event | category | flops | bytes accessed | tf_op | source)
XLA Modules:
  0.0 152.6 jit_solution(5039468684158258247)
XLA Ops:
  0.6 0.0 copy-start
  0.7 5.3 %collective-permute-start.1 = (bf16[80,1920]{1,0:T(8,128)(2,1)}, bf16[80,1920]{1,0:T(8,128)(2,1)S(1)}, u32[]{:S(2)}, u32[]{:S(2)}) collective-permute-start(bf16[80,1920]{1,0:T(8,128)(2,1)} %own_ref.3), channel_id=1, source_target_pairs={{0,257},{257,0},{1,256},{256,1},{2,259},{259,2},{3,258},{258,3},{4... | collective-permute-start | bytes 921608 | tf_op jit(solution)/shard_map/ppermute | solution.py:331
  6.0 1.7 %mel_payload.1 = bf16[4,26,16,128]{3,2,1,0:T(8,128)(2,1)} custom-call(s32[16]{0:T(128)} %length_ref.1, bf16[16,16,128]{2,1,0:T(8,128)(2,1)} %mel_ref.1), custom_call_target="tpu_custom_call" | custom-call | tf_op jit(solution)/shard_map/mel_payload/pallas_call | solution.py:332
  7.7 4.2 %all-to-all-start = ((bf16[4,26,16,128]{3,2,1,0:T(8,128)(2,1)}), bf16[4,26,16,128]{3,2,1,0:T(8,128)(2,1)S(1)}, u32[]{:S(2)}, u32[]{:S(2)}) async-start(bf16[4,26,16,128]{3,2,1,0:T(8,128)(2,1)} %mel_payload.1), calls=%async_computation | async-start | bytes 851968 | tf_op jit(solution)/shard_map/all_to_all | solution.py:293
  11.9 0.1 pad_add_fusion.where_ref
  11.9 4.8 %collective-permute-start = (bf16[80,1920]{1,0:T(8,128)(2,1)}, bf16[80,1920]{1,0:T(8,128)(2,1)S(1)}, u32[]{:S(2)}, u32[]{:S(2)}) collective-permute-start(bf16[80,1920]{1,0:T(8,128)(2,1)} %own_ref.3), channel_id=1, source_target_pairs={{0,32},{32,0},{1,33},{33,1},{2,34},{34,2},{3,35},{35,3},{4,36},{36... | collective-permute-start | bytes 921608 | tf_op jit(solution)/shard_map/ppermute | solution.py:361
  16.7 3.0 %collective-permute-start.2 = (bf16[80,1920]{1,0:T(8,128)(2,1)S(1)}, bf16[80,1920]{1,0:T(8,128)(2,1)S(1)}, u32[]{:S(2)}, u32[]{:S(2)}) collective-permute-start(bf16[80,1920]{1,0:T(8,128)(2,1)S(1)} %collective-permute-done.1.far_ref), channel_id=1, source_target_pairs={{0,32},{32,0},{1,33},{33,1},{2,34},{34,2},{3,35},{35,3},{4,36},{36... | collective-permute-start | bytes 921608 | tf_op jit(solution)/shard_map/ppermute | solution.py:363
  19.8 1.4 conv1_columns.1
  21.1 0.0 copy-start.5
  21.2 0.0 copy-start.1
  21.2 0.0 copy-start.11
  21.2 0.0 copy-start.12
  21.2 0.0 copy-start.10
  21.2 3.4 %stem_forward.1 = bf16[4,128,640]{2,1,0:T(8,128)(2,1)} custom-call(bf16[4,26,16,128]{3,2,1,0:T(8,128)(2,1)S(1)} %all-to-all-done.pay_ref, bf16[384,384]{1,0:T(8,128)(2,1)S(1)} %get-tuple-element.26.w1_ref, f32[1,384]{1,0:T(1,128)S(1)} %get-tuple-element.27.b1_ref, bf16[80,1920]{1,0:T(8,128)(2,1)S(1)} %copy-done, ...), custom_call_target="tpu_custom_call" | custom-call | tf_op jit(solution)/shard_map/stem_forward/pallas_call | solution.py:371
  24.6 3.5 %all-to-all-start.1 = ((bf16[4,128,640]{2,1,0:T(8,128)(2,1)}), bf16[4,128,640]{2,1,0:T(8,128)(2,1)S(1)}, u32[]{:S(2)}, u32[]{:S(2)}) async-start(bf16[4,128,640]{2,1,0:T(8,128)(2,1)} %stem_forward.1), calls=%async_computation.1 | async-start | bytes 1310720 | tf_op jit(solution)/shard_map/all_to_all | solution.py:293
  28.1 0.1 broadcast_in_dim.19
  28.2 0.1 broadcast_in_dim_reshape.11.owner_row_ref
  28.3 0.1 broadcast_in_dim_reshape.13.owner_col_ref
  28.4 0.1 broadcast_in_dim.18
  28.5 0.7 broadcast_in_dim_reshape.12.length_ref
  29.2 1.0 copy-done.6
  30.1 2.2 %stem_slopes.1 = (bf16[512,512]{1,0:T(8,128)(2,1)}, f32[2,512,384]{2,1,0:T(8,128)S(1)}, bf16[3,384,512]{2,1,0:T(8,128)(2,1)S(1)}) custom-call(bf16[4,26,16,128]{3,2,1,0:T(8,128)(2,1)S(1)} %all-to-all-done.pay_ref, bf16[384,384]{1,0:T(8,128)(2,1)S(1)} %copy-done.6, f32[1,384]{1,0:T(1,128)S(1)} %get-tuple-element.27.b1_ref), custom_call_target="tpu_custom_call" | custom-call | tf_op jit(solution)/shard_map/stem_slopes/pallas_call | solution.py:387
  32.3 1.0 copy-done.7
  33.3 4.7 %all-to-all-done.1.part_ref = bf16[4,128,640]{2,1,0:T(8,128)(2,1)S(1)} async-done(((bf16[4,128,640]{2,1,0:T(8,128)(2,1)}), bf16[4,128,640]{2,1,0:T(8,128)(2,1)S(1)}, u32[]{:S(2)}, u32[]{:S(2)}) %all-to-all-start.1) | async-done | bytes 655392 | tf_op jit(solution)/shard_map/all_to_all | solution.py:293
  38.0 2.2 %stem_middle.1 = (bf16[4,128,640]{2,1,0:T(8,128)(2,1)}, bf16[8,80,128]{2,1,0:T(8,128)(2,1)S(1)}, bf16[8,80,128]{2,1,0:T(8,128)(2,1)S(1)}) custom-call(s32[4]{0:T(128)S(1)} %pad_add_fusion.where_ref, bf16[4,128,640]{2,1,0:T(8,128)(2,1)S(1)} %all-to-all-done.1.part_ref, bf16[128,640]{1,0:T(8,128)(2,1)} %bitcast.15, f32[1,640]{1,0:T(1,128)S(1)} %broadcast_in_dim.17.b2_ref, ...), custom_call_target="tpu_custom_call" | custom-call | tf_op jit(solution)/shard_map/stem_middle/pallas_call | solution.py:403
  40.2 12.1 %all_to_all.35.grad_ref = bf16[4,128,640]{2,1,0:T(8,128)(2,1)S(1)} all-to-all(bf16[4,128,640]{2,1,0:T(8,128)(2,1)} %get-tuple-element.33), channel_id=1, replica_groups=mesh['xh'=2,'y'=4,'c'=2,'zh'=4,'zl'=4,'xl'=2] {'y'}, dimensions={0} | all-to-all | bytes 1310720 | tf_op jit(solution)/shard_map/all_to_all | solution.py:293
  52.4 3.4 %stem_backward.1 = (f32[2,2,896,128]{3,2,1,0:T(8,128)S(1)}, bf16[2,2,896,128]{3,2,1,0:T(8,128)(2,1)S(1)}) custom-call(s32[4]{0:T(128)S(1)} %pad_add_fusion.where_ref, bf16[4,128,640]{2,1,0:T(8,128)(2,1)S(1)} %all_to_all.35.grad_ref, bf16[80,1920]{1,0:T(8,128)(2,1)S(1)} %copy-done, bf16[80,1920]{1,0:T(8,128)(2,1)S(1)} %copy-done.2, ...), custom_call_target="tpu_custom_call" | custom-call | tf_op jit(solution)/shard_map/stem_backward/pallas_call | solution.py:421
  55.8 5.1 %collective-permute-start.3 = (bf16[2,2,896,128]{3,2,1,0:T(8,128)(2,1)S(1)}, bf16[2,2,896,128]{3,2,1,0:T(8,128)(2,1)S(1)}, u32[]{:S(2)}, u32[]{:S(2)}) collective-permute-start(bf16[2,2,896,128]{3,2,1,0:T(8,128)(2,1)S(1)} %get-tuple-element.38), channel_id=1, source_target_pairs={{0,32},{32,0},{1,33},{33,1},{2,34},{34,2},{3,35},{35,3},{4,36},{36... | collective-permute-start | bytes 2752520 | tf_op jit(solution)/shard_map/ppermute | solution.py:441
  60.9 2.1 %collective-permute-done.3 = bf16[2,2,896,128]{3,2,1,0:T(8,128)(2,1)S(1)} collective-permute-done((bf16[2,2,896,128]{3,2,1,0:T(8,128)(2,1)S(1)}, bf16[2,2,896,128]{3,2,1,0:T(8,128)(2,1)S(1)}, u32[]{:S(2)}, u32[]{:S(2)}) %collective-permute-start.3) | collective-permute-done | bytes 917536 | tf_op jit(solution)/shard_map/ppermute | solution.py:441
  63.0 0.2 add_convert_fusion
  63.2 16.9 %all_to_all.36.got_ref = bf16[4,896,128]{2,1,0:T(8,128)(2,1)S(1)} all-to-all(bf16[4,896,128]{2,1,0:T(8,128)(2,1)S(1)} %bitcast.11), channel_id=1, replica_groups=mesh['xh'=2,'y'=4,'c'=2,'zh'=4,'zl'=4,'xl'=2] {'xh','xl'}, dimensions={0} | all-to-all | bytes 1835008 | tf_op jit(solution)/shard_map/all_to_all | solution.py:293
  80.0 0.1 gradient_sum.2
  80.2 9.0 %all_to_all.37.got_ref = bf16[4,224,128]{2,1,0:T(8,128)(2,1)S(1)} all-to-all(bf16[4,224,128]{2,1,0:T(8,128)(2,1)S(1)} %bitcast.10), channel_id=1, replica_groups=mesh['xh'=2,'y'=4,'c'=2,'zh'=4,'zl'=4,'xl'=2] {'zl'}, dimensions={0} | all-to-all | bytes 458752 | tf_op jit(solution)/shard_map/all_to_all | solution.py:293
  89.2 12.7 %collective-permute-start.6 = (bf16[224,128]{1,0:T(8,128)(2,1)S(1)}, bf16[224,128]{1,0:T(8,128)(2,1)S(1)}, u32[]{:S(2)}, u32[]{:S(2)}) collective-permute-start(bf16[224,128]{1,0:T(8,128)(2,1)S(1)} %gradient_sum.3.own_ref), channel_id=1, source_target_pairs={{0,16},{8,24},{16,0},{24,8},{1,17},{9,25},{17,1},{25,9},{2,18},{10... | collective-permute-start | bytes 172040 | tf_op jit(solution)/shard_map/ppermute | solution.py:457
  102.0 3.1 %collective-permute-start.5 = (bf16[224,128]{1,0:T(8,128)(2,1)S(1)}, bf16[224,128]{1,0:T(8,128)(2,1)S(1)}, u32[]{:S(2)}, u32[]{:S(2)}) collective-permute-start(bf16[224,128]{1,0:T(8,128)(2,1)S(1)} %gradient_sum.3.own_ref), channel_id=1, source_target_pairs={{0,24},{8,16},{16,8},{24,0},{1,25},{9,17},{17,9},{25,1},{2,26},{10... | collective-permute-start | bytes 172040 | tf_op jit(solution)/shard_map/ppermute | solution.py:457
  105.1 2.9 %collective-permute-start.4 = (bf16[224,128]{1,0:T(8,128)(2,1)S(1)}, bf16[224,128]{1,0:T(8,128)(2,1)S(1)}, u32[]{:S(2)}, u32[]{:S(2)}) collective-permute-start(bf16[224,128]{1,0:T(8,128)(2,1)S(1)} %gradient_sum.3.own_ref), channel_id=1, source_target_pairs={{0,8},{8,0},{16,24},{24,16},{1,9},{9,1},{17,25},{25,17},{2,10},{10... | collective-permute-start | bytes 172040 | tf_op jit(solution)/shard_map/ppermute | solution.py:457
  108.0 5.5 %collective-permute-done.5.both_ref = bf16[224,128]{1,0:T(8,128)(2,1)S(1)} collective-permute-done((bf16[224,128]{1,0:T(8,128)(2,1)S(1)}, bf16[224,128]{1,0:T(8,128)(2,1)S(1)}, u32[]{:S(2)}, u32[]{:S(2)}) %collective-permute-start.5) | collective-permute-done | bytes 57376 | tf_op jit(solution)/shard_map/ppermute | solution.py:457
  113.5 1.7 %collective-permute-done.4.near_ref = bf16[224,128]{1,0:T(8,128)(2,1)S(1)} collective-permute-done((bf16[224,128]{1,0:T(8,128)(2,1)S(1)}, bf16[224,128]{1,0:T(8,128)(2,1)S(1)}, u32[]{:S(2)}, u32[]{:S(2)}) %collective-permute-start.4) | collective-permute-done | bytes 57376 | tf_op jit(solution)/shard_map/ppermute | solution.py:457
  115.2 9.0 %all_to_all.38 = bf16[4,224,128]{2,1,0:T(8,128)(2,1)S(1)} all-to-all(bf16[4,224,128]{2,1,0:T(8,128)(2,1)S(1)} %gradient_pairs.1), channel_id=1, replica_groups=mesh['xh'=2,'y'=4,'c'=2,'zh'=4,'zl'=4,'xl'=2] {'zl'}, dimensions={0} | all-to-all | bytes 458752 | tf_op jit(solution)/shard_map/all_to_all | solution.py:293
  124.2 0.1 broadcast_in_dim.20
  124.3 1.0 pad_maximum_fusion
  125.2 3.6 %all-to-all-start.6 = ((bf16[8,416,128]{2,1,0:T(8,128)(2,1)}), bf16[8,416,128]{2,1,0:T(8,128)(2,1)S(1)}, u32[]{:S(2)}, u32[]{:S(2)}) async-start(bf16[8,416,128]{2,1,0:T(8,128)(2,1)} %pad_maximum_fusion), calls=%async_computation.6 | async-start | bytes 1703936 | tf_op jit(solution)/shard_map/all_to_all | solution.py:293
  128.8 2.2 %collective-permute-start.7 = (bf16[640,128]{1,0:T(8,128)(2,1)S(1)}, bf16[640,128]{1,0:T(8,128)(2,1)S(1)}, u32[]{:S(2)}, u32[]{:S(2)}) collective-permute-start(bf16[640,128]{1,0:T(8,128)(2,1)S(1)} %slice.20.own_ref), channel_id=1, source_target_pairs={{0,1},{1,0},{2,3},{3,2},{4,5},{5,4},{6,7},{7,6},{8,9},{9,8},{10,11... | collective-permute-start | bytes 491528 | tf_op jit(solution)/shard_map/ppermute | solution.py:468
  131.0 6.5 %collective-permute-done.7.other_ref = bf16[640,128]{1,0:T(8,128)(2,1)S(1)} collective-permute-done((bf16[640,128]{1,0:T(8,128)(2,1)S(1)}, bf16[640,128]{1,0:T(8,128)(2,1)S(1)}, u32[]{:S(2)}, u32[]{:S(2)}) %collective-permute-start.7) | collective-permute-done | bytes 163872 | tf_op jit(solution)/shard_map/ppermute | solution.py:468
  137.5 1.2 all-to-all-done.6.got_ref
  138.7 8.9 %collective-permute-start.8 = (bf16[8,416,128]{2,1,0:T(8,128)(2,1)S(1)}, bf16[8,416,128]{2,1,0:T(8,128)(2,1)S(1)}, u32[]{:S(2)}, u32[]{:S(2)}) collective-permute-start(bf16[8,416,128]{2,1,0:T(8,128)(2,1)S(1)} %all-to-all-done.6.got_ref), channel_id=1, source_target_pairs={{0,32},{32,0},{1,33},{33,1},{2,34},{34,2},{3,35},{35,3},{4,36},{36... | collective-permute-start | bytes 2555912 | tf_op jit(solution)/shard_map/ppermute | solution.py:472
  147.6 2.0 %collective-permute-done.8.cross_ref = bf16[8,416,128]{2,1,0:T(8,128)(2,1)S(1)} collective-permute-done((bf16[8,416,128]{2,1,0:T(8,128)(2,1)S(1)}, bf16[8,416,128]{2,1,0:T(8,128)(2,1)S(1)}, u32[]{:S(2)}, u32[]{:S(2)}) %collective-permute-start.8) | collective-permute-done | bytes 852000 | tf_op jit(solution)/shard_map/ppermute | solution.py:472
  149.6 3.0 %gradient_unpack.1 = (f32[384,1280]{1,0:T(8,128)}, f32[1280]{0:T(1024)}, f32[640]{0:T(1024)}, f32[80,1920]{1,0:T(8,128)}, bf16[256,640]{1,0:T(8,128)(2,1)}) custom-call(s32[4]{0:T(128)S(1)} %pad_add_fusion.where_ref, bf16[8,416,128]{2,1,0:T(8,128)(2,1)S(1)} %all-to-all-done.6.got_ref, bf16[8,416,128]{2,1,0:T(8,128)(2,1)S(1)} %collective-permute-done.8.cross_ref, ...), custom_call_target="tpu_custom_call" | custom-call | tf_op jit(solution)/shard_map/gradient_unpack/pallas_call | solution.py:473
  (31 shorter events, 0.1 us)
Async XLA Ops:
  0.6 20.6 %copy-start = (bf16[80,1920]{1,0:T(8,128)(2,1)S(1)}, bf16[80,1920]{1,0:T(8,128)(2,1)}, u32[]{:S(2)}) copy-start(bf16[80,1920]{1,0:T(8,128)(2,1)} %own_ref.3) | copy-start | bytes 921604
  0.6 19.1 %copy-start.9 = (bf16[384,1280]{1,0:T(8,128)(2,1)S(1)}, bf16[384,1280]{1,0:T(8,128)(2,1)}, u32[]{:S(2)}) copy-start(bf16[384,1280]{1,0:T(8,128)(2,1)} %weight_ref.1) | copy-start | bytes 2949124
  0.7 16.1 %collective-permute-start.1 = (bf16[80,1920]{1,0:T(8,128)(2,1)}, bf16[80,1920]{1,0:T(8,128)(2,1)S(1)}, u32[]{:S(2)}, u32[]{:S(2)}) collective-permute-start(bf16[80,1920]{1,0:T(8,128)(2,1)} %own_ref.3), channel_id=1, source_target_pairs={{0,257},{257,0},{1,256},{256,1},{2,259},{259,2},{3,258},{258,3},{4... | collective-permute-start | bytes 921608 | tf_op jit(solution)/shard_map/ppermute | solution.py:331
  7.7 13.5 %all-to-all-start = ((bf16[4,26,16,128]{3,2,1,0:T(8,128)(2,1)}), bf16[4,26,16,128]{3,2,1,0:T(8,128)(2,1)S(1)}, u32[]{:S(2)}, u32[]{:S(2)}) async-start(bf16[4,26,16,128]{3,2,1,0:T(8,128)(2,1)} %mel_payload.1), calls=%async_computation | async-start | bytes 851968 | tf_op jit(solution)/shard_map/all_to_all | solution.py:293
  11.9 9.2 %collective-permute-start = (bf16[80,1920]{1,0:T(8,128)(2,1)}, bf16[80,1920]{1,0:T(8,128)(2,1)S(1)}, u32[]{:S(2)}, u32[]{:S(2)}) collective-permute-start(bf16[80,1920]{1,0:T(8,128)(2,1)} %own_ref.3), channel_id=1, source_target_pairs={{0,32},{32,0},{1,33},{33,1},{2,34},{34,2},{3,35},{35,3},{4,36},{36... | collective-permute-start | bytes 921608 | tf_op jit(solution)/shard_map/ppermute | solution.py:361
  16.7 4.4 %collective-permute-start.2 = (bf16[80,1920]{1,0:T(8,128)(2,1)S(1)}, bf16[80,1920]{1,0:T(8,128)(2,1)S(1)}, u32[]{:S(2)}, u32[]{:S(2)}) collective-permute-start(bf16[80,1920]{1,0:T(8,128)(2,1)S(1)} %collective-permute-done.1.far_ref), channel_id=1, source_target_pairs={{0,32},{32,0},{1,33},{33,1},{2,34},{34,2},{3,35},{35,3},{4,36},{36... | collective-permute-start | bytes 921608 | tf_op jit(solution)/shard_map/ppermute | solution.py:363
  21.1 3.5 %copy-start.5 = (bf16[384,384]{1,0:T(8,128)(2,1)}, bf16[384,384]{1,0:T(8,128)(2,1)S(1)}, u32[]{:S(2)}) copy-start(bf16[384,384]{1,0:T(8,128)(2,1)S(1)} %get-tuple-element.26.w1_ref) | copy-start | bytes 884740
  21.2 3.5 %copy-start.1 = (bf16[80,1920]{1,0:T(8,128)(2,1)}, bf16[80,1920]{1,0:T(8,128)(2,1)S(1)}, u32[]{:S(2)}) copy-start(bf16[80,1920]{1,0:T(8,128)(2,1)S(1)} %collective-permute-done.side_ref) | copy-start | bytes 921604
  21.2 3.4 %copy-start.3 = (bf16[80,1920]{1,0:T(8,128)(2,1)}, bf16[80,1920]{1,0:T(8,128)(2,1)S(1)}, u32[]{:S(2)}) copy-start(bf16[80,1920]{1,0:T(8,128)(2,1)S(1)} %collective-permute-done.2.both_ref) | copy-start | bytes 921604
  21.2 6.9 %copy-start.11 = (s32[16]{0:T(128)S(1)}, s32[16]{0:T(128)}, u32[]{:S(2)}) copy-start(s32[16]{0:T(128)} %length_ref.1) | copy-start | bytes 196
  21.2 6.9 %copy-start.12 = (s32[16,1]{0,1:T(1,128)S(1)}, s32[16,1]{0,1:T(1,128)}, u32[]{:S(2)}) copy-start(s32[16,1]{0,1:T(1,128)} %param.10) | copy-start | bytes 196
  21.2 7.2 %copy-start.10 = (f32[640]{0:T(1024)S(1)}, f32[640]{0:T(1024)}, u32[]{:S(2)}) copy-start(f32[640]{0:T(1024)} %param.14) | copy-start | bytes 7684
  24.6 13.4 %all-to-all-start.1 = ((bf16[4,128,640]{2,1,0:T(8,128)(2,1)}), bf16[4,128,640]{2,1,0:T(8,128)(2,1)S(1)}, u32[]{:S(2)}, u32[]{:S(2)}) async-start(bf16[4,128,640]{2,1,0:T(8,128)(2,1)} %stem_forward.1), calls=%async_computation.1 | async-start | bytes 1310720 | tf_op jit(solution)/shard_map/all_to_all | solution.py:293
  29.2 1.0 copy-start.6
  32.3 1.0 copy-start.7
  33.3 19.0 %copy-start.2 = (bf16[80,1920]{1,0:T(8,128)(2,1)S(1)}, bf16[80,1920]{1,0:T(8,128)(2,1)}, u32[]{:S(2)}) copy-start(bf16[80,1920]{1,0:T(8,128)(2,1)} %copy-done.1) | copy-start | bytes 921604
  38.0 14.4 %copy-start.4 = (bf16[80,1920]{1,0:T(8,128)(2,1)S(1)}, bf16[80,1920]{1,0:T(8,128)(2,1)}, u32[]{:S(2)}) copy-start(bf16[80,1920]{1,0:T(8,128)(2,1)} %copy-done.3) | copy-start | bytes 921604
  38.0 14.4 %copy-start.8 = (bf16[3,384,512]{2,1,0:T(8,128)(2,1)S(1)}, bf16[3,384,512]{2,1,0:T(8,128)(2,1)}, u32[]{:S(2)}) copy-start(bf16[3,384,512]{2,1,0:T(8,128)(2,1)} %copy-done.7) | copy-start | bytes 3538948
  55.8 7.2 %collective-permute-start.3 = (bf16[2,2,896,128]{3,2,1,0:T(8,128)(2,1)S(1)}, bf16[2,2,896,128]{3,2,1,0:T(8,128)(2,1)S(1)}, u32[]{:S(2)}, u32[]{:S(2)}) collective-permute-start(bf16[2,2,896,128]{3,2,1,0:T(8,128)(2,1)S(1)} %get-tuple-element.38), channel_id=1, source_target_pairs={{0,32},{32,0},{1,33},{33,1},{2,34},{34,2},{3,35},{35,3},{4,36},{36... | collective-permute-start | bytes 2752520 | tf_op jit(solution)/shard_map/ppermute | solution.py:441
  89.2 18.7 %collective-permute-start.6 = (bf16[224,128]{1,0:T(8,128)(2,1)S(1)}, bf16[224,128]{1,0:T(8,128)(2,1)S(1)}, u32[]{:S(2)}, u32[]{:S(2)}) collective-permute-start(bf16[224,128]{1,0:T(8,128)(2,1)S(1)} %gradient_sum.3.own_ref), channel_id=1, source_target_pairs={{0,16},{8,24},{16,0},{24,8},{1,17},{9,25},{17,1},{25,9},{2,18},{10... | collective-permute-start | bytes 172040 | tf_op jit(solution)/shard_map/ppermute | solution.py:457
  102.0 11.5 %collective-permute-start.5 = (bf16[224,128]{1,0:T(8,128)(2,1)S(1)}, bf16[224,128]{1,0:T(8,128)(2,1)S(1)}, u32[]{:S(2)}, u32[]{:S(2)}) collective-permute-start(bf16[224,128]{1,0:T(8,128)(2,1)S(1)} %gradient_sum.3.own_ref), channel_id=1, source_target_pairs={{0,24},{8,16},{16,8},{24,0},{1,25},{9,17},{17,9},{25,1},{2,26},{10... | collective-permute-start | bytes 172040 | tf_op jit(solution)/shard_map/ppermute | solution.py:457
  105.1 10.1 %collective-permute-start.4 = (bf16[224,128]{1,0:T(8,128)(2,1)S(1)}, bf16[224,128]{1,0:T(8,128)(2,1)S(1)}, u32[]{:S(2)}, u32[]{:S(2)}) collective-permute-start(bf16[224,128]{1,0:T(8,128)(2,1)S(1)} %gradient_sum.3.own_ref), channel_id=1, source_target_pairs={{0,8},{8,0},{16,24},{24,16},{1,9},{9,1},{17,25},{25,17},{2,10},{10... | collective-permute-start | bytes 172040 | tf_op jit(solution)/shard_map/ppermute | solution.py:457
  125.2 13.5 %all-to-all-start.6 = ((bf16[8,416,128]{2,1,0:T(8,128)(2,1)}), bf16[8,416,128]{2,1,0:T(8,128)(2,1)S(1)}, u32[]{:S(2)}, u32[]{:S(2)}) async-start(bf16[8,416,128]{2,1,0:T(8,128)(2,1)} %pad_maximum_fusion), calls=%async_computation.6 | async-start | bytes 1703936 | tf_op jit(solution)/shard_map/all_to_all | solution.py:293
  128.8 8.7 %collective-permute-start.7 = (bf16[640,128]{1,0:T(8,128)(2,1)S(1)}, bf16[640,128]{1,0:T(8,128)(2,1)S(1)}, u32[]{:S(2)}, u32[]{:S(2)}) collective-permute-start(bf16[640,128]{1,0:T(8,128)(2,1)S(1)} %slice.20.own_ref), channel_id=1, source_target_pairs={{0,1},{1,0},{2,3},{3,2},{4,5},{5,4},{6,7},{7,6},{8,9},{9,8},{10,11... | collective-permute-start | bytes 491528 | tf_op jit(solution)/shard_map/ppermute | solution.py:468
  138.7 10.9 %collective-permute-start.8 = (bf16[8,416,128]{2,1,0:T(8,128)(2,1)S(1)}, bf16[8,416,128]{2,1,0:T(8,128)(2,1)S(1)}, u32[]{:S(2)}, u32[]{:S(2)}) collective-permute-start(bf16[8,416,128]{2,1,0:T(8,128)(2,1)S(1)} %all-to-all-done.6.got_ref), channel_id=1, source_target_pairs={{0,32},{32,0},{1,33},{33,1},{2,34},{34,2},{3,35},{35,3},{4,36},{36... | collective-permute-start | bytes 2555912 | tf_op jit(solution)/shard_map/ppermute | solution.py:472

commit v10 on v9

--- a/solution.py
+++ b/solution.py
@@ -70,21 +70,34 @@
     return lax.dot_general(left, right, (((0,), (0,)), ((), ())), preferred_element_type=F32)
 
 
-def stack_weights(refs, w2_ref):
-    for block, ref in enumerate(refs):
-        w2_ref[block * ROWS : (block + 1) * ROWS, :] = ref[...]
-    w2_ref[BLOCKS * ROWS :, :] = jnp.zeros((WIDE - BLOCKS * ROWS, 3 * D2), BF16)
-
-
-def prepare_kernel(length_ref, mel_ref, pay_ref):
+def weight_copies(refs, w2_ref, done):
+    return [
+        pltpu.make_async_copy(ref, w2_ref.at[block * ROWS : (block + 1) * ROWS], done.at[block])
+        for block, ref in enumerate(refs)
+    ]
+
+
+def prepare_kernel(length_ref, mel_ref, pay_ref, length_here, mel_done, length_done):
+    mel_copies = [
+        pltpu.make_async_copy(mel_ref, pay_ref.at[target, :CLIPS], mel_done.at[target]) for target in range(HOLDERS)
+    ]
+    for copy in mel_copies:
+        copy.start()
     clip = lax.broadcasted_iota(jnp.int32, (CLIPS, MEL), 0)
     length = jnp.zeros((CLIPS, MEL), F32)
     for index in range(CLIPS):
         length = jnp.where(clip == index, length_ref[index].astype(F32), length)
-    for target in range(HOLDERS):
-        pay_ref[target, :CLIPS] = mel_ref[...]
-        pay_ref[target, CLIPS] = length.astype(BF16)
-        pay_ref[target, CLIPS + 1 :] = jnp.zeros((PAY - CLIPS - 1, 2 * HALF, MEL), BF16)
+    slots = length_here.shape[0]
+    for slot in range(slots):
+        length_here[slot] = length.astype(BF16)
+    length_copies = [
+        pltpu.make_async_copy(length_here, pay_ref.at[target, CLIPS:], length_done.at[target])
+        for target in range(HOLDERS)
+    ]
+    for copy in length_copies:
+        copy.start()
+    for copy in mel_copies + length_copies:
+        copy.wait()
 
 
 def columns_kernel(where_ref, weight_ref, bias_ref, w1_ref, b1_ref, picked):
@@ -130,13 +143,23 @@
 
 
 def forward_kernel(
-    pay_ref, w1_ref, b1_ref, own_ref, side_ref, far_ref, both_ref, part_ref, w2_ref, cols_ref, frames_ref
+    pay_ref, w1_ref, b1_ref, own_ref, side_ref, far_ref, both_ref, part_ref, w2_ref, cols_ref, frames_ref, done
 ):
+    copies = weight_copies((own_ref, side_ref, far_ref, both_ref), w2_ref, done)
+
     @pl.when(pl.program_id(0) == 0)
     def _():
-        stack_weights((own_ref, side_ref, far_ref, both_ref), w2_ref)
+        for copy in copies:
+            copy.start()
+        w2_ref[BLOCKS * ROWS :, :] = jnp.zeros((WIDE - BLOCKS * ROWS, 3 * D2), BF16)
 
     pre_even, pre_odd, live_even, live_odd = first_conv(pay_ref, w1_ref, b1_ref, cols_ref, frames_ref)
+
+    @pl.when(pl.program_id(0) == 0)
+    def _():
+        for copy in copies:
+            copy.wait()
+
     odd = jnp.where(live_odd, gelu_value(pre_odd), 0.0)
     total = dot(odd.astype(BF16), w2_ref[:, 2 * D2 :]) + dot(shift_down(odd).astype(BF16), w2_ref[:, :D2])
     even = jnp.where(live_even, gelu_value(pre_even), 0.0)
@@ -144,7 +167,10 @@
     part_ref[...] = total.astype(BF16).reshape(part_ref.shape)
 
 
-def slope_kernel(pay_ref, w1_ref, b1_ref, cols_ref, slope_ref, turned_ref, frames_ref):
+def slope_kernel(
+    pay_ref, w1_ref, b1_ref, grad_ref, column_ref, row_ref,
+    cols_ref, slope_ref, turned_ref, live_grad_ref, wanted_ref, frames_ref,
+):
     pre_even, pre_odd, live_even, live_odd = first_conv(pay_ref, w1_ref, b1_ref, cols_ref, frames_ref)
     value, slope = gelu_both(pre_odd)
     odd = jnp.where(live_odd, value, 0.0)
@@ -155,30 +181,39 @@
     slope_ref[0] = jnp.where(live_even, slope, 0.0)
     turned_ref[1] = jnp.where(live_even, value, 0.0).astype(BF16).T
 
+    @pl.when(pl.program_id(0) == 0)
+    def _():
+        t = (lax.broadcasted_iota(jnp.int32, (STEPS, 1), 0) & (HALF - 1)).astype(F32)
+        length = (column_ref[...] & 31).astype(F32)
+        live_grad_ref[...] = jnp.where(2.0 * t < length, grad_ref[...].astype(F32), 0.0).astype(BF16)
+        here = lax.broadcasted_iota(jnp.int32, (STEPS, STEPS), 0)
+        there = lax.broadcasted_iota(jnp.int32, (STEPS, STEPS), 1)
+        owner = row_ref[...] >> 5
+        same = ((column_ref[...] >> 5) == owner) & ((here >> 3) < (there >> 3))
+        same = same & ((here & (HALF - 1)) == 0)
+        rank = jnp.sum(jnp.where(same, 1.0, 0.0), axis=0, keepdims=True)
+        place = lax.broadcasted_iota(jnp.int32, (1, STEPS), 1) & (HALF - 1)
+        place = (owner * 2 + rank.astype(jnp.int32)) * HALF + place
+        wanted = lax.broadcasted_iota(jnp.int32, (SLOTS * HALF, STEPS), 0) == place
+        t = (lax.broadcasted_iota(jnp.int32, (1, STEPS), 1) & (HALF - 1)).astype(F32)
+        wanted = wanted & (2.0 * t < (row_ref[...] & 31).astype(F32))
+        wanted_ref[...] = jnp.where(wanted, 1.0, 0.0).astype(BF16)
+
 
 def middle_kernel(
-    where_ref, part_ref, grad_ref, b2_ref, length_ref, owner_col_ref, owner_row_ref, rep_ref, same_ref, cross_ref
+    where_ref, part_ref, b2_ref, live_grad_ref, wanted_ref, rep_ref, same_ref, cross_ref, live_grad_here, done
 ):
+    copy = pltpu.make_async_copy(live_grad_ref, live_grad_here, done)
+    copy.start()
     pre = part_ref[0].astype(F32)
     for source in range(1, HOLDERS):
         pre = pre + part_ref[source].astype(F32)
-    pre = pre + b2_ref[...]
-    t = (lax.broadcasted_iota(jnp.int32, (STEPS, 1), 0) & (HALF - 1)).astype(F32)
-    live = jnp.where(2.0 * t < length_ref[...], 1.0, 0.0)
-    value, slope = gelu_both(pre)
-    features = (value * live).astype(BF16)
-    second_grad = (grad_ref[...].astype(F32) * slope * live).astype(BF16)
+    value, slope = gelu_both(pre + b2_ref[...])
+    copy.wait()
+    second_grad = (live_grad_here[...].astype(F32) * slope).astype(BF16)
     for target in range(HOLDERS):
         rep_ref[target] = second_grad
-    here = lax.broadcasted_iota(jnp.int32, (STEPS, STEPS), 0)
-    there = lax.broadcasted_iota(jnp.int32, (STEPS, STEPS), 1)
-    same = (owner_col_ref[...] == owner_row_ref[...]) & ((here >> 3) < (there >> 3))
-    same = same & ((here & (HALF - 1)) == 0)
-    rank = jnp.sum(jnp.where(same, 1.0, 0.0), axis=0, keepdims=True)
-    place = lax.broadcasted_iota(jnp.int32, (1, STEPS), 1) & (HALF - 1)
-    place = (owner_row_ref[...] * 2 + rank.astype(jnp.int32)) * HALF + place
-    wanted = lax.broadcasted_iota(jnp.int32, (SLOTS * HALF, STEPS), 0) == place
-    placed = dot(jnp.where(wanted, 1.0, 0.0).astype(BF16), features)
+    placed = dot(wanted_ref[...], value.astype(BF16))
     first = where_ref[2] == 0
     for chip in range(CHIPS):
         for tile in range(D2 // LANES):
@@ -191,11 +226,13 @@
 
 def backward_kernel(
     where_ref, grad_ref, own_ref, side_ref, far_ref, both_ref, cols_ref, turned_ref, slope_ref, keep_ref, send_ref,
-    w2_ref, conv_sum, cols_here, cols_done,
+    w2_ref, conv_sum, cols_here, weights_done, cols_done,
 ):
-    cols_copy = pltpu.make_async_copy(cols_ref, cols_here, cols_done)
-    cols_copy.start()
-    stack_weights((own_ref, side_ref, far_ref, both_ref), w2_ref)
+    copies = weight_copies((own_ref, side_ref, far_ref, both_ref), w2_ref, weights_done)
+    copies.append(pltpu.make_async_copy(cols_ref, cols_here, cols_done))
+    for copy in copies:
+        copy.start()
+    w2_ref[BLOCKS * ROWS :, :] = jnp.zeros((WIDE - BLOCKS * ROWS, 3 * D2), BF16)
     mine = where_ref[0]
     grad = grad_ref[...].reshape(HOLDERS * STEPS, D2)
     places = []
@@ -210,11 +247,12 @@
                 piece = conv_sum[first : first + ROWS, column * LANES : (column + 1) * LANES]
                 out[target, tile // 8, (tile % 8) * ROWS : (tile % 8 + 1) * ROWS, :] = piece.astype(out.dtype)
 
+    for copy in copies:
+        copy.wait()
     even = dot_nt(grad, w2_ref[:, D2 : 2 * D2])
     even = (even * slope_ref[0]).astype(BF16)
     odd = dot_nt(grad, w2_ref[:, 2 * D2 :]) + shift_up(dot_nt(grad, w2_ref[:, :D2]))
     odd = (odd * slope_ref[1]).astype(BF16)
-    cols_copy.wait()
     cols = cols_here[...]
     conv_sum[:, : 3 * LANES] = dot_tn(even, cols[:, : 3 * LANES]) + dot_tn(odd, cols[:, LANES:])
     bias1 = jnp.sum(even.astype(F32) + odd.astype(F32), axis=0, keepdims=True)
@@ -253,8 +291,7 @@
 
 
 def last_kernel(
-    where_ref, got_ref, cross_ref, own_ref, other_ref, weight_ref, bias1_ref, bias2_ref, conv2_ref, packed_ref,
-    whole, biases,
+    where_ref, got_ref, cross_ref, weight_ref, bias1_ref, bias2_ref, packed_ref, whole, biases,
 ):
     step, core = pl.program_id(0), where_ref[2]
     rows = pl.ds(pl.multiple_of((step + 1) * ROWS, 16), ROWS)
@@ -280,13 +317,16 @@
         bias1_ref[...] = bias1.reshape(16 * ROWS)
         bias2 = jnp.concatenate([biases[0, 1 + tile : 2 + tile, :] for tile in range(D2 // LANES)], axis=1)
         bias2_ref[...] = bias2.reshape(D2)
-        lower = where_ref[1] == 0
-        for tile in range(15):
-            half, spot = tile // 8, tile % 8
-            rows = slice(spot * ROWS, (spot + 1) * ROWS)
-            own, other = own_ref[rows, :].astype(F32), other_ref[rows, :].astype(F32)
-            picked = jnp.where(lower, own, other) if half == 0 else jnp.where(lower, other, own)
-            conv2_ref[:, tile * LANES : (tile + 1) * LANES] = picked
+
+
+def unpack_kernel(where_ref, own_ref, other_ref, conv2_ref):
+    lower = where_ref[1] == 0
+    for tile in range(15):
+        half, spot = tile // 8, tile % 8
+        rows = slice(spot * ROWS, (spot + 1) * ROWS)
+        own, other = own_ref[rows, :].astype(F32), other_ref[rows, :].astype(F32)
+        picked = jnp.where(lower, own, other) if half == 0 else jnp.where(lower, other, own)
+        conv2_ref[:, tile * LANES : (tile + 1) * LANES] = picked
 
 
 def exchange(values, axes):
@@ -320,30 +360,20 @@
 
     pay = pl.pallas_call(
         prepare_kernel,
-        in_specs=[pl.BlockSpec(memory_space=pltpu.SMEM), vmem()],
-        out_specs=vmem(),
+        in_specs=[pl.BlockSpec(memory_space=pltpu.SMEM), pl.BlockSpec(memory_space=pl.ANY)],
+        out_specs=pl.BlockSpec(memory_space=pl.ANY),
         out_shape=in_hbm(HOLDERS, PAY, 2 * HALF, MEL),
+        scratch_shapes=[
+            pltpu.VMEM((PAY - CLIPS, 2 * HALF, MEL), BF16),
+            pltpu.SemaphoreType.DMA((HOLDERS,)),
+            pltpu.SemaphoreType.DMA((HOLDERS,)),
+        ],
         compiler_params=params(60),
         name="mel_payload",
-    )(lengths, mel)
+    )(lengths, from_hbm(mel))
     got_pay = exchange(pay, "y")
     cores = [(0, 1), (1, 0)]
     far_weight = lax.ppermute(conv2_weight, ("xh", "xl"), [(0, 3), (3, 0), (1, 2), (2, 1)])
-    pay = pl.pallas_call(
-        prepare_kernel,
-        in_specs=[pl.BlockSpec(memory_space=pltpu.SMEM), vmem()],
-        out_specs=vmem(),
-        out_shape=in_hbm(HOLDERS, PAY, 2 * HALF, MEL),
-        compiler_params=params(60),
-        name="mel_payload",
-    )(lengths, mel)
-    got_pay = exchange(pay, "y")
-    weights = [
-        conv2_weight,
-        lax.ppermute(conv2_weight, "c", [(0, 1), (1, 0)]),
-        lax.ppermute(conv2_weight, ("xh", "xl"), [(0, 3), (3, 0), (1, 2), (2, 1)]),
-        lax.ppermute(conv2_weight, ("xh", "c", "xl"), [(i, 7 - i) for i in range(8)]),
-    ]
 
     w1, b1 = pl.pallas_call(
         columns_kernel,
@@ -371,59 +401,61 @@
     parts = pl.pallas_call(
         forward_kernel,
         grid=(HOLDERS // 2,),
-        in_specs=[pay_spec, *[vmem()] * (2 + BLOCKS)],
+        in_specs=[pay_spec, vmem(), vmem(), *[pl.BlockSpec(memory_space=pl.ANY)] * BLOCKS],
         out_specs=pl.BlockSpec((2, STEPS, D2), pair),
         out_shape=in_hbm(HOLDERS, STEPS, D2),
         scratch_shapes=[
             pltpu.VMEM((WIDE, 3 * D2), BF16),
             pltpu.VMEM((some, 4 * LANES), BF16),
             pltpu.VMEM(frames, F32),
+            pltpu.SemaphoreType.DMA((BLOCKS,)),
         ],
         compiler_params=params(20, "arbitrary"),
         name="stem_forward",
     )(got_pay, w1, b1, *weights)
 
     got_parts = exchange(parts, "y")
-    cols, slopes, turned = pl.pallas_call(
+    code = jnp.repeat(routes[:, 0] * 32 + lengths, HALF)
+    cols, slopes, turned, live_grad, wanted = pl.pallas_call(
         slope_kernel,
         grid=(HOLDERS // 2,),
-        in_specs=[pay_spec, vmem(), vmem()],
+        in_specs=[pay_spec, *[vmem()] * 5],
         out_specs=[
             pl.BlockSpec((some, 4 * LANES), lambda i: (i, 0)),
             pl.BlockSpec((2, some, WIDE), lambda i: (0, i, 0)),
             pl.BlockSpec((3, WIDE, some), lambda i: (0, 0, i)),
-        ],
-        out_shape=[in_hbm(rows, 4 * LANES), shape(2, rows, WIDE, dtype=F32), shape(3, WIDE, rows)],
+            vmem(),
+            vmem(),
+        ],
+        out_shape=[
+            in_hbm(rows, 4 * LANES),
+            shape(2, rows, WIDE, dtype=F32),
+            shape(3, WIDE, rows),
+            in_hbm(STEPS, D2),
+            shape(SLOTS * HALF, STEPS),
+        ],
         scratch_shapes=[pltpu.VMEM(frames, F32)],
         compiler_params=params(20, "arbitrary"),
         name="stem_slopes",
-    )(got_pay, w1, b1)
+    )(got_pay, w1, b1, from_hbm(out_grad.reshape(STEPS, D2)), code[:, None], code[None])
     got_parts, slopes, turned = lax.optimization_barrier((got_parts, slopes, turned))
-    owner = jnp.repeat(routes[:, 0], HALF)
     rep, same, cross = pl.pallas_call(
         middle_kernel,
-        in_specs=[pl.BlockSpec(memory_space=pltpu.SMEM)] + [vmem()] * 6,
+        in_specs=[pl.BlockSpec(memory_space=pltpu.SMEM), vmem(), vmem(), pl.BlockSpec(memory_space=pl.ANY), vmem()],
         out_specs=[vmem()] * 3,
-        out_shape=[in_hbm(HOLDERS, STEPS, D2), shape(CHIPS, ROWS, LANES), shape(CHIPS, ROWS, LANES)],
+        out_shape=[shape(HOLDERS, STEPS, D2), shape(CHIPS, ROWS, LANES), shape(CHIPS, ROWS, LANES)],
+        scratch_shapes=[pltpu.VMEM((STEPS, D2), BF16), pltpu.SemaphoreType.DMA],
         compiler_params=params(10),
         name="stem_middle",
-    )(
-        where,
-        got_parts,
-        from_hbm(out_grad.reshape(STEPS, D2)),
-        conv2_bias[None],
-        from_hbm(jnp.repeat(lengths.astype(F32), HALF)[:, None]),
-        owner[:, None],
-        owner[None],
-    )
+    )(where, got_parts, conv2_bias[None], from_hbm(live_grad), wanted)
     got_grad = exchange(rep, "y")
 
     keep, send = pl.pallas_call(
         backward_kernel,
         in_specs=[
             pl.BlockSpec(memory_space=pltpu.SMEM),
-            *[vmem()] * (1 + BLOCKS),
-            pl.BlockSpec(memory_space=pl.ANY),
+            vmem(),
+            *[pl.BlockSpec(memory_space=pl.ANY)] * (BLOCKS + 1),
             vmem(),
             vmem(),
         ],
@@ -433,11 +465,12 @@
             pltpu.VMEM((WIDE, 3 * D2), BF16),
             pltpu.VMEM((WIDE, D2), F32),
             pltpu.VMEM((rows, 4 * LANES), BF16),
+            pltpu.SemaphoreType.DMA((BLOCKS,)),
             pltpu.SemaphoreType.DMA,
         ],
         compiler_params=params(32),
         name="stem_backward",
-    )(where, got_grad, *weights, from_hbm(cols), turned, slopes)
+    )(where, got_grad, *[from_hbm(weight) for weight in weights], from_hbm(cols), turned, slopes)
     got = lax.ppermute(send, "c", cores)
     quarters = exchange((keep + got.astype(F32)).astype(BF16).reshape(4, PACK, LANES), ("xh", "xl"))
 
@@ -470,31 +503,38 @@
     got = exchange(jnp.concatenate([same, conv1[:, : 3 * ROWS], cross, conv1[:, 3 * ROWS :]], axis=1), ("xh", "y"))
     got, other = lax.optimization_barrier((got, other))
     got_cross = lax.ppermute(got, "c", cores)
-    weight_grad, bias_grad, second_bias_grad, conv2_rows_grad, packed = pl.pallas_call(
+    conv2_rows_grad = pl.pallas_call(
+        unpack_kernel,
+        in_specs=[pl.BlockSpec(memory_space=pltpu.SMEM), vmem(), vmem()],
+        out_specs=vmem(),
+        out_shape=in_hbm(ROWS, 3 * D2, dtype=F32),
+        compiler_params=params(8),
+        name="conv2_unpack",
+    )(where, own, other)
+    weight_grad, bias_grad, second_bias_grad, packed = pl.pallas_call(
         last_kernel,
         grid=(3,),
         in_specs=[
             pl.BlockSpec(memory_space=pltpu.SMEM),
-            *[vmem()] * 4,
+            vmem(),
+            vmem(),
         ],
         out_specs=[
             pl.BlockSpec((LANES, 16 * ROWS), lambda i: (i, 0)),
             pl.BlockSpec((16 * ROWS,), lambda i: (0,)),
             pl.BlockSpec((D2,), lambda i: (0,)),
-            pl.BlockSpec((ROWS, 3 * D2), lambda i: (0, 0)),
             pl.BlockSpec((SLOTS * HALF, D2), lambda i: (0, 0)),
         ],
         out_shape=[
             shape(3 * MEL, 16 * ROWS, dtype=F32),
             shape(16 * ROWS, dtype=F32),
             shape(D2, dtype=F32),
-            shape(ROWS, 3 * D2, dtype=F32),
             shape(SLOTS * HALF, D2),
         ],
         scratch_shapes=[pltpu.VMEM((16 * ROWS, LANES), BF16), pltpu.VMEM((16, 16, LANES), F32)],
         compiler_params=params(16, "arbitrary"),
         name="gradient_unpack",
-    )(where, got, got_cross, own, other)
+    )(where, got, got_cross)
     return packed.reshape(SLOTS, HALF, D2), weight_grad, bias_grad, second_bias_grad, conv2_rows_grad
 
 

time: 153 us -> 161 us (1.052)
  Pallas kernels: 17.4 us -> 29.7 us
  waiting for transfers between devices: 23.6 us -> 20.5 us
    pallas_call x1, Pallas kernels: 1.66 us -> 9.78 us  [local(): pl.pallas_call(prepare_kernel, in_specs=[pl.BlockSpec(memory_space=pltpu....]
    pallas_call x1 -> x2, Pallas kernels: 2.17 us -> 5.21 us  [the longest x1 3.78 us: local(): pl.pallas_call(slope_kernel, grid=(HOLDERS // 2,), in_specs=[pay_spec, *[...]
  transfers between devices with their start and end apart: 12 -> 12, of which waited for: 7 -> 8; matrix products, arithmetic and copies ran while one was open for 1% -> 0% of each run, Pallas kernels for 3% -> 10%
where the time goes in v10:
time: 161 us; the launch traced here: 160 us
  starting transfers between devices  58.6 us (36%)
  blocking collectives  47.1 us (29%)
  Pallas kernels  29.7 us (18%)
  waiting for transfers between devices  20.5 us (13%)
  local copies, waits for them, and re-layouts  2.35 us (1%)
    all_to_all x4, blocking collectives, exchange(): return lax.all_to_all(values, axes, split_axis=0, concat_axis=0, tiled=True)  47.1 us
    ppermute x3, starting transfers between devices, local(): lax.ppermute(near, 'zh', [(i, i ^ flip) for i in range(4)])  18.2 us
    all_to_all x3, starting transfers between devices, exchange(): return lax.all_to_all(values, axes, split_axis=0, concat_axis=0, tiled=True)  12.2 us
    pallas_call x1, Pallas kernels, local(): pl.pallas_call(prepare_kernel, in_specs=[pl.BlockSpec(memory_space=pltpu....  9.78 us
    ppermute x1, starting transfers between devices, local(): got_cross = lax.ppermute(got, 'c', cores)  8.77 us
    ppermute x1, waiting for transfers between devices, local(): other = lax.ppermute(own, 'xl', [(0, 1), (1, 0)])  7.11 us
    ppermute x3, waiting for transfers between devices, local(): lax.ppermute(near, 'zh', [(i, i ^ flip) for i in range(4)])  6.06 us
    ppermute x1, starting transfers between devices, local(): lax.ppermute(conv2_weight, ('xh', 'xl'), [(0, 3), (3, 0), (1, 2), (2, 1)])  5.35 us
  transfers between devices with their start and end apart: 12, of which 8 were waited for; matrix products, arithmetic and copies ran while one was open for 0% of the time, Pallas kernels for 10%

profile of v10, /device:TPU:1, one launch (start us, length us, event | category | flops | bytes accessed | tf_op | source)
XLA Modules:
  0.0 160.4 jit_solution(3497505578336601212)
XLA Ops:
  0.6 0.0 copy-start
  0.7 5.3 %collective-permute-start.1 = (bf16[80,1920]{1,0:T(8,128)(2,1)}, bf16[80,1920]{1,0:T(8,128)(2,1)S(1)}, u32[]{:S(2)}, u32[]{:S(2)}) collective-permute-start(bf16[80,1920]{1,0:T(8,128)(2,1)} %own_ref.3), channel_id=1, source_target_pairs={{0,257},{257,0},{1,256},{256,1},{2,259},{259,2},{3,258},{258,3},{4... | collective-permute-start | bytes 921608 | tf_op jit(solution)/shard_map/ppermute | solution.py:376
  6.0 9.8 %mel_payload.1 = bf16[4,26,16,128]{3,2,1,0:T(8,128)(2,1)} custom-call(s32[16]{0:T(128)} %length_ref.1, bf16[16,16,128]{2,1,0:T(8,128)(2,1)} %mel_ref.1), custom_call_target="tpu_custom_call" | custom-call | tf_op jit(solution)/shard_map/mel_payload/pallas_call | solution.py:361
  15.8 4.2 %all-to-all-start = ((bf16[4,26,16,128]{3,2,1,0:T(8,128)(2,1)}), bf16[4,26,16,128]{3,2,1,0:T(8,128)(2,1)S(1)}, u32[]{:S(2)}, u32[]{:S(2)}) async-start(bf16[4,26,16,128]{3,2,1,0:T(8,128)(2,1)} %mel_payload.1), calls=%async_computation | async-start | bytes 851968 | tf_op jit(solution)/shard_map/all_to_all | solution.py:333
  20.0 0.1 pad_add_fusion.where_ref
  20.1 4.8 %collective-permute-start = (bf16[80,1920]{1,0:T(8,128)(2,1)}, bf16[80,1920]{1,0:T(8,128)(2,1)S(1)}, u32[]{:S(2)}, u32[]{:S(2)}) collective-permute-start(bf16[80,1920]{1,0:T(8,128)(2,1)} %own_ref.3), channel_id=1, source_target_pairs={{0,32},{32,0},{1,33},{33,1},{2,34},{34,2},{3,35},{35,3},{4,36},{36... | collective-permute-start | bytes 921608 | tf_op jit(solution)/shard_map/ppermute | solution.py:391
  24.9 1.9 %collective-permute-start.2 = (bf16[80,1920]{1,0:T(8,128)(2,1)S(1)}, bf16[80,1920]{1,0:T(8,128)(2,1)S(1)}, u32[]{:S(2)}, u32[]{:S(2)}) collective-permute-start(bf16[80,1920]{1,0:T(8,128)(2,1)S(1)} %collective-permute-done.1.far_ref), channel_id=1, source_target_pairs={{0,32},{32,0},{1,33},{33,1},{2,34},{34,2},{3,35},{35,3},{4,36},{36... | collective-permute-start | bytes 921608 | tf_op jit(solution)/shard_map/ppermute | solution.py:393
  26.8 1.4 conv1_columns.1
  28.2 0.0 copy-start.6
  28.2 0.0 collective-permute-done.side_ref
  28.2 0.0 copy-start.2
  28.2 0.1 collective-permute-done.2.both_ref
  28.4 0.0 copy-start.9
  28.4 3.8 %stem_forward.1 = bf16[4,128,640]{2,1,0:T(8,128)(2,1)} custom-call(bf16[4,26,16,128]{3,2,1,0:T(8,128)(2,1)S(1)} %all-to-all-done.pay_ref, bf16[384,384]{1,0:T(8,128)(2,1)S(1)} %get-tuple-element.27.w1_ref, f32[1,384]{1,0:T(1,128)S(1)} %get-tuple-element.28.b1_ref, bf16[80,1920]{1,0:T(8,128)(2,1)S(1)} %copy-done, ...), custom_call_target="tpu_custom_call" | custom-call | tf_op jit(solution)/shard_map/stem_forward/pallas_call | solution.py:401
  32.2 4.5 %all-to-all-start.1 = ((bf16[4,128,640]{2,1,0:T(8,128)(2,1)}), bf16[4,128,640]{2,1,0:T(8,128)(2,1)S(1)}, u32[]{:S(2)}, u32[]{:S(2)}) async-start(bf16[4,128,640]{2,1,0:T(8,128)(2,1)} %stem_forward.1), calls=%async_computation.1 | async-start | bytes 1310720 | tf_op jit(solution)/shard_map/all_to_all | solution.py:333
  36.7 0.1 broadcast_in_dim.14
  36.8 0.1 broadcast_in_dim_reshape.7.row_ref
  36.9 0.1 broadcast_in_dim_reshape.8.column_ref
  37.0 0.0 copy-start.7
  37.0 1.0 copy-done.7
  38.0 3.8 %stem_slopes.1 = (bf16[512,512]{1,0:T(8,128)(2,1)}, f32[2,512,384]{2,1,0:T(8,128)S(1)}, bf16[3,384,512]{2,1,0:T(8,128)(2,1)S(1)}, bf16[128,640]{1,0:T(8,128)(2,1)}, bf16[256,128]{1,0:T(8,128)(2,1)S(1)}) custom-call(bf16[4,26,16,128]{3,2,1,0:T(8,128)(2,1)S(1)} %all-to-all-done.pay_ref, bf16[384,384]{1,0:T(8,128)(2,1)S(1)} %copy-done.7, ...), custom_call_target="tpu_custom_call" | custom-call | tf_op jit(solution)/shard_map/stem_slopes/pallas_call | solution.py:419
  41.7 1.0 copy-done.4
  42.8 3.9 %all-to-all-done.1.part_ref = bf16[4,128,640]{2,1,0:T(8,128)(2,1)S(1)} async-done(((bf16[4,128,640]{2,1,0:T(8,128)(2,1)}), bf16[4,128,640]{2,1,0:T(8,128)(2,1)S(1)}, u32[]{:S(2)}, u32[]{:S(2)}) %all-to-all-start.1) | async-done | bytes 655392 | tf_op jit(solution)/shard_map/all_to_all | solution.py:333
  46.6 1.7 %stem_middle.1 = (bf16[4,128,640]{2,1,0:T(8,128)(2,1)S(1)}, bf16[8,80,128]{2,1,0:T(8,128)(2,1)S(1)}, bf16[8,80,128]{2,1,0:T(8,128)(2,1)S(1)}) custom-call(s32[4]{0:T(128)S(1)} %pad_add_fusion.where_ref, bf16[4,128,640]{2,1,0:T(8,128)(2,1)S(1)} %all-to-all-done.1.part_ref, f32[1,640]{1,0:T(1,128)S(1)} %broadcast_in_dim.15.b2_ref, ...), custom_call_target="tpu_custom_call" | custom-call | tf_op jit(solution)/shard_map/stem_middle/pallas_call | solution.py:442
  48.4 11.1 %all_to_all.35.grad_ref = bf16[4,128,640]{2,1,0:T(8,128)(2,1)S(1)} all-to-all(bf16[4,128,640]{2,1,0:T(8,128)(2,1)S(1)} %get-tuple-element.36), channel_id=1, replica_groups=mesh['xh'=2,'y'=4,'c'=2,'zh'=4,'zl'=4,'xl'=2] {'y'}, dimensions={0} | all-to-all | bytes 1310720 | tf_op jit(solution)/shard_map/all_to_all | solution.py:333
  59.5 4.8 %stem_backward.1 = (f32[2,2,896,128]{3,2,1,0:T(8,128)S(1)}, bf16[2,2,896,128]{3,2,1,0:T(8,128)(2,1)S(1)}) custom-call(s32[4]{0:T(128)S(1)} %pad_add_fusion.where_ref, bf16[4,128,640]{2,1,0:T(8,128)(2,1)S(1)} %all_to_all.35.grad_ref, bf16[80,1920]{1,0:T(8,128)(2,1)} %own_ref.3, bf16[80,1920]{1,0:T(8,128)(2,1)} %copy-done.2, bf16[80,1920]{1,0:T(8,128)(2,1)} %copy-done.1, ...), custom_call_target="tpu_custom_call" | custom-call | tf_op jit(solution)/shard_map/stem_backward/pallas_call | solution.py:453
  64.3 5.1 %collective-permute-start.3 = (bf16[2,2,896,128]{3,2,1,0:T(8,128)(2,1)S(1)}, bf16[2,2,896,128]{3,2,1,0:T(8,128)(2,1)S(1)}, u32[]{:S(2)}, u32[]{:S(2)}) collective-permute-start(bf16[2,2,896,128]{3,2,1,0:T(8,128)(2,1)S(1)} %get-tuple-element.41), channel_id=1, source_target_pairs={{0,32},{32,0},{1,33},{33,1},{2,34},{34,2},{3,35},{35,3},{4,36},{36... | collective-permute-start | bytes 2752520 | tf_op jit(solution)/shard_map/ppermute | solution.py:474
  69.3 2.1 %collective-permute-done.3 = bf16[2,2,896,128]{3,2,1,0:T(8,128)(2,1)S(1)} collective-permute-done((bf16[2,2,896,128]{3,2,1,0:T(8,128)(2,1)S(1)}, bf16[2,2,896,128]{3,2,1,0:T(8,128)(2,1)S(1)}, u32[]{:S(2)}, u32[]{:S(2)}) %collective-permute-start.3) | collective-permute-done | bytes 917536 | tf_op jit(solution)/shard_map/ppermute | solution.py:474
  71.4 0.2 add_convert_fusion
  71.6 16.8 %all_to_all.36.got_ref = bf16[4,896,128]{2,1,0:T(8,128)(2,1)S(1)} all-to-all(bf16[4,896,128]{2,1,0:T(8,128)(2,1)S(1)} %bitcast.12), channel_id=1, replica_groups=mesh['xh'=2,'y'=4,'c'=2,'zh'=4,'zl'=4,'xl'=2] {'xh','xl'}, dimensions={0} | all-to-all | bytes 1835008 | tf_op jit(solution)/shard_map/all_to_all | solution.py:333
  88.4 0.1 gradient_sum.2
  88.6 8.1 %all_to_all.37.got_ref = bf16[4,224,128]{2,1,0:T(8,128)(2,1)S(1)} all-to-all(bf16[4,224,128]{2,1,0:T(8,128)(2,1)S(1)} %bitcast.11), channel_id=1, replica_groups=mesh['xh'=2,'y'=4,'c'=2,'zh'=4,'zl'=4,'xl'=2] {'zl'}, dimensions={0} | all-to-all | bytes 458752 | tf_op jit(solution)/shard_map/all_to_all | solution.py:333
  96.7 12.3 %collective-permute-start.6 = (bf16[224,128]{1,0:T(8,128)(2,1)S(1)}, bf16[224,128]{1,0:T(8,128)(2,1)S(1)}, u32[]{:S(2)}, u32[]{:S(2)}) collective-permute-start(bf16[224,128]{1,0:T(8,128)(2,1)S(1)} %gradient_sum.3.own_ref), channel_id=1, source_target_pairs={{0,16},{8,24},{16,0},{24,8},{1,17},{9,25},{17,1},{25,9},{2,18},{10... | collective-permute-start | bytes 172040 | tf_op jit(solution)/shard_map/ppermute | solution.py:490
  109.1 3.1 %collective-permute-start.5 = (bf16[224,128]{1,0:T(8,128)(2,1)S(1)}, bf16[224,128]{1,0:T(8,128)(2,1)S(1)}, u32[]{:S(2)}, u32[]{:S(2)}) collective-permute-start(bf16[224,128]{1,0:T(8,128)(2,1)S(1)} %gradient_sum.3.own_ref), channel_id=1, source_target_pairs={{0,24},{8,16},{16,8},{24,0},{1,25},{9,17},{17,9},{25,1},{2,26},{10... | collective-permute-start | bytes 172040 | tf_op jit(solution)/shard_map/ppermute | solution.py:490
  112.2 2.9 %collective-permute-start.4 = (bf16[224,128]{1,0:T(8,128)(2,1)S(1)}, bf16[224,128]{1,0:T(8,128)(2,1)S(1)}, u32[]{:S(2)}, u32[]{:S(2)}) collective-permute-start(bf16[224,128]{1,0:T(8,128)(2,1)S(1)} %gradient_sum.3.own_ref), channel_id=1, source_target_pairs={{0,8},{8,0},{16,24},{24,16},{1,9},{9,1},{17,25},{25,17},{2,10},{10... | collective-permute-start | bytes 172040 | tf_op jit(solution)/shard_map/ppermute | solution.py:490
  115.0 6.0 %collective-permute-done.5.both_ref = bf16[224,128]{1,0:T(8,128)(2,1)S(1)} collective-permute-done((bf16[224,128]{1,0:T(8,128)(2,1)S(1)}, bf16[224,128]{1,0:T(8,128)(2,1)S(1)}, u32[]{:S(2)}, u32[]{:S(2)}) %collective-permute-start.5) | collective-permute-done | bytes 57376 | tf_op jit(solution)/shard_map/ppermute | solution.py:490
  121.0 0.1 collective-permute-done.4.near_ref
  121.1 11.1 %all_to_all.38 = bf16[4,224,128]{2,1,0:T(8,128)(2,1)S(1)} all-to-all(bf16[4,224,128]{2,1,0:T(8,128)(2,1)S(1)} %gradient_pairs.1), channel_id=1, replica_groups=mesh['xh'=2,'y'=4,'c'=2,'zh'=4,'zl'=4,'xl'=2] {'zl'}, dimensions={0} | all-to-all | bytes 458752 | tf_op jit(solution)/shard_map/all_to_all | solution.py:333
  132.2 0.1 broadcast_in_dim.16
  132.3 1.0 pad_maximum_fusion
  133.2 3.6 %all-to-all-start.6 = ((bf16[8,416,128]{2,1,0:T(8,128)(2,1)}), bf16[8,416,128]{2,1,0:T(8,128)(2,1)S(1)}, u32[]{:S(2)}, u32[]{:S(2)}) async-start(bf16[8,416,128]{2,1,0:T(8,128)(2,1)} %pad_maximum_fusion), calls=%async_computation.6 | async-start | bytes 1703936 | tf_op jit(solution)/shard_map/all_to_all | solution.py:333
  136.8 2.2 %collective-permute-start.7 = (bf16[640,128]{1,0:T(8,128)(2,1)S(1)}, bf16[640,128]{1,0:T(8,128)(2,1)S(1)}, u32[]{:S(2)}, u32[]{:S(2)}) collective-permute-start(bf16[640,128]{1,0:T(8,128)(2,1)S(1)} %slice.20.own_ref), channel_id=1, source_target_pairs={{0,1},{1,0},{2,3},{3,2},{4,5},{5,4},{6,7},{7,6},{8,9},{9,8},{10,11... | collective-permute-start | bytes 491528 | tf_op jit(solution)/shard_map/ppermute | solution.py:501
  139.0 7.1 %collective-permute-done.7.other_ref = bf16[640,128]{1,0:T(8,128)(2,1)S(1)} collective-permute-done((bf16[640,128]{1,0:T(8,128)(2,1)S(1)}, bf16[640,128]{1,0:T(8,128)(2,1)S(1)}, u32[]{:S(2)}, u32[]{:S(2)}) %collective-permute-start.7) | collective-permute-done | bytes 163872 | tf_op jit(solution)/shard_map/ppermute | solution.py:501
  146.1 0.7 all-to-all-done.6.got_ref
  146.8 8.8 %collective-permute-start.8 = (bf16[8,416,128]{2,1,0:T(8,128)(2,1)S(1)}, bf16[8,416,128]{2,1,0:T(8,128)(2,1)S(1)}, u32[]{:S(2)}, u32[]{:S(2)}) collective-permute-start(bf16[8,416,128]{2,1,0:T(8,128)(2,1)S(1)} %all-to-all-done.6.got_ref), channel_id=1, source_target_pairs={{0,32},{32,0},{1,33},{33,1},{2,34},{34,2},{3,35},{35,3},{4,36},{36... | collective-permute-start | bytes 2555912 | tf_op jit(solution)/shard_map/ppermute | solution.py:505
  155.6 1.4 conv2_unpack.1
  157.0 0.6 collective-permute-done.8.cross_ref
  157.6 2.8 %gradient_unpack.1 = (f32[384,1280]{1,0:T(8,128)}, f32[1280]{0:T(1024)}, f32[640]{0:T(1024)}, bf16[256,640]{1,0:T(8,128)(2,1)}) custom-call(s32[4]{0:T(128)S(1)} %pad_add_fusion.where_ref, bf16[8,416,128]{2,1,0:T(8,128)(2,1)S(1)} %all-to-all-done.6.got_ref, bf16[8,416,128]{2,1,0:T(8,128)(2,1)S(1)} %collective-permute-done.8.cross_ref), custom_call_target="tpu_custom_call" | custom-call | tf_op jit(solution)/shard_map/gradient_unpack/pallas_call | solution.py:514
  (28 shorter events, 0.1 us)
Async XLA Ops:
  0.6 27.8 %copy-start = (bf16[80,1920]{1,0:T(8,128)(2,1)S(1)}, bf16[80,1920]{1,0:T(8,128)(2,1)}, u32[]{:S(2)}) copy-start(bf16[80,1920]{1,0:T(8,128)(2,1)} %own_ref.3) | copy-start | bytes 921604
  0.6 26.2 %copy-start.8 = (bf16[384,1280]{1,0:T(8,128)(2,1)S(1)}, bf16[384,1280]{1,0:T(8,128)(2,1)}, u32[]{:S(2)}) copy-start(bf16[384,1280]{1,0:T(8,128)(2,1)} %weight_ref.1) | copy-start | bytes 2949124
  0.7 24.2 %collective-permute-start.1 = (bf16[80,1920]{1,0:T(8,128)(2,1)}, bf16[80,1920]{1,0:T(8,128)(2,1)S(1)}, u32[]{:S(2)}, u32[]{:S(2)}) collective-permute-start(bf16[80,1920]{1,0:T(8,128)(2,1)} %own_ref.3), channel_id=1, source_target_pairs={{0,257},{257,0},{1,256},{256,1},{2,259},{259,2},{3,258},{258,3},{4... | collective-permute-start | bytes 921608 | tf_op jit(solution)/shard_map/ppermute | solution.py:376
  15.8 12.4 %all-to-all-start = ((bf16[4,26,16,128]{3,2,1,0:T(8,128)(2,1)}), bf16[4,26,16,128]{3,2,1,0:T(8,128)(2,1)S(1)}, u32[]{:S(2)}, u32[]{:S(2)}) async-start(bf16[4,26,16,128]{3,2,1,0:T(8,128)(2,1)} %mel_payload.1), calls=%async_computation | async-start | bytes 851968 | tf_op jit(solution)/shard_map/all_to_all | solution.py:333
  20.1 8.1 %collective-permute-start = (bf16[80,1920]{1,0:T(8,128)(2,1)}, bf16[80,1920]{1,0:T(8,128)(2,1)S(1)}, u32[]{:S(2)}, u32[]{:S(2)}) collective-permute-start(bf16[80,1920]{1,0:T(8,128)(2,1)} %own_ref.3), channel_id=1, source_target_pairs={{0,32},{32,0},{1,33},{33,1},{2,34},{34,2},{3,35},{35,3},{4,36},{36... | collective-permute-start | bytes 921608 | tf_op jit(solution)/shard_map/ppermute | solution.py:391
  24.9 7.3 %copy-start.1 = (bf16[80,1920]{1,0:T(8,128)(2,1)}, bf16[80,1920]{1,0:T(8,128)(2,1)S(1)}, u32[]{:S(2)}) copy-start(bf16[80,1920]{1,0:T(8,128)(2,1)S(1)} %collective-permute-done.1.far_ref) | copy-start | bytes 921604
  24.9 3.5 %collective-permute-start.2 = (bf16[80,1920]{1,0:T(8,128)(2,1)S(1)}, bf16[80,1920]{1,0:T(8,128)(2,1)S(1)}, u32[]{:S(2)}, u32[]{:S(2)}) collective-permute-start(bf16[80,1920]{1,0:T(8,128)(2,1)S(1)} %collective-permute-done.1.far_ref), channel_id=1, source_target_pairs={{0,32},{32,0},{1,33},{33,1},{2,34},{34,2},{3,35},{35,3},{4,36},{36... | collective-permute-start | bytes 921608 | tf_op jit(solution)/shard_map/ppermute | solution.py:393
  28.2 4.0 %copy-start.6 = (bf16[384,384]{1,0:T(8,128)(2,1)}, bf16[384,384]{1,0:T(8,128)(2,1)S(1)}, u32[]{:S(2)}) copy-start(bf16[384,384]{1,0:T(8,128)(2,1)S(1)} %get-tuple-element.27.w1_ref) | copy-start | bytes 884740
  28.2 4.0 %copy-start.2 = (bf16[80,1920]{1,0:T(8,128)(2,1)}, bf16[80,1920]{1,0:T(8,128)(2,1)S(1)}, u32[]{:S(2)}) copy-start(bf16[80,1920]{1,0:T(8,128)(2,1)S(1)} %collective-permute-done.side_ref) | copy-start | bytes 921604
  28.4 3.8 %copy-start.3 = (bf16[80,1920]{1,0:T(8,128)(2,1)}, bf16[80,1920]{1,0:T(8,128)(2,1)S(1)}, u32[]{:S(2)}) copy-start(bf16[80,1920]{1,0:T(8,128)(2,1)S(1)} %collective-permute-done.2.both_ref) | copy-start | bytes 921604
  28.4 8.3 %copy-start.10 = (s32[16]{0:T(128)S(1)}, s32[16]{0:T(128)}, u32[]{:S(2)}) copy-start(s32[16]{0:T(128)} %length_ref.1) | copy-start | bytes 196
  28.4 8.3 %copy-start.11 = (s32[16,1]{0,1:T(1,128)S(1)}, s32[16,1]{0,1:T(1,128)}, u32[]{:S(2)}) copy-start(s32[16,1]{0,1:T(1,128)} %param.10) | copy-start | bytes 196
  28.4 8.6 %copy-start.9 = (f32[640]{0:T(1024)S(1)}, f32[640]{0:T(1024)}, u32[]{:S(2)}) copy-start(f32[640]{0:T(1024)} %param.14) | copy-start | bytes 7684
  32.2 14.4 %all-to-all-start.1 = ((bf16[4,128,640]{2,1,0:T(8,128)(2,1)}), bf16[4,128,640]{2,1,0:T(8,128)(2,1)S(1)}, u32[]{:S(2)}, u32[]{:S(2)}) async-start(bf16[4,128,640]{2,1,0:T(8,128)(2,1)} %stem_forward.1), calls=%async_computation.1 | async-start | bytes 1310720 | tf_op jit(solution)/shard_map/all_to_all | solution.py:333
  37.0 1.0 copy-start.7
  41.7 1.0 copy-start.4
  46.6 12.8 %copy-start.5 = (bf16[3,384,512]{2,1,0:T(8,128)(2,1)S(1)}, bf16[3,384,512]{2,1,0:T(8,128)(2,1)}, u32[]{:S(2)}) copy-start(bf16[3,384,512]{2,1,0:T(8,128)(2,1)} %copy-done.4) | copy-start | bytes 3538948
  64.3 7.1 %collective-permute-start.3 = (bf16[2,2,896,128]{3,2,1,0:T(8,128)(2,1)S(1)}, bf16[2,2,896,128]{3,2,1,0:T(8,128)(2,1)S(1)}, u32[]{:S(2)}, u32[]{:S(2)}) collective-permute-start(bf16[2,2,896,128]{3,2,1,0:T(8,128)(2,1)S(1)} %get-tuple-element.41), channel_id=1, source_target_pairs={{0,32},{32,0},{1,33},{33,1},{2,34},{34,2},{3,35},{35,3},{4,36},{36... | collective-permute-start | bytes 2752520 | tf_op jit(solution)/shard_map/ppermute | solution.py:474
  96.7 18.3 %collective-permute-start.6 = (bf16[224,128]{1,0:T(8,128)(2,1)S(1)}, bf16[224,128]{1,0:T(8,128)(2,1)S(1)}, u32[]{:S(2)}, u32[]{:S(2)}) collective-permute-start(bf16[224,128]{1,0:T(8,128)(2,1)S(1)} %gradient_sum.3.own_ref), channel_id=1, source_target_pairs={{0,16},{8,24},{16,0},{24,8},{1,17},{9,25},{17,1},{25,9},{2,18},{10... | collective-permute-start | bytes 172040 | tf_op jit(solution)/shard_map/ppermute | solution.py:490
  109.1 12.0 %collective-permute-start.5 = (bf16[224,128]{1,0:T(8,128)(2,1)S(1)}, bf16[224,128]{1,0:T(8,128)(2,1)S(1)}, u32[]{:S(2)}, u32[]{:S(2)}) collective-permute-start(bf16[224,128]{1,0:T(8,128)(2,1)S(1)} %gradient_sum.3.own_ref), channel_id=1, source_target_pairs={{0,24},{8,16},{16,8},{24,0},{1,25},{9,17},{17,9},{25,1},{2,26},{10... | collective-permute-start | bytes 172040 | tf_op jit(solution)/shard_map/ppermute | solution.py:490
  112.2 8.9 %collective-permute-start.4 = (bf16[224,128]{1,0:T(8,128)(2,1)S(1)}, bf16[224,128]{1,0:T(8,128)(2,1)S(1)}, u32[]{:S(2)}, u32[]{:S(2)}) collective-permute-start(bf16[224,128]{1,0:T(8,128)(2,1)S(1)} %gradient_sum.3.own_ref), channel_id=1, source_target_pairs={{0,8},{8,0},{16,24},{24,16},{1,9},{9,1},{17,25},{25,17},{2,10},{10... | collective-permute-start | bytes 172040 | tf_op jit(solution)/shard_map/ppermute | solution.py:490
  133.2 13.6 %all-to-all-start.6 = ((bf16[8,416,128]{2,1,0:T(8,128)(2,1)}), bf16[8,416,128]{2,1,0:T(8,128)(2,1)S(1)}, u32[]{:S(2)}, u32[]{:S(2)}) async-start(bf16[8,416,128]{2,1,0:T(8,128)(2,1)} %pad_maximum_fusion), calls=%async_computation.6 | async-start | bytes 1703936 | tf_op jit(solution)/shard_map/all_to_all | solution.py:333
  136.8 9.3 %collective-permute-start.7 = (bf16[640,128]{1,0:T(8,128)(2,1)S(1)}, bf16[640,128]{1,0:T(8,128)(2,1)S(1)}, u32[]{:S(2)}, u32[]{:S(2)}) collective-permute-start(bf16[640,128]{1,0:T(8,128)(2,1)S(1)} %slice.20.own_ref), channel_id=1, source_target_pairs={{0,1},{1,0},{2,3},{3,2},{4,5},{5,4},{6,7},{7,6},{8,9},{9,8},{10,11... | collective-permute-start | bytes 491528 | tf_op jit(solution)/shard_map/ppermute | solution.py:501
  146.8 10.8 %collective-permute-start.8 = (bf16[8,416,128]{2,1,0:T(8,128)(2,1)S(1)}, bf16[8,416,128]{2,1,0:T(8,128)(2,1)S(1)}, u32[]{:S(2)}, u32[]{:S(2)}) collective-permute-start(bf16[8,416,128]{2,1,0:T(8,128)(2,1)S(1)} %all-to-all-done.6.got_ref), channel_id=1, source_target_pairs={{0,32},{32,0},{1,33},{33,1},{2,34},{34,2},{3,35},{35,3},{4,36},{36... | collective-permute-start | bytes 2555912 | tf_op jit(solution)/shard_map/ppermute | solution.py:505

commit v11 on v10

--- a/solution.py
+++ b/solution.py
@@ -70,34 +70,21 @@
     return lax.dot_general(left, right, (((0,), (0,)), ((), ())), preferred_element_type=F32)
 
 
-def weight_copies(refs, w2_ref, done):
-    return [
-        pltpu.make_async_copy(ref, w2_ref.at[block * ROWS : (block + 1) * ROWS], done.at[block])
-        for block, ref in enumerate(refs)
-    ]
-
-
-def prepare_kernel(length_ref, mel_ref, pay_ref, length_here, mel_done, length_done):
-    mel_copies = [
-        pltpu.make_async_copy(mel_ref, pay_ref.at[target, :CLIPS], mel_done.at[target]) for target in range(HOLDERS)
-    ]
-    for copy in mel_copies:
-        copy.start()
+def stack_weights(refs, w2_ref):
+    for block, ref in enumerate(refs):
+        w2_ref[block * ROWS : (block + 1) * ROWS, :] = ref[...]
+    w2_ref[BLOCKS * ROWS :, :] = jnp.zeros((WIDE - BLOCKS * ROWS, 3 * D2), BF16)
+
+
+def prepare_kernel(length_ref, mel_ref, pay_ref):
     clip = lax.broadcasted_iota(jnp.int32, (CLIPS, MEL), 0)
     length = jnp.zeros((CLIPS, MEL), F32)
     for index in range(CLIPS):
         length = jnp.where(clip == index, length_ref[index].astype(F32), length)
-    slots = length_here.shape[0]
-    for slot in range(slots):
-        length_here[slot] = length.astype(BF16)
-    length_copies = [
-        pltpu.make_async_copy(length_here, pay_ref.at[target, CLIPS:], length_done.at[target])
-        for target in range(HOLDERS)
-    ]
-    for copy in length_copies:
-        copy.start()
-    for copy in mel_copies + length_copies:
-        copy.wait()
+    for target in range(HOLDERS):
+        pay_ref[target, :CLIPS] = mel_ref[...]
+        pay_ref[target, CLIPS] = length.astype(BF16)
+        pay_ref[target, CLIPS + 1 :] = jnp.zeros((PAY - CLIPS - 1, 2 * HALF, MEL), BF16)
 
 
 def columns_kernel(where_ref, weight_ref, bias_ref, w1_ref, b1_ref, picked):
@@ -143,23 +130,13 @@
 
 
 def forward_kernel(
-    pay_ref, w1_ref, b1_ref, own_ref, side_ref, far_ref, both_ref, part_ref, w2_ref, cols_ref, frames_ref, done
+    pay_ref, w1_ref, b1_ref, own_ref, side_ref, far_ref, both_ref, part_ref, w2_ref, cols_ref, frames_ref
 ):
-    copies = weight_copies((own_ref, side_ref, far_ref, both_ref), w2_ref, done)
-
     @pl.when(pl.program_id(0) == 0)
     def _():
-        for copy in copies:
-            copy.start()
-        w2_ref[BLOCKS * ROWS :, :] = jnp.zeros((WIDE - BLOCKS * ROWS, 3 * D2), BF16)
+        stack_weights((own_ref, side_ref, far_ref, both_ref), w2_ref)
 
     pre_even, pre_odd, live_even, live_odd = first_conv(pay_ref, w1_ref, b1_ref, cols_ref, frames_ref)
-
-    @pl.when(pl.program_id(0) == 0)
-    def _():
-        for copy in copies:
-            copy.wait()
-
     odd = jnp.where(live_odd, gelu_value(pre_odd), 0.0)
     total = dot(odd.astype(BF16), w2_ref[:, 2 * D2 :]) + dot(shift_down(odd).astype(BF16), w2_ref[:, :D2])
     even = jnp.where(live_even, gelu_value(pre_even), 0.0)
@@ -226,13 +203,11 @@
 
 def backward_kernel(
     where_ref, grad_ref, own_ref, side_ref, far_ref, both_ref, cols_ref, turned_ref, slope_ref, keep_ref, send_ref,
-    w2_ref, conv_sum, cols_here, weights_done, cols_done,
+    w2_ref, conv_sum, cols_here, cols_done,
 ):
-    copies = weight_copies((own_ref, side_ref, far_ref, both_ref), w2_ref, weights_done)
-    copies.append(pltpu.make_async_copy(cols_ref, cols_here, cols_done))
-    for copy in copies:
-        copy.start()
-    w2_ref[BLOCKS * ROWS :, :] = jnp.zeros((WIDE - BLOCKS * ROWS, 3 * D2), BF16)
+    cols_copy = pltpu.make_async_copy(cols_ref, cols_here, cols_done)
+    cols_copy.start()
+    stack_weights((own_ref, side_ref, far_ref, both_ref), w2_ref)
     mine = where_ref[0]
     grad = grad_ref[...].reshape(HOLDERS * STEPS, D2)
     places = []
@@ -247,12 +222,11 @@
                 piece = conv_sum[first : first + ROWS, column * LANES : (column + 1) * LANES]
                 out[target, tile // 8, (tile % 8) * ROWS : (tile % 8 + 1) * ROWS, :] = piece.astype(out.dtype)
 
-    for copy in copies:
-        copy.wait()
     even = dot_nt(grad, w2_ref[:, D2 : 2 * D2])
     even = (even * slope_ref[0]).astype(BF16)
     odd = dot_nt(grad, w2_ref[:, 2 * D2 :]) + shift_up(dot_nt(grad, w2_ref[:, :D2]))
     odd = (odd * slope_ref[1]).astype(BF16)
+    cols_copy.wait()
     cols = cols_here[...]
     conv_sum[:, : 3 * LANES] = dot_tn(even, cols[:, : 3 * LANES]) + dot_tn(odd, cols[:, LANES:])
     bias1 = jnp.sum(even.astype(F32) + odd.astype(F32), axis=0, keepdims=True)
@@ -360,17 +334,12 @@
 
     pay = pl.pallas_call(
         prepare_kernel,
-        in_specs=[pl.BlockSpec(memory_space=pltpu.SMEM), pl.BlockSpec(memory_space=pl.ANY)],
-        out_specs=pl.BlockSpec(memory_space=pl.ANY),
+        in_specs=[pl.BlockSpec(memory_space=pltpu.SMEM), vmem()],
+        out_specs=vmem(),
         out_shape=in_hbm(HOLDERS, PAY, 2 * HALF, MEL),
-        scratch_shapes=[
-            pltpu.VMEM((PAY - CLIPS, 2 * HALF, MEL), BF16),
-            pltpu.SemaphoreType.DMA((HOLDERS,)),
-            pltpu.SemaphoreType.DMA((HOLDERS,)),
-        ],
         compiler_params=params(60),
         name="mel_payload",
-    )(lengths, from_hbm(mel))
+    )(lengths, mel)
     got_pay = exchange(pay, "y")
     cores = [(0, 1), (1, 0)]
     far_weight = lax.ppermute(conv2_weight, ("xh", "xl"), [(0, 3), (3, 0), (1, 2), (2, 1)])
@@ -401,14 +370,13 @@
     parts = pl.pallas_call(
         forward_kernel,
         grid=(HOLDERS // 2,),
-        in_specs=[pay_spec, vmem(), vmem(), *[pl.BlockSpec(memory_space=pl.ANY)] * BLOCKS],
+        in_specs=[pay_spec, *[vmem()] * (2 + BLOCKS)],
         out_specs=pl.BlockSpec((2, STEPS, D2), pair),
         out_shape=in_hbm(HOLDERS, STEPS, D2),
         scratch_shapes=[
             pltpu.VMEM((WIDE, 3 * D2), BF16),
             pltpu.VMEM((some, 4 * LANES), BF16),
             pltpu.VMEM(frames, F32),
-            pltpu.SemaphoreType.DMA((BLOCKS,)),
         ],
         compiler_params=params(20, "arbitrary"),
         name="stem_forward",
@@ -454,8 +422,8 @@
         backward_kernel,
         in_specs=[
             pl.BlockSpec(memory_space=pltpu.SMEM),
-            vmem(),
-            *[pl.BlockSpec(memory_space=pl.ANY)] * (BLOCKS + 1),
+            *[vmem()] * (1 + BLOCKS),
+            pl.BlockSpec(memory_space=pl.ANY),
             vmem(),
             vmem(),
         ],
@@ -465,12 +433,11 @@
             pltpu.VMEM((WIDE, 3 * D2), BF16),
             pltpu.VMEM((WIDE, D2), F32),
             pltpu.VMEM((rows, 4 * LANES), BF16),
-            pltpu.SemaphoreType.DMA((BLOCKS,)),
             pltpu.SemaphoreType.DMA,
         ],
         compiler_params=params(32),
         name="stem_backward",
-    )(where, got_grad, *[from_hbm(weight) for weight in weights], from_hbm(cols), turned, slopes)
+    )(where, got_grad, *weights, from_hbm(cols), turned, slopes)
     got = lax.ppermute(send, "c", cores)
     quarters = exchange((keep + got.astype(F32)).astype(BF16).reshape(4, PACK, LANES), ("xh", "xl"))
 

time: 161 us -> 152 us (0.944)
  Pallas kernels: 29.7 us -> 19.8 us
    pallas_call x1, Pallas kernels: 9.78 us -> 1.66 us  [local(): pl.pallas_call(prepare_kernel, in_specs=[pl.BlockSpec(memory_space=pltpu....]
  transfers between devices with their start and end apart: 12 -> 12, of which waited for: 8 -> 7; matrix products, arithmetic and copies ran while one was open for 0% -> 0% of each run, Pallas kernels for 10% -> 5%
where the time goes in v11:
time: 152 us; the launch traced here: 151 us
  starting transfers between devices  59.2 us (39%)
  blocking collectives  46 us (30%)
  waiting for transfers between devices  21.4 us (14%)
  Pallas kernels  19.8 us (13%)
  local copies, waits for them, and re-layouts  2.36 us (2%)
    all_to_all x4, blocking collectives, exchange(): return lax.all_to_all(values, axes, split_axis=0, concat_axis=0, tiled=True)  46 us
    ppermute x3, starting transfers between devices, local(): lax.ppermute(near, 'zh', [(i, i ^ flip) for i in range(4)])  18.7 us
    all_to_all x3, starting transfers between devices, exchange(): return lax.all_to_all(values, axes, split_axis=0, concat_axis=0, tiled=True)  11.2 us
    ppermute x1, starting transfers between devices, local(): got_cross = lax.ppermute(got, 'c', cores)  8.88 us
    ppermute x3, waiting for transfers between devices, local(): lax.ppermute(near, 'zh', [(i, i ^ flip) for i in range(4)])  7.21 us
    ppermute x1, waiting for transfers between devices, local(): other = lax.ppermute(own, 'xl', [(0, 1), (1, 0)])  6.48 us
    ppermute x1, starting transfers between devices, local(): lax.ppermute(conv2_weight, ('xh', 'xl'), [(0, 3), (3, 0), (1, 2), (2, 1)])  5.35 us
    ppermute x1, starting transfers between devices, local(): got = lax.ppermute(send, 'c', cores)  5.07 us
  transfers between devices with their start and end apart: 12, of which 7 were waited for; matrix products, arithmetic and copies ran while one was open for 0% of the time, Pallas kernels for 5%

profile of v11, /device:TPU:1, one launch (start us, length us, event | category | flops | bytes accessed | tf_op | source)
XLA Modules:
  0.0 150.9 jit_solution(11023367261650378776)
XLA Ops:
  0.6 0.0 copy-start
  0.7 5.3 %collective-permute-start.1 = (bf16[80,1920]{1,0:T(8,128)(2,1)}, bf16[80,1920]{1,0:T(8,128)(2,1)S(1)}, u32[]{:S(2)}, u32[]{:S(2)}) collective-permute-start(bf16[80,1920]{1,0:T(8,128)(2,1)} %own_ref.3), channel_id=1, source_target_pairs={{0,257},{257,0},{1,256},{256,1},{2,259},{259,2},{3,258},{258,3},{4... | collective-permute-start | bytes 921608 | tf_op jit(solution)/shard_map/ppermute | solution.py:345
  6.0 1.7 %mel_payload.1 = bf16[4,26,16,128]{3,2,1,0:T(8,128)(2,1)} custom-call(s32[16]{0:T(128)} %length_ref.1, bf16[16,16,128]{2,1,0:T(8,128)(2,1)} %mel_ref.1), custom_call_target="tpu_custom_call" | custom-call | tf_op jit(solution)/shard_map/mel_payload/pallas_call | solution.py:335
  7.7 4.2 %all-to-all-start = ((bf16[4,26,16,128]{3,2,1,0:T(8,128)(2,1)}), bf16[4,26,16,128]{3,2,1,0:T(8,128)(2,1)S(1)}, u32[]{:S(2)}, u32[]{:S(2)}) async-start(bf16[4,26,16,128]{3,2,1,0:T(8,128)(2,1)} %mel_payload.1), calls=%async_computation | async-start | bytes 851968 | tf_op jit(solution)/shard_map/all_to_all | solution.py:307
  11.9 0.1 pad_add_fusion.where_ref
  11.9 4.8 %collective-permute-start = (bf16[80,1920]{1,0:T(8,128)(2,1)}, bf16[80,1920]{1,0:T(8,128)(2,1)S(1)}, u32[]{:S(2)}, u32[]{:S(2)}) collective-permute-start(bf16[80,1920]{1,0:T(8,128)(2,1)} %own_ref.3), channel_id=1, source_target_pairs={{0,32},{32,0},{1,33},{33,1},{2,34},{34,2},{3,35},{35,3},{4,36},{36... | collective-permute-start | bytes 921608 | tf_op jit(solution)/shard_map/ppermute | solution.py:360
  16.7 3.0 %collective-permute-start.2 = (bf16[80,1920]{1,0:T(8,128)(2,1)S(1)}, bf16[80,1920]{1,0:T(8,128)(2,1)S(1)}, u32[]{:S(2)}, u32[]{:S(2)}) collective-permute-start(bf16[80,1920]{1,0:T(8,128)(2,1)S(1)} %collective-permute-done.1.far_ref), channel_id=1, source_target_pairs={{0,32},{32,0},{1,33},{33,1},{2,34},{34,2},{3,35},{35,3},{4,36},{36... | collective-permute-start | bytes 921608 | tf_op jit(solution)/shard_map/ppermute | solution.py:362
  19.8 1.4 conv1_columns.1
  21.1 0.0 copy-start.7
  21.2 0.0 copy-start.1
  21.2 0.0 copy-start.11
  21.2 0.0 copy-start.12
  21.2 0.0 copy-start.10
  21.2 3.4 %stem_forward.1 = bf16[4,128,640]{2,1,0:T(8,128)(2,1)} custom-call(bf16[4,26,16,128]{3,2,1,0:T(8,128)(2,1)S(1)} %all-to-all-done.pay_ref, bf16[384,384]{1,0:T(8,128)(2,1)S(1)} %get-tuple-element.27.w1_ref, f32[1,384]{1,0:T(1,128)S(1)} %get-tuple-element.28.b1_ref, bf16[80,1920]{1,0:T(8,128)(2,1)S(1)} %copy-done, ...), custom_call_target="tpu_custom_call" | custom-call | tf_op jit(solution)/shard_map/stem_forward/pallas_call | solution.py:370
  24.6 3.5 %all-to-all-start.1 = ((bf16[4,128,640]{2,1,0:T(8,128)(2,1)}), bf16[4,128,640]{2,1,0:T(8,128)(2,1)S(1)}, u32[]{:S(2)}, u32[]{:S(2)}) async-start(bf16[4,128,640]{2,1,0:T(8,128)(2,1)} %stem_forward.1), calls=%async_computation.1 | async-start | bytes 1310720 | tf_op jit(solution)/shard_map/all_to_all | solution.py:307
  28.1 0.1 broadcast_in_dim.14
  28.2 0.1 broadcast_in_dim_reshape.7.row_ref
  28.3 0.1 broadcast_in_dim_reshape.8.column_ref
  28.4 0.0 copy-start.8
  28.4 1.0 copy-done.8
  29.4 3.8 %stem_slopes.1 = (bf16[512,512]{1,0:T(8,128)(2,1)}, f32[2,512,384]{2,1,0:T(8,128)S(1)}, bf16[3,384,512]{2,1,0:T(8,128)(2,1)S(1)}, bf16[128,640]{1,0:T(8,128)(2,1)}, bf16[256,128]{1,0:T(8,128)(2,1)S(1)}) custom-call(bf16[4,26,16,128]{3,2,1,0:T(8,128)(2,1)S(1)} %all-to-all-done.pay_ref, bf16[384,384]{1,0:T(8,128)(2,1)S(1)} %copy-done.8, ...), custom_call_target="tpu_custom_call" | custom-call | tf_op jit(solution)/shard_map/stem_slopes/pallas_call | solution.py:387
  33.2 1.0 copy-done.5
  34.2 3.8 %all-to-all-done.1.part_ref = bf16[4,128,640]{2,1,0:T(8,128)(2,1)S(1)} async-done(((bf16[4,128,640]{2,1,0:T(8,128)(2,1)}), bf16[4,128,640]{2,1,0:T(8,128)(2,1)S(1)}, u32[]{:S(2)}, u32[]{:S(2)}) %all-to-all-start.1) | async-done | bytes 655392 | tf_op jit(solution)/shard_map/all_to_all | solution.py:307
  38.0 1.7 %stem_middle.1 = (bf16[4,128,640]{2,1,0:T(8,128)(2,1)S(1)}, bf16[8,80,128]{2,1,0:T(8,128)(2,1)S(1)}, bf16[8,80,128]{2,1,0:T(8,128)(2,1)S(1)}) custom-call(s32[4]{0:T(128)S(1)} %pad_add_fusion.where_ref, bf16[4,128,640]{2,1,0:T(8,128)(2,1)S(1)} %all-to-all-done.1.part_ref, f32[1,640]{1,0:T(1,128)S(1)} %broadcast_in_dim.15.b2_ref, ...), custom_call_target="tpu_custom_call" | custom-call | tf_op jit(solution)/shard_map/stem_middle/pallas_call | solution.py:410
  39.7 11.1 %all_to_all.35.grad_ref = bf16[4,128,640]{2,1,0:T(8,128)(2,1)S(1)} all-to-all(bf16[4,128,640]{2,1,0:T(8,128)(2,1)S(1)} %get-tuple-element.36), channel_id=1, replica_groups=mesh['xh'=2,'y'=4,'c'=2,'zh'=4,'zl'=4,'xl'=2] {'y'}, dimensions={0} | all-to-all | bytes 1310720 | tf_op jit(solution)/shard_map/all_to_all | solution.py:307
  50.8 3.4 %stem_backward.1 = (f32[2,2,896,128]{3,2,1,0:T(8,128)S(1)}, bf16[2,2,896,128]{3,2,1,0:T(8,128)(2,1)S(1)}) custom-call(s32[4]{0:T(128)S(1)} %pad_add_fusion.where_ref, bf16[4,128,640]{2,1,0:T(8,128)(2,1)S(1)} %all_to_all.35.grad_ref, bf16[80,1920]{1,0:T(8,128)(2,1)S(1)} %copy-done, bf16[80,1920]{1,0:T(8,128)(2,1)S(1)} %copy-done.2, ...), custom_call_target="tpu_custom_call" | custom-call | tf_op jit(solution)/shard_map/stem_backward/pallas_call | solution.py:421
  54.3 5.1 %collective-permute-start.3 = (bf16[2,2,896,128]{3,2,1,0:T(8,128)(2,1)S(1)}, bf16[2,2,896,128]{3,2,1,0:T(8,128)(2,1)S(1)}, u32[]{:S(2)}, u32[]{:S(2)}) collective-permute-start(bf16[2,2,896,128]{3,2,1,0:T(8,128)(2,1)S(1)} %get-tuple-element.41), channel_id=1, source_target_pairs={{0,32},{32,0},{1,33},{33,1},{2,34},{34,2},{3,35},{35,3},{4,36},{36... | collective-permute-start | bytes 2752520 | tf_op jit(solution)/shard_map/ppermute | solution.py:441
  59.4 2.1 %collective-permute-done.3 = bf16[2,2,896,128]{3,2,1,0:T(8,128)(2,1)S(1)} collective-permute-done((bf16[2,2,896,128]{3,2,1,0:T(8,128)(2,1)S(1)}, bf16[2,2,896,128]{3,2,1,0:T(8,128)(2,1)S(1)}, u32[]{:S(2)}, u32[]{:S(2)}) %collective-permute-start.3) | collective-permute-done | bytes 917536 | tf_op jit(solution)/shard_map/ppermute | solution.py:441
  61.4 0.2 add_convert_fusion
  61.7 16.9 %all_to_all.36.got_ref = bf16[4,896,128]{2,1,0:T(8,128)(2,1)S(1)} all-to-all(bf16[4,896,128]{2,1,0:T(8,128)(2,1)S(1)} %bitcast.12), channel_id=1, replica_groups=mesh['xh'=2,'y'=4,'c'=2,'zh'=4,'zl'=4,'xl'=2] {'xh','xl'}, dimensions={0} | all-to-all | bytes 1835008 | tf_op jit(solution)/shard_map/all_to_all | solution.py:307
  78.5 0.1 gradient_sum.2
  78.6 9.0 %all_to_all.37.got_ref = bf16[4,224,128]{2,1,0:T(8,128)(2,1)S(1)} all-to-all(bf16[4,224,128]{2,1,0:T(8,128)(2,1)S(1)} %bitcast.11), channel_id=1, replica_groups=mesh['xh'=2,'y'=4,'c'=2,'zh'=4,'zl'=4,'xl'=2] {'zl'}, dimensions={0} | all-to-all | bytes 458752 | tf_op jit(solution)/shard_map/all_to_all | solution.py:307
  87.7 12.7 %collective-permute-start.6 = (bf16[224,128]{1,0:T(8,128)(2,1)S(1)}, bf16[224,128]{1,0:T(8,128)(2,1)S(1)}, u32[]{:S(2)}, u32[]{:S(2)}) collective-permute-start(bf16[224,128]{1,0:T(8,128)(2,1)S(1)} %gradient_sum.3.own_ref), channel_id=1, source_target_pairs={{0,16},{8,24},{16,0},{24,8},{1,17},{9,25},{17,1},{25,9},{2,18},{10... | collective-permute-start | bytes 172040 | tf_op jit(solution)/shard_map/ppermute | solution.py:457
  100.5 3.1 %collective-permute-start.5 = (bf16[224,128]{1,0:T(8,128)(2,1)S(1)}, bf16[224,128]{1,0:T(8,128)(2,1)S(1)}, u32[]{:S(2)}, u32[]{:S(2)}) collective-permute-start(bf16[224,128]{1,0:T(8,128)(2,1)S(1)} %gradient_sum.3.own_ref), channel_id=1, source_target_pairs={{0,24},{8,16},{16,8},{24,0},{1,25},{9,17},{17,9},{25,1},{2,26},{10... | collective-permute-start | bytes 172040 | tf_op jit(solution)/shard_map/ppermute | solution.py:457
  103.6 2.9 %collective-permute-start.4 = (bf16[224,128]{1,0:T(8,128)(2,1)S(1)}, bf16[224,128]{1,0:T(8,128)(2,1)S(1)}, u32[]{:S(2)}, u32[]{:S(2)}) collective-permute-start(bf16[224,128]{1,0:T(8,128)(2,1)S(1)} %gradient_sum.3.own_ref), channel_id=1, source_target_pairs={{0,8},{8,0},{16,24},{24,16},{1,9},{9,1},{17,25},{25,17},{2,10},{10... | collective-permute-start | bytes 172040 | tf_op jit(solution)/shard_map/ppermute | solution.py:457
  106.4 5.5 %collective-permute-done.5.both_ref = bf16[224,128]{1,0:T(8,128)(2,1)S(1)} collective-permute-done((bf16[224,128]{1,0:T(8,128)(2,1)S(1)}, bf16[224,128]{1,0:T(8,128)(2,1)S(1)}, u32[]{:S(2)}, u32[]{:S(2)}) %collective-permute-start.5) | collective-permute-done | bytes 57376 | tf_op jit(solution)/shard_map/ppermute | solution.py:457
  112.0 1.7 %collective-permute-done.4.near_ref = bf16[224,128]{1,0:T(8,128)(2,1)S(1)} collective-permute-done((bf16[224,128]{1,0:T(8,128)(2,1)S(1)}, bf16[224,128]{1,0:T(8,128)(2,1)S(1)}, u32[]{:S(2)}, u32[]{:S(2)}) %collective-permute-start.4) | collective-permute-done | bytes 57376 | tf_op jit(solution)/shard_map/ppermute | solution.py:457
  113.7 9.0 %all_to_all.38 = bf16[4,224,128]{2,1,0:T(8,128)(2,1)S(1)} all-to-all(bf16[4,224,128]{2,1,0:T(8,128)(2,1)S(1)} %gradient_pairs.1), channel_id=1, replica_groups=mesh['xh'=2,'y'=4,'c'=2,'zh'=4,'zl'=4,'xl'=2] {'zl'}, dimensions={0} | all-to-all | bytes 458752 | tf_op jit(solution)/shard_map/all_to_all | solution.py:307
  122.7 0.1 broadcast_in_dim.16
  122.8 1.0 pad_maximum_fusion
  123.7 3.6 %all-to-all-start.6 = ((bf16[8,416,128]{2,1,0:T(8,128)(2,1)}), bf16[8,416,128]{2,1,0:T(8,128)(2,1)S(1)}, u32[]{:S(2)}, u32[]{:S(2)}) async-start(bf16[8,416,128]{2,1,0:T(8,128)(2,1)} %pad_maximum_fusion), calls=%async_computation.6 | async-start | bytes 1703936 | tf_op jit(solution)/shard_map/all_to_all | solution.py:307
  127.3 2.2 %collective-permute-start.7 = (bf16[640,128]{1,0:T(8,128)(2,1)S(1)}, bf16[640,128]{1,0:T(8,128)(2,1)S(1)}, u32[]{:S(2)}, u32[]{:S(2)}) collective-permute-start(bf16[640,128]{1,0:T(8,128)(2,1)S(1)} %slice.20.own_ref), channel_id=1, source_target_pairs={{0,1},{1,0},{2,3},{3,2},{4,5},{5,4},{6,7},{7,6},{8,9},{9,8},{10,11... | collective-permute-start | bytes 491528 | tf_op jit(solution)/shard_map/ppermute | solution.py:468
  129.5 6.5 %collective-permute-done.7.other_ref = bf16[640,128]{1,0:T(8,128)(2,1)S(1)} collective-permute-done((bf16[640,128]{1,0:T(8,128)(2,1)S(1)}, bf16[640,128]{1,0:T(8,128)(2,1)S(1)}, u32[]{:S(2)}, u32[]{:S(2)}) %collective-permute-start.7) | collective-permute-done | bytes 163872 | tf_op jit(solution)/shard_map/ppermute | solution.py:468
  136.0 1.2 all-to-all-done.6.got_ref
  137.2 8.9 %collective-permute-start.8 = (bf16[8,416,128]{2,1,0:T(8,128)(2,1)S(1)}, bf16[8,416,128]{2,1,0:T(8,128)(2,1)S(1)}, u32[]{:S(2)}, u32[]{:S(2)}) collective-permute-start(bf16[8,416,128]{2,1,0:T(8,128)(2,1)S(1)} %all-to-all-done.6.got_ref), channel_id=1, source_target_pairs={{0,32},{32,0},{1,33},{33,1},{2,34},{34,2},{3,35},{35,3},{4,36},{36... | collective-permute-start | bytes 2555912 | tf_op jit(solution)/shard_map/ppermute | solution.py:472
  146.1 1.4 conv2_unpack.1
  147.5 0.6 collective-permute-done.8.cross_ref
  148.1 2.8 %gradient_unpack.1 = (f32[384,1280]{1,0:T(8,128)}, f32[1280]{0:T(1024)}, f32[640]{0:T(1024)}, bf16[256,640]{1,0:T(8,128)(2,1)}) custom-call(s32[4]{0:T(128)S(1)} %pad_add_fusion.where_ref, bf16[8,416,128]{2,1,0:T(8,128)(2,1)S(1)} %all-to-all-done.6.got_ref, bf16[8,416,128]{2,1,0:T(8,128)(2,1)S(1)} %collective-permute-done.8.cross_ref), custom_call_target="tpu_custom_call" | custom-call | tf_op jit(solution)/shard_map/gradient_unpack/pallas_call | solution.py:481
  (30 shorter events, 0.1 us)
Async XLA Ops:
  0.6 20.6 %copy-start = (bf16[80,1920]{1,0:T(8,128)(2,1)S(1)}, bf16[80,1920]{1,0:T(8,128)(2,1)}, u32[]{:S(2)}) copy-start(bf16[80,1920]{1,0:T(8,128)(2,1)} %own_ref.3) | copy-start | bytes 921604
  0.6 19.1 %copy-start.9 = (bf16[384,1280]{1,0:T(8,128)(2,1)S(1)}, bf16[384,1280]{1,0:T(8,128)(2,1)}, u32[]{:S(2)}) copy-start(bf16[384,1280]{1,0:T(8,128)(2,1)} %weight_ref.1) | copy-start | bytes 2949124
  0.7 16.1 %collective-permute-start.1 = (bf16[80,1920]{1,0:T(8,128)(2,1)}, bf16[80,1920]{1,0:T(8,128)(2,1)S(1)}, u32[]{:S(2)}, u32[]{:S(2)}) collective-permute-start(bf16[80,1920]{1,0:T(8,128)(2,1)} %own_ref.3), channel_id=1, source_target_pairs={{0,257},{257,0},{1,256},{256,1},{2,259},{259,2},{3,258},{258,3},{4... | collective-permute-start | bytes 921608 | tf_op jit(solution)/shard_map/ppermute | solution.py:345
  7.7 13.5 %all-to-all-start = ((bf16[4,26,16,128]{3,2,1,0:T(8,128)(2,1)}), bf16[4,26,16,128]{3,2,1,0:T(8,128)(2,1)S(1)}, u32[]{:S(2)}, u32[]{:S(2)}) async-start(bf16[4,26,16,128]{3,2,1,0:T(8,128)(2,1)} %mel_payload.1), calls=%async_computation | async-start | bytes 851968 | tf_op jit(solution)/shard_map/all_to_all | solution.py:307
  11.9 9.2 %collective-permute-start = (bf16[80,1920]{1,0:T(8,128)(2,1)}, bf16[80,1920]{1,0:T(8,128)(2,1)S(1)}, u32[]{:S(2)}, u32[]{:S(2)}) collective-permute-start(bf16[80,1920]{1,0:T(8,128)(2,1)} %own_ref.3), channel_id=1, source_target_pairs={{0,32},{32,0},{1,33},{33,1},{2,34},{34,2},{3,35},{35,3},{4,36},{36... | collective-permute-start | bytes 921608 | tf_op jit(solution)/shard_map/ppermute | solution.py:360
  16.7 4.4 %collective-permute-start.2 = (bf16[80,1920]{1,0:T(8,128)(2,1)S(1)}, bf16[80,1920]{1,0:T(8,128)(2,1)S(1)}, u32[]{:S(2)}, u32[]{:S(2)}) collective-permute-start(bf16[80,1920]{1,0:T(8,128)(2,1)S(1)} %collective-permute-done.1.far_ref), channel_id=1, source_target_pairs={{0,32},{32,0},{1,33},{33,1},{2,34},{34,2},{3,35},{35,3},{4,36},{36... | collective-permute-start | bytes 921608 | tf_op jit(solution)/shard_map/ppermute | solution.py:362
  21.1 3.5 %copy-start.7 = (bf16[384,384]{1,0:T(8,128)(2,1)}, bf16[384,384]{1,0:T(8,128)(2,1)S(1)}, u32[]{:S(2)}) copy-start(bf16[384,384]{1,0:T(8,128)(2,1)S(1)} %get-tuple-element.27.w1_ref) | copy-start | bytes 884740
  21.2 3.5 %copy-start.1 = (bf16[80,1920]{1,0:T(8,128)(2,1)}, bf16[80,1920]{1,0:T(8,128)(2,1)S(1)}, u32[]{:S(2)}) copy-start(bf16[80,1920]{1,0:T(8,128)(2,1)S(1)} %collective-permute-done.side_ref) | copy-start | bytes 921604
  21.2 3.4 %copy-start.3 = (bf16[80,1920]{1,0:T(8,128)(2,1)}, bf16[80,1920]{1,0:T(8,128)(2,1)S(1)}, u32[]{:S(2)}) copy-start(bf16[80,1920]{1,0:T(8,128)(2,1)S(1)} %collective-permute-done.2.both_ref) | copy-start | bytes 921604
  21.2 6.9 %copy-start.11 = (s32[16]{0:T(128)S(1)}, s32[16]{0:T(128)}, u32[]{:S(2)}) copy-start(s32[16]{0:T(128)} %length_ref.1) | copy-start | bytes 196
  21.2 6.9 %copy-start.12 = (s32[16,1]{0,1:T(1,128)S(1)}, s32[16,1]{0,1:T(1,128)}, u32[]{:S(2)}) copy-start(s32[16,1]{0,1:T(1,128)} %param.10) | copy-start | bytes 196
  21.2 7.2 %copy-start.10 = (f32[640]{0:T(1024)S(1)}, f32[640]{0:T(1024)}, u32[]{:S(2)}) copy-start(f32[640]{0:T(1024)} %param.14) | copy-start | bytes 7684
  24.6 13.4 %all-to-all-start.1 = ((bf16[4,128,640]{2,1,0:T(8,128)(2,1)}), bf16[4,128,640]{2,1,0:T(8,128)(2,1)S(1)}, u32[]{:S(2)}, u32[]{:S(2)}) async-start(bf16[4,128,640]{2,1,0:T(8,128)(2,1)} %stem_forward.1), calls=%async_computation.1 | async-start | bytes 1310720 | tf_op jit(solution)/shard_map/all_to_all | solution.py:307
  28.4 1.0 copy-start.8
  33.2 1.0 copy-start.5
  34.2 16.7 %copy-start.2 = (bf16[80,1920]{1,0:T(8,128)(2,1)S(1)}, bf16[80,1920]{1,0:T(8,128)(2,1)}, u32[]{:S(2)}) copy-start(bf16[80,1920]{1,0:T(8,128)(2,1)} %copy-done.1) | copy-start | bytes 921604
  38.0 12.8 %copy-start.4 = (bf16[80,1920]{1,0:T(8,128)(2,1)S(1)}, bf16[80,1920]{1,0:T(8,128)(2,1)}, u32[]{:S(2)}) copy-start(bf16[80,1920]{1,0:T(8,128)(2,1)} %copy-done.3) | copy-start | bytes 921604
  38.0 12.8 %copy-start.6 = (bf16[3,384,512]{2,1,0:T(8,128)(2,1)S(1)}, bf16[3,384,512]{2,1,0:T(8,128)(2,1)}, u32[]{:S(2)}) copy-start(bf16[3,384,512]{2,1,0:T(8,128)(2,1)} %copy-done.5) | copy-start | bytes 3538948
  54.3 7.2 %collective-permute-start.3 = (bf16[2,2,896,128]{3,2,1,0:T(8,128)(2,1)S(1)}, bf16[2,2,896,128]{3,2,1,0:T(8,128)(2,1)S(1)}, u32[]{:S(2)}, u32[]{:S(2)}) collective-permute-start(bf16[2,2,896,128]{3,2,1,0:T(8,128)(2,1)S(1)} %get-tuple-element.41), channel_id=1, source_target_pairs={{0,32},{32,0},{1,33},{33,1},{2,34},{34,2},{3,35},{35,3},{4,36},{36... | collective-permute-start | bytes 2752520 | tf_op jit(solution)/shard_map/ppermute | solution.py:441
  87.7 18.7 %collective-permute-start.6 = (bf16[224,128]{1,0:T(8,128)(2,1)S(1)}, bf16[224,128]{1,0:T(8,128)(2,1)S(1)}, u32[]{:S(2)}, u32[]{:S(2)}) collective-permute-start(bf16[224,128]{1,0:T(8,128)(2,1)S(1)} %gradient_sum.3.own_ref), channel_id=1, source_target_pairs={{0,16},{8,24},{16,0},{24,8},{1,17},{9,25},{17,1},{25,9},{2,18},{10... | collective-permute-start | bytes 172040 | tf_op jit(solution)/shard_map/ppermute | solution.py:457
  100.5 11.5 %collective-permute-start.5 = (bf16[224,128]{1,0:T(8,128)(2,1)S(1)}, bf16[224,128]{1,0:T(8,128)(2,1)S(1)}, u32[]{:S(2)}, u32[]{:S(2)}) collective-permute-start(bf16[224,128]{1,0:T(8,128)(2,1)S(1)} %gradient_sum.3.own_ref), channel_id=1, source_target_pairs={{0,24},{8,16},{16,8},{24,0},{1,25},{9,17},{17,9},{25,1},{2,26},{10... | collective-permute-start | bytes 172040 | tf_op jit(solution)/shard_map/ppermute | solution.py:457
  103.6 10.1 %collective-permute-start.4 = (bf16[224,128]{1,0:T(8,128)(2,1)S(1)}, bf16[224,128]{1,0:T(8,128)(2,1)S(1)}, u32[]{:S(2)}, u32[]{:S(2)}) collective-permute-start(bf16[224,128]{1,0:T(8,128)(2,1)S(1)} %gradient_sum.3.own_ref), channel_id=1, source_target_pairs={{0,8},{8,0},{16,24},{24,16},{1,9},{9,1},{17,25},{25,17},{2,10},{10... | collective-permute-start | bytes 172040 | tf_op jit(solution)/shard_map/ppermute | solution.py:457
  123.7 13.5 %all-to-all-start.6 = ((bf16[8,416,128]{2,1,0:T(8,128)(2,1)}), bf16[8,416,128]{2,1,0:T(8,128)(2,1)S(1)}, u32[]{:S(2)}, u32[]{:S(2)}) async-start(bf16[8,416,128]{2,1,0:T(8,128)(2,1)} %pad_maximum_fusion), calls=%async_computation.6 | async-start | bytes 1703936 | tf_op jit(solution)/shard_map/all_to_all | solution.py:307
  127.3 8.7 %collective-permute-start.7 = (bf16[640,128]{1,0:T(8,128)(2,1)S(1)}, bf16[640,128]{1,0:T(8,128)(2,1)S(1)}, u32[]{:S(2)}, u32[]{:S(2)}) collective-permute-start(bf16[640,128]{1,0:T(8,128)(2,1)S(1)} %slice.20.own_ref), channel_id=1, source_target_pairs={{0,1},{1,0},{2,3},{3,2},{4,5},{5,4},{6,7},{7,6},{8,9},{9,8},{10,11... | collective-permute-start | bytes 491528 | tf_op jit(solution)/shard_map/ppermute | solution.py:468
  137.2 10.9 %collective-permute-start.8 = (bf16[8,416,128]{2,1,0:T(8,128)(2,1)S(1)}, bf16[8,416,128]{2,1,0:T(8,128)(2,1)S(1)}, u32[]{:S(2)}, u32[]{:S(2)}) collective-permute-start(bf16[8,416,128]{2,1,0:T(8,128)(2,1)S(1)} %all-to-all-done.6.got_ref), channel_id=1, source_target_pairs={{0,32},{32,0},{1,33},{33,1},{2,34},{34,2},{3,35},{35,3},{4,36},{36... | collective-permute-start | bytes 2555912 | tf_op jit(solution)/shard_map/ppermute | solution.py:472

commit v12 on v11

--- a/solution.py
+++ b/solution.py
@@ -257,11 +257,13 @@
             out_ref[target] = total
 
 
-def pairs_kernel(own_ref, near_ref, both_ref, far_ref, out_ref):
-    own, near, far, both = (ref[...].astype(F32) for ref in (own_ref, near_ref, far_ref, both_ref))
-    total = ((own + near) + (far + both)).astype(BF16)
-    for target in range(out_ref.shape[0]):
-        out_ref[target] = total
+def pair_kernel(own_ref, other_ref, out_ref):
+    total = (own_ref[...].astype(F32) + other_ref[...].astype(F32)).astype(BF16)
+    if len(out_ref.shape) == 2:
+        out_ref[...] = total
+    else:
+        for target in range(out_ref.shape[0]):
+            out_ref[target] = total
 
 
 def last_kernel(
@@ -454,15 +456,18 @@
     half = summed(quarters, PACK, LANES)
     quarter = PACK // 4
     near = summed(exchange(half.reshape(4, quarter, LANES), "zl"), quarter, LANES)
-    far = {flip: lax.ppermute(near, "zh", [(i, i ^ flip) for i in range(4)]) for flip in (2, 3, 1)}
-    far = pl.pallas_call(
-        pairs_kernel,
-        in_specs=[vmem()] * 4,
-        out_specs=vmem(),
-        out_shape=shape(4, quarter, LANES),
-        compiler_params=params(8),
-        name="gradient_pairs",
-    )(near, far[1], far[3], far[2])
+
+    def with_group(values, flip, *dims):
+        return pl.pallas_call(
+            pair_kernel,
+            in_specs=[vmem()] * 2,
+            out_specs=vmem(),
+            out_shape=shape(*dims),
+            compiler_params=params(8),
+            name="gradient_pair",
+        )(values, lax.ppermute(values, "zh", [(i, i ^ flip) for i in range(4)]))
+
+    far = with_group(with_group(near, 1, quarter, LANES), 3, 4, quarter, LANES)
     half = exchange(far, "zl").reshape(PACK, LANES)
     own = half[:HALF_ROWS]
     other = lax.ppermute(own, "xl", [(0, 1), (1, 0)])

time: 152 us -> 148 us (0.974)
  starting transfers between devices: 59.2 us -> 56.4 us
  waiting for transfers between devices: 21.4 us -> 19.3 us
    ppermute x3 -> x2, starting transfers between devices: 18.7 us -> 16 us  [with_group(): lax.ppermute(values, 'zh', [(i, i ^ flip) for i in range(4)])]
    ppermute x3 -> x2, waiting for transfers between devices: 7.21 us -> 5.06 us  [with_group(): lax.ppermute(values, 'zh', [(i, i ^ flip) for i in range(4)])]
  transfers between devices with their start and end apart: 12 -> 11, of which waited for: 7 -> 7; matrix products, arithmetic and copies ran while one was open for 0% -> 0% of each run, Pallas kernels for 5% -> 6%
where the time goes in v12:
time: 148 us; the launch traced here: 147 us
  starting transfers between devices  56.4 us (38%)
  blocking collectives  47.3 us (32%)
  Pallas kernels  19.8 us (13%)
  waiting for transfers between devices  19.3 us (13%)
  local copies, waits for them, and re-layouts  2.36 us (2%)
    all_to_all x4, blocking collectives, exchange(): return lax.all_to_all(values, axes, split_axis=0, concat_axis=0, tiled=True)  47.3 us
    ppermute x2, starting transfers between devices, with_group(): lax.ppermute(values, 'zh', [(i, i ^ flip) for i in range(4)])  16 us
    all_to_all x3, starting transfers between devices, exchange(): return lax.all_to_all(values, axes, split_axis=0, concat_axis=0, tiled=True)  11.2 us
    ppermute x1, starting transfers between devices, local(): got_cross = lax.ppermute(got, 'c', cores)  8.81 us
    ppermute x1, waiting for transfers between devices, local(): other = lax.ppermute(own, 'xl', [(0, 1), (1, 0)])  6.95 us
    ppermute x1, starting transfers between devices, local(): lax.ppermute(conv2_weight, ('xh', 'xl'), [(0, 3), (3, 0), (1, 2), (2, 1)])  5.35 us
    ppermute x1, starting transfers between devices, local(): got = lax.ppermute(send, 'c', cores)  5.06 us
    ppermute x2, waiting for transfers between devices, with_group(): lax.ppermute(values, 'zh', [(i, i ^ flip) for i in range(4)])  5.06 us
  transfers between devices with their start and end apart: 11, of which 7 were waited for; matrix products, arithmetic and copies ran while one was open for 0% of the time, Pallas kernels for 6%

profile of v12, /device:TPU:1, one launch (start us, length us, event | category | flops | bytes accessed | tf_op | source)
XLA Modules:
  0.0 147.4 jit_solution(10704221155555696442)
XLA Ops:
  0.6 0.0 copy-start
  0.7 5.3 %collective-permute-start.1 = (bf16[80,1920]{1,0:T(8,128)(2,1)}, bf16[80,1920]{1,0:T(8,128)(2,1)S(1)}, u32[]{:S(2)}, u32[]{:S(2)}) collective-permute-start(bf16[80,1920]{1,0:T(8,128)(2,1)} %own_ref.3), channel_id=1, source_target_pairs={{0,257},{257,0},{1,256},{256,1},{2,259},{259,2},{3,258},{258,3},{4... | collective-permute-start | bytes 921608 | tf_op jit(solution)/shard_map/ppermute | solution.py:347
  6.0 1.7 %mel_payload.1 = bf16[4,26,16,128]{3,2,1,0:T(8,128)(2,1)} custom-call(s32[16]{0:T(128)} %length_ref.1, bf16[16,16,128]{2,1,0:T(8,128)(2,1)} %mel_ref.1), custom_call_target="tpu_custom_call" | custom-call | tf_op jit(solution)/shard_map/mel_payload/pallas_call | solution.py:337
  7.7 4.2 %all-to-all-start = ((bf16[4,26,16,128]{3,2,1,0:T(8,128)(2,1)}), bf16[4,26,16,128]{3,2,1,0:T(8,128)(2,1)S(1)}, u32[]{:S(2)}, u32[]{:S(2)}) async-start(bf16[4,26,16,128]{3,2,1,0:T(8,128)(2,1)} %mel_payload.1), calls=%async_computation | async-start | bytes 851968 | tf_op jit(solution)/shard_map/all_to_all | solution.py:309
  11.9 0.1 pad_add_fusion.where_ref
  11.9 4.8 %collective-permute-start = (bf16[80,1920]{1,0:T(8,128)(2,1)}, bf16[80,1920]{1,0:T(8,128)(2,1)S(1)}, u32[]{:S(2)}, u32[]{:S(2)}) collective-permute-start(bf16[80,1920]{1,0:T(8,128)(2,1)} %own_ref.3), channel_id=1, source_target_pairs={{0,32},{32,0},{1,33},{33,1},{2,34},{34,2},{3,35},{35,3},{4,36},{36... | collective-permute-start | bytes 921608 | tf_op jit(solution)/shard_map/ppermute | solution.py:362
  16.7 0.0 collective-permute-done.1.far_ref
  16.7 3.0 %collective-permute-start.2 = (bf16[80,1920]{1,0:T(8,128)(2,1)S(1)}, bf16[80,1920]{1,0:T(8,128)(2,1)S(1)}, u32[]{:S(2)}, u32[]{:S(2)}) collective-permute-start(bf16[80,1920]{1,0:T(8,128)(2,1)S(1)} %collective-permute-done.1.far_ref), channel_id=1, source_target_pairs={{0,32},{32,0},{1,33},{33,1},{2,34},{34,2},{3,35},{35,3},{4,36},{36... | collective-permute-start | bytes 921608 | tf_op jit(solution)/shard_map/ppermute | solution.py:364
  19.8 1.4 conv1_columns.1
  21.1 0.0 copy-start.7
  21.2 0.0 copy-start.1
  21.2 0.0 copy-start.11
  21.2 0.0 copy-start.12
  21.2 0.0 copy-start.10
  21.2 3.3 %stem_forward.1 = bf16[4,128,640]{2,1,0:T(8,128)(2,1)} custom-call(bf16[4,26,16,128]{3,2,1,0:T(8,128)(2,1)S(1)} %all-to-all-done.pay_ref, bf16[384,384]{1,0:T(8,128)(2,1)S(1)} %get-tuple-element.27.w1_ref, f32[1,384]{1,0:T(1,128)S(1)} %get-tuple-element.28.b1_ref, bf16[80,1920]{1,0:T(8,128)(2,1)S(1)} %copy-done, ...), custom_call_target="tpu_custom_call" | custom-call | tf_op jit(solution)/shard_map/stem_forward/pallas_call | solution.py:372
  24.6 3.5 %all-to-all-start.1 = ((bf16[4,128,640]{2,1,0:T(8,128)(2,1)}), bf16[4,128,640]{2,1,0:T(8,128)(2,1)S(1)}, u32[]{:S(2)}, u32[]{:S(2)}) async-start(bf16[4,128,640]{2,1,0:T(8,128)(2,1)} %stem_forward.1), calls=%async_computation.1 | async-start | bytes 1310720 | tf_op jit(solution)/shard_map/all_to_all | solution.py:309
  28.1 0.1 broadcast_in_dim.14
  28.2 0.1 broadcast_in_dim_reshape.7.row_ref
  28.3 0.1 broadcast_in_dim_reshape.8.column_ref
  28.4 0.0 copy-start.8
  28.4 1.0 copy-done.8
  29.4 3.8 %stem_slopes.1 = (bf16[512,512]{1,0:T(8,128)(2,1)}, f32[2,512,384]{2,1,0:T(8,128)S(1)}, bf16[3,384,512]{2,1,0:T(8,128)(2,1)S(1)}, bf16[128,640]{1,0:T(8,128)(2,1)}, bf16[256,128]{1,0:T(8,128)(2,1)S(1)}) custom-call(bf16[4,26,16,128]{3,2,1,0:T(8,128)(2,1)S(1)} %all-to-all-done.pay_ref, bf16[384,384]{1,0:T(8,128)(2,1)S(1)} %copy-done.8, ...), custom_call_target="tpu_custom_call" | custom-call | tf_op jit(solution)/shard_map/stem_slopes/pallas_call | solution.py:389
  33.2 1.0 copy-done.5
  34.2 3.8 %all-to-all-done.1.part_ref = bf16[4,128,640]{2,1,0:T(8,128)(2,1)S(1)} async-done(((bf16[4,128,640]{2,1,0:T(8,128)(2,1)}), bf16[4,128,640]{2,1,0:T(8,128)(2,1)S(1)}, u32[]{:S(2)}, u32[]{:S(2)}) %all-to-all-start.1) | async-done | bytes 655392 | tf_op jit(solution)/shard_map/all_to_all | solution.py:309
  38.0 1.7 %stem_middle.1 = (bf16[4,128,640]{2,1,0:T(8,128)(2,1)S(1)}, bf16[8,80,128]{2,1,0:T(8,128)(2,1)S(1)}, bf16[8,80,128]{2,1,0:T(8,128)(2,1)S(1)}) custom-call(s32[4]{0:T(128)S(1)} %pad_add_fusion.where_ref, bf16[4,128,640]{2,1,0:T(8,128)(2,1)S(1)} %all-to-all-done.1.part_ref, f32[1,640]{1,0:T(1,128)S(1)} %broadcast_in_dim.15.b2_ref, ...), custom_call_target="tpu_custom_call" | custom-call | tf_op jit(solution)/shard_map/stem_middle/pallas_call | solution.py:412
  39.7 11.1 %all_to_all.35.grad_ref = bf16[4,128,640]{2,1,0:T(8,128)(2,1)S(1)} all-to-all(bf16[4,128,640]{2,1,0:T(8,128)(2,1)S(1)} %get-tuple-element.36), channel_id=1, replica_groups=mesh['xh'=2,'y'=4,'c'=2,'zh'=4,'zl'=4,'xl'=2] {'y'}, dimensions={0} | all-to-all | bytes 1310720 | tf_op jit(solution)/shard_map/all_to_all | solution.py:309
  50.8 3.4 %stem_backward.1 = (f32[2,2,896,128]{3,2,1,0:T(8,128)S(1)}, bf16[2,2,896,128]{3,2,1,0:T(8,128)(2,1)S(1)}) custom-call(s32[4]{0:T(128)S(1)} %pad_add_fusion.where_ref, bf16[4,128,640]{2,1,0:T(8,128)(2,1)S(1)} %all_to_all.35.grad_ref, bf16[80,1920]{1,0:T(8,128)(2,1)S(1)} %copy-done, bf16[80,1920]{1,0:T(8,128)(2,1)S(1)} %copy-done.2, ...), custom_call_target="tpu_custom_call" | custom-call | tf_op jit(solution)/shard_map/stem_backward/pallas_call | solution.py:423
  54.3 5.1 %collective-permute-start.3 = (bf16[2,2,896,128]{3,2,1,0:T(8,128)(2,1)S(1)}, bf16[2,2,896,128]{3,2,1,0:T(8,128)(2,1)S(1)}, u32[]{:S(2)}, u32[]{:S(2)}) collective-permute-start(bf16[2,2,896,128]{3,2,1,0:T(8,128)(2,1)S(1)} %get-tuple-element.41), channel_id=1, source_target_pairs={{0,32},{32,0},{1,33},{33,1},{2,34},{34,2},{3,35},{35,3},{4,36},{36... | collective-permute-start | bytes 2752520 | tf_op jit(solution)/shard_map/ppermute | solution.py:443
  59.4 2.1 %collective-permute-done.3 = bf16[2,2,896,128]{3,2,1,0:T(8,128)(2,1)S(1)} collective-permute-done((bf16[2,2,896,128]{3,2,1,0:T(8,128)(2,1)S(1)}, bf16[2,2,896,128]{3,2,1,0:T(8,128)(2,1)S(1)}, u32[]{:S(2)}, u32[]{:S(2)}) %collective-permute-start.3) | collective-permute-done | bytes 917536 | tf_op jit(solution)/shard_map/ppermute | solution.py:443
  61.4 0.2 add_convert_fusion
  61.7 16.9 %all_to_all.36.got_ref = bf16[4,896,128]{2,1,0:T(8,128)(2,1)S(1)} all-to-all(bf16[4,896,128]{2,1,0:T(8,128)(2,1)S(1)} %bitcast.12), channel_id=1, replica_groups=mesh['xh'=2,'y'=4,'c'=2,'zh'=4,'zl'=4,'xl'=2] {'xh','xl'}, dimensions={0} | all-to-all | bytes 1835008 | tf_op jit(solution)/shard_map/all_to_all | solution.py:309
  78.5 0.1 gradient_sum.2
  78.6 9.0 %all_to_all.37.got_ref = bf16[4,224,128]{2,1,0:T(8,128)(2,1)S(1)} all-to-all(bf16[4,224,128]{2,1,0:T(8,128)(2,1)S(1)} %bitcast.11), channel_id=1, replica_groups=mesh['xh'=2,'y'=4,'c'=2,'zh'=4,'zl'=4,'xl'=2] {'zl'}, dimensions={0} | all-to-all | bytes 458752 | tf_op jit(solution)/shard_map/all_to_all | solution.py:309
  87.7 8.8 %collective-permute-start.4 = (bf16[224,128]{1,0:T(8,128)(2,1)S(1)}, bf16[224,128]{1,0:T(8,128)(2,1)S(1)}, u32[]{:S(2)}, u32[]{:S(2)}) collective-permute-start(bf16[224,128]{1,0:T(8,128)(2,1)S(1)} %gradient_sum.3.own_ref), channel_id=1, source_target_pairs={{0,8},{8,0},{16,24},{24,16},{1,9},{9,1},{17,25},{25,17},{2,10},{10... | collective-permute-start | bytes 172040 | tf_op jit(solution)/shard_map/ppermute | solution.py:468
  96.5 2.8 %collective-permute-done.4.other_ref = bf16[224,128]{1,0:T(8,128)(2,1)S(1)} collective-permute-done((bf16[224,128]{1,0:T(8,128)(2,1)S(1)}, bf16[224,128]{1,0:T(8,128)(2,1)S(1)}, u32[]{:S(2)}, u32[]{:S(2)}) %collective-permute-start.4) | collective-permute-done | bytes 57376 | tf_op jit(solution)/shard_map/ppermute | solution.py:468
  99.3 7.2 %collective-permute-start.5 = (bf16[224,128]{1,0:T(8,128)(2,1)S(1)}, bf16[224,128]{1,0:T(8,128)(2,1)S(1)}, u32[]{:S(2)}, u32[]{:S(2)}) collective-permute-start(bf16[224,128]{1,0:T(8,128)(2,1)S(1)} %gradient_pair.2.own_ref), channel_id=1, source_target_pairs={{0,24},{8,16},{16,8},{24,0},{1,25},{9,17},{17,9},{25,1},{2,26},{10... | collective-permute-start | bytes 172040 | tf_op jit(solution)/shard_map/ppermute | solution.py:468
  106.5 2.3 %collective-permute-done.5.other_ref = bf16[224,128]{1,0:T(8,128)(2,1)S(1)} collective-permute-done((bf16[224,128]{1,0:T(8,128)(2,1)S(1)}, bf16[224,128]{1,0:T(8,128)(2,1)S(1)}, u32[]{:S(2)}, u32[]{:S(2)}) %collective-permute-start.5) | collective-permute-done | bytes 57376 | tf_op jit(solution)/shard_map/ppermute | solution.py:468
  108.8 10.3 %all_to_all.38 = bf16[4,224,128]{2,1,0:T(8,128)(2,1)S(1)} all-to-all(bf16[4,224,128]{2,1,0:T(8,128)(2,1)S(1)} %gradient_pair.3), channel_id=1, replica_groups=mesh['xh'=2,'y'=4,'c'=2,'zh'=4,'zl'=4,'xl'=2] {'zl'}, dimensions={0} | all-to-all | bytes 458752 | tf_op jit(solution)/shard_map/all_to_all | solution.py:309
  119.2 0.1 broadcast_in_dim.16
  119.3 1.0 pad_maximum_fusion
  120.2 3.6 %all-to-all-start.6 = ((bf16[8,416,128]{2,1,0:T(8,128)(2,1)}), bf16[8,416,128]{2,1,0:T(8,128)(2,1)S(1)}, u32[]{:S(2)}, u32[]{:S(2)}) async-start(bf16[8,416,128]{2,1,0:T(8,128)(2,1)} %pad_maximum_fusion), calls=%async_computation.6 | async-start | bytes 1703936 | tf_op jit(solution)/shard_map/all_to_all | solution.py:309
  123.8 2.2 %collective-permute-start.6 = (bf16[640,128]{1,0:T(8,128)(2,1)S(1)}, bf16[640,128]{1,0:T(8,128)(2,1)S(1)}, u32[]{:S(2)}, u32[]{:S(2)}) collective-permute-start(bf16[640,128]{1,0:T(8,128)(2,1)S(1)} %slice.20.own_ref), channel_id=1, source_target_pairs={{0,1},{1,0},{2,3},{3,2},{4,5},{5,4},{6,7},{7,6},{8,9},{9,8},{10,11... | collective-permute-start | bytes 491528 | tf_op jit(solution)/shard_map/ppermute | solution.py:473
  126.0 7.0 %collective-permute-done.6.other_ref = bf16[640,128]{1,0:T(8,128)(2,1)S(1)} collective-permute-done((bf16[640,128]{1,0:T(8,128)(2,1)S(1)}, bf16[640,128]{1,0:T(8,128)(2,1)S(1)}, u32[]{:S(2)}, u32[]{:S(2)}) %collective-permute-start.6) | collective-permute-done | bytes 163872 | tf_op jit(solution)/shard_map/ppermute | solution.py:473
  133.0 0.8 all-to-all-done.6.got_ref
  133.8 8.8 %collective-permute-start.7 = (bf16[8,416,128]{2,1,0:T(8,128)(2,1)S(1)}, bf16[8,416,128]{2,1,0:T(8,128)(2,1)S(1)}, u32[]{:S(2)}, u32[]{:S(2)}) collective-permute-start(bf16[8,416,128]{2,1,0:T(8,128)(2,1)S(1)} %all-to-all-done.6.got_ref), channel_id=1, source_target_pairs={{0,32},{32,0},{1,33},{33,1},{2,34},{34,2},{3,35},{35,3},{4,36},{36... | collective-permute-start | bytes 2555912 | tf_op jit(solution)/shard_map/ppermute | solution.py:477
  142.6 1.4 conv2_unpack.1
  144.0 0.6 collective-permute-done.7.cross_ref
  144.6 2.8 %gradient_unpack.1 = (f32[384,1280]{1,0:T(8,128)}, f32[1280]{0:T(1024)}, f32[640]{0:T(1024)}, bf16[256,640]{1,0:T(8,128)(2,1)}) custom-call(s32[4]{0:T(128)S(1)} %pad_add_fusion.where_ref, bf16[8,416,128]{2,1,0:T(8,128)(2,1)S(1)} %all-to-all-done.6.got_ref, bf16[8,416,128]{2,1,0:T(8,128)(2,1)S(1)} %collective-permute-done.7.cross_ref), custom_call_target="tpu_custom_call" | custom-call | tf_op jit(solution)/shard_map/gradient_unpack/pallas_call | solution.py:486
  (29 shorter events, 0.1 us)
Async XLA Ops:
  0.6 20.6 %copy-start = (bf16[80,1920]{1,0:T(8,128)(2,1)S(1)}, bf16[80,1920]{1,0:T(8,128)(2,1)}, u32[]{:S(2)}) copy-start(bf16[80,1920]{1,0:T(8,128)(2,1)} %own_ref.3) | copy-start | bytes 921604
  0.6 19.1 %copy-start.9 = (bf16[384,1280]{1,0:T(8,128)(2,1)S(1)}, bf16[384,1280]{1,0:T(8,128)(2,1)}, u32[]{:S(2)}) copy-start(bf16[384,1280]{1,0:T(8,128)(2,1)} %weight_ref.1) | copy-start | bytes 2949124
  0.7 16.1 %collective-permute-start.1 = (bf16[80,1920]{1,0:T(8,128)(2,1)}, bf16[80,1920]{1,0:T(8,128)(2,1)S(1)}, u32[]{:S(2)}, u32[]{:S(2)}) collective-permute-start(bf16[80,1920]{1,0:T(8,128)(2,1)} %own_ref.3), channel_id=1, source_target_pairs={{0,257},{257,0},{1,256},{256,1},{2,259},{259,2},{3,258},{258,3},{4... | collective-permute-start | bytes 921608 | tf_op jit(solution)/shard_map/ppermute | solution.py:347
  7.7 13.5 %all-to-all-start = ((bf16[4,26,16,128]{3,2,1,0:T(8,128)(2,1)}), bf16[4,26,16,128]{3,2,1,0:T(8,128)(2,1)S(1)}, u32[]{:S(2)}, u32[]{:S(2)}) async-start(bf16[4,26,16,128]{3,2,1,0:T(8,128)(2,1)} %mel_payload.1), calls=%async_computation | async-start | bytes 851968 | tf_op jit(solution)/shard_map/all_to_all | solution.py:309
  11.9 9.2 %collective-permute-start = (bf16[80,1920]{1,0:T(8,128)(2,1)}, bf16[80,1920]{1,0:T(8,128)(2,1)S(1)}, u32[]{:S(2)}, u32[]{:S(2)}) collective-permute-start(bf16[80,1920]{1,0:T(8,128)(2,1)} %own_ref.3), channel_id=1, source_target_pairs={{0,32},{32,0},{1,33},{33,1},{2,34},{34,2},{3,35},{35,3},{4,36},{36... | collective-permute-start | bytes 921608 | tf_op jit(solution)/shard_map/ppermute | solution.py:362
  16.7 4.4 %collective-permute-start.2 = (bf16[80,1920]{1,0:T(8,128)(2,1)S(1)}, bf16[80,1920]{1,0:T(8,128)(2,1)S(1)}, u32[]{:S(2)}, u32[]{:S(2)}) collective-permute-start(bf16[80,1920]{1,0:T(8,128)(2,1)S(1)} %collective-permute-done.1.far_ref), channel_id=1, source_target_pairs={{0,32},{32,0},{1,33},{33,1},{2,34},{34,2},{3,35},{35,3},{4,36},{36... | collective-permute-start | bytes 921608 | tf_op jit(solution)/shard_map/ppermute | solution.py:364
  21.1 3.5 %copy-start.7 = (bf16[384,384]{1,0:T(8,128)(2,1)}, bf16[384,384]{1,0:T(8,128)(2,1)S(1)}, u32[]{:S(2)}) copy-start(bf16[384,384]{1,0:T(8,128)(2,1)S(1)} %get-tuple-element.27.w1_ref) | copy-start | bytes 884740
  21.2 3.4 %copy-start.1 = (bf16[80,1920]{1,0:T(8,128)(2,1)}, bf16[80,1920]{1,0:T(8,128)(2,1)S(1)}, u32[]{:S(2)}) copy-start(bf16[80,1920]{1,0:T(8,128)(2,1)S(1)} %collective-permute-done.side_ref) | copy-start | bytes 921604
  21.2 3.4 %copy-start.3 = (bf16[80,1920]{1,0:T(8,128)(2,1)}, bf16[80,1920]{1,0:T(8,128)(2,1)S(1)}, u32[]{:S(2)}) copy-start(bf16[80,1920]{1,0:T(8,128)(2,1)S(1)} %collective-permute-done.2.both_ref) | copy-start | bytes 921604
  21.2 6.9 %copy-start.11 = (s32[16]{0:T(128)S(1)}, s32[16]{0:T(128)}, u32[]{:S(2)}) copy-start(s32[16]{0:T(128)} %length_ref.1) | copy-start | bytes 196
  21.2 6.9 %copy-start.12 = (s32[16,1]{0,1:T(1,128)S(1)}, s32[16,1]{0,1:T(1,128)}, u32[]{:S(2)}) copy-start(s32[16,1]{0,1:T(1,128)} %param.10) | copy-start | bytes 196
  21.2 7.2 %copy-start.10 = (f32[640]{0:T(1024)S(1)}, f32[640]{0:T(1024)}, u32[]{:S(2)}) copy-start(f32[640]{0:T(1024)} %param.14) | copy-start | bytes 7684
  24.6 13.4 %all-to-all-start.1 = ((bf16[4,128,640]{2,1,0:T(8,128)(2,1)}), bf16[4,128,640]{2,1,0:T(8,128)(2,1)S(1)}, u32[]{:S(2)}, u32[]{:S(2)}) async-start(bf16[4,128,640]{2,1,0:T(8,128)(2,1)} %stem_forward.1), calls=%async_computation.1 | async-start | bytes 1310720 | tf_op jit(solution)/shard_map/all_to_all | solution.py:309
  28.4 1.0 copy-start.8
  33.2 1.0 copy-start.5
  34.2 16.7 %copy-start.2 = (bf16[80,1920]{1,0:T(8,128)(2,1)S(1)}, bf16[80,1920]{1,0:T(8,128)(2,1)}, u32[]{:S(2)}) copy-start(bf16[80,1920]{1,0:T(8,128)(2,1)} %copy-done.1) | copy-start | bytes 921604
  38.0 12.8 %copy-start.4 = (bf16[80,1920]{1,0:T(8,128)(2,1)S(1)}, bf16[80,1920]{1,0:T(8,128)(2,1)}, u32[]{:S(2)}) copy-start(bf16[80,1920]{1,0:T(8,128)(2,1)} %copy-done.3) | copy-start | bytes 921604
  38.0 12.8 %copy-start.6 = (bf16[3,384,512]{2,1,0:T(8,128)(2,1)S(1)}, bf16[3,384,512]{2,1,0:T(8,128)(2,1)}, u32[]{:S(2)}) copy-start(bf16[3,384,512]{2,1,0:T(8,128)(2,1)} %copy-done.5) | copy-start | bytes 3538948
  54.3 7.1 %collective-permute-start.3 = (bf16[2,2,896,128]{3,2,1,0:T(8,128)(2,1)S(1)}, bf16[2,2,896,128]{3,2,1,0:T(8,128)(2,1)S(1)}, u32[]{:S(2)}, u32[]{:S(2)}) collective-permute-start(bf16[2,2,896,128]{3,2,1,0:T(8,128)(2,1)S(1)} %get-tuple-element.41), channel_id=1, source_target_pairs={{0,32},{32,0},{1,33},{33,1},{2,34},{34,2},{3,35},{35,3},{4,36},{36... | collective-permute-start | bytes 2752520 | tf_op jit(solution)/shard_map/ppermute | solution.py:443
  87.7 11.6 %collective-permute-start.4 = (bf16[224,128]{1,0:T(8,128)(2,1)S(1)}, bf16[224,128]{1,0:T(8,128)(2,1)S(1)}, u32[]{:S(2)}, u32[]{:S(2)}) collective-permute-start(bf16[224,128]{1,0:T(8,128)(2,1)S(1)} %gradient_sum.3.own_ref), channel_id=1, source_target_pairs={{0,8},{8,0},{16,24},{24,16},{1,9},{9,1},{17,25},{25,17},{2,10},{10... | collective-permute-start | bytes 172040 | tf_op jit(solution)/shard_map/ppermute | solution.py:468
  99.3 9.5 %collective-permute-start.5 = (bf16[224,128]{1,0:T(8,128)(2,1)S(1)}, bf16[224,128]{1,0:T(8,128)(2,1)S(1)}, u32[]{:S(2)}, u32[]{:S(2)}) collective-permute-start(bf16[224,128]{1,0:T(8,128)(2,1)S(1)} %gradient_pair.2.own_ref), channel_id=1, source_target_pairs={{0,24},{8,16},{16,8},{24,0},{1,25},{9,17},{17,9},{25,1},{2,26},{10... | collective-permute-start | bytes 172040 | tf_op jit(solution)/shard_map/ppermute | solution.py:468
  120.2 13.5 %all-to-all-start.6 = ((bf16[8,416,128]{2,1,0:T(8,128)(2,1)}), bf16[8,416,128]{2,1,0:T(8,128)(2,1)S(1)}, u32[]{:S(2)}, u32[]{:S(2)}) async-start(bf16[8,416,128]{2,1,0:T(8,128)(2,1)} %pad_maximum_fusion), calls=%async_computation.6 | async-start | bytes 1703936 | tf_op jit(solution)/shard_map/all_to_all | solution.py:309
  123.8 9.1 %collective-permute-start.6 = (bf16[640,128]{1,0:T(8,128)(2,1)S(1)}, bf16[640,128]{1,0:T(8,128)(2,1)S(1)}, u32[]{:S(2)}, u32[]{:S(2)}) collective-permute-start(bf16[640,128]{1,0:T(8,128)(2,1)S(1)} %slice.20.own_ref), channel_id=1, source_target_pairs={{0,1},{1,0},{2,3},{3,2},{4,5},{5,4},{6,7},{7,6},{8,9},{9,8},{10,11... | collective-permute-start | bytes 491528 | tf_op jit(solution)/shard_map/ppermute | solution.py:473
  133.8 10.8 %collective-permute-start.7 = (bf16[8,416,128]{2,1,0:T(8,128)(2,1)S(1)}, bf16[8,416,128]{2,1,0:T(8,128)(2,1)S(1)}, u32[]{:S(2)}, u32[]{:S(2)}) collective-permute-start(bf16[8,416,128]{2,1,0:T(8,128)(2,1)S(1)} %all-to-all-done.6.got_ref), channel_id=1, source_target_pairs={{0,32},{32,0},{1,33},{33,1},{2,34},{34,2},{3,35},{35,3},{4,36},{36... | collective-permute-start | bytes 2555912 | tf_op jit(solution)/shard_map/ppermute | solution.py:477

commit v13 on v12

--- a/solution.py
+++ b/solution.py
@@ -249,21 +249,19 @@
     total = got_ref[0].astype(F32)
     for source in range(1, got_ref.shape[0]):
         total = total + got_ref[source].astype(F32)
-    total = total.astype(BF16)
-    if len(out_ref.shape) == 2:
-        out_ref[...] = total
-    else:
-        for target in range(out_ref.shape[0]):
-            out_ref[target] = total
+    out_ref[...] = total.astype(BF16)
+
+
+def split_kernel(got_ref, conv2_ref, conv1_ref):
+    total = got_ref[0].astype(F32)
+    for source in range(1, got_ref.shape[0]):
+        total = total + got_ref[source].astype(F32)
+    conv2_ref[...] = total[:HALF_ROWS].astype(BF16)
+    conv1_ref[...] = total[HALF_ROWS:].astype(BF16)
 
 
 def pair_kernel(own_ref, other_ref, out_ref):
-    total = (own_ref[...].astype(F32) + other_ref[...].astype(F32)).astype(BF16)
-    if len(out_ref.shape) == 2:
-        out_ref[...] = total
-    else:
-        for target in range(out_ref.shape[0]):
-            out_ref[target] = total
+    out_ref[...] = (own_ref[...].astype(F32) + other_ref[...].astype(F32)).astype(BF16)
 
 
 def last_kernel(
@@ -295,14 +293,17 @@
         bias2_ref[...] = bias2.reshape(D2)
 
 
-def unpack_kernel(where_ref, own_ref, other_ref, conv2_ref):
-    lower = where_ref[1] == 0
-    for tile in range(15):
-        half, spot = tile // 8, tile % 8
-        rows = slice(spot * ROWS, (spot + 1) * ROWS)
-        own, other = own_ref[rows, :].astype(F32), other_ref[rows, :].astype(F32)
-        picked = jnp.where(lower, own, other) if half == 0 else jnp.where(lower, other, own)
-        conv2_ref[:, tile * LANES : (tile + 1) * LANES] = picked
+def unpack_kernel(where_ref, own_ref, first_ref, second_ref, third_ref, conv2_ref):
+    for flip, ref in enumerate((own_ref, first_ref, second_ref, third_ref)):
+        for side in range(2):
+            for spot in range(2):
+                tile = 8 * (where_ref[1] ^ side) + 2 * (where_ref[4] ^ flip) + spot
+                rows = slice((2 * side + spot) * ROWS, (2 * side + spot + 1) * ROWS)
+
+                @pl.when(tile < 15)
+                def _(ref=ref, rows=rows, tile=tile):
+                    lanes = pl.ds(pl.multiple_of(tile * LANES, LANES), LANES)
+                    conv2_ref[:, lanes] = ref[rows, :].astype(F32)
 
 
 def exchange(values, axes):
@@ -323,7 +324,8 @@
 
 def local(mel, lengths, routes, conv1_weight, conv1_bias, conv2_weight, conv2_bias, out_grad):
     x_hi, y, core = lax.axis_index("xh"), lax.axis_index("y"), lax.axis_index("c")
-    where = jnp.stack([x_hi, lax.axis_index("xl"), core, (x_hi * HOLDERS + y) * 2 + core]).astype(jnp.int32)
+    where = jnp.stack([x_hi, lax.axis_index("xl"), core, (x_hi * HOLDERS + y) * 2 + core, lax.axis_index("zl")])
+    where = where.astype(jnp.int32)
 
     def shape(*dims, dtype=BF16):
         return jax.ShapeDtypeStruct(dims, dtype)
@@ -443,46 +445,52 @@
     got = lax.ppermute(send, "c", cores)
     quarters = exchange((keep + got.astype(F32)).astype(BF16).reshape(4, PACK, LANES), ("xh", "xl"))
 
-    def summed(values, *dims):
-        return pl.pallas_call(
-            sum_kernel,
-            in_specs=[vmem()],
-            out_specs=vmem(),
-            out_shape=shape(*dims),
-            compiler_params=params(8),
-            name="gradient_sum",
-        )(values)
-
-    half = summed(quarters, PACK, LANES)
-    quarter = PACK // 4
-    near = summed(exchange(half.reshape(4, quarter, LANES), "zl"), quarter, LANES)
-
-    def with_group(values, flip, *dims):
+    def with_other(values, axis, flip):
         return pl.pallas_call(
             pair_kernel,
             in_specs=[vmem()] * 2,
             out_specs=vmem(),
-            out_shape=shape(*dims),
+            out_shape=shape(*values.shape),
             compiler_params=params(8),
             name="gradient_pair",
-        )(values, lax.ppermute(values, "zh", [(i, i ^ flip) for i in range(4)]))
-
-    far = with_group(with_group(near, 1, quarter, LANES), 3, 4, quarter, LANES)
-    half = exchange(far, "zl").reshape(PACK, LANES)
-    own = half[:HALF_ROWS]
-    other = lax.ppermute(own, "xl", [(0, 1), (1, 0)])
-    conv1 = spread_to(half[HALF_ROWS:], CHIPS)
+        )(values, lax.ppermute(values, axis, [(i, i ^ flip) for i in range(4)]))
+
+    conv2, conv1 = pl.pallas_call(
+        split_kernel,
+        in_specs=[vmem()],
+        out_specs=[vmem()] * 2,
+        out_shape=[shape(HALF_ROWS, LANES), shape(PACK - HALF_ROWS, LANES)],
+        compiler_params=params(8),
+        name="gradient_sum",
+    )(quarters)
+    quarter = HALF_ROWS // 4
+    conv2 = exchange(conv2.reshape(4, quarter, LANES), "zl")
+    conv2 = pl.pallas_call(
+        sum_kernel,
+        in_specs=[vmem()],
+        out_specs=vmem(),
+        out_shape=shape(quarter, LANES),
+        compiler_params=params(8),
+        name="gradient_sum",
+    )(conv2)
+    conv1 = with_other(with_other(conv1, "zl", 1), "zl", 2)
+    conv2 = with_other(with_other(conv2, "zh", 1), "zh", 3)
+    conv1 = with_other(with_other(conv1, "zh", 1), "zh", 3)
+    conv2 = jnp.concatenate([conv2, lax.ppermute(conv2, "xl", [(0, 1), (1, 0)])], axis=0)
+    conv2, conv1 = lax.optimization_barrier((conv2, conv1))
+    others = [lax.ppermute(conv2, "zl", [(i, i ^ flip) for i in range(4)]) for flip in (1, 2, 3)]
+    conv1 = spread_to(conv1, CHIPS)
     got = exchange(jnp.concatenate([same, conv1[:, : 3 * ROWS], cross, conv1[:, 3 * ROWS :]], axis=1), ("xh", "y"))
-    got, other = lax.optimization_barrier((got, other))
+    got, *others = lax.optimization_barrier((got, *others))
     got_cross = lax.ppermute(got, "c", cores)
     conv2_rows_grad = pl.pallas_call(
         unpack_kernel,
-        in_specs=[pl.BlockSpec(memory_space=pltpu.SMEM), vmem(), vmem()],
+        in_specs=[pl.BlockSpec(memory_space=pltpu.SMEM), *[vmem()] * 4],
         out_specs=vmem(),
         out_shape=in_hbm(ROWS, 3 * D2, dtype=F32),
         compiler_params=params(8),
         name="conv2_unpack",
-    )(where, own, other)
+    )(where, conv2, *others)
     weight_grad, bias_grad, second_bias_grad, packed = pl.pallas_call(
         last_kernel,
         grid=(3,),

time: 148 us -> 163 us (1.10)
  starting transfers between devices: 56.4 us -> 80.5 us
  blocking collectives: 47.3 us -> 27.9 us
  waiting for transfers between devices: 19.3 us -> 27.7 us
    ppermute x3 -> x10, starting transfers between devices: 18.2 us -> 40 us  [the longest x6 26.8 us: with_other(): lax.ppermute(values, axis, [(i, i ^ flip) for i in range(4)])]
    all_to_all x4 -> x2, blocking collectives: 47.3 us -> 27.9 us  [exchange(): return lax.all_to_all(values, axes, split_axis=0, concat_axis=0, tiled=True)]
    ppermute x3 -> x10, waiting for transfers between devices: 12 us -> 21.4 us  [the longest x6 16.9 us: with_other(): lax.ppermute(values, axis, [(i, i ^ flip) for i in range(4)])]
    all_to_all x3 -> x4, starting transfers between devices: 11.2 us -> 14.6 us  [exchange(): return lax.all_to_all(values, axes, split_axis=0, concat_axis=0, tiled=True)]
    all_to_all x3 -> x4, waiting for transfers between devices: 4.63 us -> 3.82 us  [exchange(): return lax.all_to_all(values, axes, split_axis=0, concat_axis=0, tiled=True)]
  transfers between devices with their start and end apart: 11 -> 19, of which waited for: 7 -> 9; matrix products, arithmetic and copies ran while one was open for 0% -> 0% of each run, Pallas kernels for 6% -> 5%
where the time goes in v13:
time: 163 us; the launch traced here: 161 us
  starting transfers between devices  80.5 us (49%)
  blocking collectives  27.9 us (17%)
  waiting for transfers between devices  27.7 us (17%)
  Pallas kernels  20.6 us (13%)
  local copies, waits for them, and re-layouts  2.44 us (1%)
    all_to_all x2, blocking collectives, exchange(): return lax.all_to_all(values, axes, split_axis=0, concat_axis=0, tiled=True)  27.9 us
    ppermute x6, starting transfers between devices, with_other(): lax.ppermute(values, axis, [(i, i ^ flip) for i in range(4)])  26.8 us
    ppermute x6, waiting for transfers between devices, with_other(): lax.ppermute(values, axis, [(i, i ^ flip) for i in range(4)])  16.9 us
    all_to_all x4, starting transfers between devices, exchange(): return lax.all_to_all(values, axes, split_axis=0, concat_axis=0, tiled=True)  14.6 us
    ppermute x3, starting transfers between devices, local(): lax.ppermute(conv2, 'zl', [(i, i ^ flip) for i in range(4)])  11 us
    ppermute x1, starting transfers between devices, local(): got_cross = lax.ppermute(got, 'c', cores)  7.65 us
    ppermute x1, starting transfers between devices, local(): lax.ppermute(conv2_weight, ('xh', 'xl'), [(0, 3), (3, 0), (1, 2), (2, 1)])  5.35 us
    ppermute x1, starting transfers between devices, local(): got = lax.ppermute(send, 'c', cores)  5.06 us
  transfers between devices with their start and end apart: 19, of which 9 were waited for; matrix products, arithmetic and copies ran while one was open for 0% of the time, Pallas kernels for 5%

profile of v13, /device:TPU:1, one launch (start us, length us, event | category | flops | bytes accessed | tf_op | source)
XLA Modules:
  0.0 161.5 jit_solution(2687872874426341233)
XLA Ops:
  0.7 5.3 %collective-permute-start.1 = (bf16[80,1920]{1,0:T(8,128)(2,1)}, bf16[80,1920]{1,0:T(8,128)(2,1)S(1)}, u32[]{:S(2)}, u32[]{:S(2)}) collective-permute-start(bf16[80,1920]{1,0:T(8,128)(2,1)} %own_ref.3), channel_id=1, source_target_pairs={{0,257},{257,0},{1,256},{256,1},{2,259},{259,2},{3,258},{258,3},{4... | collective-permute-start | bytes 921608 | tf_op jit(solution)/shard_map/ppermute | solution.py:349
  6.0 1.7 %mel_payload.1 = bf16[4,26,16,128]{3,2,1,0:T(8,128)(2,1)} custom-call(s32[16]{0:T(128)} %length_ref.1, bf16[16,16,128]{2,1,0:T(8,128)(2,1)} %mel_ref.1), custom_call_target="tpu_custom_call" | custom-call | tf_op jit(solution)/shard_map/mel_payload/pallas_call | solution.py:339
  7.7 4.2 %all-to-all-start = ((bf16[4,26,16,128]{3,2,1,0:T(8,128)(2,1)}), bf16[4,26,16,128]{3,2,1,0:T(8,128)(2,1)S(1)}, u32[]{:S(2)}, u32[]{:S(2)}) async-start(bf16[4,26,16,128]{3,2,1,0:T(8,128)(2,1)} %mel_payload.1), calls=%async_computation | async-start | bytes 851968 | tf_op jit(solution)/shard_map/all_to_all | solution.py:310
  11.9 0.1 stack.23.where_ref
  11.9 4.8 %collective-permute-start = (bf16[80,1920]{1,0:T(8,128)(2,1)}, bf16[80,1920]{1,0:T(8,128)(2,1)S(1)}, u32[]{:S(2)}, u32[]{:S(2)}) collective-permute-start(bf16[80,1920]{1,0:T(8,128)(2,1)} %own_ref.3), channel_id=1, source_target_pairs={{0,32},{32,0},{1,33},{33,1},{2,34},{34,2},{3,35},{35,3},{4,36},{36... | collective-permute-start | bytes 921608 | tf_op jit(solution)/shard_map/ppermute | solution.py:364
  16.7 3.0 %collective-permute-start.2 = (bf16[80,1920]{1,0:T(8,128)(2,1)S(1)}, bf16[80,1920]{1,0:T(8,128)(2,1)S(1)}, u32[]{:S(2)}, u32[]{:S(2)}) collective-permute-start(bf16[80,1920]{1,0:T(8,128)(2,1)S(1)} %collective-permute-done.1.far_ref), channel_id=1, source_target_pairs={{0,32},{32,0},{1,33},{33,1},{2,34},{34,2},{3,35},{35,3},{4,36},{36... | collective-permute-start | bytes 921608 | tf_op jit(solution)/shard_map/ppermute | solution.py:366
  19.8 1.4 conv1_columns.1
  21.2 3.4 %stem_forward.1 = bf16[4,128,640]{2,1,0:T(8,128)(2,1)} custom-call(bf16[4,26,16,128]{3,2,1,0:T(8,128)(2,1)S(1)} %all-to-all-done.pay_ref, bf16[384,384]{1,0:T(8,128)(2,1)S(1)} %get-tuple-element.33.w1_ref, f32[1,384]{1,0:T(1,128)S(1)} %get-tuple-element.34.b1_ref, bf16[80,1920]{1,0:T(8,128)(2,1)S(1)} %copy-done, ...), custom_call_target="tpu_custom_call" | custom-call | tf_op jit(solution)/shard_map/stem_forward/pallas_call | solution.py:374
  24.6 3.5 %all-to-all-start.1 = ((bf16[4,128,640]{2,1,0:T(8,128)(2,1)}), bf16[4,128,640]{2,1,0:T(8,128)(2,1)S(1)}, u32[]{:S(2)}, u32[]{:S(2)}) async-start(bf16[4,128,640]{2,1,0:T(8,128)(2,1)} %stem_forward.1), calls=%async_computation.1 | async-start | bytes 1310720 | tf_op jit(solution)/shard_map/all_to_all | solution.py:310
  28.2 0.1 broadcast_in_dim.14
  28.2 0.1 broadcast_in_dim_reshape.7.row_ref
  28.3 0.1 broadcast_in_dim_reshape.8.column_ref
  28.4 1.0 copy-done.8
  29.4 3.8 %stem_slopes.1 = (bf16[512,512]{1,0:T(8,128)(2,1)}, f32[2,512,384]{2,1,0:T(8,128)S(1)}, bf16[3,384,512]{2,1,0:T(8,128)(2,1)S(1)}, bf16[128,640]{1,0:T(8,128)(2,1)}, bf16[256,128]{1,0:T(8,128)(2,1)S(1)}) custom-call(bf16[4,26,16,128]{3,2,1,0:T(8,128)(2,1)S(1)} %all-to-all-done.pay_ref, bf16[384,384]{1,0:T(8,128)(2,1)S(1)} %copy-done.8, ...), custom_call_target="tpu_custom_call" | custom-call | tf_op jit(solution)/shard_map/stem_slopes/pallas_call | solution.py:391
  33.2 1.0 copy-done.5
  34.2 3.8 %all-to-all-done.1.part_ref = bf16[4,128,640]{2,1,0:T(8,128)(2,1)S(1)} async-done(((bf16[4,128,640]{2,1,0:T(8,128)(2,1)}), bf16[4,128,640]{2,1,0:T(8,128)(2,1)S(1)}, u32[]{:S(2)}, u32[]{:S(2)}) %all-to-all-start.1) | async-done | bytes 655392 | tf_op jit(solution)/shard_map/all_to_all | solution.py:310
  38.0 1.7 %stem_middle.1 = (bf16[4,128,640]{2,1,0:T(8,128)(2,1)S(1)}, bf16[8,80,128]{2,1,0:T(8,128)(2,1)S(1)}, bf16[8,80,128]{2,1,0:T(8,128)(2,1)S(1)}) custom-call(s32[5]{0:T(128)S(1)} %stack.23.where_ref, bf16[4,128,640]{2,1,0:T(8,128)(2,1)S(1)} %all-to-all-done.1.part_ref, f32[1,640]{1,0:T(1,128)S(1)} %broadcast_in_dim.15.b2_ref, ...), custom_call_target="tpu_custom_call" | custom-call | tf_op jit(solution)/shard_map/stem_middle/pallas_call | solution.py:414
  39.8 11.1 %all_to_all.30.grad_ref = bf16[4,128,640]{2,1,0:T(8,128)(2,1)S(1)} all-to-all(bf16[4,128,640]{2,1,0:T(8,128)(2,1)S(1)} %get-tuple-element.42), channel_id=1, replica_groups=mesh['xh'=2,'y'=4,'c'=2,'zh'=4,'zl'=4,'xl'=2] {'y'}, dimensions={0} | all-to-all | bytes 1310720 | tf_op jit(solution)/shard_map/all_to_all | solution.py:310
  50.9 3.4 %stem_backward.1 = (f32[2,2,896,128]{3,2,1,0:T(8,128)S(1)}, bf16[2,2,896,128]{3,2,1,0:T(8,128)(2,1)S(1)}) custom-call(s32[5]{0:T(128)S(1)} %stack.23.where_ref, bf16[4,128,640]{2,1,0:T(8,128)(2,1)S(1)} %all_to_all.30.grad_ref, bf16[80,1920]{1,0:T(8,128)(2,1)S(1)} %copy-done, bf16[80,1920]{1,0:T(8,128)(2,1)S(1)} %copy-done.2, ...), custom_call_target="tpu_custom_call" | custom-call | tf_op jit(solution)/shard_map/stem_backward/pallas_call | solution.py:425
  54.4 5.1 %collective-permute-start.3 = (bf16[2,2,896,128]{3,2,1,0:T(8,128)(2,1)S(1)}, bf16[2,2,896,128]{3,2,1,0:T(8,128)(2,1)S(1)}, u32[]{:S(2)}, u32[]{:S(2)}) collective-permute-start(bf16[2,2,896,128]{3,2,1,0:T(8,128)(2,1)S(1)} %get-tuple-element.47), channel_id=1, source_target_pairs={{0,32},{32,0},{1,33},{33,1},{2,34},{34,2},{3,35},{35,3},{4,36},{36... | collective-permute-start | bytes 2752520 | tf_op jit(solution)/shard_map/ppermute | solution.py:445
  59.4 2.1 %collective-permute-done.3 = bf16[2,2,896,128]{3,2,1,0:T(8,128)(2,1)S(1)} collective-permute-done((bf16[2,2,896,128]{3,2,1,0:T(8,128)(2,1)S(1)}, bf16[2,2,896,128]{3,2,1,0:T(8,128)(2,1)S(1)}, u32[]{:S(2)}, u32[]{:S(2)}) %collective-permute-start.3) | collective-permute-done | bytes 917536 | tf_op jit(solution)/shard_map/ppermute | solution.py:445
  61.5 0.2 add_convert_fusion
  61.7 16.8 %all_to_all.31.got_ref = bf16[4,896,128]{2,1,0:T(8,128)(2,1)S(1)} all-to-all(bf16[4,896,128]{2,1,0:T(8,128)(2,1)S(1)} %bitcast.11), channel_id=1, replica_groups=mesh['xh'=2,'y'=4,'c'=2,'zh'=4,'zl'=4,'xl'=2] {'xh','xl'}, dimensions={0} | all-to-all | bytes 1835008 | tf_op jit(solution)/shard_map/all_to_all | solution.py:310
  78.6 0.7 gradient_sum.2
  79.3 3.4 %all-to-all-start.4 = ((bf16[4,160,128]{2,1,0:T(8,128)(2,1)}), bf16[4,160,128]{2,1,0:T(8,128)(2,1)S(1)}, u32[]{:S(2)}, u32[]{:S(2)}) async-start(bf16[4,160,128]{2,1,0:T(8,128)(2,1)} %bitcast.8), calls=%async_computation.4 | async-start | bytes 327680 | tf_op jit(solution)/shard_map/all_to_all | solution.py:310
  82.7 3.4 %collective-permute-start.7 = (bf16[256,128]{1,0:T(8,128)(2,1)S(1)}, bf16[256,128]{1,0:T(8,128)(2,1)S(1)}, u32[]{:S(2)}, u32[]{:S(2)}) collective-permute-start(bf16[256,128]{1,0:T(8,128)(2,1)S(1)} %get-tuple-element.49.own_ref), channel_id=1, source_target_pairs={{0,2},{2,0},{4,6},{6,4},{1,3},{3,1},{5,7},{7,5},{8,10},{10,8},{12,... | collective-permute-start | bytes 196616 | tf_op jit(solution)/shard_map/ppermute | solution.py:456
  86.1 2.8 %collective-permute-done.7.other_ref = bf16[256,128]{1,0:T(8,128)(2,1)S(1)} collective-permute-done((bf16[256,128]{1,0:T(8,128)(2,1)S(1)}, bf16[256,128]{1,0:T(8,128)(2,1)S(1)}, u32[]{:S(2)}, u32[]{:S(2)}) %collective-permute-start.7) | collective-permute-done | bytes 65568 | tf_op jit(solution)/shard_map/ppermute | solution.py:456
  88.9 3.5 %collective-permute-start.8 = (bf16[256,128]{1,0:T(8,128)(2,1)S(1)}, bf16[256,128]{1,0:T(8,128)(2,1)S(1)}, u32[]{:S(2)}, u32[]{:S(2)}) collective-permute-start(bf16[256,128]{1,0:T(8,128)(2,1)S(1)} %gradient_pair.8.own_ref), channel_id=1, source_target_pairs={{0,4},{2,6},{4,0},{6,2},{1,5},{3,7},{5,1},{7,3},{8,12},{10,14},{12... | collective-permute-start | bytes 196616 | tf_op jit(solution)/shard_map/ppermute | solution.py:456
  92.5 2.4 %collective-permute-done.8.other_ref = bf16[256,128]{1,0:T(8,128)(2,1)S(1)} collective-permute-done((bf16[256,128]{1,0:T(8,128)(2,1)S(1)}, bf16[256,128]{1,0:T(8,128)(2,1)S(1)}, u32[]{:S(2)}, u32[]{:S(2)}) %collective-permute-start.8) | collective-permute-done | bytes 65568 | tf_op jit(solution)/shard_map/ppermute | solution.py:456
  94.9 8.8 %collective-permute-start.9 = (bf16[256,128]{1,0:T(8,128)(2,1)S(1)}, bf16[256,128]{1,0:T(8,128)(2,1)S(1)}, u32[]{:S(2)}, u32[]{:S(2)}) collective-permute-start(bf16[256,128]{1,0:T(8,128)(2,1)S(1)} %gradient_pair.9.own_ref), channel_id=1, source_target_pairs={{0,8},{8,0},{16,24},{24,16},{1,9},{9,1},{17,25},{25,17},{2,10},{10... | collective-permute-start | bytes 196616 | tf_op jit(solution)/shard_map/ppermute | solution.py:456
  103.7 1.9 %collective-permute-start.4 = (bf16[160,128]{1,0:T(8,128)(2,1)S(1)}, bf16[160,128]{1,0:T(8,128)(2,1)S(1)}, u32[]{:S(2)}, u32[]{:S(2)}) collective-permute-start(bf16[160,128]{1,0:T(8,128)(2,1)S(1)} %gradient_sum.3.own_ref), channel_id=1, source_target_pairs={{0,8},{8,0},{16,24},{24,16},{1,9},{9,1},{17,25},{25,17},{2,10},{10... | collective-permute-start | bytes 122888 | tf_op jit(solution)/shard_map/ppermute | solution.py:456
  105.7 8.3 %collective-permute-done.4.other_ref = bf16[160,128]{1,0:T(8,128)(2,1)S(1)} collective-permute-done((bf16[160,128]{1,0:T(8,128)(2,1)S(1)}, bf16[160,128]{1,0:T(8,128)(2,1)S(1)}, u32[]{:S(2)}, u32[]{:S(2)}) %collective-permute-start.4) | collective-permute-done | bytes 40992 | tf_op jit(solution)/shard_map/ppermute | solution.py:456
  114.0 5.7 %collective-permute-start.5 = (bf16[160,128]{1,0:T(8,128)(2,1)S(1)}, bf16[160,128]{1,0:T(8,128)(2,1)S(1)}, u32[]{:S(2)}, u32[]{:S(2)}) collective-permute-start(bf16[160,128]{1,0:T(8,128)(2,1)S(1)} %gradient_pair.6.own_ref), channel_id=1, source_target_pairs={{0,24},{8,16},{16,8},{24,0},{1,25},{9,17},{17,9},{25,1},{2,26},{10... | collective-permute-start | bytes 122888 | tf_op jit(solution)/shard_map/ppermute | solution.py:456
  119.7 3.5 %collective-permute-start.10 = (bf16[256,128]{1,0:T(8,128)(2,1)S(1)}, bf16[256,128]{1,0:T(8,128)(2,1)S(1)}, u32[]{:S(2)}, u32[]{:S(2)}) collective-permute-start(bf16[256,128]{1,0:T(8,128)(2,1)S(1)} %gradient_pair.10.own_ref), channel_id=1, source_target_pairs={{0,24},{8,16},{16,8},{24,0},{1,25},{9,17},{17,9},{25,1},{2,26},{10... | collective-permute-start | bytes 196616 | tf_op jit(solution)/shard_map/ppermute | solution.py:456
  123.3 2.2 %collective-permute-start.6 = (bf16[160,128]{1,0:T(8,128)(2,1)S(1)}, bf16[160,128]{1,0:T(8,128)(2,1)S(1)}, u32[]{:S(2)}, u32[]{:S(2)}) collective-permute-start(bf16[160,128]{1,0:T(8,128)(2,1)S(1)} %gradient_pair.7), channel_id=1, source_target_pairs={{0,1},{1,0},{2,3},{3,2},{4,5},{5,4},{6,7},{7,6},{8,9},{9,8},{10,11... | collective-permute-start | bytes 122888 | tf_op jit(solution)/shard_map/ppermute | solution.py:479
  125.5 3.4 %collective-permute-done.10.other_ref = bf16[256,128]{1,0:T(8,128)(2,1)S(1)} collective-permute-done((bf16[256,128]{1,0:T(8,128)(2,1)S(1)}, bf16[256,128]{1,0:T(8,128)(2,1)S(1)}, u32[]{:S(2)}, u32[]{:S(2)}) %collective-permute-start.10) | collective-permute-done | bytes 65568 | tf_op jit(solution)/shard_map/ppermute | solution.py:456
  128.9 0.1 broadcast_in_dim.16
  129.0 1.0 pad_maximum_fusion
  130.0 3.6 %all-to-all-start.5 = ((bf16[8,416,128]{2,1,0:T(8,128)(2,1)}), bf16[8,416,128]{2,1,0:T(8,128)(2,1)S(1)}, u32[]{:S(2)}, u32[]{:S(2)}) async-start(bf16[8,416,128]{2,1,0:T(8,128)(2,1)} %pad_maximum_fusion), calls=%async_computation.5 | async-start | bytes 1703936 | tf_op jit(solution)/shard_map/all_to_all | solution.py:310
  133.5 6.9 %collective-permute-start.13 = (bf16[320,128]{1,0:T(8,128)(2,1)S(1)}, bf16[320,128]{1,0:T(8,128)(2,1)S(1)}, u32[]{:S(2)}, u32[]{:S(2)}) collective-permute-start(bf16[320,128]{1,0:T(8,128)(2,1)S(1)} %pad_maximum_fusion.1.own_ref), channel_id=1, source_target_pairs={{0,6},{2,4},{4,2},{6,0},{1,7},{3,5},{5,3},{7,1},{8,14},{10,12},{12... | collective-permute-start | bytes 245768 | tf_op jit(solution)/shard_map/ppermute | solution.py:481
  140.4 1.9 %collective-permute-start.12 = (bf16[320,128]{1,0:T(8,128)(2,1)S(1)}, bf16[320,128]{1,0:T(8,128)(2,1)S(1)}, u32[]{:S(2)}, u32[]{:S(2)}) collective-permute-start(bf16[320,128]{1,0:T(8,128)(2,1)S(1)} %pad_maximum_fusion.1.own_ref), channel_id=1, source_target_pairs={{0,4},{2,6},{4,0},{6,2},{1,5},{3,7},{5,1},{7,3},{8,12},{10,14},{12... | collective-permute-start | bytes 245768 | tf_op jit(solution)/shard_map/ppermute | solution.py:481
  142.3 2.2 %collective-permute-start.11 = (bf16[320,128]{1,0:T(8,128)(2,1)S(1)}, bf16[320,128]{1,0:T(8,128)(2,1)S(1)}, u32[]{:S(2)}, u32[]{:S(2)}) collective-permute-start(bf16[320,128]{1,0:T(8,128)(2,1)S(1)} %pad_maximum_fusion.1.own_ref), channel_id=1, source_target_pairs={{0,2},{2,0},{4,6},{6,4},{1,3},{3,1},{5,7},{7,5},{8,10},{10,8},{12,... | collective-permute-start | bytes 245768 | tf_op jit(solution)/shard_map/ppermute | solution.py:481
  144.5 3.1 %collective-permute-done.12.second_ref = bf16[320,128]{1,0:T(8,128)(2,1)S(1)} collective-permute-done((bf16[320,128]{1,0:T(8,128)(2,1)S(1)}, bf16[320,128]{1,0:T(8,128)(2,1)S(1)}, u32[]{:S(2)}, u32[]{:S(2)}) %collective-permute-start.12) | collective-permute-done | bytes 81952 | tf_op jit(solution)/shard_map/ppermute | solution.py:481
  147.6 1.4 collective-permute-done.11.first_ref
  149.0 7.6 %collective-permute-start.14 = (bf16[8,416,128]{2,1,0:T(8,128)(2,1)S(1)}, bf16[8,416,128]{2,1,0:T(8,128)(2,1)S(1)}, u32[]{:S(2)}, u32[]{:S(2)}) collective-permute-start(bf16[8,416,128]{2,1,0:T(8,128)(2,1)S(1)} %all-to-all-done.5.got_ref), channel_id=1, source_target_pairs={{0,32},{32,0},{1,33},{33,1},{2,34},{34,2},{3,35},{35,3},{4,36},{36... | collective-permute-start | bytes 2555912 | tf_op jit(solution)/shard_map/ppermute | solution.py:485
  156.7 1.5 conv2_unpack.1
  158.2 0.4 collective-permute-done.14.cross_ref
  158.7 2.8 %gradient_unpack.1 = (f32[384,1280]{1,0:T(8,128)}, f32[1280]{0:T(1024)}, f32[640]{0:T(1024)}, bf16[256,640]{1,0:T(8,128)(2,1)}) custom-call(s32[5]{0:T(128)S(1)} %stack.23.where_ref, bf16[8,416,128]{2,1,0:T(8,128)(2,1)S(1)} %all-to-all-done.5.got_ref, bf16[8,416,128]{2,1,0:T(8,128)(2,1)S(1)} %collective-permute-done.14.cross_ref), custom_call_target="tpu_custom_call" | custom-call | tf_op jit(solution)/shard_map/gradient_unpack/pallas_call | solution.py:494
  (51 shorter events, 0.3 us)
Async XLA Ops:
  0.6 20.6 %copy-start = (bf16[80,1920]{1,0:T(8,128)(2,1)S(1)}, bf16[80,1920]{1,0:T(8,128)(2,1)}, u32[]{:S(2)}) copy-start(bf16[80,1920]{1,0:T(8,128)(2,1)} %own_ref.3) | copy-start | bytes 921604
  0.6 19.1 %copy-start.9 = (bf16[384,1280]{1,0:T(8,128)(2,1)S(1)}, bf16[384,1280]{1,0:T(8,128)(2,1)}, u32[]{:S(2)}) copy-start(bf16[384,1280]{1,0:T(8,128)(2,1)} %weight_ref.1) | copy-start | bytes 2949124
  0.7 16.1 %collective-permute-start.1 = (bf16[80,1920]{1,0:T(8,128)(2,1)}, bf16[80,1920]{1,0:T(8,128)(2,1)S(1)}, u32[]{:S(2)}, u32[]{:S(2)}) collective-permute-start(bf16[80,1920]{1,0:T(8,128)(2,1)} %own_ref.3), channel_id=1, source_target_pairs={{0,257},{257,0},{1,256},{256,1},{2,259},{259,2},{3,258},{258,3},{4... | collective-permute-start | bytes 921608 | tf_op jit(solution)/shard_map/ppermute | solution.py:349
  7.7 13.5 %all-to-all-start = ((bf16[4,26,16,128]{3,2,1,0:T(8,128)(2,1)}), bf16[4,26,16,128]{3,2,1,0:T(8,128)(2,1)S(1)}, u32[]{:S(2)}, u32[]{:S(2)}) async-start(bf16[4,26,16,128]{3,2,1,0:T(8,128)(2,1)} %mel_payload.1), calls=%async_computation | async-start | bytes 851968 | tf_op jit(solution)/shard_map/all_to_all | solution.py:310
  11.9 9.2 %collective-permute-start = (bf16[80,1920]{1,0:T(8,128)(2,1)}, bf16[80,1920]{1,0:T(8,128)(2,1)S(1)}, u32[]{:S(2)}, u32[]{:S(2)}) collective-permute-start(bf16[80,1920]{1,0:T(8,128)(2,1)} %own_ref.3), channel_id=1, source_target_pairs={{0,32},{32,0},{1,33},{33,1},{2,34},{34,2},{3,35},{35,3},{4,36},{36... | collective-permute-start | bytes 921608 | tf_op jit(solution)/shard_map/ppermute | solution.py:364
  16.7 4.4 %collective-permute-start.2 = (bf16[80,1920]{1,0:T(8,128)(2,1)S(1)}, bf16[80,1920]{1,0:T(8,128)(2,1)S(1)}, u32[]{:S(2)}, u32[]{:S(2)}) collective-permute-start(bf16[80,1920]{1,0:T(8,128)(2,1)S(1)} %collective-permute-done.1.far_ref), channel_id=1, source_target_pairs={{0,32},{32,0},{1,33},{33,1},{2,34},{34,2},{3,35},{35,3},{4,36},{36... | collective-permute-start | bytes 921608 | tf_op jit(solution)/shard_map/ppermute | solution.py:366
  21.1 3.5 %copy-start.7 = (bf16[384,384]{1,0:T(8,128)(2,1)}, bf16[384,384]{1,0:T(8,128)(2,1)S(1)}, u32[]{:S(2)}) copy-start(bf16[384,384]{1,0:T(8,128)(2,1)S(1)} %get-tuple-element.33.w1_ref) | copy-start | bytes 884740
  21.2 3.5 %copy-start.1 = (bf16[80,1920]{1,0:T(8,128)(2,1)}, bf16[80,1920]{1,0:T(8,128)(2,1)S(1)}, u32[]{:S(2)}) copy-start(bf16[80,1920]{1,0:T(8,128)(2,1)S(1)} %collective-permute-done.side_ref) | copy-start | bytes 921604
  21.2 3.4 %copy-start.3 = (bf16[80,1920]{1,0:T(8,128)(2,1)}, bf16[80,1920]{1,0:T(8,128)(2,1)S(1)}, u32[]{:S(2)}) copy-start(bf16[80,1920]{1,0:T(8,128)(2,1)S(1)} %collective-permute-done.2.both_ref) | copy-start | bytes 921604
  21.2 6.9 %copy-start.13 = (s32[16]{0:T(128)S(1)}, s32[16]{0:T(128)}, u32[]{:S(2)}) copy-start(s32[16]{0:T(128)} %length_ref.1) | copy-start | bytes 196
  21.2 6.9 %copy-start.14 = (s32[16,1]{0,1:T(1,128)S(1)}, s32[16,1]{0,1:T(1,128)}, u32[]{:S(2)}) copy-start(s32[16,1]{0,1:T(1,128)} %param.10) | copy-start | bytes 196
  21.2 7.2 %copy-start.12 = (f32[640]{0:T(1024)S(1)}, f32[640]{0:T(1024)}, u32[]{:S(2)}) copy-start(f32[640]{0:T(1024)} %param.14) | copy-start | bytes 7684
  24.6 13.4 %all-to-all-start.1 = ((bf16[4,128,640]{2,1,0:T(8,128)(2,1)}), bf16[4,128,640]{2,1,0:T(8,128)(2,1)S(1)}, u32[]{:S(2)}, u32[]{:S(2)}) async-start(bf16[4,128,640]{2,1,0:T(8,128)(2,1)} %stem_forward.1), calls=%async_computation.1 | async-start | bytes 1310720 | tf_op jit(solution)/shard_map/all_to_all | solution.py:310
  28.4 1.0 copy-start.8
  33.2 1.0 copy-start.5
  34.2 16.7 %copy-start.2 = (bf16[80,1920]{1,0:T(8,128)(2,1)S(1)}, bf16[80,1920]{1,0:T(8,128)(2,1)}, u32[]{:S(2)}) copy-start(bf16[80,1920]{1,0:T(8,128)(2,1)} %copy-done.1) | copy-start | bytes 921604
  38.0 12.9 %copy-start.4 = (bf16[80,1920]{1,0:T(8,128)(2,1)S(1)}, bf16[80,1920]{1,0:T(8,128)(2,1)}, u32[]{:S(2)}) copy-start(bf16[80,1920]{1,0:T(8,128)(2,1)} %copy-done.3) | copy-start | bytes 921604
  38.0 12.9 %copy-start.6 = (bf16[3,384,512]{2,1,0:T(8,128)(2,1)S(1)}, bf16[3,384,512]{2,1,0:T(8,128)(2,1)}, u32[]{:S(2)}) copy-start(bf16[3,384,512]{2,1,0:T(8,128)(2,1)} %copy-done.5) | copy-start | bytes 3538948
  39.8 11.1 %copy-start.10 = (bf16[8,80,128]{2,1,0:T(8,128)(2,1)}, bf16[8,80,128]{2,1,0:T(8,128)(2,1)S(1)}, u32[]{:S(2)}) copy-start(bf16[8,80,128]{2,1,0:T(8,128)(2,1)S(1)} %get-tuple-element.51) | copy-start | bytes 491524
  54.4 7.1 %collective-permute-start.3 = (bf16[2,2,896,128]{3,2,1,0:T(8,128)(2,1)S(1)}, bf16[2,2,896,128]{3,2,1,0:T(8,128)(2,1)S(1)}, u32[]{:S(2)}, u32[]{:S(2)}) collective-permute-start(bf16[2,2,896,128]{3,2,1,0:T(8,128)(2,1)S(1)} %get-tuple-element.47), channel_id=1, source_target_pairs={{0,32},{32,0},{1,33},{33,1},{2,34},{34,2},{3,35},{35,3},{4,36},{36... | collective-permute-start | bytes 2752520 | tf_op jit(solution)/shard_map/ppermute | solution.py:445
  78.6 50.4 %copy-start.11 = (bf16[8,80,128]{2,1,0:T(8,128)(2,1)S(1)}, bf16[8,80,128]{2,1,0:T(8,128)(2,1)}, u32[]{:S(2)}) copy-start(bf16[8,80,128]{2,1,0:T(8,128)(2,1)} %copy-done.10) | copy-start | bytes 491524
  79.3 24.4 %all-to-all-start.4 = ((bf16[4,160,128]{2,1,0:T(8,128)(2,1)}), bf16[4,160,128]{2,1,0:T(8,128)(2,1)S(1)}, u32[]{:S(2)}, u32[]{:S(2)}) async-start(bf16[4,160,128]{2,1,0:T(8,128)(2,1)} %bitcast.8), calls=%async_computation.4 | async-start | bytes 327680 | tf_op jit(solution)/shard_map/all_to_all | solution.py:310
  82.7 6.2 %collective-permute-start.7 = (bf16[256,128]{1,0:T(8,128)(2,1)S(1)}, bf16[256,128]{1,0:T(8,128)(2,1)S(1)}, u32[]{:S(2)}, u32[]{:S(2)}) collective-permute-start(bf16[256,128]{1,0:T(8,128)(2,1)S(1)} %get-tuple-element.49.own_ref), channel_id=1, source_target_pairs={{0,2},{2,0},{4,6},{6,4},{1,3},{3,1},{5,7},{7,5},{8,10},{10,8},{12,... | collective-permute-start | bytes 196616 | tf_op jit(solution)/shard_map/ppermute | solution.py:456
  88.9 5.9 %collective-permute-start.8 = (bf16[256,128]{1,0:T(8,128)(2,1)S(1)}, bf16[256,128]{1,0:T(8,128)(2,1)S(1)}, u32[]{:S(2)}, u32[]{:S(2)}) collective-permute-start(bf16[256,128]{1,0:T(8,128)(2,1)S(1)} %gradient_pair.8.own_ref), channel_id=1, source_target_pairs={{0,4},{2,6},{4,0},{6,2},{1,5},{3,7},{5,1},{7,3},{8,12},{10,14},{12... | collective-permute-start | bytes 196616 | tf_op jit(solution)/shard_map/ppermute | solution.py:456
  94.9 24.8 %collective-permute-start.9 = (bf16[256,128]{1,0:T(8,128)(2,1)S(1)}, bf16[256,128]{1,0:T(8,128)(2,1)S(1)}, u32[]{:S(2)}, u32[]{:S(2)}) collective-permute-start(bf16[256,128]{1,0:T(8,128)(2,1)S(1)} %gradient_pair.9.own_ref), channel_id=1, source_target_pairs={{0,8},{8,0},{16,24},{24,16},{1,9},{9,1},{17,25},{25,17},{2,10},{10... | collective-permute-start | bytes 196616 | tf_op jit(solution)/shard_map/ppermute | solution.py:456
  103.7 10.2 %collective-permute-start.4 = (bf16[160,128]{1,0:T(8,128)(2,1)S(1)}, bf16[160,128]{1,0:T(8,128)(2,1)S(1)}, u32[]{:S(2)}, u32[]{:S(2)}) collective-permute-start(bf16[160,128]{1,0:T(8,128)(2,1)S(1)} %gradient_sum.3.own_ref), channel_id=1, source_target_pairs={{0,8},{8,0},{16,24},{24,16},{1,9},{9,1},{17,25},{25,17},{2,10},{10... | collective-permute-start | bytes 122888 | tf_op jit(solution)/shard_map/ppermute | solution.py:456
  114.0 9.2 %collective-permute-start.5 = (bf16[160,128]{1,0:T(8,128)(2,1)S(1)}, bf16[160,128]{1,0:T(8,128)(2,1)S(1)}, u32[]{:S(2)}, u32[]{:S(2)}) collective-permute-start(bf16[160,128]{1,0:T(8,128)(2,1)S(1)} %gradient_pair.6.own_ref), channel_id=1, source_target_pairs={{0,24},{8,16},{16,8},{24,0},{1,25},{9,17},{17,9},{25,1},{2,26},{10... | collective-permute-start | bytes 122888 | tf_op jit(solution)/shard_map/ppermute | solution.py:456
  119.7 9.1 %collective-permute-start.10 = (bf16[256,128]{1,0:T(8,128)(2,1)S(1)}, bf16[256,128]{1,0:T(8,128)(2,1)S(1)}, u32[]{:S(2)}, u32[]{:S(2)}) collective-permute-start(bf16[256,128]{1,0:T(8,128)(2,1)S(1)} %gradient_pair.10.own_ref), channel_id=1, source_target_pairs={{0,24},{8,16},{16,8},{24,0},{1,25},{9,17},{17,9},{25,1},{2,26},{10... | collective-permute-start | bytes 196616 | tf_op jit(solution)/shard_map/ppermute | solution.py:456
  123.3 5.6 %collective-permute-start.6 = (bf16[160,128]{1,0:T(8,128)(2,1)S(1)}, bf16[160,128]{1,0:T(8,128)(2,1)S(1)}, u32[]{:S(2)}, u32[]{:S(2)}) collective-permute-start(bf16[160,128]{1,0:T(8,128)(2,1)S(1)} %gradient_pair.7), channel_id=1, source_target_pairs={{0,1},{1,0},{2,3},{3,2},{4,5},{5,4},{6,7},{7,6},{8,9},{9,8},{10,11... | collective-permute-start | bytes 122888 | tf_op jit(solution)/shard_map/ppermute | solution.py:479
  130.0 19.1 %all-to-all-start.5 = ((bf16[8,416,128]{2,1,0:T(8,128)(2,1)}), bf16[8,416,128]{2,1,0:T(8,128)(2,1)S(1)}, u32[]{:S(2)}, u32[]{:S(2)}) async-start(bf16[8,416,128]{2,1,0:T(8,128)(2,1)} %pad_maximum_fusion), calls=%async_computation.5 | async-start | bytes 1703936 | tf_op jit(solution)/shard_map/all_to_all | solution.py:310
  133.5 11.0 %collective-permute-start.13 = (bf16[320,128]{1,0:T(8,128)(2,1)S(1)}, bf16[320,128]{1,0:T(8,128)(2,1)S(1)}, u32[]{:S(2)}, u32[]{:S(2)}) collective-permute-start(bf16[320,128]{1,0:T(8,128)(2,1)S(1)} %pad_maximum_fusion.1.own_ref), channel_id=1, source_target_pairs={{0,6},{2,4},{4,2},{6,0},{1,7},{3,5},{5,3},{7,1},{8,14},{10,12},{12... | collective-permute-start | bytes 245768 | tf_op jit(solution)/shard_map/ppermute | solution.py:481
  140.4 7.2 %collective-permute-start.12 = (bf16[320,128]{1,0:T(8,128)(2,1)S(1)}, bf16[320,128]{1,0:T(8,128)(2,1)S(1)}, u32[]{:S(2)}, u32[]{:S(2)}) collective-permute-start(bf16[320,128]{1,0:T(8,128)(2,1)S(1)} %pad_maximum_fusion.1.own_ref), channel_id=1, source_target_pairs={{0,4},{2,6},{4,0},{6,2},{1,5},{3,7},{5,1},{7,3},{8,12},{10,14},{12... | collective-permute-start | bytes 245768 | tf_op jit(solution)/shard_map/ppermute | solution.py:481
  142.3 6.7 %collective-permute-start.11 = (bf16[320,128]{1,0:T(8,128)(2,1)S(1)}, bf16[320,128]{1,0:T(8,128)(2,1)S(1)}, u32[]{:S(2)}, u32[]{:S(2)}) collective-permute-start(bf16[320,128]{1,0:T(8,128)(2,1)S(1)} %pad_maximum_fusion.1.own_ref), channel_id=1, source_target_pairs={{0,2},{2,0},{4,6},{6,4},{1,3},{3,1},{5,7},{7,5},{8,10},{10,8},{12,... | collective-permute-start | bytes 245768 | tf_op jit(solution)/shard_map/ppermute | solution.py:481
  149.0 9.6 %collective-permute-start.14 = (bf16[8,416,128]{2,1,0:T(8,128)(2,1)S(1)}, bf16[8,416,128]{2,1,0:T(8,128)(2,1)S(1)}, u32[]{:S(2)}, u32[]{:S(2)}) collective-permute-start(bf16[8,416,128]{2,1,0:T(8,128)(2,1)S(1)} %all-to-all-done.5.got_ref), channel_id=1, source_target_pairs={{0,32},{32,0},{1,33},{33,1},{2,34},{34,2},{3,35},{35,3},{4,36},{36... | collective-permute-start | bytes 2555912 | tf_op jit(solution)/shard_map/ppermute | solution.py:485

commit v14 on v12

--- a/solution.py
+++ b/solution.py
@@ -70,24 +70,24 @@
     return lax.dot_general(left, right, (((0,), (0,)), ((), ())), preferred_element_type=F32)
 
 
-def stack_weights(refs, w2_ref):
-    for block, ref in enumerate(refs):
-        w2_ref[block * ROWS : (block + 1) * ROWS, :] = ref[...]
-    w2_ref[BLOCKS * ROWS :, :] = jnp.zeros((WIDE - BLOCKS * ROWS, 3 * D2), BF16)
-
-
-def prepare_kernel(length_ref, mel_ref, pay_ref):
+def prepare_kernel(length_ref, mel_ref, pay_ref, slots, mel_done, pay_done):
+    mel_copy = pltpu.make_async_copy(mel_ref, slots.at[:CLIPS], mel_done)
+    mel_copy.start()
     clip = lax.broadcasted_iota(jnp.int32, (CLIPS, MEL), 0)
     length = jnp.zeros((CLIPS, MEL), F32)
     for index in range(CLIPS):
         length = jnp.where(clip == index, length_ref[index].astype(F32), length)
-    for target in range(HOLDERS):
-        pay_ref[target, :CLIPS] = mel_ref[...]
-        pay_ref[target, CLIPS] = length.astype(BF16)
-        pay_ref[target, CLIPS + 1 :] = jnp.zeros((PAY - CLIPS - 1, 2 * HALF, MEL), BF16)
-
-
-def columns_kernel(where_ref, weight_ref, bias_ref, w1_ref, b1_ref, picked):
+    for slot in range(CLIPS, PAY):
+        slots[slot] = length.astype(BF16)
+    mel_copy.wait()
+    copies = [pltpu.make_async_copy(slots, pay_ref.at[target], pay_done.at[target]) for target in range(HOLDERS)]
+    for copy in copies:
+        copy.start()
+    for copy in copies:
+        copy.wait()
+
+
+def pick_columns(where_ref, weight_ref, bias_ref, w1_ref, b1_ref, picked):
     picked[...] = jnp.zeros_like(picked)
     b1_ref[...] = jnp.zeros_like(b1_ref)
     for block, flip in enumerate((0, 1, 2 * HOLDERS, 2 * HOLDERS + 1)):
@@ -130,11 +130,19 @@
 
 
 def forward_kernel(
-    pay_ref, w1_ref, b1_ref, own_ref, side_ref, far_ref, both_ref, part_ref, w2_ref, cols_ref, frames_ref
+    where_ref, pay_ref, weight_ref, bias_ref, own_ref, side_ref, far_ref, both_ref, part_ref,
+    w2_ref, cols_ref, frames_ref, w1_ref, b1_ref, picked, own_done,
 ):
+    own_copy = pltpu.make_async_copy(own_ref, w2_ref.at[:ROWS], own_done)
+
     @pl.when(pl.program_id(0) == 0)
     def _():
-        stack_weights((own_ref, side_ref, far_ref, both_ref), w2_ref)
+        own_copy.start()
+        pick_columns(where_ref, weight_ref, bias_ref, w1_ref, b1_ref, picked)
+        for block, ref in enumerate((side_ref, far_ref, both_ref)):
+            w2_ref[(block + 1) * ROWS : (block + 2) * ROWS, :] = ref[...]
+        w2_ref[BLOCKS * ROWS :, :] = jnp.zeros((WIDE - BLOCKS * ROWS, 3 * D2), BF16)
+        own_copy.wait()
 
     pre_even, pre_odd, live_even, live_odd = first_conv(pay_ref, w1_ref, b1_ref, cols_ref, frames_ref)
     odd = jnp.where(live_odd, gelu_value(pre_odd), 0.0)
@@ -145,9 +153,13 @@
 
 
 def slope_kernel(
-    pay_ref, w1_ref, b1_ref, grad_ref, column_ref, row_ref,
-    cols_ref, slope_ref, turned_ref, live_grad_ref, wanted_ref, frames_ref,
+    where_ref, pay_ref, weight_ref, bias_ref, grad_ref, column_ref, row_ref,
+    cols_ref, slope_ref, turned_ref, live_grad_ref, wanted_ref, frames_ref, w1_ref, b1_ref, picked,
 ):
+    @pl.when(pl.program_id(0) == 0)
+    def _():
+        pick_columns(where_ref, weight_ref, bias_ref, w1_ref, b1_ref, picked)
+
     pre_even, pre_odd, live_even, live_odd = first_conv(pay_ref, w1_ref, b1_ref, cols_ref, frames_ref)
     value, slope = gelu_both(pre_odd)
     odd = jnp.where(live_odd, value, 0.0)
@@ -203,11 +215,15 @@
 
 def backward_kernel(
     where_ref, grad_ref, own_ref, side_ref, far_ref, both_ref, cols_ref, turned_ref, slope_ref, keep_ref, send_ref,
-    w2_ref, conv_sum, cols_here, cols_done,
+    w2_ref, conv_sum, cols_here, cols_done, both_done,
 ):
     cols_copy = pltpu.make_async_copy(cols_ref, cols_here, cols_done)
     cols_copy.start()
-    stack_weights((own_ref, side_ref, far_ref, both_ref), w2_ref)
+    both_copy = pltpu.make_async_copy(both_ref, w2_ref.at[3 * ROWS : 4 * ROWS], both_done)
+    both_copy.start()
+    for block, ref in enumerate((own_ref, side_ref, far_ref)):
+        w2_ref[block * ROWS : (block + 1) * ROWS, :] = ref[...]
+    w2_ref[BLOCKS * ROWS :, :] = jnp.zeros((WIDE - BLOCKS * ROWS, 3 * D2), BF16)
     mine = where_ref[0]
     grad = grad_ref[...].reshape(HOLDERS * STEPS, D2)
     places = []
@@ -222,6 +238,7 @@
                 piece = conv_sum[first : first + ROWS, column * LANES : (column + 1) * LANES]
                 out[target, tile // 8, (tile % 8) * ROWS : (tile % 8 + 1) * ROWS, :] = piece.astype(out.dtype)
 
+    both_copy.wait()
     even = dot_nt(grad, w2_ref[:, D2 : 2 * D2])
     even = (even * slope_ref[0]).astype(BF16)
     odd = dot_nt(grad, w2_ref[:, 2 * D2 :]) + shift_up(dot_nt(grad, w2_ref[:, :D2]))
@@ -336,25 +353,21 @@
 
     pay = pl.pallas_call(
         prepare_kernel,
-        in_specs=[pl.BlockSpec(memory_space=pltpu.SMEM), vmem()],
-        out_specs=vmem(),
+        in_specs=[pl.BlockSpec(memory_space=pltpu.SMEM), pl.BlockSpec(memory_space=pl.ANY)],
+        out_specs=pl.BlockSpec(memory_space=pl.ANY),
         out_shape=in_hbm(HOLDERS, PAY, 2 * HALF, MEL),
+        scratch_shapes=[
+            pltpu.VMEM((PAY, 2 * HALF, MEL), BF16),
+            pltpu.SemaphoreType.DMA,
+            pltpu.SemaphoreType.DMA((HOLDERS,)),
+        ],
         compiler_params=params(60),
         name="mel_payload",
-    )(lengths, mel)
+    )(lengths, from_hbm(mel))
     got_pay = exchange(pay, "y")
     cores = [(0, 1), (1, 0)]
     far_weight = lax.ppermute(conv2_weight, ("xh", "xl"), [(0, 3), (3, 0), (1, 2), (2, 1)])
 
-    w1, b1 = pl.pallas_call(
-        columns_kernel,
-        in_specs=[pl.BlockSpec(memory_space=pltpu.SMEM), vmem(), vmem()],
-        out_specs=[vmem()] * 2,
-        out_shape=[shape(3 * MEL, WIDE), shape(1, WIDE, dtype=F32)],
-        scratch_shapes=[pltpu.VMEM((3 * MEL, WIDE), F32)],
-        compiler_params=params(10),
-        name="conv1_columns",
-    )(where, conv1_weight, from_hbm(conv1_bias))
     own_weight, place = lax.optimization_barrier((conv2_weight, where))
     far_weight, place = lax.optimization_barrier((far_weight, place))
     weights = [
@@ -369,27 +382,35 @@
     rows, some = HOLDERS * STEPS, 2 * STEPS
     frames = (2, 2 * STEPS, MEL)
     pay_spec = pl.BlockSpec((2, PAY, 2 * HALF, MEL), pair4)
+    smem = pl.BlockSpec(memory_space=pltpu.SMEM)
+    columns = [
+        pltpu.VMEM((3 * MEL, WIDE), BF16),
+        pltpu.VMEM((1, WIDE), F32),
+        pltpu.VMEM((3 * MEL, WIDE), F32),
+    ]
     parts = pl.pallas_call(
         forward_kernel,
         grid=(HOLDERS // 2,),
-        in_specs=[pay_spec, *[vmem()] * (2 + BLOCKS)],
+        in_specs=[smem, pay_spec, vmem(), vmem(), pl.BlockSpec(memory_space=pl.ANY), *[vmem()] * (BLOCKS - 1)],
         out_specs=pl.BlockSpec((2, STEPS, D2), pair),
         out_shape=in_hbm(HOLDERS, STEPS, D2),
         scratch_shapes=[
             pltpu.VMEM((WIDE, 3 * D2), BF16),
             pltpu.VMEM((some, 4 * LANES), BF16),
             pltpu.VMEM(frames, F32),
+            *columns,
+            pltpu.SemaphoreType.DMA,
         ],
         compiler_params=params(20, "arbitrary"),
         name="stem_forward",
-    )(got_pay, w1, b1, *weights)
+    )(where, got_pay, conv1_weight, from_hbm(conv1_bias), from_hbm(conv2_weight), *weights[1:])
 
     got_parts = exchange(parts, "y")
     code = jnp.repeat(routes[:, 0] * 32 + lengths, HALF)
     cols, slopes, turned, live_grad, wanted = pl.pallas_call(
         slope_kernel,
         grid=(HOLDERS // 2,),
-        in_specs=[pay_spec, *[vmem()] * 5],
+        in_specs=[smem, pay_spec, *[vmem()] * 5],
         out_specs=[
             pl.BlockSpec((some, 4 * LANES), lambda i: (i, 0)),
             pl.BlockSpec((2, some, WIDE), lambda i: (0, i, 0)),
@@ -404,10 +425,10 @@
             in_hbm(STEPS, D2),
             shape(SLOTS * HALF, STEPS),
         ],
-        scratch_shapes=[pltpu.VMEM(frames, F32)],
+        scratch_shapes=[pltpu.VMEM(frames, F32), *columns],
         compiler_params=params(20, "arbitrary"),
         name="stem_slopes",
-    )(got_pay, w1, b1, from_hbm(out_grad.reshape(STEPS, D2)), code[:, None], code[None])
+    )(where, got_pay, from_hbm(conv1_weight), from_hbm(conv1_bias), from_hbm(out_grad.reshape(STEPS, D2)), code[:, None], code[None])
     got_parts, slopes, turned = lax.optimization_barrier((got_parts, slopes, turned))
     rep, same, cross = pl.pallas_call(
         middle_kernel,
@@ -424,7 +445,8 @@
         backward_kernel,
         in_specs=[
             pl.BlockSpec(memory_space=pltpu.SMEM),
-            *[vmem()] * (1 + BLOCKS),
+            *[vmem()] * BLOCKS,
+            pl.BlockSpec(memory_space=pl.ANY),
             pl.BlockSpec(memory_space=pl.ANY),
             vmem(),
             vmem(),
@@ -436,10 +458,11 @@
             pltpu.VMEM((WIDE, D2), F32),
             pltpu.VMEM((rows, 4 * LANES), BF16),
             pltpu.SemaphoreType.DMA,
+            pltpu.SemaphoreType.DMA,
         ],
         compiler_params=params(32),
         name="stem_backward",
-    )(where, got_grad, *weights, from_hbm(cols), turned, slopes)
+    )(where, got_grad, *weights[:3], from_hbm(weights[3]), from_hbm(cols), turned, slopes)
     got = lax.ppermute(send, "c", cores)
     quarters = exchange((keep + got.astype(F32)).astype(BF16).reshape(4, PACK, LANES), ("xh", "xl"))
 

time: 148 us -> 153 us (1.034)
  Pallas kernels: 19.8 us -> 23.3 us
  blocking collectives: 47.3 us -> 49.2 us
    all_to_all x4, blocking collectives: 47.3 us -> 49.2 us  [exchange(): return lax.all_to_all(values, axes, split_axis=0, concat_axis=0, tiled=True)]
    ppermute x2, waiting for transfers between devices: 5.06 us -> 3.25 us  [with_group(): lax.ppermute(values, 'zh', [(i, i ^ flip) for i in range(4)])]
    pallas_call x3 -> x2, Pallas kernels: 8.5 us -> 10.3 us  [the longest x1 5.33 us: local(): pl.pallas_call(forward_kernel, grid=(HOLDERS // 2,), in_specs=[smem, pay_...]
where the time goes in v14:
time: 153 us; the launch traced here: 152 us
  starting transfers between devices  56.8 us (37%)
  blocking collectives  49.2 us (32%)
  Pallas kernels  23.3 us (15%)
  waiting for transfers between devices  19 us (12%)
    all_to_all x4, blocking collectives, exchange(): return lax.all_to_all(values, axes, split_axis=0, concat_axis=0, tiled=True)  49.2 us
    ppermute x2, starting transfers between devices, with_group(): lax.ppermute(values, 'zh', [(i, i ^ flip) for i in range(4)])  16.8 us
    all_to_all x3, starting transfers between devices, exchange(): return lax.all_to_all(values, axes, split_axis=0, concat_axis=0, tiled=True)  12.2 us
    ppermute x1, starting transfers between devices, local(): got_cross = lax.ppermute(got, 'c', cores)  8.43 us
    ppermute x1, waiting for transfers between devices, local(): other = lax.ppermute(own, 'xl', [(0, 1), (1, 0)])  8.1 us
    ppermute x1, starting transfers between devices, local(): lax.ppermute(conv2_weight, ('xh', 'xl'), [(0, 3), (3, 0), (1, 2), (2, 1)])  5.35 us
    pallas_call x1, Pallas kernels, local(): pl.pallas_call(forward_kernel, grid=(HOLDERS // 2,), in_specs=[smem, pay_...  5.33 us
    pallas_call x1, Pallas kernels, local(): pl.pallas_call(slope_kernel, grid=(HOLDERS // 2,), in_specs=[smem, pay_sp...  4.93 us
  transfers between devices with their start and end apart: 11, of which 7 were waited for; matrix products, arithmetic and copies ran while one was open for 0% of the time, Pallas kernels for 6%

profile of v14, /device:TPU:1, one launch (start us, length us, event | category | flops | bytes accessed | tf_op | source)
XLA Modules:
  0.0 151.8 jit_solution(8372956353205704357)
XLA Ops:
  0.6 0.0 copy-start
  0.6 5.3 %collective-permute-start.1 = (bf16[80,1920]{1,0:T(8,128)(2,1)}, bf16[80,1920]{1,0:T(8,128)(2,1)S(1)}, u32[]{:S(2)}, u32[]{:S(2)}) collective-permute-start(bf16[80,1920]{1,0:T(8,128)(2,1)} %own_ref.3), channel_id=1, source_target_pairs={{0,257},{257,0},{1,256},{256,1},{2,259},{259,2},{3,258},{258,3},{4... | collective-permute-start | bytes 921608 | tf_op jit(solution)/shard_map/ppermute | solution.py:369
  6.0 2.3 %mel_payload.1 = bf16[4,26,16,128]{3,2,1,0:T(8,128)(2,1)} custom-call(s32[16]{0:T(128)} %length_ref.1, bf16[16,16,128]{2,1,0:T(8,128)(2,1)} %mel_ref.1), custom_call_target="tpu_custom_call" | custom-call | tf_op jit(solution)/shard_map/mel_payload/pallas_call | solution.py:354
  8.3 4.2 %all-to-all-start = ((bf16[4,26,16,128]{3,2,1,0:T(8,128)(2,1)}), bf16[4,26,16,128]{3,2,1,0:T(8,128)(2,1)S(1)}, u32[]{:S(2)}, u32[]{:S(2)}) async-start(bf16[4,26,16,128]{3,2,1,0:T(8,128)(2,1)} %mel_payload.1), calls=%async_computation | async-start | bytes 851968 | tf_op jit(solution)/shard_map/all_to_all | solution.py:326
  12.5 0.1 pad_add_fusion.where_ref
  12.6 4.9 %collective-permute-start = (bf16[80,1920]{1,0:T(8,128)(2,1)}, bf16[80,1920]{1,0:T(8,128)(2,1)S(1)}, u32[]{:S(2)}, u32[]{:S(2)}) collective-permute-start(bf16[80,1920]{1,0:T(8,128)(2,1)} %own_ref.3), channel_id=1, source_target_pairs={{0,32},{32,0},{1,33},{33,1},{2,34},{34,2},{3,35},{35,3},{4,36},{36... | collective-permute-start | bytes 921608 | tf_op jit(solution)/shard_map/ppermute | solution.py:375
  17.5 0.0 collective-permute-done.1.far_ref
  17.5 2.2 %collective-permute-start.2 = (bf16[80,1920]{1,0:T(8,128)(2,1)S(1)}, bf16[80,1920]{1,0:T(8,128)(2,1)S(1)}, u32[]{:S(2)}, u32[]{:S(2)}) collective-permute-start(bf16[80,1920]{1,0:T(8,128)(2,1)S(1)} %collective-permute-done.1.far_ref), channel_id=1, source_target_pairs={{0,32},{32,0},{1,33},{33,1},{2,34},{34,2},{3,35},{35,3},{4,36},{36... | collective-permute-start | bytes 921608 | tf_op jit(solution)/shard_map/ppermute | solution.py:377
  19.7 0.0 collective-permute-done.side_ref
  19.7 0.0 copy-start.2
  19.8 0.0 all-to-all-done.pay_ref
  19.8 1.2 collective-permute-done.2.both_ref
  21.0 0.0 copy-done
  21.0 5.3 %stem_forward.1 = bf16[4,128,640]{2,1,0:T(8,128)(2,1)} custom-call(s32[4]{0:T(128)S(1)} %pad_add_fusion.where_ref, bf16[4,26,16,128]{3,2,1,0:T(8,128)(2,1)S(1)} %all-to-all-done.pay_ref, bf16[384,1280]{1,0:T(8,128)(2,1)S(1)} %copy-done, f32[1280]{0:T(1024)} %bias_ref.3, bf16[80,1920]{1,0:T(8,128)(2,1)} %own_ref.3, ...), custom_call_target="tpu_custom_call" | custom-call | tf_op jit(solution)/shard_map/stem_forward/pallas_call | solution.py:391
  26.4 0.0 copy-done.2
  26.4 4.5 %all-to-all-start.1 = ((bf16[4,128,640]{2,1,0:T(8,128)(2,1)}), bf16[4,128,640]{2,1,0:T(8,128)(2,1)S(1)}, u32[]{:S(2)}, u32[]{:S(2)}) async-start(bf16[4,128,640]{2,1,0:T(8,128)(2,1)} %stem_forward.1), calls=%async_computation.1 | async-start | bytes 1310720 | tf_op jit(solution)/shard_map/all_to_all | solution.py:326
  30.9 0.1 broadcast_in_dim.14
  30.9 0.1 broadcast_in_dim_reshape.7.row_ref
  31.0 0.1 broadcast_in_dim_reshape.8.column_ref
  31.1 0.0 copy-done.7
  31.1 0.0 copy-start.1
  31.2 4.9 %stem_slopes.1 = (bf16[512,512]{1,0:T(8,128)(2,1)}, f32[2,512,384]{2,1,0:T(8,128)S(1)}, bf16[3,384,512]{2,1,0:T(8,128)(2,1)S(1)}, bf16[128,640]{1,0:T(8,128)(2,1)}, bf16[256,128]{1,0:T(8,128)(2,1)S(1)}) custom-call(s32[4]{0:T(128)S(1)} %pad_add_fusion.where_ref, bf16[4,26,16,128]{3,2,1,0:T(8,128)(2,1)S(1)} %all-to-all-done.pay_ref, ...), custom_call_target="tpu_custom_call" | custom-call | tf_op jit(solution)/shard_map/stem_slopes/pallas_call | solution.py:410
  36.1 1.0 copy-done.5
  37.1 3.8 %all-to-all-done.1.part_ref = bf16[4,128,640]{2,1,0:T(8,128)(2,1)S(1)} async-done(((bf16[4,128,640]{2,1,0:T(8,128)(2,1)}), bf16[4,128,640]{2,1,0:T(8,128)(2,1)S(1)}, u32[]{:S(2)}, u32[]{:S(2)}) %all-to-all-start.1) | async-done | bytes 655392 | tf_op jit(solution)/shard_map/all_to_all | solution.py:326
  40.9 1.7 %stem_middle.1 = (bf16[4,128,640]{2,1,0:T(8,128)(2,1)S(1)}, bf16[8,80,128]{2,1,0:T(8,128)(2,1)S(1)}, bf16[8,80,128]{2,1,0:T(8,128)(2,1)S(1)}) custom-call(s32[4]{0:T(128)S(1)} %pad_add_fusion.where_ref, bf16[4,128,640]{2,1,0:T(8,128)(2,1)S(1)} %all-to-all-done.1.part_ref, f32[1,640]{1,0:T(1,128)S(1)} %broadcast_in_dim.15.b2_ref, ...), custom_call_target="tpu_custom_call" | custom-call | tf_op jit(solution)/shard_map/stem_middle/pallas_call | solution.py:433
  42.6 11.5 %all_to_all.35.grad_ref = bf16[4,128,640]{2,1,0:T(8,128)(2,1)S(1)} all-to-all(bf16[4,128,640]{2,1,0:T(8,128)(2,1)S(1)} %get-tuple-element.32), channel_id=1, replica_groups=mesh['xh'=2,'y'=4,'c'=2,'zh'=4,'zl'=4,'xl'=2] {'y'}, dimensions={0} | all-to-all | bytes 1310720 | tf_op jit(solution)/shard_map/all_to_all | solution.py:326
  54.1 4.6 %stem_backward.1 = (f32[2,2,896,128]{3,2,1,0:T(8,128)S(1)}, bf16[2,2,896,128]{3,2,1,0:T(8,128)(2,1)S(1)}) custom-call(s32[4]{0:T(128)S(1)} %pad_add_fusion.where_ref, bf16[4,128,640]{2,1,0:T(8,128)(2,1)S(1)} %all_to_all.35.grad_ref, bf16[80,1920]{1,0:T(8,128)(2,1)S(1)} %copy-done.1, bf16[80,1920]{1,0:T(8,128)(2,1)S(1)} %copy-done.3, ...), custom_call_target="tpu_custom_call" | custom-call | tf_op jit(solution)/shard_map/stem_backward/pallas_call | solution.py:444
  58.7 4.7 %collective-permute-start.3 = (bf16[2,2,896,128]{3,2,1,0:T(8,128)(2,1)S(1)}, bf16[2,2,896,128]{3,2,1,0:T(8,128)(2,1)S(1)}, u32[]{:S(2)}, u32[]{:S(2)}) collective-permute-start(bf16[2,2,896,128]{3,2,1,0:T(8,128)(2,1)S(1)} %get-tuple-element.37), channel_id=1, source_target_pairs={{0,32},{32,0},{1,33},{33,1},{2,34},{34,2},{3,35},{35,3},{4,36},{36... | collective-permute-start | bytes 2752520 | tf_op jit(solution)/shard_map/ppermute | solution.py:466
  63.4 2.1 %collective-permute-done.3 = bf16[2,2,896,128]{3,2,1,0:T(8,128)(2,1)S(1)} collective-permute-done((bf16[2,2,896,128]{3,2,1,0:T(8,128)(2,1)S(1)}, bf16[2,2,896,128]{3,2,1,0:T(8,128)(2,1)S(1)}, u32[]{:S(2)}, u32[]{:S(2)}) %collective-permute-start.3) | collective-permute-done | bytes 917536 | tf_op jit(solution)/shard_map/ppermute | solution.py:466
  65.5 0.2 add_convert_fusion
  65.7 16.8 %all_to_all.36.got_ref = bf16[4,896,128]{2,1,0:T(8,128)(2,1)S(1)} all-to-all(bf16[4,896,128]{2,1,0:T(8,128)(2,1)S(1)} %bitcast.12), channel_id=1, replica_groups=mesh['xh'=2,'y'=4,'c'=2,'zh'=4,'zl'=4,'xl'=2] {'xh','xl'}, dimensions={0} | all-to-all | bytes 1835008 | tf_op jit(solution)/shard_map/all_to_all | solution.py:326
  82.5 0.1 gradient_sum.2
  82.6 8.1 %all_to_all.37.got_ref = bf16[4,224,128]{2,1,0:T(8,128)(2,1)S(1)} all-to-all(bf16[4,224,128]{2,1,0:T(8,128)(2,1)S(1)} %bitcast.11), channel_id=1, replica_groups=mesh['xh'=2,'y'=4,'c'=2,'zh'=4,'zl'=4,'xl'=2] {'zl'}, dimensions={0} | all-to-all | bytes 458752 | tf_op jit(solution)/shard_map/all_to_all | solution.py:326
  90.8 8.3 %collective-permute-start.4 = (bf16[224,128]{1,0:T(8,128)(2,1)S(1)}, bf16[224,128]{1,0:T(8,128)(2,1)S(1)}, u32[]{:S(2)}, u32[]{:S(2)}) collective-permute-start(bf16[224,128]{1,0:T(8,128)(2,1)S(1)} %gradient_sum.3.own_ref), channel_id=1, source_target_pairs={{0,8},{8,0},{16,24},{24,16},{1,9},{9,1},{17,25},{25,17},{2,10},{10... | collective-permute-start | bytes 172040 | tf_op jit(solution)/shard_map/ppermute | solution.py:491
  99.2 1.6 %collective-permute-done.4.other_ref = bf16[224,128]{1,0:T(8,128)(2,1)S(1)} collective-permute-done((bf16[224,128]{1,0:T(8,128)(2,1)S(1)}, bf16[224,128]{1,0:T(8,128)(2,1)S(1)}, u32[]{:S(2)}, u32[]{:S(2)}) %collective-permute-start.4) | collective-permute-done | bytes 57376 | tf_op jit(solution)/shard_map/ppermute | solution.py:491
  100.8 8.4 %collective-permute-start.5 = (bf16[224,128]{1,0:T(8,128)(2,1)S(1)}, bf16[224,128]{1,0:T(8,128)(2,1)S(1)}, u32[]{:S(2)}, u32[]{:S(2)}) collective-permute-start(bf16[224,128]{1,0:T(8,128)(2,1)S(1)} %gradient_pair.2.own_ref), channel_id=1, source_target_pairs={{0,24},{8,16},{16,8},{24,0},{1,25},{9,17},{17,9},{25,1},{2,26},{10... | collective-permute-start | bytes 172040 | tf_op jit(solution)/shard_map/ppermute | solution.py:491
  109.2 1.7 %collective-permute-done.5.other_ref = bf16[224,128]{1,0:T(8,128)(2,1)S(1)} collective-permute-done((bf16[224,128]{1,0:T(8,128)(2,1)S(1)}, bf16[224,128]{1,0:T(8,128)(2,1)S(1)}, u32[]{:S(2)}, u32[]{:S(2)}) %collective-permute-start.5) | collective-permute-done | bytes 57376 | tf_op jit(solution)/shard_map/ppermute | solution.py:491
  110.9 12.7 %all_to_all.38 = bf16[4,224,128]{2,1,0:T(8,128)(2,1)S(1)} all-to-all(bf16[4,224,128]{2,1,0:T(8,128)(2,1)S(1)} %gradient_pair.3), channel_id=1, replica_groups=mesh['xh'=2,'y'=4,'c'=2,'zh'=4,'zl'=4,'xl'=2] {'zl'}, dimensions={0} | all-to-all | bytes 458752 | tf_op jit(solution)/shard_map/all_to_all | solution.py:326
  123.7 0.1 broadcast_in_dim.16
  123.7 1.0 pad_maximum_fusion
  124.7 3.6 %all-to-all-start.6 = ((bf16[8,416,128]{2,1,0:T(8,128)(2,1)}), bf16[8,416,128]{2,1,0:T(8,128)(2,1)S(1)}, u32[]{:S(2)}, u32[]{:S(2)}) async-start(bf16[8,416,128]{2,1,0:T(8,128)(2,1)} %pad_maximum_fusion), calls=%async_computation.6 | async-start | bytes 1703936 | tf_op jit(solution)/shard_map/all_to_all | solution.py:326
  128.3 2.2 %collective-permute-start.6 = (bf16[640,128]{1,0:T(8,128)(2,1)S(1)}, bf16[640,128]{1,0:T(8,128)(2,1)S(1)}, u32[]{:S(2)}, u32[]{:S(2)}) collective-permute-start(bf16[640,128]{1,0:T(8,128)(2,1)S(1)} %slice.20.own_ref), channel_id=1, source_target_pairs={{0,1},{1,0},{2,3},{3,2},{4,5},{5,4},{6,7},{7,6},{8,9},{9,8},{10,11... | collective-permute-start | bytes 491528 | tf_op jit(solution)/shard_map/ppermute | solution.py:496
  130.5 8.1 %collective-permute-done.6.other_ref = bf16[640,128]{1,0:T(8,128)(2,1)S(1)} collective-permute-done((bf16[640,128]{1,0:T(8,128)(2,1)S(1)}, bf16[640,128]{1,0:T(8,128)(2,1)S(1)}, u32[]{:S(2)}, u32[]{:S(2)}) %collective-permute-start.6) | collective-permute-done | bytes 163872 | tf_op jit(solution)/shard_map/ppermute | solution.py:496
  138.6 0.0 all-to-all-done.6.got_ref
  138.6 8.4 %collective-permute-start.7 = (bf16[8,416,128]{2,1,0:T(8,128)(2,1)S(1)}, bf16[8,416,128]{2,1,0:T(8,128)(2,1)S(1)}, u32[]{:S(2)}, u32[]{:S(2)}) collective-permute-start(bf16[8,416,128]{2,1,0:T(8,128)(2,1)S(1)} %all-to-all-done.6.got_ref), channel_id=1, source_target_pairs={{0,32},{32,0},{1,33},{33,1},{2,34},{34,2},{3,35},{35,3},{4,36},{36... | collective-permute-start | bytes 2555912 | tf_op jit(solution)/shard_map/ppermute | solution.py:500
  147.0 1.4 conv2_unpack.1
  148.5 0.6 collective-permute-done.7.cross_ref
  149.0 2.8 %gradient_unpack.1 = (f32[384,1280]{1,0:T(8,128)}, f32[1280]{0:T(1024)}, f32[640]{0:T(1024)}, bf16[256,640]{1,0:T(8,128)(2,1)}) custom-call(s32[4]{0:T(128)S(1)} %pad_add_fusion.where_ref, bf16[8,416,128]{2,1,0:T(8,128)(2,1)S(1)} %all-to-all-done.6.got_ref, bf16[8,416,128]{2,1,0:T(8,128)(2,1)S(1)} %collective-permute-done.7.cross_ref), custom_call_target="tpu_custom_call" | custom-call | tf_op jit(solution)/shard_map/gradient_unpack/pallas_call | solution.py:509
  (22 shorter events, 0.1 us)
Async XLA Ops:
  0.6 20.4 %copy-start = (bf16[384,1280]{1,0:T(8,128)(2,1)S(1)}, bf16[384,1280]{1,0:T(8,128)(2,1)}, u32[]{:S(2)}) copy-start(bf16[384,1280]{1,0:T(8,128)(2,1)} %weight_ref.3) | copy-start | bytes 2949124
  0.6 16.9 %collective-permute-start.1 = (bf16[80,1920]{1,0:T(8,128)(2,1)}, bf16[80,1920]{1,0:T(8,128)(2,1)S(1)}, u32[]{:S(2)}, u32[]{:S(2)}) collective-permute-start(bf16[80,1920]{1,0:T(8,128)(2,1)} %own_ref.3), channel_id=1, source_target_pairs={{0,257},{257,0},{1,256},{256,1},{2,259},{259,2},{3,258},{258,3},{4... | collective-permute-start | bytes 921608 | tf_op jit(solution)/shard_map/ppermute | solution.py:369
  8.3 11.5 %all-to-all-start = ((bf16[4,26,16,128]{3,2,1,0:T(8,128)(2,1)}), bf16[4,26,16,128]{3,2,1,0:T(8,128)(2,1)S(1)}, u32[]{:S(2)}, u32[]{:S(2)}) async-start(bf16[4,26,16,128]{3,2,1,0:T(8,128)(2,1)} %mel_payload.1), calls=%async_computation | async-start | bytes 851968 | tf_op jit(solution)/shard_map/all_to_all | solution.py:326
  12.6 18.3 %copy-start.8 = (s32[16]{0:T(128)S(1)}, s32[16]{0:T(128)}, u32[]{:S(2)}) copy-start(s32[16]{0:T(128)} %length_ref.1) | copy-start | bytes 196
  12.6 18.3 %copy-start.9 = (s32[16,1]{0,1:T(1,128)S(1)}, s32[16,1]{0,1:T(1,128)}, u32[]{:S(2)}) copy-start(s32[16,1]{0,1:T(1,128)} %param.10) | copy-start | bytes 196
  12.6 18.5 %copy-start.7 = (f32[640]{0:T(1024)S(1)}, f32[640]{0:T(1024)}, u32[]{:S(2)}) copy-start(f32[640]{0:T(1024)} %param.14) | copy-start | bytes 7684
  12.6 7.2 %collective-permute-start = (bf16[80,1920]{1,0:T(8,128)(2,1)}, bf16[80,1920]{1,0:T(8,128)(2,1)S(1)}, u32[]{:S(2)}, u32[]{:S(2)}) collective-permute-start(bf16[80,1920]{1,0:T(8,128)(2,1)} %own_ref.3), channel_id=1, source_target_pairs={{0,32},{32,0},{1,33},{33,1},{2,34},{34,2},{3,35},{35,3},{4,36},{36... | collective-permute-start | bytes 921608 | tf_op jit(solution)/shard_map/ppermute | solution.py:375
  17.5 3.5 %collective-permute-start.2 = (bf16[80,1920]{1,0:T(8,128)(2,1)S(1)}, bf16[80,1920]{1,0:T(8,128)(2,1)S(1)}, u32[]{:S(2)}, u32[]{:S(2)}) collective-permute-start(bf16[80,1920]{1,0:T(8,128)(2,1)S(1)} %collective-permute-done.1.far_ref), channel_id=1, source_target_pairs={{0,32},{32,0},{1,33},{33,1},{2,34},{34,2},{3,35},{35,3},{4,36},{36... | collective-permute-start | bytes 921608 | tf_op jit(solution)/shard_map/ppermute | solution.py:377
  19.7 6.6 %copy-start.2 = (bf16[80,1920]{1,0:T(8,128)(2,1)}, bf16[80,1920]{1,0:T(8,128)(2,1)S(1)}, u32[]{:S(2)}) copy-start(bf16[80,1920]{1,0:T(8,128)(2,1)S(1)} %collective-permute-done.side_ref) | copy-start | bytes 921604
  21.0 5.4 %copy-start.4 = (bf16[80,1920]{1,0:T(8,128)(2,1)}, bf16[80,1920]{1,0:T(8,128)(2,1)S(1)}, u32[]{:S(2)}) copy-start(bf16[80,1920]{1,0:T(8,128)(2,1)S(1)} %collective-permute-done.2.both_ref) | copy-start | bytes 921604
  26.4 14.5 %all-to-all-start.1 = ((bf16[4,128,640]{2,1,0:T(8,128)(2,1)}), bf16[4,128,640]{2,1,0:T(8,128)(2,1)S(1)}, u32[]{:S(2)}, u32[]{:S(2)}) async-start(bf16[4,128,640]{2,1,0:T(8,128)(2,1)} %stem_forward.1), calls=%async_computation.1 | async-start | bytes 1310720 | tf_op jit(solution)/shard_map/all_to_all | solution.py:326
  31.1 22.9 %copy-start.1 = (bf16[80,1920]{1,0:T(8,128)(2,1)S(1)}, bf16[80,1920]{1,0:T(8,128)(2,1)}, u32[]{:S(2)}) copy-start(bf16[80,1920]{1,0:T(8,128)(2,1)} %own_ref.3) | copy-start | bytes 921604
  36.1 1.0 copy-start.5
  37.1 17.0 %copy-start.3 = (bf16[80,1920]{1,0:T(8,128)(2,1)S(1)}, bf16[80,1920]{1,0:T(8,128)(2,1)}, u32[]{:S(2)}) copy-start(bf16[80,1920]{1,0:T(8,128)(2,1)} %copy-done.2) | copy-start | bytes 921604
  40.9 13.2 %copy-start.6 = (bf16[3,384,512]{2,1,0:T(8,128)(2,1)S(1)}, bf16[3,384,512]{2,1,0:T(8,128)(2,1)}, u32[]{:S(2)}) copy-start(bf16[3,384,512]{2,1,0:T(8,128)(2,1)} %copy-done.5) | copy-start | bytes 3538948
  58.7 6.8 %collective-permute-start.3 = (bf16[2,2,896,128]{3,2,1,0:T(8,128)(2,1)S(1)}, bf16[2,2,896,128]{3,2,1,0:T(8,128)(2,1)S(1)}, u32[]{:S(2)}, u32[]{:S(2)}) collective-permute-start(bf16[2,2,896,128]{3,2,1,0:T(8,128)(2,1)S(1)} %get-tuple-element.37), channel_id=1, source_target_pairs={{0,32},{32,0},{1,33},{33,1},{2,34},{34,2},{3,35},{35,3},{4,36},{36... | collective-permute-start | bytes 2752520 | tf_op jit(solution)/shard_map/ppermute | solution.py:466
  90.8 9.9 %collective-permute-start.4 = (bf16[224,128]{1,0:T(8,128)(2,1)S(1)}, bf16[224,128]{1,0:T(8,128)(2,1)S(1)}, u32[]{:S(2)}, u32[]{:S(2)}) collective-permute-start(bf16[224,128]{1,0:T(8,128)(2,1)S(1)} %gradient_sum.3.own_ref), channel_id=1, source_target_pairs={{0,8},{8,0},{16,24},{24,16},{1,9},{9,1},{17,25},{25,17},{2,10},{10... | collective-permute-start | bytes 172040 | tf_op jit(solution)/shard_map/ppermute | solution.py:491
  100.8 10.1 %collective-permute-start.5 = (bf16[224,128]{1,0:T(8,128)(2,1)S(1)}, bf16[224,128]{1,0:T(8,128)(2,1)S(1)}, u32[]{:S(2)}, u32[]{:S(2)}) collective-permute-start(bf16[224,128]{1,0:T(8,128)(2,1)S(1)} %gradient_pair.2.own_ref), channel_id=1, source_target_pairs={{0,24},{8,16},{16,8},{24,0},{1,25},{9,17},{17,9},{25,1},{2,26},{10... | collective-permute-start | bytes 172040 | tf_op jit(solution)/shard_map/ppermute | solution.py:491
  124.7 13.9 %all-to-all-start.6 = ((bf16[8,416,128]{2,1,0:T(8,128)(2,1)}), bf16[8,416,128]{2,1,0:T(8,128)(2,1)S(1)}, u32[]{:S(2)}, u32[]{:S(2)}) async-start(bf16[8,416,128]{2,1,0:T(8,128)(2,1)} %pad_maximum_fusion), calls=%async_computation.6 | async-start | bytes 1703936 | tf_op jit(solution)/shard_map/all_to_all | solution.py:326
  128.3 10.3 %collective-permute-start.6 = (bf16[640,128]{1,0:T(8,128)(2,1)S(1)}, bf16[640,128]{1,0:T(8,128)(2,1)S(1)}, u32[]{:S(2)}, u32[]{:S(2)}) collective-permute-start(bf16[640,128]{1,0:T(8,128)(2,1)S(1)} %slice.20.own_ref), channel_id=1, source_target_pairs={{0,1},{1,0},{2,3},{3,2},{4,5},{5,4},{6,7},{7,6},{8,9},{9,8},{10,11... | collective-permute-start | bytes 491528 | tf_op jit(solution)/shard_map/ppermute | solution.py:496
  138.6 10.4 %collective-permute-start.7 = (bf16[8,416,128]{2,1,0:T(8,128)(2,1)S(1)}, bf16[8,416,128]{2,1,0:T(8,128)(2,1)S(1)}, u32[]{:S(2)}, u32[]{:S(2)}) collective-permute-start(bf16[8,416,128]{2,1,0:T(8,128)(2,1)S(1)} %all-to-all-done.6.got_ref), channel_id=1, source_target_pairs={{0,32},{32,0},{1,33},{33,1},{2,34},{34,2},{3,35},{35,3},{4,36},{36... | collective-permute-start | bytes 2555912 | tf_op jit(solution)/shard_map/ppermute | solution.py:500

commit v15 on v12

--- a/solution.py
+++ b/solution.py
@@ -146,17 +146,20 @@
 
 def slope_kernel(
     pay_ref, w1_ref, b1_ref, grad_ref, column_ref, row_ref,
-    cols_ref, slope_ref, turned_ref, live_grad_ref, wanted_ref, frames_ref,
+    slope_ref, turned_ref, live_grad_ref, wanted_ref, frames_ref, cols_ref,
 ):
     pre_even, pre_odd, live_even, live_odd = first_conv(pay_ref, w1_ref, b1_ref, cols_ref, frames_ref)
+    some = pre_odd.shape[0]
+    lanes = pl.ds(pl.multiple_of(pl.program_id(0) * some, some), some)
+    turned_ref[pl.ds(pl.multiple_of(3 * WIDE + pl.program_id(0) * some, some // 2), some), :] = cols_ref[...]
     value, slope = gelu_both(pre_odd)
     odd = jnp.where(live_odd, value, 0.0)
     slope_ref[1] = jnp.where(live_odd, slope, 0.0)
-    turned_ref[0] = shift_down(odd).astype(BF16).T
-    turned_ref[2] = odd.astype(BF16).T
+    turned_ref[:WIDE, lanes] = shift_down(odd).astype(BF16).T
+    turned_ref[2 * WIDE : 3 * WIDE, lanes] = odd.astype(BF16).T
     value, slope = gelu_both(pre_even)
     slope_ref[0] = jnp.where(live_even, slope, 0.0)
-    turned_ref[1] = jnp.where(live_even, value, 0.0).astype(BF16).T
+    turned_ref[WIDE : 2 * WIDE, lanes] = jnp.where(live_even, value, 0.0).astype(BF16).T
 
     @pl.when(pl.program_id(0) == 0)
     def _():
@@ -202,11 +205,9 @@
 
 
 def backward_kernel(
-    where_ref, grad_ref, own_ref, side_ref, far_ref, both_ref, cols_ref, turned_ref, slope_ref, keep_ref, send_ref,
-    w2_ref, conv_sum, cols_here, cols_done,
+    where_ref, grad_ref, own_ref, side_ref, far_ref, both_ref, turned_ref, slope_ref, keep_ref, send_ref,
+    w2_ref, conv_sum,
 ):
-    cols_copy = pltpu.make_async_copy(cols_ref, cols_here, cols_done)
-    cols_copy.start()
     stack_weights((own_ref, side_ref, far_ref, both_ref), w2_ref)
     mine = where_ref[0]
     grad = grad_ref[...].reshape(HOLDERS * STEPS, D2)
@@ -215,7 +216,7 @@
         places.append((keep_ref if block % 2 == 0 else send_ref, mine if block < 2 else 1 - mine, block * ROWS))
 
     for tap in range(3):
-        conv_sum[...] = dot(turned_ref[tap], grad)
+        conv_sum[...] = dot(turned_ref[tap * WIDE : (tap + 1) * WIDE, :], grad)
         for out, target, first in places:
             for column in range(D2 // LANES):
                 tile = tap * (D2 // LANES) + column
@@ -226,8 +227,7 @@
     even = (even * slope_ref[0]).astype(BF16)
     odd = dot_nt(grad, w2_ref[:, 2 * D2 :]) + shift_up(dot_nt(grad, w2_ref[:, :D2]))
     odd = (odd * slope_ref[1]).astype(BF16)
-    cols_copy.wait()
-    cols = cols_here[...]
+    cols = turned_ref[3 * WIDE :, :]
     conv_sum[:, : 3 * LANES] = dot_tn(even, cols[:, : 3 * LANES]) + dot_tn(odd, cols[:, LANES:])
     bias1 = jnp.sum(even.astype(F32) + odd.astype(F32), axis=0, keepdims=True)
     bias2 = jnp.sum(grad.astype(F32), axis=0, keepdims=True)
@@ -386,25 +386,18 @@
 
     got_parts = exchange(parts, "y")
     code = jnp.repeat(routes[:, 0] * 32 + lengths, HALF)
-    cols, slopes, turned, live_grad, wanted = pl.pallas_call(
+    slopes, turned, live_grad, wanted = pl.pallas_call(
         slope_kernel,
         grid=(HOLDERS // 2,),
         in_specs=[pay_spec, *[vmem()] * 5],
-        out_specs=[
-            pl.BlockSpec((some, 4 * LANES), lambda i: (i, 0)),
-            pl.BlockSpec((2, some, WIDE), lambda i: (0, i, 0)),
-            pl.BlockSpec((3, WIDE, some), lambda i: (0, 0, i)),
-            vmem(),
-            vmem(),
-        ],
+        out_specs=[pl.BlockSpec((2, some, WIDE), lambda i: (0, i, 0)), vmem(), vmem(), vmem()],
         out_shape=[
-            in_hbm(rows, 4 * LANES),
             shape(2, rows, WIDE, dtype=F32),
-            shape(3, WIDE, rows),
+            shape(3 * WIDE + rows, rows),
             in_hbm(STEPS, D2),
             shape(SLOTS * HALF, STEPS),
         ],
-        scratch_shapes=[pltpu.VMEM(frames, F32)],
+        scratch_shapes=[pltpu.VMEM(frames, F32), pltpu.VMEM((some, 4 * LANES), BF16)],
         compiler_params=params(20, "arbitrary"),
         name="stem_slopes",
     )(got_pay, w1, b1, from_hbm(out_grad.reshape(STEPS, D2)), code[:, None], code[None])
@@ -424,22 +417,17 @@
         backward_kernel,
         in_specs=[
             pl.BlockSpec(memory_space=pltpu.SMEM),
-            *[vmem()] * (1 + BLOCKS),
-            pl.BlockSpec(memory_space=pl.ANY),
-            vmem(),
-            vmem(),
+            *[vmem()] * (3 + BLOCKS),
         ],
         out_specs=[vmem()] * 2,
         out_shape=[shape(2, 2, PACK, LANES, dtype=F32), shape(2, 2, PACK, LANES)],
         scratch_shapes=[
             pltpu.VMEM((WIDE, 3 * D2), BF16),
             pltpu.VMEM((WIDE, D2), F32),
-            pltpu.VMEM((rows, 4 * LANES), BF16),
-            pltpu.SemaphoreType.DMA,
         ],
         compiler_params=params(32),
         name="stem_backward",
-    )(where, got_grad, *weights, from_hbm(cols), turned, slopes)
+    )(where, got_grad, *weights, turned, slopes)
     got = lax.ppermute(send, "c", cores)
     quarters = exchange((keep + got.astype(F32)).astype(BF16).reshape(4, PACK, LANES), ("xh", "xl"))
 

time: 148 us -> 148 us (level)
  no operation moved by 1% of the time
where the time goes in v15:
time: 148 us; the launch traced here: 147 us
  starting transfers between devices  56.4 us (38%)
  blocking collectives  47.3 us (32%)
  Pallas kernels  19.7 us (13%)
  waiting for transfers between devices  19.2 us (13%)
  local copies, waits for them, and re-layouts  2.49 us (2%)
    all_to_all x4, blocking collectives, exchange(): return lax.all_to_all(values, axes, split_axis=0, concat_axis=0, tiled=True)  47.3 us
    ppermute x2, starting transfers between devices, with_group(): lax.ppermute(values, 'zh', [(i, i ^ flip) for i in range(4)])  16 us
    all_to_all x3, starting transfers between devices, exchange(): return lax.all_to_all(values, axes, split_axis=0, concat_axis=0, tiled=True)  11.2 us
    ppermute x1, starting transfers between devices, local(): got_cross = lax.ppermute(got, 'c', cores)  8.81 us
    ppermute x1, waiting for transfers between devices, local(): other = lax.ppermute(own, 'xl', [(0, 1), (1, 0)])  6.95 us
    ppermute x1, starting transfers between devices, local(): lax.ppermute(conv2_weight, ('xh', 'xl'), [(0, 3), (3, 0), (1, 2), (2, 1)])  5.35 us
    ppermute x1, starting transfers between devices, local(): got = lax.ppermute(send, 'c', cores)  5.07 us
    ppermute x2, waiting for transfers between devices, with_group(): lax.ppermute(values, 'zh', [(i, i ^ flip) for i in range(4)])  5.06 us
  transfers between devices with their start and end apart: 11, of which 7 were waited for; matrix products, arithmetic and copies ran while one was open for 0% of the time, Pallas kernels for 6%

profile of v15, /device:TPU:1, one launch (start us, length us, event | category | flops | bytes accessed | tf_op | source)
XLA Modules:
  0.0 147.4 jit_solution(14497360115538817874)
XLA Ops:
  0.6 0.0 copy-start.2
  0.7 5.3 %collective-permute-start.1 = (bf16[80,1920]{1,0:T(8,128)(2,1)}, bf16[80,1920]{1,0:T(8,128)(2,1)S(1)}, u32[]{:S(2)}, u32[]{:S(2)}) collective-permute-start(bf16[80,1920]{1,0:T(8,128)(2,1)} %own_ref.3), channel_id=1, source_target_pairs={{0,257},{257,0},{1,256},{256,1},{2,259},{259,2},{3,258},{258,3},{4... | collective-permute-start | bytes 921608 | tf_op jit(solution)/shard_map/ppermute | solution.py:347
  6.0 1.7 %mel_payload.1 = bf16[4,26,16,128]{3,2,1,0:T(8,128)(2,1)} custom-call(s32[16]{0:T(128)} %length_ref.1, bf16[16,16,128]{2,1,0:T(8,128)(2,1)} %mel_ref.1), custom_call_target="tpu_custom_call" | custom-call | tf_op jit(solution)/shard_map/mel_payload/pallas_call | solution.py:337
  7.7 4.2 %all-to-all-start = ((bf16[4,26,16,128]{3,2,1,0:T(8,128)(2,1)}), bf16[4,26,16,128]{3,2,1,0:T(8,128)(2,1)S(1)}, u32[]{:S(2)}, u32[]{:S(2)}) async-start(bf16[4,26,16,128]{3,2,1,0:T(8,128)(2,1)} %mel_payload.1), calls=%async_computation | async-start | bytes 851968 | tf_op jit(solution)/shard_map/all_to_all | solution.py:309
  11.9 0.1 pad_add_fusion.where_ref
  11.9 4.8 %collective-permute-start = (bf16[80,1920]{1,0:T(8,128)(2,1)}, bf16[80,1920]{1,0:T(8,128)(2,1)S(1)}, u32[]{:S(2)}, u32[]{:S(2)}) collective-permute-start(bf16[80,1920]{1,0:T(8,128)(2,1)} %own_ref.3), channel_id=1, source_target_pairs={{0,32},{32,0},{1,33},{33,1},{2,34},{34,2},{3,35},{35,3},{4,36},{36... | collective-permute-start | bytes 921608 | tf_op jit(solution)/shard_map/ppermute | solution.py:362
  16.7 3.0 %collective-permute-start.2 = (bf16[80,1920]{1,0:T(8,128)(2,1)S(1)}, bf16[80,1920]{1,0:T(8,128)(2,1)S(1)}, u32[]{:S(2)}, u32[]{:S(2)}) collective-permute-start(bf16[80,1920]{1,0:T(8,128)(2,1)S(1)} %collective-permute-done.1.far_ref), channel_id=1, source_target_pairs={{0,32},{32,0},{1,33},{33,1},{2,34},{34,2},{3,35},{35,3},{4,36},{36... | collective-permute-start | bytes 921608 | tf_op jit(solution)/shard_map/ppermute | solution.py:364
  19.8 1.4 conv1_columns.1
  21.1 0.0 copy-start.7
  21.2 0.0 copy-start.3
  21.2 0.0 copy-start.5
  21.2 0.0 copy-start.11
  21.2 0.0 copy-start.12
  21.2 0.0 copy-start.10
  21.2 3.3 %stem_forward.1 = bf16[4,128,640]{2,1,0:T(8,128)(2,1)} custom-call(bf16[4,26,16,128]{3,2,1,0:T(8,128)(2,1)S(1)} %all-to-all-done.pay_ref, bf16[384,384]{1,0:T(8,128)(2,1)S(1)} %get-tuple-element.26.w1_ref, f32[1,384]{1,0:T(1,128)S(1)} %get-tuple-element.27.b1_ref, bf16[80,1920]{1,0:T(8,128)(2,1)S(1)} %copy-done.2, ...), custom_call_target="tpu_custom_call" | custom-call | tf_op jit(solution)/shard_map/stem_forward/pallas_call | solution.py:372
  24.6 3.5 %all-to-all-start.1 = ((bf16[4,128,640]{2,1,0:T(8,128)(2,1)}), bf16[4,128,640]{2,1,0:T(8,128)(2,1)S(1)}, u32[]{:S(2)}, u32[]{:S(2)}) async-start(bf16[4,128,640]{2,1,0:T(8,128)(2,1)} %stem_forward.1), calls=%async_computation.1 | async-start | bytes 1310720 | tf_op jit(solution)/shard_map/all_to_all | solution.py:309
  28.1 0.1 broadcast_in_dim.14
  28.2 0.1 broadcast_in_dim_reshape.7.row_ref
  28.3 0.1 broadcast_in_dim_reshape.8.column_ref
  28.4 0.0 copy-start.8
  28.4 1.0 copy-done.8
  29.4 3.7 %stem_slopes.1 = (f32[2,512,384]{2,1,0:T(8,128)S(1)}, bf16[1664,512]{1,0:T(8,128)(2,1)S(1)}, bf16[128,640]{1,0:T(8,128)(2,1)}, bf16[256,128]{1,0:T(8,128)(2,1)S(1)}) custom-call(bf16[4,26,16,128]{3,2,1,0:T(8,128)(2,1)S(1)} %all-to-all-done.pay_ref, bf16[384,384]{1,0:T(8,128)(2,1)S(1)} %copy-done.8, f32[1,384]{1,0:T(1,128)S(1)} %get-tuple-element.27.b1_ref, ...), custom_call_target="tpu_custom_call" | custom-call | tf_op jit(solution)/shard_map/stem_slopes/pallas_call | solution.py:389
  33.1 1.1 copy-done
  34.3 3.7 %all-to-all-done.1.part_ref = bf16[4,128,640]{2,1,0:T(8,128)(2,1)S(1)} async-done(((bf16[4,128,640]{2,1,0:T(8,128)(2,1)}), bf16[4,128,640]{2,1,0:T(8,128)(2,1)S(1)}, u32[]{:S(2)}, u32[]{:S(2)}) %all-to-all-start.1) | async-done | bytes 655392 | tf_op jit(solution)/shard_map/all_to_all | solution.py:309
  38.0 1.8 %stem_middle.1 = (bf16[4,128,640]{2,1,0:T(8,128)(2,1)S(1)}, bf16[8,80,128]{2,1,0:T(8,128)(2,1)S(1)}, bf16[8,80,128]{2,1,0:T(8,128)(2,1)S(1)}) custom-call(s32[4]{0:T(128)S(1)} %pad_add_fusion.where_ref, bf16[4,128,640]{2,1,0:T(8,128)(2,1)S(1)} %all-to-all-done.1.part_ref, f32[1,640]{1,0:T(1,128)S(1)} %broadcast_in_dim.15.b2_ref, ...), custom_call_target="tpu_custom_call" | custom-call | tf_op jit(solution)/shard_map/stem_middle/pallas_call | solution.py:405
  39.8 11.1 %all_to_all.35.grad_ref = bf16[4,128,640]{2,1,0:T(8,128)(2,1)S(1)} all-to-all(bf16[4,128,640]{2,1,0:T(8,128)(2,1)S(1)} %get-tuple-element.35), channel_id=1, replica_groups=mesh['xh'=2,'y'=4,'c'=2,'zh'=4,'zl'=4,'xl'=2] {'y'}, dimensions={0} | all-to-all | bytes 1310720 | tf_op jit(solution)/shard_map/all_to_all | solution.py:309
  50.9 3.4 %stem_backward.1 = (f32[2,2,896,128]{3,2,1,0:T(8,128)S(1)}, bf16[2,2,896,128]{3,2,1,0:T(8,128)(2,1)S(1)}) custom-call(s32[4]{0:T(128)S(1)} %pad_add_fusion.where_ref, bf16[4,128,640]{2,1,0:T(8,128)(2,1)S(1)} %all_to_all.35.grad_ref, bf16[80,1920]{1,0:T(8,128)(2,1)S(1)} %copy-done.2, bf16[80,1920]{1,0:T(8,128)(2,1)S(1)} %copy-done.4, ...), custom_call_target="tpu_custom_call" | custom-call | tf_op jit(solution)/shard_map/stem_backward/pallas_call | solution.py:416
  54.3 5.1 %collective-permute-start.3 = (bf16[2,2,896,128]{3,2,1,0:T(8,128)(2,1)S(1)}, bf16[2,2,896,128]{3,2,1,0:T(8,128)(2,1)S(1)}, u32[]{:S(2)}, u32[]{:S(2)}) collective-permute-start(bf16[2,2,896,128]{3,2,1,0:T(8,128)(2,1)S(1)} %get-tuple-element.39), channel_id=1, source_target_pairs={{0,32},{32,0},{1,33},{33,1},{2,34},{34,2},{3,35},{35,3},{4,36},{36... | collective-permute-start | bytes 2752520 | tf_op jit(solution)/shard_map/ppermute | solution.py:431
  59.4 2.1 %collective-permute-done.3 = bf16[2,2,896,128]{3,2,1,0:T(8,128)(2,1)S(1)} collective-permute-done((bf16[2,2,896,128]{3,2,1,0:T(8,128)(2,1)S(1)}, bf16[2,2,896,128]{3,2,1,0:T(8,128)(2,1)S(1)}, u32[]{:S(2)}, u32[]{:S(2)}) %collective-permute-start.3) | collective-permute-done | bytes 917536 | tf_op jit(solution)/shard_map/ppermute | solution.py:431
  61.5 0.2 add_convert_fusion
  61.7 16.9 %all_to_all.36.got_ref = bf16[4,896,128]{2,1,0:T(8,128)(2,1)S(1)} all-to-all(bf16[4,896,128]{2,1,0:T(8,128)(2,1)S(1)} %bitcast.12), channel_id=1, replica_groups=mesh['xh'=2,'y'=4,'c'=2,'zh'=4,'zl'=4,'xl'=2] {'xh','xl'}, dimensions={0} | all-to-all | bytes 1835008 | tf_op jit(solution)/shard_map/all_to_all | solution.py:309
  78.5 0.1 gradient_sum.2
  78.7 9.0 %all_to_all.37.got_ref = bf16[4,224,128]{2,1,0:T(8,128)(2,1)S(1)} all-to-all(bf16[4,224,128]{2,1,0:T(8,128)(2,1)S(1)} %bitcast.11), channel_id=1, replica_groups=mesh['xh'=2,'y'=4,'c'=2,'zh'=4,'zl'=4,'xl'=2] {'zl'}, dimensions={0} | all-to-all | bytes 458752 | tf_op jit(solution)/shard_map/all_to_all | solution.py:309
  87.7 8.8 %collective-permute-start.4 = (bf16[224,128]{1,0:T(8,128)(2,1)S(1)}, bf16[224,128]{1,0:T(8,128)(2,1)S(1)}, u32[]{:S(2)}, u32[]{:S(2)}) collective-permute-start(bf16[224,128]{1,0:T(8,128)(2,1)S(1)} %gradient_sum.3.own_ref), channel_id=1, source_target_pairs={{0,8},{8,0},{16,24},{24,16},{1,9},{9,1},{17,25},{25,17},{2,10},{10... | collective-permute-start | bytes 172040 | tf_op jit(solution)/shard_map/ppermute | solution.py:456
  96.6 2.8 %collective-permute-done.4.other_ref = bf16[224,128]{1,0:T(8,128)(2,1)S(1)} collective-permute-done((bf16[224,128]{1,0:T(8,128)(2,1)S(1)}, bf16[224,128]{1,0:T(8,128)(2,1)S(1)}, u32[]{:S(2)}, u32[]{:S(2)}) %collective-permute-start.4) | collective-permute-done | bytes 57376 | tf_op jit(solution)/shard_map/ppermute | solution.py:456
  99.4 7.2 %collective-permute-start.5 = (bf16[224,128]{1,0:T(8,128)(2,1)S(1)}, bf16[224,128]{1,0:T(8,128)(2,1)S(1)}, u32[]{:S(2)}, u32[]{:S(2)}) collective-permute-start(bf16[224,128]{1,0:T(8,128)(2,1)S(1)} %gradient_pair.2.own_ref), channel_id=1, source_target_pairs={{0,24},{8,16},{16,8},{24,0},{1,25},{9,17},{17,9},{25,1},{2,26},{10... | collective-permute-start | bytes 172040 | tf_op jit(solution)/shard_map/ppermute | solution.py:456
  106.6 2.3 %collective-permute-done.5.other_ref = bf16[224,128]{1,0:T(8,128)(2,1)S(1)} collective-permute-done((bf16[224,128]{1,0:T(8,128)(2,1)S(1)}, bf16[224,128]{1,0:T(8,128)(2,1)S(1)}, u32[]{:S(2)}, u32[]{:S(2)}) %collective-permute-start.5) | collective-permute-done | bytes 57376 | tf_op jit(solution)/shard_map/ppermute | solution.py:456
  108.9 10.3 %all_to_all.38 = bf16[4,224,128]{2,1,0:T(8,128)(2,1)S(1)} all-to-all(bf16[4,224,128]{2,1,0:T(8,128)(2,1)S(1)} %gradient_pair.3), channel_id=1, replica_groups=mesh['xh'=2,'y'=4,'c'=2,'zh'=4,'zl'=4,'xl'=2] {'zl'}, dimensions={0} | all-to-all | bytes 458752 | tf_op jit(solution)/shard_map/all_to_all | solution.py:309
  119.2 0.1 broadcast_in_dim.16
  119.3 1.0 pad_maximum_fusion
  120.3 3.6 %all-to-all-start.6 = ((bf16[8,416,128]{2,1,0:T(8,128)(2,1)}), bf16[8,416,128]{2,1,0:T(8,128)(2,1)S(1)}, u32[]{:S(2)}, u32[]{:S(2)}) async-start(bf16[8,416,128]{2,1,0:T(8,128)(2,1)} %pad_maximum_fusion), calls=%async_computation.6 | async-start | bytes 1703936 | tf_op jit(solution)/shard_map/all_to_all | solution.py:309
  123.8 2.2 %collective-permute-start.6 = (bf16[640,128]{1,0:T(8,128)(2,1)S(1)}, bf16[640,128]{1,0:T(8,128)(2,1)S(1)}, u32[]{:S(2)}, u32[]{:S(2)}) collective-permute-start(bf16[640,128]{1,0:T(8,128)(2,1)S(1)} %slice.20.own_ref), channel_id=1, source_target_pairs={{0,1},{1,0},{2,3},{3,2},{4,5},{5,4},{6,7},{7,6},{8,9},{9,8},{10,11... | collective-permute-start | bytes 491528 | tf_op jit(solution)/shard_map/ppermute | solution.py:461
  126.0 7.0 %collective-permute-done.6.other_ref = bf16[640,128]{1,0:T(8,128)(2,1)S(1)} collective-permute-done((bf16[640,128]{1,0:T(8,128)(2,1)S(1)}, bf16[640,128]{1,0:T(8,128)(2,1)S(1)}, u32[]{:S(2)}, u32[]{:S(2)}) %collective-permute-start.6) | collective-permute-done | bytes 163872 | tf_op jit(solution)/shard_map/ppermute | solution.py:461
  133.0 0.8 all-to-all-done.6.got_ref
  133.8 8.8 %collective-permute-start.7 = (bf16[8,416,128]{2,1,0:T(8,128)(2,1)S(1)}, bf16[8,416,128]{2,1,0:T(8,128)(2,1)S(1)}, u32[]{:S(2)}, u32[]{:S(2)}) collective-permute-start(bf16[8,416,128]{2,1,0:T(8,128)(2,1)S(1)} %all-to-all-done.6.got_ref), channel_id=1, source_target_pairs={{0,32},{32,0},{1,33},{33,1},{2,34},{34,2},{3,35},{35,3},{4,36},{36... | collective-permute-start | bytes 2555912 | tf_op jit(solution)/shard_map/ppermute | solution.py:465
  142.6 1.4 conv2_unpack.1
  144.0 0.6 collective-permute-done.7.cross_ref
  144.6 2.8 %gradient_unpack.1 = (f32[384,1280]{1,0:T(8,128)}, f32[1280]{0:T(1024)}, f32[640]{0:T(1024)}, bf16[256,640]{1,0:T(8,128)(2,1)}) custom-call(s32[4]{0:T(128)S(1)} %pad_add_fusion.where_ref, bf16[8,416,128]{2,1,0:T(8,128)(2,1)S(1)} %all-to-all-done.6.got_ref, bf16[8,416,128]{2,1,0:T(8,128)(2,1)S(1)} %collective-permute-done.7.cross_ref), custom_call_target="tpu_custom_call" | custom-call | tf_op jit(solution)/shard_map/gradient_unpack/pallas_call | solution.py:474
  (29 shorter events, 0.1 us)
Async XLA Ops:
  0.6 20.6 %copy-start.2 = (bf16[80,1920]{1,0:T(8,128)(2,1)S(1)}, bf16[80,1920]{1,0:T(8,128)(2,1)}, u32[]{:S(2)}) copy-start(bf16[80,1920]{1,0:T(8,128)(2,1)} %own_ref.3) | copy-start | bytes 921604
  0.6 19.1 %copy-start.9 = (bf16[384,1280]{1,0:T(8,128)(2,1)S(1)}, bf16[384,1280]{1,0:T(8,128)(2,1)}, u32[]{:S(2)}) copy-start(bf16[384,1280]{1,0:T(8,128)(2,1)} %weight_ref.1) | copy-start | bytes 2949124
  0.7 16.1 %collective-permute-start.1 = (bf16[80,1920]{1,0:T(8,128)(2,1)}, bf16[80,1920]{1,0:T(8,128)(2,1)S(1)}, u32[]{:S(2)}, u32[]{:S(2)}) collective-permute-start(bf16[80,1920]{1,0:T(8,128)(2,1)} %own_ref.3), channel_id=1, source_target_pairs={{0,257},{257,0},{1,256},{256,1},{2,259},{259,2},{3,258},{258,3},{4... | collective-permute-start | bytes 921608 | tf_op jit(solution)/shard_map/ppermute | solution.py:347
  7.7 13.5 %all-to-all-start = ((bf16[4,26,16,128]{3,2,1,0:T(8,128)(2,1)}), bf16[4,26,16,128]{3,2,1,0:T(8,128)(2,1)S(1)}, u32[]{:S(2)}, u32[]{:S(2)}) async-start(bf16[4,26,16,128]{3,2,1,0:T(8,128)(2,1)} %mel_payload.1), calls=%async_computation | async-start | bytes 851968 | tf_op jit(solution)/shard_map/all_to_all | solution.py:309
  11.9 9.2 %collective-permute-start = (bf16[80,1920]{1,0:T(8,128)(2,1)}, bf16[80,1920]{1,0:T(8,128)(2,1)S(1)}, u32[]{:S(2)}, u32[]{:S(2)}) collective-permute-start(bf16[80,1920]{1,0:T(8,128)(2,1)} %own_ref.3), channel_id=1, source_target_pairs={{0,32},{32,0},{1,33},{33,1},{2,34},{34,2},{3,35},{35,3},{4,36},{36... | collective-permute-start | bytes 921608 | tf_op jit(solution)/shard_map/ppermute | solution.py:362
  16.7 4.4 %collective-permute-start.2 = (bf16[80,1920]{1,0:T(8,128)(2,1)S(1)}, bf16[80,1920]{1,0:T(8,128)(2,1)S(1)}, u32[]{:S(2)}, u32[]{:S(2)}) collective-permute-start(bf16[80,1920]{1,0:T(8,128)(2,1)S(1)} %collective-permute-done.1.far_ref), channel_id=1, source_target_pairs={{0,32},{32,0},{1,33},{33,1},{2,34},{34,2},{3,35},{35,3},{4,36},{36... | collective-permute-start | bytes 921608 | tf_op jit(solution)/shard_map/ppermute | solution.py:364
  21.1 3.5 %copy-start.7 = (bf16[384,384]{1,0:T(8,128)(2,1)}, bf16[384,384]{1,0:T(8,128)(2,1)S(1)}, u32[]{:S(2)}) copy-start(bf16[384,384]{1,0:T(8,128)(2,1)S(1)} %get-tuple-element.26.w1_ref) | copy-start | bytes 884740
  21.2 3.4 %copy-start.3 = (bf16[80,1920]{1,0:T(8,128)(2,1)}, bf16[80,1920]{1,0:T(8,128)(2,1)S(1)}, u32[]{:S(2)}) copy-start(bf16[80,1920]{1,0:T(8,128)(2,1)S(1)} %collective-permute-done.side_ref) | copy-start | bytes 921604
  21.2 3.4 %copy-start.5 = (bf16[80,1920]{1,0:T(8,128)(2,1)}, bf16[80,1920]{1,0:T(8,128)(2,1)S(1)}, u32[]{:S(2)}) copy-start(bf16[80,1920]{1,0:T(8,128)(2,1)S(1)} %collective-permute-done.2.both_ref) | copy-start | bytes 921604
  21.2 6.9 %copy-start.11 = (s32[16]{0:T(128)S(1)}, s32[16]{0:T(128)}, u32[]{:S(2)}) copy-start(s32[16]{0:T(128)} %length_ref.1) | copy-start | bytes 196
  21.2 6.9 %copy-start.12 = (s32[16,1]{0,1:T(1,128)S(1)}, s32[16,1]{0,1:T(1,128)}, u32[]{:S(2)}) copy-start(s32[16,1]{0,1:T(1,128)} %param.10) | copy-start | bytes 196
  21.2 7.2 %copy-start.10 = (f32[640]{0:T(1024)S(1)}, f32[640]{0:T(1024)}, u32[]{:S(2)}) copy-start(f32[640]{0:T(1024)} %param.14) | copy-start | bytes 7684
  24.6 13.4 %all-to-all-start.1 = ((bf16[4,128,640]{2,1,0:T(8,128)(2,1)}), bf16[4,128,640]{2,1,0:T(8,128)(2,1)S(1)}, u32[]{:S(2)}, u32[]{:S(2)}) async-start(bf16[4,128,640]{2,1,0:T(8,128)(2,1)} %stem_forward.1), calls=%async_computation.1 | async-start | bytes 1310720 | tf_op jit(solution)/shard_map/all_to_all | solution.py:309
  28.4 1.0 copy-start.8
  33.1 1.1 copy-start
  34.2 16.6 %copy-start.4 = (bf16[80,1920]{1,0:T(8,128)(2,1)S(1)}, bf16[80,1920]{1,0:T(8,128)(2,1)}, u32[]{:S(2)}) copy-start(bf16[80,1920]{1,0:T(8,128)(2,1)} %copy-done.3) | copy-start | bytes 921604
  38.0 12.9 %copy-start.1 = (f32[2,512,384]{2,1,0:T(8,128)S(1)}, f32[2,512,384]{2,1,0:T(8,128)}, u32[]{:S(2)}) copy-start(f32[2,512,384]{2,1,0:T(8,128)} %copy-done) | copy-start | bytes 4718596
  38.0 12.9 %copy-start.6 = (bf16[80,1920]{1,0:T(8,128)(2,1)S(1)}, bf16[80,1920]{1,0:T(8,128)(2,1)}, u32[]{:S(2)}) copy-start(bf16[80,1920]{1,0:T(8,128)(2,1)} %copy-done.5) | copy-start | bytes 921604
  54.3 7.2 %collective-permute-start.3 = (bf16[2,2,896,128]{3,2,1,0:T(8,128)(2,1)S(1)}, bf16[2,2,896,128]{3,2,1,0:T(8,128)(2,1)S(1)}, u32[]{:S(2)}, u32[]{:S(2)}) collective-permute-start(bf16[2,2,896,128]{3,2,1,0:T(8,128)(2,1)S(1)} %get-tuple-element.39), channel_id=1, source_target_pairs={{0,32},{32,0},{1,33},{33,1},{2,34},{34,2},{3,35},{35,3},{4,36},{36... | collective-permute-start | bytes 2752520 | tf_op jit(solution)/shard_map/ppermute | solution.py:431
  87.7 11.6 %collective-permute-start.4 = (bf16[224,128]{1,0:T(8,128)(2,1)S(1)}, bf16[224,128]{1,0:T(8,128)(2,1)S(1)}, u32[]{:S(2)}, u32[]{:S(2)}) collective-permute-start(bf16[224,128]{1,0:T(8,128)(2,1)S(1)} %gradient_sum.3.own_ref), channel_id=1, source_target_pairs={{0,8},{8,0},{16,24},{24,16},{1,9},{9,1},{17,25},{25,17},{2,10},{10... | collective-permute-start | bytes 172040 | tf_op jit(solution)/shard_map/ppermute | solution.py:456
  99.4 9.5 %collective-permute-start.5 = (bf16[224,128]{1,0:T(8,128)(2,1)S(1)}, bf16[224,128]{1,0:T(8,128)(2,1)S(1)}, u32[]{:S(2)}, u32[]{:S(2)}) collective-permute-start(bf16[224,128]{1,0:T(8,128)(2,1)S(1)} %gradient_pair.2.own_ref), channel_id=1, source_target_pairs={{0,24},{8,16},{16,8},{24,0},{1,25},{9,17},{17,9},{25,1},{2,26},{10... | collective-permute-start | bytes 172040 | tf_op jit(solution)/shard_map/ppermute | solution.py:456
  120.3 13.5 %all-to-all-start.6 = ((bf16[8,416,128]{2,1,0:T(8,128)(2,1)}), bf16[8,416,128]{2,1,0:T(8,128)(2,1)S(1)}, u32[]{:S(2)}, u32[]{:S(2)}) async-start(bf16[8,416,128]{2,1,0:T(8,128)(2,1)} %pad_maximum_fusion), calls=%async_computation.6 | async-start | bytes 1703936 | tf_op jit(solution)/shard_map/all_to_all | solution.py:309
  123.8 9.1 %collective-permute-start.6 = (bf16[640,128]{1,0:T(8,128)(2,1)S(1)}, bf16[640,128]{1,0:T(8,128)(2,1)S(1)}, u32[]{:S(2)}, u32[]{:S(2)}) collective-permute-start(bf16[640,128]{1,0:T(8,128)(2,1)S(1)} %slice.20.own_ref), channel_id=1, source_target_pairs={{0,1},{1,0},{2,3},{3,2},{4,5},{5,4},{6,7},{7,6},{8,9},{9,8},{10,11... | collective-permute-start | bytes 491528 | tf_op jit(solution)/shard_map/ppermute | solution.py:461
  133.8 10.8 %collective-permute-start.7 = (bf16[8,416,128]{2,1,0:T(8,128)(2,1)S(1)}, bf16[8,416,128]{2,1,0:T(8,128)(2,1)S(1)}, u32[]{:S(2)}, u32[]{:S(2)}) collective-permute-start(bf16[8,416,128]{2,1,0:T(8,128)(2,1)S(1)} %all-to-all-done.6.got_ref), channel_id=1, source_target_pairs={{0,32},{32,0},{1,33},{33,1},{2,34},{34,2},{3,35},{35,3},{4,36},{36... | collective-permute-start | bytes 2555912 | tf_op jit(solution)/shard_map/ppermute | solution.py:465

commit v16 on v15

--- a/solution.py
+++ b/solution.py
@@ -130,36 +130,30 @@
 
 
 def forward_kernel(
-    pay_ref, w1_ref, b1_ref, own_ref, side_ref, far_ref, both_ref, part_ref, w2_ref, cols_ref, frames_ref
+    pay_ref, w1_ref, b1_ref, own_ref, side_ref, far_ref, both_ref, grad_ref, column_ref, row_ref,
+    part_ref, slope_ref, turned_ref, live_grad_ref, wanted_ref, w2_ref, cols_ref, frames_ref,
 ):
     @pl.when(pl.program_id(0) == 0)
     def _():
         stack_weights((own_ref, side_ref, far_ref, both_ref), w2_ref)
 
     pre_even, pre_odd, live_even, live_odd = first_conv(pay_ref, w1_ref, b1_ref, cols_ref, frames_ref)
-    odd = jnp.where(live_odd, gelu_value(pre_odd), 0.0)
-    total = dot(odd.astype(BF16), w2_ref[:, 2 * D2 :]) + dot(shift_down(odd).astype(BF16), w2_ref[:, :D2])
-    even = jnp.where(live_even, gelu_value(pre_even), 0.0)
-    total = total + dot(even.astype(BF16), w2_ref[:, D2 : 2 * D2])
-    part_ref[...] = total.astype(BF16).reshape(part_ref.shape)
-
-
-def slope_kernel(
-    pay_ref, w1_ref, b1_ref, grad_ref, column_ref, row_ref,
-    slope_ref, turned_ref, live_grad_ref, wanted_ref, frames_ref, cols_ref,
-):
-    pre_even, pre_odd, live_even, live_odd = first_conv(pay_ref, w1_ref, b1_ref, cols_ref, frames_ref)
     some = pre_odd.shape[0]
     lanes = pl.ds(pl.multiple_of(pl.program_id(0) * some, some), some)
+    value, slope = gelu_both(pre_odd)
+    value = jnp.where(live_odd, value, 0.0)
+    odd, prior = value.astype(BF16), shift_down(value).astype(BF16)
+    slope_ref[1] = jnp.where(live_odd, slope, 0.0)
+    total = dot(odd, w2_ref[:, 2 * D2 :]) + dot(prior, w2_ref[:, :D2])
+    value, slope = gelu_both(pre_even)
+    even = jnp.where(live_even, value, 0.0).astype(BF16)
+    slope_ref[0] = jnp.where(live_even, slope, 0.0)
+    total = total + dot(even, w2_ref[:, D2 : 2 * D2])
+    part_ref[...] = total.astype(BF16).reshape(part_ref.shape)
     turned_ref[pl.ds(pl.multiple_of(3 * WIDE + pl.program_id(0) * some, some // 2), some), :] = cols_ref[...]
-    value, slope = gelu_both(pre_odd)
-    odd = jnp.where(live_odd, value, 0.0)
-    slope_ref[1] = jnp.where(live_odd, slope, 0.0)
-    turned_ref[:WIDE, lanes] = shift_down(odd).astype(BF16).T
-    turned_ref[2 * WIDE : 3 * WIDE, lanes] = odd.astype(BF16).T
-    value, slope = gelu_both(pre_even)
-    slope_ref[0] = jnp.where(live_even, slope, 0.0)
-    turned_ref[WIDE : 2 * WIDE, lanes] = jnp.where(live_even, value, 0.0).astype(BF16).T
+    turned_ref[:WIDE, lanes] = prior.T
+    turned_ref[WIDE : 2 * WIDE, lanes] = even.T
+    turned_ref[2 * WIDE : 3 * WIDE, lanes] = odd.T
 
     @pl.when(pl.program_id(0) == 0)
     def _():
@@ -188,7 +182,7 @@
     pre = part_ref[0].astype(F32)
     for source in range(1, HOLDERS):
         pre = pre + part_ref[source].astype(F32)
-    value, slope = gelu_both(pre + b2_ref[...])
+    value, slope = gelu_both(pre + b2_ref[...].reshape(1, D2))
     copy.wait()
     second_grad = (live_grad_here[...].astype(F32) * slope).astype(BF16)
     for target in range(HOLDERS):
@@ -369,39 +363,32 @@
     rows, some = HOLDERS * STEPS, 2 * STEPS
     frames = (2, 2 * STEPS, MEL)
     pay_spec = pl.BlockSpec((2, PAY, 2 * HALF, MEL), pair4)
-    parts = pl.pallas_call(
+    code = jnp.repeat(routes[:, 0] * 32 + lengths, HALF)
+    parts, slopes, turned, live_grad, wanted = pl.pallas_call(
         forward_kernel,
         grid=(HOLDERS // 2,),
-        in_specs=[pay_spec, *[vmem()] * (2 + BLOCKS)],
-        out_specs=pl.BlockSpec((2, STEPS, D2), pair),
-        out_shape=in_hbm(HOLDERS, STEPS, D2),
+        in_specs=[pay_spec, *[vmem()] * (5 + BLOCKS)],
+        out_specs=[
+            pl.BlockSpec((2, STEPS, D2), pair),
+            pl.BlockSpec((2, some, WIDE), lambda i: (0, i, 0)),
+            *[vmem()] * 3,
+        ],
+        out_shape=[
+            shape(HOLDERS, STEPS, D2),
+            shape(2, rows, WIDE, dtype=F32),
+            shape(3 * WIDE + rows, rows),
+            in_hbm(STEPS, D2),
+            shape(SLOTS * HALF, STEPS),
+        ],
         scratch_shapes=[
             pltpu.VMEM((WIDE, 3 * D2), BF16),
             pltpu.VMEM((some, 4 * LANES), BF16),
             pltpu.VMEM(frames, F32),
         ],
-        compiler_params=params(20, "arbitrary"),
+        compiler_params=params(24, "arbitrary"),
         name="stem_forward",
-    )(got_pay, w1, b1, *weights)
-
+    )(got_pay, w1, b1, *weights, from_hbm(out_grad.reshape(STEPS, D2)), code[:, None], code[None])
     got_parts = exchange(parts, "y")
-    code = jnp.repeat(routes[:, 0] * 32 + lengths, HALF)
-    slopes, turned, live_grad, wanted = pl.pallas_call(
-        slope_kernel,
-        grid=(HOLDERS // 2,),
-        in_specs=[pay_spec, *[vmem()] * 5],
-        out_specs=[pl.BlockSpec((2, some, WIDE), lambda i: (0, i, 0)), vmem(), vmem(), vmem()],
-        out_shape=[
-            shape(2, rows, WIDE, dtype=F32),
-            shape(3 * WIDE + rows, rows),
-            in_hbm(STEPS, D2),
-            shape(SLOTS * HALF, STEPS),
-        ],
-        scratch_shapes=[pltpu.VMEM(frames, F32), pltpu.VMEM((some, 4 * LANES), BF16)],
-        compiler_params=params(20, "arbitrary"),
-        name="stem_slopes",
-    )(got_pay, w1, b1, from_hbm(out_grad.reshape(STEPS, D2)), code[:, None], code[None])
-    got_parts, slopes, turned = lax.optimization_barrier((got_parts, slopes, turned))
     rep, same, cross = pl.pallas_call(
         middle_kernel,
         in_specs=[pl.BlockSpec(memory_space=pltpu.SMEM), vmem(), vmem(), pl.BlockSpec(memory_space=pl.ANY), vmem()],
@@ -410,7 +397,7 @@
         scratch_shapes=[pltpu.VMEM((STEPS, D2), BF16), pltpu.SemaphoreType.DMA],
         compiler_params=params(10),
         name="stem_middle",
-    )(where, got_parts, conv2_bias[None], from_hbm(live_grad), wanted)
+    )(where, got_parts, conv2_bias, from_hbm(live_grad), wanted)
     got_grad = exchange(rep, "y")
 
     keep, send = pl.pallas_call(

time: 148 us -> 150 us (1.014)
  blocking collectives: 47.3 us -> 60.5 us
  waiting for transfers between devices: 19.2 us -> 15.5 us
  starting transfers between devices: 56.4 us -> 52.9 us
  local copies, waits for them, and re-layouts: 2.49 us -> 0.35 us
  Pallas kernels: 19.7 us -> 17.6 us
    all_to_all x4 -> x5, blocking collectives: 47.3 us -> 60.5 us  [exchange(): return lax.all_to_all(values, axes, split_axis=0, concat_axis=0, tiled=True)]
    all_to_all x3 -> x2, waiting for transfers between devices: 4.55 us -> 0.81 us  [exchange(): return lax.all_to_all(values, axes, split_axis=0, concat_axis=0, tiled=True)]
    pallas_call x1 -> x0, Pallas kernels: 3.73 us -> none  [local(): pl.pallas_call(slope_kernel, grid=(HOLDERS // 2,), in_specs=[pay_spec, *[...]
    all_to_all x3 -> x2, starting transfers between devices: 11.2 us -> 7.73 us  [exchange(): return lax.all_to_all(values, axes, split_axis=0, concat_axis=0, tiled=True)]
    unnamed x26 -> x6, local copies, waits for them, and re-layouts: 2.16 us -> 0.02 us
    pallas_call x1, Pallas kernels: 3.35 us -> 5 us  [local(): pl.pallas_call(forward_kernel, grid=(HOLDERS // 2,), in_specs=[pay_spec,...]
  transfers between devices with their start and end apart: 11 -> 10, of which waited for: 7 -> 6; matrix products, arithmetic and copies ran while one was open for 0% -> 1% of each run, Pallas kernels for 6% -> 3%
where the time goes in v16:
time: 150 us
  blocking collectives  60.5 us (40%)
  starting transfers between devices  52.9 us (35%)
  Pallas kernels  17.6 us (12%)
  waiting for transfers between devices  15.5 us (10%)
  other arithmetic  1.89 us (1%)
    all_to_all x5, blocking collectives, exchange(): return lax.all_to_all(values, axes, split_axis=0, concat_axis=0, tiled=True)  60.5 us
    ppermute x2, starting transfers between devices, with_group(): lax.ppermute(values, 'zh', [(i, i ^ flip) for i in range(4)])  16 us
    ppermute x1, starting transfers between devices, local(): got_cross = lax.ppermute(got, 'c', cores)  8.81 us
    all_to_all x2, starting transfers between devices, exchange(): return lax.all_to_all(values, axes, split_axis=0, concat_axis=0, tiled=True)  7.73 us
    ppermute x1, waiting for transfers between devices, local(): other = lax.ppermute(own, 'xl', [(0, 1), (1, 0)])  6.95 us
    ppermute x1, starting transfers between devices, local(): lax.ppermute(conv2_weight, ('xh', 'xl'), [(0, 3), (3, 0), (1, 2), (2, 1)])  5.35 us
    ppermute x2, waiting for transfers between devices, with_group(): lax.ppermute(values, 'zh', [(i, i ^ flip) for i in range(4)])  5.06 us
    ppermute x1, starting transfers between devices, local(): got = lax.ppermute(send, 'c', cores)  5.04 us
  transfers between devices with their start and end apart: 10, of which 6 were waited for; matrix products, arithmetic and copies ran while one was open for 1% of the time, Pallas kernels for 3%

profile of v16, /device:TPU:1, one launch (start us, length us, event | category | flops | bytes accessed | tf_op | source)
XLA Modules:
  0.0 149.6 jit_solution(13852567236616378988)
XLA Ops:
  0.6 0.0 copy-start
  0.6 0.0 copy-start.1
  0.7 5.3 %collective-permute-start.1 = (bf16[80,1920]{1,0:T(8,128)(2,1)}, bf16[80,1920]{1,0:T(8,128)(2,1)S(1)}, u32[]{:S(2)}, u32[]{:S(2)}) collective-permute-start(bf16[80,1920]{1,0:T(8,128)(2,1)} %own_ref.3), channel_id=1, source_target_pairs={{0,257},{257,0},{1,256},{256,1},{2,259},{259,2},{3,258},{258,3},{4... | collective-permute-start | bytes 921608 | tf_op jit(solution)/shard_map/ppermute | solution.py:341
  6.0 1.7 %mel_payload.1 = bf16[4,26,16,128]{3,2,1,0:T(8,128)(2,1)} custom-call(s32[16]{0:T(128)} %length_ref.1, bf16[16,16,128]{2,1,0:T(8,128)(2,1)} %mel_ref.1), custom_call_target="tpu_custom_call" | custom-call | tf_op jit(solution)/shard_map/mel_payload/pallas_call | solution.py:331
  7.7 4.2 %all-to-all-start = ((bf16[4,26,16,128]{3,2,1,0:T(8,128)(2,1)}), bf16[4,26,16,128]{3,2,1,0:T(8,128)(2,1)S(1)}, u32[]{:S(2)}, u32[]{:S(2)}) async-start(bf16[4,26,16,128]{3,2,1,0:T(8,128)(2,1)} %mel_payload.1), calls=%async_computation | async-start | bytes 851968 | tf_op jit(solution)/shard_map/all_to_all | solution.py:303
  11.9 0.1 pad_add_fusion.where_ref
  11.9 4.8 %collective-permute-start = (bf16[80,1920]{1,0:T(8,128)(2,1)}, bf16[80,1920]{1,0:T(8,128)(2,1)S(1)}, u32[]{:S(2)}, u32[]{:S(2)}) collective-permute-start(bf16[80,1920]{1,0:T(8,128)(2,1)} %own_ref.3), channel_id=1, source_target_pairs={{0,32},{32,0},{1,33},{33,1},{2,34},{34,2},{3,35},{35,3},{4,36},{36... | collective-permute-start | bytes 921608 | tf_op jit(solution)/shard_map/ppermute | solution.py:356
  16.7 0.0 collective-permute-done.1.far_ref
  16.7 3.0 %collective-permute-start.2 = (bf16[80,1920]{1,0:T(8,128)(2,1)S(1)}, bf16[80,1920]{1,0:T(8,128)(2,1)S(1)}, u32[]{:S(2)}, u32[]{:S(2)}) collective-permute-start(bf16[80,1920]{1,0:T(8,128)(2,1)S(1)} %collective-permute-done.1.far_ref), channel_id=1, source_target_pairs={{0,32},{32,0},{1,33},{33,1},{2,34},{34,2},{3,35},{35,3},{4,36},{36... | collective-permute-start | bytes 921608 | tf_op jit(solution)/shard_map/ppermute | solution.py:358
  19.7 0.7 bitcast_add_fusion
  20.4 0.1 broadcast_in_dim.11
  20.5 0.1 broadcast_in_dim_reshape.7.row_ref
  20.6 0.1 broadcast_in_dim_reshape.8.column_ref
  20.7 0.0 copy-done.1
  20.7 1.4 conv1_columns.1
  22.1 0.0 collective-permute-done.side_ref
  22.1 0.0 all-to-all-done.pay_ref
  22.1 0.0 collective-permute-done.2.both_ref
  22.1 0.0 copy-done
  22.1 0.0 copy-start.2
  22.1 5.0 %stem_forward.1 = (bf16[4,128,640]{2,1,0:T(8,128)(2,1)S(1)}, f32[2,512,384]{2,1,0:T(8,128)S(1)}, bf16[1664,512]{1,0:T(8,128)(2,1)S(1)}, bf16[128,640]{1,0:T(8,128)(2,1)}, bf16[256,128]{1,0:T(8,128)(2,1)S(1)}) custom-call(bf16[4,26,16,128]{3,2,1,0:T(8,128)(2,1)S(1)} %all-to-all-done.pay_ref, bf16[384,384]{1,0:T(8,128)(2,1)S(1)} %get-tuple-element.24.w1_ref, ...), custom_call_target="tpu_custom_call" | custom-call | tf_op jit(solution)/shard_map/stem_forward/pallas_call | solution.py:367
  27.1 13.1 %all_to_all.35.part_ref = bf16[4,128,640]{2,1,0:T(8,128)(2,1)S(1)} all-to-all(bf16[4,128,640]{2,1,0:T(8,128)(2,1)S(1)} %get-tuple-element.27), channel_id=1, replica_groups=mesh['xh'=2,'y'=4,'c'=2,'zh'=4,'zl'=4,'xl'=2] {'y'}, dimensions={0} | all-to-all | bytes 1310720 | tf_op jit(solution)/shard_map/all_to_all | solution.py:303
  40.2 0.0 copy-done.2
  40.2 1.7 %stem_middle.1 = (bf16[4,128,640]{2,1,0:T(8,128)(2,1)S(1)}, bf16[8,80,128]{2,1,0:T(8,128)(2,1)S(1)}, bf16[8,80,128]{2,1,0:T(8,128)(2,1)S(1)}) custom-call(s32[4]{0:T(128)S(1)} %pad_add_fusion.where_ref, bf16[4,128,640]{2,1,0:T(8,128)(2,1)S(1)} %all_to_all.35.part_ref, f32[640]{0:T(1024)S(1)} %copy-done.2, bf16[128,640]{1,0:T(8,128)(2,1)} %get-tuple-element.28.live_grad_ref, ...), custom_call_target="tpu_custom_call" | custom-call | tf_op jit(solution)/shard_map/stem_middle/pallas_call | solution.py:392
  41.9 11.1 %all_to_all.36.grad_ref = bf16[4,128,640]{2,1,0:T(8,128)(2,1)S(1)} all-to-all(bf16[4,128,640]{2,1,0:T(8,128)(2,1)S(1)} %get-tuple-element.31), channel_id=1, replica_groups=mesh['xh'=2,'y'=4,'c'=2,'zh'=4,'zl'=4,'xl'=2] {'y'}, dimensions={0} | all-to-all | bytes 1310720 | tf_op jit(solution)/shard_map/all_to_all | solution.py:303
  53.0 3.4 %stem_backward.1 = (f32[2,2,896,128]{3,2,1,0:T(8,128)S(1)}, bf16[2,2,896,128]{3,2,1,0:T(8,128)(2,1)S(1)}) custom-call(s32[4]{0:T(128)S(1)} %pad_add_fusion.where_ref, bf16[4,128,640]{2,1,0:T(8,128)(2,1)S(1)} %all_to_all.36.grad_ref, bf16[80,1920]{1,0:T(8,128)(2,1)S(1)} %copy-done, bf16[80,1920]{1,0:T(8,128)(2,1)S(1)} %collective-permute-done.side_ref, ...), custom_call_target="tpu_custom_call" | custom-call | tf_op jit(solution)/shard_map/stem_backward/pallas_call | solution.py:403
  56.5 5.0 %collective-permute-start.3 = (bf16[2,2,896,128]{3,2,1,0:T(8,128)(2,1)S(1)}, bf16[2,2,896,128]{3,2,1,0:T(8,128)(2,1)S(1)}, u32[]{:S(2)}, u32[]{:S(2)}) collective-permute-start(bf16[2,2,896,128]{3,2,1,0:T(8,128)(2,1)S(1)} %get-tuple-element.35), channel_id=1, source_target_pairs={{0,32},{32,0},{1,33},{33,1},{2,34},{34,2},{3,35},{35,3},{4,36},{36... | collective-permute-start | bytes 2752520 | tf_op jit(solution)/shard_map/ppermute | solution.py:418
  61.5 2.1 %collective-permute-done.3 = bf16[2,2,896,128]{3,2,1,0:T(8,128)(2,1)S(1)} collective-permute-done((bf16[2,2,896,128]{3,2,1,0:T(8,128)(2,1)S(1)}, bf16[2,2,896,128]{3,2,1,0:T(8,128)(2,1)S(1)}, u32[]{:S(2)}, u32[]{:S(2)}) %collective-permute-start.3) | collective-permute-done | bytes 917536 | tf_op jit(solution)/shard_map/ppermute | solution.py:418
  63.6 0.2 add_convert_fusion
  63.8 16.9 %all_to_all.37.got_ref = bf16[4,896,128]{2,1,0:T(8,128)(2,1)S(1)} all-to-all(bf16[4,896,128]{2,1,0:T(8,128)(2,1)S(1)} %bitcast.12), channel_id=1, replica_groups=mesh['xh'=2,'y'=4,'c'=2,'zh'=4,'zl'=4,'xl'=2] {'xh','xl'}, dimensions={0} | all-to-all | bytes 1835008 | tf_op jit(solution)/shard_map/all_to_all | solution.py:303
  80.6 0.1 gradient_sum.2
  80.7 9.1 %all_to_all.38.got_ref = bf16[4,224,128]{2,1,0:T(8,128)(2,1)S(1)} all-to-all(bf16[4,224,128]{2,1,0:T(8,128)(2,1)S(1)} %bitcast.11), channel_id=1, replica_groups=mesh['xh'=2,'y'=4,'c'=2,'zh'=4,'zl'=4,'xl'=2] {'zl'}, dimensions={0} | all-to-all | bytes 458752 | tf_op jit(solution)/shard_map/all_to_all | solution.py:303
  89.9 8.9 %collective-permute-start.4 = (bf16[224,128]{1,0:T(8,128)(2,1)S(1)}, bf16[224,128]{1,0:T(8,128)(2,1)S(1)}, u32[]{:S(2)}, u32[]{:S(2)}) collective-permute-start(bf16[224,128]{1,0:T(8,128)(2,1)S(1)} %gradient_sum.3.own_ref), channel_id=1, source_target_pairs={{0,8},{8,0},{16,24},{24,16},{1,9},{9,1},{17,25},{25,17},{2,10},{10... | collective-permute-start | bytes 172040 | tf_op jit(solution)/shard_map/ppermute | solution.py:443
  98.8 2.8 %collective-permute-done.4.other_ref = bf16[224,128]{1,0:T(8,128)(2,1)S(1)} collective-permute-done((bf16[224,128]{1,0:T(8,128)(2,1)S(1)}, bf16[224,128]{1,0:T(8,128)(2,1)S(1)}, u32[]{:S(2)}, u32[]{:S(2)}) %collective-permute-start.4) | collective-permute-done | bytes 57376 | tf_op jit(solution)/shard_map/ppermute | solution.py:443
  101.6 7.2 %collective-permute-start.5 = (bf16[224,128]{1,0:T(8,128)(2,1)S(1)}, bf16[224,128]{1,0:T(8,128)(2,1)S(1)}, u32[]{:S(2)}, u32[]{:S(2)}) collective-permute-start(bf16[224,128]{1,0:T(8,128)(2,1)S(1)} %gradient_pair.2.own_ref), channel_id=1, source_target_pairs={{0,24},{8,16},{16,8},{24,0},{1,25},{9,17},{17,9},{25,1},{2,26},{10... | collective-permute-start | bytes 172040 | tf_op jit(solution)/shard_map/ppermute | solution.py:443
  108.8 2.3 %collective-permute-done.5.other_ref = bf16[224,128]{1,0:T(8,128)(2,1)S(1)} collective-permute-done((bf16[224,128]{1,0:T(8,128)(2,1)S(1)}, bf16[224,128]{1,0:T(8,128)(2,1)S(1)}, u32[]{:S(2)}, u32[]{:S(2)}) %collective-permute-start.5) | collective-permute-done | bytes 57376 | tf_op jit(solution)/shard_map/ppermute | solution.py:443
  111.1 10.3 %all_to_all.39 = bf16[4,224,128]{2,1,0:T(8,128)(2,1)S(1)} all-to-all(bf16[4,224,128]{2,1,0:T(8,128)(2,1)S(1)} %gradient_pair.3), channel_id=1, replica_groups=mesh['xh'=2,'y'=4,'c'=2,'zh'=4,'zl'=4,'xl'=2] {'zl'}, dimensions={0} | all-to-all | bytes 458752 | tf_op jit(solution)/shard_map/all_to_all | solution.py:303
  121.4 0.1 broadcast_in_dim.12
  121.5 1.0 pad_maximum_fusion
  122.5 3.6 %all-to-all-start.6 = ((bf16[8,416,128]{2,1,0:T(8,128)(2,1)}), bf16[8,416,128]{2,1,0:T(8,128)(2,1)S(1)}, u32[]{:S(2)}, u32[]{:S(2)}) async-start(bf16[8,416,128]{2,1,0:T(8,128)(2,1)} %pad_maximum_fusion), calls=%async_computation.6 | async-start | bytes 1703936 | tf_op jit(solution)/shard_map/all_to_all | solution.py:303
  126.0 2.2 %collective-permute-start.6 = (bf16[640,128]{1,0:T(8,128)(2,1)S(1)}, bf16[640,128]{1,0:T(8,128)(2,1)S(1)}, u32[]{:S(2)}, u32[]{:S(2)}) collective-permute-start(bf16[640,128]{1,0:T(8,128)(2,1)S(1)} %slice.20.own_ref), channel_id=1, source_target_pairs={{0,1},{1,0},{2,3},{3,2},{4,5},{5,4},{6,7},{7,6},{8,9},{9,8},{10,11... | collective-permute-start | bytes 491528 | tf_op jit(solution)/shard_map/ppermute | solution.py:448
  128.2 7.0 %collective-permute-done.6.other_ref = bf16[640,128]{1,0:T(8,128)(2,1)S(1)} collective-permute-done((bf16[640,128]{1,0:T(8,128)(2,1)S(1)}, bf16[640,128]{1,0:T(8,128)(2,1)S(1)}, u32[]{:S(2)}, u32[]{:S(2)}) %collective-permute-start.6) | collective-permute-done | bytes 163872 | tf_op jit(solution)/shard_map/ppermute | solution.py:448
  135.2 0.8 all-to-all-done.6.got_ref
  136.0 8.8 %collective-permute-start.7 = (bf16[8,416,128]{2,1,0:T(8,128)(2,1)S(1)}, bf16[8,416,128]{2,1,0:T(8,128)(2,1)S(1)}, u32[]{:S(2)}, u32[]{:S(2)}) collective-permute-start(bf16[8,416,128]{2,1,0:T(8,128)(2,1)S(1)} %all-to-all-done.6.got_ref), channel_id=1, source_target_pairs={{0,32},{32,0},{1,33},{33,1},{2,34},{34,2},{3,35},{35,3},{4,36},{36... | collective-permute-start | bytes 2555912 | tf_op jit(solution)/shard_map/ppermute | solution.py:452
  144.8 1.4 conv2_unpack.1
  146.3 0.6 collective-permute-done.7.cross_ref
  146.8 2.8 %gradient_unpack.1 = (f32[384,1280]{1,0:T(8,128)}, f32[1280]{0:T(1024)}, f32[640]{0:T(1024)}, bf16[256,640]{1,0:T(8,128)(2,1)}) custom-call(s32[4]{0:T(128)S(1)} %pad_add_fusion.where_ref, bf16[8,416,128]{2,1,0:T(8,128)(2,1)S(1)} %all-to-all-done.6.got_ref, bf16[8,416,128]{2,1,0:T(8,128)(2,1)S(1)} %collective-permute-done.7.cross_ref), custom_call_target="tpu_custom_call" | custom-call | tf_op jit(solution)/shard_map/gradient_unpack/pallas_call | solution.py:461
  (7 shorter events, 0.1 us)
Async XLA Ops:
  0.6 21.5 %copy-start = (bf16[80,1920]{1,0:T(8,128)(2,1)S(1)}, bf16[80,1920]{1,0:T(8,128)(2,1)}, u32[]{:S(2)}) copy-start(bf16[80,1920]{1,0:T(8,128)(2,1)} %own_ref.3) | copy-start | bytes 921604
  0.6 20.0 %copy-start.1 = (bf16[384,1280]{1,0:T(8,128)(2,1)S(1)}, bf16[384,1280]{1,0:T(8,128)(2,1)}, u32[]{:S(2)}) copy-start(bf16[384,1280]{1,0:T(8,128)(2,1)} %weight_ref.1) | copy-start | bytes 2949124
  0.7 16.1 %collective-permute-start.1 = (bf16[80,1920]{1,0:T(8,128)(2,1)}, bf16[80,1920]{1,0:T(8,128)(2,1)S(1)}, u32[]{:S(2)}, u32[]{:S(2)}) collective-permute-start(bf16[80,1920]{1,0:T(8,128)(2,1)} %own_ref.3), channel_id=1, source_target_pairs={{0,257},{257,0},{1,256},{256,1},{2,259},{259,2},{3,258},{258,3},{4... | collective-permute-start | bytes 921608 | tf_op jit(solution)/shard_map/ppermute | solution.py:341
  7.7 14.4 %all-to-all-start = ((bf16[4,26,16,128]{3,2,1,0:T(8,128)(2,1)}), bf16[4,26,16,128]{3,2,1,0:T(8,128)(2,1)S(1)}, u32[]{:S(2)}, u32[]{:S(2)}) async-start(bf16[4,26,16,128]{3,2,1,0:T(8,128)(2,1)} %mel_payload.1), calls=%async_computation | async-start | bytes 851968 | tf_op jit(solution)/shard_map/all_to_all | solution.py:303
  11.9 10.1 %collective-permute-start = (bf16[80,1920]{1,0:T(8,128)(2,1)}, bf16[80,1920]{1,0:T(8,128)(2,1)S(1)}, u32[]{:S(2)}, u32[]{:S(2)}) collective-permute-start(bf16[80,1920]{1,0:T(8,128)(2,1)} %own_ref.3), channel_id=1, source_target_pairs={{0,32},{32,0},{1,33},{33,1},{2,34},{34,2},{3,35},{35,3},{4,36},{36... | collective-permute-start | bytes 921608 | tf_op jit(solution)/shard_map/ppermute | solution.py:356
  16.7 5.3 %collective-permute-start.2 = (bf16[80,1920]{1,0:T(8,128)(2,1)S(1)}, bf16[80,1920]{1,0:T(8,128)(2,1)S(1)}, u32[]{:S(2)}, u32[]{:S(2)}) collective-permute-start(bf16[80,1920]{1,0:T(8,128)(2,1)S(1)} %collective-permute-done.1.far_ref), channel_id=1, source_target_pairs={{0,32},{32,0},{1,33},{33,1},{2,34},{34,2},{3,35},{35,3},{4,36},{36... | collective-permute-start | bytes 921608 | tf_op jit(solution)/shard_map/ppermute | solution.py:358
  22.1 18.1 %copy-start.2 = (f32[640]{0:T(1024)S(1)}, f32[640]{0:T(1024)}, u32[]{:S(2)}) copy-start(f32[640]{0:T(1024)} %b2_ref.1) | copy-start | bytes 7684
  56.5 7.1 %collective-permute-start.3 = (bf16[2,2,896,128]{3,2,1,0:T(8,128)(2,1)S(1)}, bf16[2,2,896,128]{3,2,1,0:T(8,128)(2,1)S(1)}, u32[]{:S(2)}, u32[]{:S(2)}) collective-permute-start(bf16[2,2,896,128]{3,2,1,0:T(8,128)(2,1)S(1)} %get-tuple-element.35), channel_id=1, source_target_pairs={{0,32},{32,0},{1,33},{33,1},{2,34},{34,2},{3,35},{35,3},{4,36},{36... | collective-permute-start | bytes 2752520 | tf_op jit(solution)/shard_map/ppermute | solution.py:418
  89.9 11.7 %collective-permute-start.4 = (bf16[224,128]{1,0:T(8,128)(2,1)S(1)}, bf16[224,128]{1,0:T(8,128)(2,1)S(1)}, u32[]{:S(2)}, u32[]{:S(2)}) collective-permute-start(bf16[224,128]{1,0:T(8,128)(2,1)S(1)} %gradient_sum.3.own_ref), channel_id=1, source_target_pairs={{0,8},{8,0},{16,24},{24,16},{1,9},{9,1},{17,25},{25,17},{2,10},{10... | collective-permute-start | bytes 172040 | tf_op jit(solution)/shard_map/ppermute | solution.py:443
  101.6 9.5 %collective-permute-start.5 = (bf16[224,128]{1,0:T(8,128)(2,1)S(1)}, bf16[224,128]{1,0:T(8,128)(2,1)S(1)}, u32[]{:S(2)}, u32[]{:S(2)}) collective-permute-start(bf16[224,128]{1,0:T(8,128)(2,1)S(1)} %gradient_pair.2.own_ref), channel_id=1, source_target_pairs={{0,24},{8,16},{16,8},{24,0},{1,25},{9,17},{17,9},{25,1},{2,26},{10... | collective-permute-start | bytes 172040 | tf_op jit(solution)/shard_map/ppermute | solution.py:443
  122.5 13.5 %all-to-all-start.6 = ((bf16[8,416,128]{2,1,0:T(8,128)(2,1)}), bf16[8,416,128]{2,1,0:T(8,128)(2,1)S(1)}, u32[]{:S(2)}, u32[]{:S(2)}) async-start(bf16[8,416,128]{2,1,0:T(8,128)(2,1)} %pad_maximum_fusion), calls=%async_computation.6 | async-start | bytes 1703936 | tf_op jit(solution)/shard_map/all_to_all | solution.py:303
  126.0 9.1 %collective-permute-start.6 = (bf16[640,128]{1,0:T(8,128)(2,1)S(1)}, bf16[640,128]{1,0:T(8,128)(2,1)S(1)}, u32[]{:S(2)}, u32[]{:S(2)}) collective-permute-start(bf16[640,128]{1,0:T(8,128)(2,1)S(1)} %slice.20.own_ref), channel_id=1, source_target_pairs={{0,1},{1,0},{2,3},{3,2},{4,5},{5,4},{6,7},{7,6},{8,9},{9,8},{10,11... | collective-permute-start | bytes 491528 | tf_op jit(solution)/shard_map/ppermute | solution.py:448
  136.0 10.8 %collective-permute-start.7 = (bf16[8,416,128]{2,1,0:T(8,128)(2,1)S(1)}, bf16[8,416,128]{2,1,0:T(8,128)(2,1)S(1)}, u32[]{:S(2)}, u32[]{:S(2)}) collective-permute-start(bf16[8,416,128]{2,1,0:T(8,128)(2,1)S(1)} %all-to-all-done.6.got_ref), channel_id=1, source_target_pairs={{0,32},{32,0},{1,33},{33,1},{2,34},{34,2},{3,35},{35,3},{4,36},{36... | collective-permute-start | bytes 2555912 | tf_op jit(solution)/shard_map/ppermute | solution.py:452

commit v17 on v15

--- a/solution.py
+++ b/solution.py
@@ -205,19 +205,20 @@
 
 
 def backward_kernel(
-    where_ref, grad_ref, own_ref, side_ref, far_ref, both_ref, turned_ref, slope_ref, keep_ref, send_ref,
+    where_ref, grad_ref, own_ref, side_ref, far_ref, both_ref, turned_ref, slope_ref, out,
     w2_ref, conv_sum,
 ):
     stack_weights((own_ref, side_ref, far_ref, both_ref), w2_ref)
-    mine = where_ref[0]
+    mine, core = where_ref[0], where_ref[2]
     grad = grad_ref[...].reshape(HOLDERS * STEPS, D2)
     places = []
     for block in range(BLOCKS):
-        places.append((keep_ref if block % 2 == 0 else send_ref, mine if block < 2 else 1 - mine, block * ROWS))
+        to_core = core if block % 2 == 0 else 1 - core
+        places.append((2 * to_core + (mine if block < 2 else 1 - mine), block * ROWS))
 
     for tap in range(3):
         conv_sum[...] = dot(turned_ref[tap * WIDE : (tap + 1) * WIDE, :], grad)
-        for out, target, first in places:
+        for target, first in places:
             for column in range(D2 // LANES):
                 tile = tap * (D2 // LANES) + column
                 piece = conv_sum[first : first + ROWS, column * LANES : (column + 1) * LANES]
@@ -231,7 +232,7 @@
     conv_sum[:, : 3 * LANES] = dot_tn(even, cols[:, : 3 * LANES]) + dot_tn(odd, cols[:, LANES:])
     bias1 = jnp.sum(even.astype(F32) + odd.astype(F32), axis=0, keepdims=True)
     bias2 = jnp.sum(grad.astype(F32), axis=0, keepdims=True)
-    for out, target, first in places:
+    for target, first in places:
         out[target, 1, 7 * ROWS : 8 * ROWS, :] = jnp.zeros((ROWS, LANES), out.dtype)
         biases = [jnp.concatenate([bias1[:, first : first + ROWS], jnp.zeros((1, LANES - ROWS), F32)], axis=1)]
         for tile in range(D2 // LANES):
@@ -413,14 +414,14 @@
     )(where, got_parts, conv2_bias[None], from_hbm(live_grad), wanted)
     got_grad = exchange(rep, "y")
 
-    keep, send = pl.pallas_call(
+    pack = pl.pallas_call(
         backward_kernel,
         in_specs=[
             pl.BlockSpec(memory_space=pltpu.SMEM),
             *[vmem()] * (3 + BLOCKS),
         ],
-        out_specs=[vmem()] * 2,
-        out_shape=[shape(2, 2, PACK, LANES, dtype=F32), shape(2, 2, PACK, LANES)],
+        out_specs=vmem(),
+        out_shape=shape(4, 2, PACK, LANES),
         scratch_shapes=[
             pltpu.VMEM((WIDE, 3 * D2), BF16),
             pltpu.VMEM((WIDE, D2), F32),
@@ -428,9 +429,6 @@
         compiler_params=params(32),
         name="stem_backward",
     )(where, got_grad, *weights, turned, slopes)
-    got = lax.ppermute(send, "c", cores)
-    quarters = exchange((keep + got.astype(F32)).astype(BF16).reshape(4, PACK, LANES), ("xh", "xl"))
-
     def summed(values, *dims):
         return pl.pallas_call(
             sum_kernel,
@@ -441,7 +439,8 @@
             name="gradient_sum",
         )(values)
 
-    half = summed(quarters, PACK, LANES)
+    pack = summed(exchange(pack.reshape(2, 4 * PACK, LANES), "c"), 4 * PACK, LANES)
+    half = summed(exchange(pack.reshape(4, PACK, LANES), ("xh", "xl")), PACK, LANES)
     quarter = PACK // 4
     near = summed(exchange(half.reshape(4, quarter, LANES), "zl"), quarter, LANES)
 

time: 148 us -> 149 us (level)
  blocking collectives: 47.3 us -> 55.3 us
  starting transfers between devices: 56.4 us -> 51.4 us
  waiting for transfers between devices: 19.2 us -> 17.1 us
    all_to_all x4 -> x5, blocking collectives: 47.3 us -> 55.3 us  [exchange(): return lax.all_to_all(values, axes, split_axis=0, concat_axis=0, tiled=True)]
    ppermute x1 -> x0, starting transfers between devices: 5.07 us -> none  [local(): got = lax.ppermute(send, 'c', cores)]
    ppermute x1 -> x0, waiting for transfers between devices: 2.08 us -> none  [local(): got = lax.ppermute(send, 'c', cores)]
  transfers between devices with their start and end apart: 11 -> 10, of which waited for: 7 -> 6; matrix products, arithmetic and copies ran while one was open for 0% -> 0% of each run, Pallas kernels for 6% -> 6%
where the time goes in v17:
time: 149 us; the launch traced here: 148 us
  blocking collectives  55.3 us (37%)
  starting transfers between devices  51.4 us (34%)
  Pallas kernels  20 us (13%)
  waiting for transfers between devices  17.1 us (11%)
  local copies, waits for them, and re-layouts  2.49 us (2%)
    all_to_all x5, blocking collectives, exchange(): return lax.all_to_all(values, axes, split_axis=0, concat_axis=0, tiled=True)  55.3 us
    ppermute x2, starting transfers between devices, with_group(): lax.ppermute(values, 'zh', [(i, i ^ flip) for i in range(4)])  16 us
    all_to_all x3, starting transfers between devices, exchange(): return lax.all_to_all(values, axes, split_axis=0, concat_axis=0, tiled=True)  11.2 us
    ppermute x1, starting transfers between devices, local(): got_cross = lax.ppermute(got, 'c', cores)  8.81 us
    ppermute x1, waiting for transfers between devices, local(): other = lax.ppermute(own, 'xl', [(0, 1), (1, 0)])  6.95 us
    ppermute x1, starting transfers between devices, local(): lax.ppermute(conv2_weight, ('xh', 'xl'), [(0, 3), (3, 0), (1, 2), (2, 1)])  5.35 us
    ppermute x2, waiting for transfers between devices, with_group(): lax.ppermute(values, 'zh', [(i, i ^ flip) for i in range(4)])  5.06 us
    ppermute x1, starting transfers between devices, local(): lax.ppermute(own_weight, 'c', cores)  4.78 us
  transfers between devices with their start and end apart: 10, of which 6 were waited for; matrix products, arithmetic and copies ran while one was open for 0% of the time, Pallas kernels for 6%

profile of v17, /device:TPU:1, one launch (start us, length us, event | category | flops | bytes accessed | tf_op | source)
XLA Modules:
  0.0 148.2 jit_solution(8569960210073512877)
XLA Ops:
  0.6 0.0 copy-start.2
  0.7 5.3 %collective-permute-start.1 = (bf16[80,1920]{1,0:T(8,128)(2,1)}, bf16[80,1920]{1,0:T(8,128)(2,1)S(1)}, u32[]{:S(2)}, u32[]{:S(2)}) collective-permute-start(bf16[80,1920]{1,0:T(8,128)(2,1)} %own_ref.3), channel_id=1, source_target_pairs={{0,257},{257,0},{1,256},{256,1},{2,259},{259,2},{3,258},{258,3},{4... | collective-permute-start | bytes 921608 | tf_op jit(solution)/shard_map/ppermute | solution.py:348
  6.0 1.7 %mel_payload.1 = bf16[4,26,16,128]{3,2,1,0:T(8,128)(2,1)} custom-call(s32[16]{0:T(128)} %length_ref.1, bf16[16,16,128]{2,1,0:T(8,128)(2,1)} %mel_ref.1), custom_call_target="tpu_custom_call" | custom-call | tf_op jit(solution)/shard_map/mel_payload/pallas_call | solution.py:338
  7.7 4.2 %all-to-all-start = ((bf16[4,26,16,128]{3,2,1,0:T(8,128)(2,1)}), bf16[4,26,16,128]{3,2,1,0:T(8,128)(2,1)S(1)}, u32[]{:S(2)}, u32[]{:S(2)}) async-start(bf16[4,26,16,128]{3,2,1,0:T(8,128)(2,1)} %mel_payload.1), calls=%async_computation | async-start | bytes 851968 | tf_op jit(solution)/shard_map/all_to_all | solution.py:310
  11.9 0.1 pad_add_fusion.where_ref
  11.9 4.8 %collective-permute-start = (bf16[80,1920]{1,0:T(8,128)(2,1)}, bf16[80,1920]{1,0:T(8,128)(2,1)S(1)}, u32[]{:S(2)}, u32[]{:S(2)}) collective-permute-start(bf16[80,1920]{1,0:T(8,128)(2,1)} %own_ref.3), channel_id=1, source_target_pairs={{0,32},{32,0},{1,33},{33,1},{2,34},{34,2},{3,35},{35,3},{4,36},{36... | collective-permute-start | bytes 921608 | tf_op jit(solution)/shard_map/ppermute | solution.py:363
  16.7 0.0 collective-permute-done.1.far_ref
  16.7 3.0 %collective-permute-start.2 = (bf16[80,1920]{1,0:T(8,128)(2,1)S(1)}, bf16[80,1920]{1,0:T(8,128)(2,1)S(1)}, u32[]{:S(2)}, u32[]{:S(2)}) collective-permute-start(bf16[80,1920]{1,0:T(8,128)(2,1)S(1)} %collective-permute-done.1.far_ref), channel_id=1, source_target_pairs={{0,32},{32,0},{1,33},{33,1},{2,34},{34,2},{3,35},{35,3},{4,36},{36... | collective-permute-start | bytes 921608 | tf_op jit(solution)/shard_map/ppermute | solution.py:365
  19.8 1.4 conv1_columns.1
  21.1 0.0 copy-start.7
  21.2 0.0 copy-start.3
  21.2 0.0 copy-start.5
  21.2 0.0 copy-start.11
  21.2 0.0 copy-start.12
  21.2 0.0 copy-start.10
  21.2 3.4 %stem_forward.1 = bf16[4,128,640]{2,1,0:T(8,128)(2,1)} custom-call(bf16[4,26,16,128]{3,2,1,0:T(8,128)(2,1)S(1)} %all-to-all-done.pay_ref, bf16[384,384]{1,0:T(8,128)(2,1)S(1)} %get-tuple-element.24.w1_ref, f32[1,384]{1,0:T(1,128)S(1)} %get-tuple-element.25.b1_ref, bf16[80,1920]{1,0:T(8,128)(2,1)S(1)} %copy-done.2, ...), custom_call_target="tpu_custom_call" | custom-call | tf_op jit(solution)/shard_map/stem_forward/pallas_call | solution.py:373
  24.6 3.5 %all-to-all-start.1 = ((bf16[4,128,640]{2,1,0:T(8,128)(2,1)}), bf16[4,128,640]{2,1,0:T(8,128)(2,1)S(1)}, u32[]{:S(2)}, u32[]{:S(2)}) async-start(bf16[4,128,640]{2,1,0:T(8,128)(2,1)} %stem_forward.1), calls=%async_computation.1 | async-start | bytes 1310720 | tf_op jit(solution)/shard_map/all_to_all | solution.py:310
  28.1 0.1 broadcast_in_dim.14
  28.2 0.1 broadcast_in_dim_reshape.7.row_ref
  28.3 0.1 broadcast_in_dim_reshape.8.column_ref
  28.4 0.0 copy-start.8
  28.4 1.0 copy-done.8
  29.4 3.7 %stem_slopes.1 = (f32[2,512,384]{2,1,0:T(8,128)S(1)}, bf16[1664,512]{1,0:T(8,128)(2,1)S(1)}, bf16[128,640]{1,0:T(8,128)(2,1)}, bf16[256,128]{1,0:T(8,128)(2,1)S(1)}) custom-call(bf16[4,26,16,128]{3,2,1,0:T(8,128)(2,1)S(1)} %all-to-all-done.pay_ref, bf16[384,384]{1,0:T(8,128)(2,1)S(1)} %copy-done.8, f32[1,384]{1,0:T(1,128)S(1)} %get-tuple-element.25.b1_ref, ...), custom_call_target="tpu_custom_call" | custom-call | tf_op jit(solution)/shard_map/stem_slopes/pallas_call | solution.py:390
  33.1 1.1 copy-done
  34.2 3.7 %all-to-all-done.1.part_ref = bf16[4,128,640]{2,1,0:T(8,128)(2,1)S(1)} async-done(((bf16[4,128,640]{2,1,0:T(8,128)(2,1)}), bf16[4,128,640]{2,1,0:T(8,128)(2,1)S(1)}, u32[]{:S(2)}, u32[]{:S(2)}) %all-to-all-start.1) | async-done | bytes 655392 | tf_op jit(solution)/shard_map/all_to_all | solution.py:310
  38.0 1.8 %stem_middle.1 = (bf16[4,128,640]{2,1,0:T(8,128)(2,1)S(1)}, bf16[8,80,128]{2,1,0:T(8,128)(2,1)S(1)}, bf16[8,80,128]{2,1,0:T(8,128)(2,1)S(1)}) custom-call(s32[4]{0:T(128)S(1)} %pad_add_fusion.where_ref, bf16[4,128,640]{2,1,0:T(8,128)(2,1)S(1)} %all-to-all-done.1.part_ref, f32[1,640]{1,0:T(1,128)S(1)} %broadcast_in_dim.15.b2_ref, ...), custom_call_target="tpu_custom_call" | custom-call | tf_op jit(solution)/shard_map/stem_middle/pallas_call | solution.py:406
  39.8 11.1 %all_to_all.40.grad_ref = bf16[4,128,640]{2,1,0:T(8,128)(2,1)S(1)} all-to-all(bf16[4,128,640]{2,1,0:T(8,128)(2,1)S(1)} %get-tuple-element.33), channel_id=1, replica_groups=mesh['xh'=2,'y'=4,'c'=2,'zh'=4,'zl'=4,'xl'=2] {'y'}, dimensions={0} | all-to-all | bytes 1310720 | tf_op jit(solution)/shard_map/all_to_all | solution.py:310
  50.9 3.4 %stem_backward.1 = bf16[4,2,896,128]{3,2,1,0:T(8,128)(2,1)S(1)} custom-call(s32[4]{0:T(128)S(1)} %pad_add_fusion.where_ref, bf16[4,128,640]{2,1,0:T(8,128)(2,1)S(1)} %all_to_all.40.grad_ref, bf16[80,1920]{1,0:T(8,128)(2,1)S(1)} %copy-done.2, bf16[80,1920]{1,0:T(8,128)(2,1)S(1)} %copy-done.4, bf16[80,1920]{1,0:T(8,128)(2,1)S(1)} %collective-permute-done.1.far_ref, ...), custom_call_target="tpu_custom_call" | custom-call | tf_op jit(solution)/shard_map/stem_backward/pallas_call | solution.py:417
  54.3 8.0 %all_to_all.41.got_ref = bf16[2,3584,128]{2,1,0:T(8,128)(2,1)S(1)} all-to-all(bf16[2,3584,128]{2,1,0:T(8,128)(2,1)S(1)} %bitcast.12), channel_id=1, replica_groups=mesh['xh'=2,'y'=4,'c'=2,'zh'=4,'zl'=4,'xl'=2] {'c'}, dimensions={0} | all-to-all | bytes 3670016 | tf_op jit(solution)/shard_map/all_to_all | solution.py:310
  62.3 0.2 gradient_sum.3
  62.5 16.9 %all_to_all.42.got_ref = bf16[4,896,128]{2,1,0:T(8,128)(2,1)S(1)} all-to-all(bf16[4,896,128]{2,1,0:T(8,128)(2,1)S(1)} %bitcast.13), channel_id=1, replica_groups=mesh['xh'=2,'y'=4,'c'=2,'zh'=4,'zl'=4,'xl'=2] {'xh','xl'}, dimensions={0} | all-to-all | bytes 1835008 | tf_op jit(solution)/shard_map/all_to_all | solution.py:310
  79.4 0.1 gradient_sum.4
  79.5 9.0 %all_to_all.43.got_ref = bf16[4,224,128]{2,1,0:T(8,128)(2,1)S(1)} all-to-all(bf16[4,224,128]{2,1,0:T(8,128)(2,1)S(1)} %bitcast.14), channel_id=1, replica_groups=mesh['xh'=2,'y'=4,'c'=2,'zh'=4,'zl'=4,'xl'=2] {'zl'}, dimensions={0} | all-to-all | bytes 458752 | tf_op jit(solution)/shard_map/all_to_all | solution.py:310
  88.6 8.8 %collective-permute-start.3 = (bf16[224,128]{1,0:T(8,128)(2,1)S(1)}, bf16[224,128]{1,0:T(8,128)(2,1)S(1)}, u32[]{:S(2)}, u32[]{:S(2)}) collective-permute-start(bf16[224,128]{1,0:T(8,128)(2,1)S(1)} %gradient_sum.5.own_ref), channel_id=1, source_target_pairs={{0,8},{8,0},{16,24},{24,16},{1,9},{9,1},{17,25},{25,17},{2,10},{10... | collective-permute-start | bytes 172040 | tf_op jit(solution)/shard_map/ppermute | solution.py:455
  97.4 2.8 %collective-permute-done.3.other_ref = bf16[224,128]{1,0:T(8,128)(2,1)S(1)} collective-permute-done((bf16[224,128]{1,0:T(8,128)(2,1)S(1)}, bf16[224,128]{1,0:T(8,128)(2,1)S(1)}, u32[]{:S(2)}, u32[]{:S(2)}) %collective-permute-start.3) | collective-permute-done | bytes 57376 | tf_op jit(solution)/shard_map/ppermute | solution.py:455
  100.2 7.2 %collective-permute-start.4 = (bf16[224,128]{1,0:T(8,128)(2,1)S(1)}, bf16[224,128]{1,0:T(8,128)(2,1)S(1)}, u32[]{:S(2)}, u32[]{:S(2)}) collective-permute-start(bf16[224,128]{1,0:T(8,128)(2,1)S(1)} %gradient_pair.2.own_ref), channel_id=1, source_target_pairs={{0,24},{8,16},{16,8},{24,0},{1,25},{9,17},{17,9},{25,1},{2,26},{10... | collective-permute-start | bytes 172040 | tf_op jit(solution)/shard_map/ppermute | solution.py:455
  107.4 2.3 %collective-permute-done.4.other_ref = bf16[224,128]{1,0:T(8,128)(2,1)S(1)} collective-permute-done((bf16[224,128]{1,0:T(8,128)(2,1)S(1)}, bf16[224,128]{1,0:T(8,128)(2,1)S(1)}, u32[]{:S(2)}, u32[]{:S(2)}) %collective-permute-start.4) | collective-permute-done | bytes 57376 | tf_op jit(solution)/shard_map/ppermute | solution.py:455
  109.7 10.3 %all_to_all.44 = bf16[4,224,128]{2,1,0:T(8,128)(2,1)S(1)} all-to-all(bf16[4,224,128]{2,1,0:T(8,128)(2,1)S(1)} %gradient_pair.3), channel_id=1, replica_groups=mesh['xh'=2,'y'=4,'c'=2,'zh'=4,'zl'=4,'xl'=2] {'zl'}, dimensions={0} | all-to-all | bytes 458752 | tf_op jit(solution)/shard_map/all_to_all | solution.py:310
  120.1 0.1 broadcast_in_dim.16
  120.1 1.0 pad_maximum_fusion
  121.1 3.6 %all-to-all-start.7 = ((bf16[8,416,128]{2,1,0:T(8,128)(2,1)}), bf16[8,416,128]{2,1,0:T(8,128)(2,1)S(1)}, u32[]{:S(2)}, u32[]{:S(2)}) async-start(bf16[8,416,128]{2,1,0:T(8,128)(2,1)} %pad_maximum_fusion), calls=%async_computation.7 | async-start | bytes 1703936 | tf_op jit(solution)/shard_map/all_to_all | solution.py:310
  124.7 2.2 %collective-permute-start.5 = (bf16[640,128]{1,0:T(8,128)(2,1)S(1)}, bf16[640,128]{1,0:T(8,128)(2,1)S(1)}, u32[]{:S(2)}, u32[]{:S(2)}) collective-permute-start(bf16[640,128]{1,0:T(8,128)(2,1)S(1)} %slice.20.own_ref), channel_id=1, source_target_pairs={{0,1},{1,0},{2,3},{3,2},{4,5},{5,4},{6,7},{7,6},{8,9},{9,8},{10,11... | collective-permute-start | bytes 491528 | tf_op jit(solution)/shard_map/ppermute | solution.py:460
  126.9 7.0 %collective-permute-done.5.other_ref = bf16[640,128]{1,0:T(8,128)(2,1)S(1)} collective-permute-done((bf16[640,128]{1,0:T(8,128)(2,1)S(1)}, bf16[640,128]{1,0:T(8,128)(2,1)S(1)}, u32[]{:S(2)}, u32[]{:S(2)}) %collective-permute-start.5) | collective-permute-done | bytes 163872 | tf_op jit(solution)/shard_map/ppermute | solution.py:460
  133.8 0.8 all-to-all-done.7.got_ref
  134.6 8.8 %collective-permute-start.6 = (bf16[8,416,128]{2,1,0:T(8,128)(2,1)S(1)}, bf16[8,416,128]{2,1,0:T(8,128)(2,1)S(1)}, u32[]{:S(2)}, u32[]{:S(2)}) collective-permute-start(bf16[8,416,128]{2,1,0:T(8,128)(2,1)S(1)} %all-to-all-done.7.got_ref), channel_id=1, source_target_pairs={{0,32},{32,0},{1,33},{33,1},{2,34},{34,2},{3,35},{35,3},{4,36},{36... | collective-permute-start | bytes 2555912 | tf_op jit(solution)/shard_map/ppermute | solution.py:464
  143.4 1.4 conv2_unpack.1
  144.9 0.6 collective-permute-done.6.cross_ref
  145.4 2.8 %gradient_unpack.1 = (f32[384,1280]{1,0:T(8,128)}, f32[1280]{0:T(1024)}, f32[640]{0:T(1024)}, bf16[256,640]{1,0:T(8,128)(2,1)}) custom-call(s32[4]{0:T(128)S(1)} %pad_add_fusion.where_ref, bf16[8,416,128]{2,1,0:T(8,128)(2,1)S(1)} %all-to-all-done.7.got_ref, bf16[8,416,128]{2,1,0:T(8,128)(2,1)S(1)} %collective-permute-done.6.cross_ref), custom_call_target="tpu_custom_call" | custom-call | tf_op jit(solution)/shard_map/gradient_unpack/pallas_call | solution.py:473
  (28 shorter events, 0.1 us)
Async XLA Ops:
  0.6 20.6 %copy-start.2 = (bf16[80,1920]{1,0:T(8,128)(2,1)S(1)}, bf16[80,1920]{1,0:T(8,128)(2,1)}, u32[]{:S(2)}) copy-start(bf16[80,1920]{1,0:T(8,128)(2,1)} %own_ref.3) | copy-start | bytes 921604
  0.6 19.1 %copy-start.9 = (bf16[384,1280]{1,0:T(8,128)(2,1)S(1)}, bf16[384,1280]{1,0:T(8,128)(2,1)}, u32[]{:S(2)}) copy-start(bf16[384,1280]{1,0:T(8,128)(2,1)} %weight_ref.1) | copy-start | bytes 2949124
  0.7 16.1 %collective-permute-start.1 = (bf16[80,1920]{1,0:T(8,128)(2,1)}, bf16[80,1920]{1,0:T(8,128)(2,1)S(1)}, u32[]{:S(2)}, u32[]{:S(2)}) collective-permute-start(bf16[80,1920]{1,0:T(8,128)(2,1)} %own_ref.3), channel_id=1, source_target_pairs={{0,257},{257,0},{1,256},{256,1},{2,259},{259,2},{3,258},{258,3},{4... | collective-permute-start | bytes 921608 | tf_op jit(solution)/shard_map/ppermute | solution.py:348
  7.7 13.5 %all-to-all-start = ((bf16[4,26,16,128]{3,2,1,0:T(8,128)(2,1)}), bf16[4,26,16,128]{3,2,1,0:T(8,128)(2,1)S(1)}, u32[]{:S(2)}, u32[]{:S(2)}) async-start(bf16[4,26,16,128]{3,2,1,0:T(8,128)(2,1)} %mel_payload.1), calls=%async_computation | async-start | bytes 851968 | tf_op jit(solution)/shard_map/all_to_all | solution.py:310
  11.9 9.2 %collective-permute-start = (bf16[80,1920]{1,0:T(8,128)(2,1)}, bf16[80,1920]{1,0:T(8,128)(2,1)S(1)}, u32[]{:S(2)}, u32[]{:S(2)}) collective-permute-start(bf16[80,1920]{1,0:T(8,128)(2,1)} %own_ref.3), channel_id=1, source_target_pairs={{0,32},{32,0},{1,33},{33,1},{2,34},{34,2},{3,35},{35,3},{4,36},{36... | collective-permute-start | bytes 921608 | tf_op jit(solution)/shard_map/ppermute | solution.py:363
  16.7 4.4 %collective-permute-start.2 = (bf16[80,1920]{1,0:T(8,128)(2,1)S(1)}, bf16[80,1920]{1,0:T(8,128)(2,1)S(1)}, u32[]{:S(2)}, u32[]{:S(2)}) collective-permute-start(bf16[80,1920]{1,0:T(8,128)(2,1)S(1)} %collective-permute-done.1.far_ref), channel_id=1, source_target_pairs={{0,32},{32,0},{1,33},{33,1},{2,34},{34,2},{3,35},{35,3},{4,36},{36... | collective-permute-start | bytes 921608 | tf_op jit(solution)/shard_map/ppermute | solution.py:365
  21.1 3.5 %copy-start.7 = (bf16[384,384]{1,0:T(8,128)(2,1)}, bf16[384,384]{1,0:T(8,128)(2,1)S(1)}, u32[]{:S(2)}) copy-start(bf16[384,384]{1,0:T(8,128)(2,1)S(1)} %get-tuple-element.24.w1_ref) | copy-start | bytes 884740
  21.2 3.5 %copy-start.3 = (bf16[80,1920]{1,0:T(8,128)(2,1)}, bf16[80,1920]{1,0:T(8,128)(2,1)S(1)}, u32[]{:S(2)}) copy-start(bf16[80,1920]{1,0:T(8,128)(2,1)S(1)} %collective-permute-done.side_ref) | copy-start | bytes 921604
  21.2 3.4 %copy-start.5 = (bf16[80,1920]{1,0:T(8,128)(2,1)}, bf16[80,1920]{1,0:T(8,128)(2,1)S(1)}, u32[]{:S(2)}) copy-start(bf16[80,1920]{1,0:T(8,128)(2,1)S(1)} %collective-permute-done.2.both_ref) | copy-start | bytes 921604
  21.2 6.9 %copy-start.11 = (s32[16]{0:T(128)S(1)}, s32[16]{0:T(128)}, u32[]{:S(2)}) copy-start(s32[16]{0:T(128)} %length_ref.1) | copy-start | bytes 196
  21.2 6.9 %copy-start.12 = (s32[16,1]{0,1:T(1,128)S(1)}, s32[16,1]{0,1:T(1,128)}, u32[]{:S(2)}) copy-start(s32[16,1]{0,1:T(1,128)} %param.10) | copy-start | bytes 196
  21.2 7.2 %copy-start.10 = (f32[640]{0:T(1024)S(1)}, f32[640]{0:T(1024)}, u32[]{:S(2)}) copy-start(f32[640]{0:T(1024)} %param.14) | copy-start | bytes 7684
  24.6 13.4 %all-to-all-start.1 = ((bf16[4,128,640]{2,1,0:T(8,128)(2,1)}), bf16[4,128,640]{2,1,0:T(8,128)(2,1)S(1)}, u32[]{:S(2)}, u32[]{:S(2)}) async-start(bf16[4,128,640]{2,1,0:T(8,128)(2,1)} %stem_forward.1), calls=%async_computation.1 | async-start | bytes 1310720 | tf_op jit(solution)/shard_map/all_to_all | solution.py:310
  28.4 1.0 copy-start.8
  33.1 1.1 copy-start
  34.2 16.6 %copy-start.4 = (bf16[80,1920]{1,0:T(8,128)(2,1)S(1)}, bf16[80,1920]{1,0:T(8,128)(2,1)}, u32[]{:S(2)}) copy-start(bf16[80,1920]{1,0:T(8,128)(2,1)} %copy-done.3) | copy-start | bytes 921604
  38.0 12.9 %copy-start.1 = (f32[2,512,384]{2,1,0:T(8,128)S(1)}, f32[2,512,384]{2,1,0:T(8,128)}, u32[]{:S(2)}) copy-start(f32[2,512,384]{2,1,0:T(8,128)} %copy-done) | copy-start | bytes 4718596
  38.0 12.9 %copy-start.6 = (bf16[80,1920]{1,0:T(8,128)(2,1)S(1)}, bf16[80,1920]{1,0:T(8,128)(2,1)}, u32[]{:S(2)}) copy-start(bf16[80,1920]{1,0:T(8,128)(2,1)} %copy-done.5) | copy-start | bytes 921604
  88.6 11.6 %collective-permute-start.3 = (bf16[224,128]{1,0:T(8,128)(2,1)S(1)}, bf16[224,128]{1,0:T(8,128)(2,1)S(1)}, u32[]{:S(2)}, u32[]{:S(2)}) collective-permute-start(bf16[224,128]{1,0:T(8,128)(2,1)S(1)} %gradient_sum.5.own_ref), channel_id=1, source_target_pairs={{0,8},{8,0},{16,24},{24,16},{1,9},{9,1},{17,25},{25,17},{2,10},{10... | collective-permute-start | bytes 172040 | tf_op jit(solution)/shard_map/ppermute | solution.py:455
  100.2 9.5 %collective-permute-start.4 = (bf16[224,128]{1,0:T(8,128)(2,1)S(1)}, bf16[224,128]{1,0:T(8,128)(2,1)S(1)}, u32[]{:S(2)}, u32[]{:S(2)}) collective-permute-start(bf16[224,128]{1,0:T(8,128)(2,1)S(1)} %gradient_pair.2.own_ref), channel_id=1, source_target_pairs={{0,24},{8,16},{16,8},{24,0},{1,25},{9,17},{17,9},{25,1},{2,26},{10... | collective-permute-start | bytes 172040 | tf_op jit(solution)/shard_map/ppermute | solution.py:455
  121.1 13.5 %all-to-all-start.7 = ((bf16[8,416,128]{2,1,0:T(8,128)(2,1)}), bf16[8,416,128]{2,1,0:T(8,128)(2,1)S(1)}, u32[]{:S(2)}, u32[]{:S(2)}) async-start(bf16[8,416,128]{2,1,0:T(8,128)(2,1)} %pad_maximum_fusion), calls=%async_computation.7 | async-start | bytes 1703936 | tf_op jit(solution)/shard_map/all_to_all | solution.py:310
  124.7 9.1 %collective-permute-start.5 = (bf16[640,128]{1,0:T(8,128)(2,1)S(1)}, bf16[640,128]{1,0:T(8,128)(2,1)S(1)}, u32[]{:S(2)}, u32[]{:S(2)}) collective-permute-start(bf16[640,128]{1,0:T(8,128)(2,1)S(1)} %slice.20.own_ref), channel_id=1, source_target_pairs={{0,1},{1,0},{2,3},{3,2},{4,5},{5,4},{6,7},{7,6},{8,9},{9,8},{10,11... | collective-permute-start | bytes 491528 | tf_op jit(solution)/shard_map/ppermute | solution.py:460
  134.6 10.8 %collective-permute-start.6 = (bf16[8,416,128]{2,1,0:T(8,128)(2,1)S(1)}, bf16[8,416,128]{2,1,0:T(8,128)(2,1)S(1)}, u32[]{:S(2)}, u32[]{:S(2)}) collective-permute-start(bf16[8,416,128]{2,1,0:T(8,128)(2,1)S(1)} %all-to-all-done.7.got_ref), channel_id=1, source_target_pairs={{0,32},{32,0},{1,33},{33,1},{2,34},{34,2},{3,35},{35,3},{4,36},{36... | collective-permute-start | bytes 2555912 | tf_op jit(solution)/shard_map/ppermute | solution.py:464
